TPU v7x, 32 devices: a whole 2x2x4 slice. The times are simulated.
32 devices in a mesh: seq: 8 (over y, x, core), head: 4 (over z).
Axes of the slice: x: 2, y: 2, z: 4, core: 2. Of those that a mesh axis runs over, the one named last changes fastest.
Arguments:
- queries: bfloat16 [1024, 4096], P('seq', 'head'), may hold values from -64 to 64
- keys: bfloat16 [1024, 4096], P('seq', 'head'), may hold values from -8 to 8
- values: bfloat16 [1024, 4096], P('seq', 'head'), may hold values from -8 to 8
- gate: float32 [32], P('head'), may hold values from -6 to 6
- out_weight: bfloat16 [4096, 4096], P('head'), may hold values from -0.09375 to 0.09375
- out_grad: bfloat16 [1024, 4096], P('seq', 'head'), may hold values from -6 to 6
- valid: int32 [8], P('seq'), may hold values from 32 to 128, as said below
- starts: int32 [8], P('seq'), may hold values from 0 to 1, as said below
Outputs:
- output: bfloat16 [1024, 4096], P('seq', 'head')
- query_grad: bfloat16 [1024, 4096], P('seq', 'head')
- key_grad: bfloat16 [1024, 4096], P('seq', 'head')
- value_grad: bfloat16 [1024, 4096], P('seq', 'head')
Inputs may be any that keep to these rules, and one draw needn't show every extreme that they name: `valid`: A segment with fewer than 128 live tokens is followed by a segment that starts a document, or is the last one. The first segment starts a document and the second does not.
All inputs are finite; a program needn't handle non-finite values.
Results may differ from a plain program's by a relative error of at most 0.029.
Values may be sent and summed in bfloat16 or wider, within the bound.
No kernel may reach another device: no remote copies, remote signals or barrier semaphores. Data moves between devices by JAX's collectives and lax.ppermute only.
A program may use at most 64 MiB of HBM per device.

v0:
```python
import jax
import jax.numpy as jnp
from jax import lax
from jax.sharding import PartitionSpec as P

DH = 128


precise = lax.Precision.HIGHEST


def carried_in(value, axis, join, neutral):
    count, mine = (lax.axis_size(axis), lax.axis_index(axis))
    pieces = jax.tree.map(lambda part: lax.all_gather(part, axis), value)
    total = jax.tree.map(
        lambda part, zero: jnp.full_like(part, 0) + jnp.asarray(zero, part.dtype), value, neutral
    )

    def carried_turn(position, total):
        longer = join(total, jax.tree.map(lambda part: part[position], pieces))
        return jax.tree.map(lambda new, old: jnp.where(position < mine, new, old), longer, total)

    return lax.fori_loop(0, count - 1, carried_turn, total)


def entering(shard, axis, combine, identity):
    devices, position = (lax.axis_size(axis), lax.axis_index(axis))
    everything = jax.tree.map(
        lambda part, kind: lax.all_gather(part.astype(kind), axis),
        shard,
        jax.tree.map(lambda a: jnp.bfloat16 if a.dtype == jnp.float32 else a.dtype, shard),
    )
    start = jax.tree.map(
        lambda part, zero: jnp.broadcast_to(jnp.asarray(zero, part.dtype), part.shape),
        shard,
        identity,
    )

    def entering_turn(k, before):
        at = devices - 1 - k
        reached = at > position
        new = combine(
            before, jax.tree.map(lambda part, own: part[at].astype(own.dtype), everything, shard)
        )
        return jax.tree.map(lambda a, b: jnp.where(reached, a, b), new, before)

    return lax.fori_loop(0, devices, entering_turn, start)


def feature_map(inputs):
    return jnp.where(inputs > 0, inputs + 1.0, jnp.exp(jnp.minimum(inputs, 0.0)))


def segment_state(key_vals, value_vals, live_mask):
    length = key_vals.shape[0]
    sig_keys = feature_map(key_vals.reshape(length, -1, DH)) * live_mask[:, None, None]
    val_heads = value_vals.reshape(length, -1, DH) * live_mask[:, None, None]
    memory = jnp.einsum("thd,the->hde", sig_keys, val_heads, precision=precise)
    return (memory, jnp.sum(sig_keys, axis=0))


def segment_read(query_vals, key_vals, value_vals, live_mask, memory, norm_sum, gate_weight):
    length = query_vals.shape[0]
    query_heads = query_vals.reshape(length, -1, DH)
    query_low = query_heads.astype(jnp.bfloat16)
    key_low = key_vals.reshape(length, -1, DH).astype(jnp.bfloat16)
    value_low = value_vals.reshape(length, -1, DH).astype(jnp.bfloat16)
    sig_query = feature_map(query_heads)
    numer = jnp.einsum("thd,hde->the", sig_query, memory, precision=precise)
    denom = jnp.einsum("thd,hd->th", sig_query, norm_sum, precision=precise) + 1.0
    memory_read = numer / denom[:, :, None]
    scores = jnp.einsum(
        "thd,shd->hts", query_low, key_low, preferred_element_type=jnp.float32
    ) * DH ** (-0.5)
    where_pos = jnp.arange(length)
    allowed = (where_pos[None, :] <= where_pos[:, None]) & (live_mask[None, :] > 0)
    scores = jnp.where(allowed[None], scores, -1e30)
    row_top = lax.stop_gradient(jnp.max(scores, axis=-1, keepdims=True))
    expo = jnp.exp(scores - row_top)
    probs = expo / jnp.sum(expo, axis=-1, keepdims=True)
    probs_low = probs.astype(jnp.bfloat16)
    local_read = jnp.einsum(
        "hts,she->the", probs_low, value_low, preferred_element_type=jnp.float32
    )
    mixed = (
        gate_weight[None, :, None] * memory_read + (1.0 - gate_weight)[None, :, None] * local_read
    )
    return (mixed * live_mask[:, None, None]).reshape(length, -1)


def join_forward(earlier, later):
    keep = 1.0 - later[0]
    return (
        jnp.maximum(earlier[0], later[0]),
        later[1] + keep * earlier[1],
        later[2] + keep * earlier[2],
    )


def join_reverse(earlier, later):
    keep = 1.0 - later[0]
    return (
        jnp.maximum(earlier[0], later[0]),
        later[1] + keep * earlier[1],
        later[2] + keep * earlier[2],
    )


def shards(queries, keys, values, gate, out_weight, out_grad, valid, starts):
    length = queries.shape[0]
    live_mask = (jnp.arange(length) < valid[0]).astype(jnp.float32)
    query_full = queries.astype(jnp.float32)
    key_full = keys.astype(jnp.float32)
    value_full = values.astype(jnp.float32)
    gate_weight = jax.nn.sigmoid(gate)
    start_flag = starts.astype(jnp.float32)
    opened = 1.0 - start_flag
    memory_local, norm_local = segment_state(key_full, value_full, live_mask)
    empty = (jnp.zeros((1,), jnp.float32), jnp.zeros_like(memory_local), jnp.zeros_like(norm_local))
    _, memory_prev, norm_prev = carried_in(
        (start_flag, memory_local, norm_local), "seq", join_forward, empty
    )
    memory_in = opened * memory_prev
    norm_in = opened * norm_prev

    def read_local(query_arg, key_arg, value_arg, memory_arg, norm_arg):
        return segment_read(
            query_arg, key_arg, value_arg, live_mask, memory_arg, norm_arg, gate_weight
        )

    mixed, pullback = jax.vjp(read_local, query_full, key_full, value_full, memory_in, norm_in)
    mixed_heads = mixed.astype(jnp.bfloat16)
    weight_part = out_weight
    projected = lax.psum_scatter(
        lax.dot_general(
            weight_part, mixed_heads, (((0,), (1,)), ((), ())), preferred_element_type=jnp.float32
        ),
        "head",
        scatter_dimension=0,
        tiled=True,
    ).T
    output = projected.astype(jnp.bfloat16)
    weight_part = out_weight
    mixed_grad = lax.dot_general(
        lax.all_gather(out_grad, "head", axis=1, tiled=True),
        weight_part,
        (((1,), (1,)), ((), ())),
        preferred_element_type=jnp.float32,
    )
    mixed_grad = lax.optimization_barrier(mixed_grad.astype(jnp.bfloat16)).astype(jnp.float32)
    query_part, key_part, value_part, memory_grad, norm_grad = pullback(mixed_grad)
    passed = (start_flag, opened * memory_grad, opened * norm_grad)
    _, memory_back, norm_back = entering(passed, "seq", join_reverse, empty)

    def state_local(key_arg, value_arg):
        return segment_state(key_arg, value_arg, live_mask)

    _, state_pull = jax.vjp(state_local, key_full, value_full)
    key_more, value_more = state_pull((memory_back, norm_back))
    query_grad = query_part.astype(jnp.bfloat16)
    key_grad = (key_part + key_more).astype(jnp.bfloat16)
    value_grad = (value_part + value_more).astype(jnp.bfloat16)
    return (output, query_grad, key_grad, value_grad)


def solution(mesh):
    placed = (
        P("seq", "head"),
        P("seq", "head"),
        P("seq", "head"),
        P("head"),
        P("head", None),
        P("seq", "head"),
        P("seq"),
        P("seq"),
    )
    return jax.shard_map(
        shards,
        mesh=mesh,
        in_specs=placed,
        out_specs=(P("seq", "head"), P("seq", "head"), P("seq", "head"), P("seq", "head")),
        check_vma=False,
    )
```

profile of v0, /device:TPU:0, one launch (start us, length us, event | category | flops | bytes accessed | tf_op | source)
XLA Modules:
  0.0 203.5 jit_solution(2501752228977129905)
XLA Ops:
  8.6 2.0 select_select_fusion
  13.4 2.1 %fusion.34 = f32[8,128,128]{2,1,0:T(8,128)} fusion(bf16[128,8,128]{0,2,1:T(8,128)(2,1)S(1)} %bitcast.149, f32[128]{0:T(128)S(1)} %compare_convert_fusion, pred[128,8,128]{0,2,1:T(32,128)(4,1)S(1)} %bitcast.157, f32[128,8,128]{0,2,1:T(8,128)S(1)} %bitcast.143, f32[128,8,128]{0,2,1:T(8,128)S(1)} %bitcast.140), kind=kOutput, calls=%fused_computation.71 | convolution fusion | flops 201850880 | bytes 1966592 | tf_op jit(solution)/shard_map/thd,the->hde/dot_general | solution.py:58
  20.1 16.4 %all-reduce.1 = bf16[8]{0:T(256)(128)(2,1)} all-reduce(bf16[8]{0:T(256)(128)(2,1)S(1)} %dynamic-update-slice.1), channel_id=5, replica_groups=mesh['seq'=8,'head'=4] {'seq'}, use_global_device_ids=true, to_apply=%add.1 | all-reduce | flops 8 | bytes 32
  36.5 12.7 %all-reduce = f32[8]{0:T(128)} all-reduce(f32[8]{0:T(128)S(1)} %convert_dynamic-update-slice_fusion), channel_id=3, replica_groups=mesh['seq'=8,'head'=4] {'seq'}, use_global_device_ids=true, to_apply=%add | all-reduce | flops 8 | bytes 64
  53.1 2.1 %copy.47 = f32[128,1024]{0,1:T(8,128)} copy(f32[128,1024]{1,0:T(8,128)} %get-tuple-element.401) | data formatting | bytes 1048576 | tf_op jit(solution)/shard_map/jvp()/exp | solution.py:51
  55.1 2.0 copy.46
  57.5 2.1 %copy.61 = f32[128,1024]{0,1:T(8,128)} copy(f32[128,1024]{1,0:T(8,128)} %get-tuple-element.396) | data formatting | bytes 1048576 | tf_op jit(solution)/shard_map/jvp()/select_n | solution.py:51
  61.8 9.2 %all_gather.44 = f32[8,8,128]{2,1,0:T(8,128)} all-gather(f32[1,8,128]{2,1,0:T(8,128)S(1)} %bitcast.176), channel_id=1, replica_groups=mesh['seq'=8,'head'=4] {'seq'}, dimensions={0}, use_global_device_ids=true | all-gather | bytes 36864 | tf_op jit(solution)/shard_map/all_gather | solution.py:14
  73.0 7.4 %convolution_convert_fusion.4 = bf16[128,1024]{1,0:T(8,128)(2,1)} fusion(bf16[128,4096]{1,0:T(8,128)(2,1)} %all-gather.9.cloned.1.call-done, bf16[1024,4096]{1,0:T(8,128)(2,1)} %param.16), kind=kOutput, calls=%fused_computation.46 | convolution fusion | flops 1073872896 | bytes 9699328 | tf_op jit(solution)/shard_map/dot_general | solution.py:144
  81.5 32.9 %while.34 = (s32[]{:T(128)}, f32[8,128,128]{2,1,0:T(8,128)S(1)}, f32[8,128]{1,0:T(8,128)S(1)}, s32[]{:T(128)}, f32[8,8,128,128]{3,2,1,0:T(8,128)}, /*index=5*/f3...) while((s32[]{:T(128)}, f32[8,128,128]{2,1,0:T(8,128)S(1)}, f32[8,128]{1,0:T(8,128)S(1)}, ...), condition=%wide.region_2.3_spmd.clone, body=%wide.region_1.2_spmd.clone.sunk | while | flops 528389 | bytes 1585295 | solution.py:23
  82.8 2.1 %fusion.86 = f32[8,128,128]{2,1,0:T(8,128)S(1)} fusion(f32[8,128,128]{2,1,0:T(8,128)S(1)} %get-tuple-element.507, f32[8,8,128,128]{3,2,1,0:T(8,128)} %get-tuple-element.519, s32[]{:T(128)} %get-tuple-element.506, f32[]{:T(128)} %bitcast.134, pred[]{:T(512)S(6)} %compare.6, pred[]{:T(512)S(6)} %lt.69), kind=kLoop, calls=%fused_computation.1.clone.1 | loop fusion | flops 524288 | bytes 1572874 | tf_op jit(solution)/shard_map/while/body/eval_jaxpr/jit(_where)/select_n | solution.py:21
  87.5 2.1 %fusion.86 = f32[8,128,128]{2,1,0:T(8,128)S(1)} fusion(f32[8,128,128]{2,1,0:T(8,128)S(1)} %get-tuple-element.507, f32[8,8,128,128]{3,2,1,0:T(8,128)} %get-tuple-element.519, s32[]{:T(128)} %get-tuple-element.506, f32[]{:T(128)} %bitcast.134, pred[]{:T(512)S(6)} %compare.6, pred[]{:T(512)S(6)} %lt.69), kind=kLoop, calls=%fused_computation.1.clone.1 | loop fusion | flops 524288 | bytes 1572874 | tf_op jit(solution)/shard_map/while/body/eval_jaxpr/jit(_where)/select_n | solution.py:21
  92.2 2.1 %fusion.86 = f32[8,128,128]{2,1,0:T(8,128)S(1)} fusion(f32[8,128,128]{2,1,0:T(8,128)S(1)} %get-tuple-element.507, f32[8,8,128,128]{3,2,1,0:T(8,128)} %get-tuple-element.519, s32[]{:T(128)} %get-tuple-element.506, f32[]{:T(128)} %bitcast.134, pred[]{:T(512)S(6)} %compare.6, pred[]{:T(512)S(6)} %lt.69), kind=kLoop, calls=%fused_computation.1.clone.1 | loop fusion | flops 524288 | bytes 1572874 | tf_op jit(solution)/shard_map/while/body/eval_jaxpr/jit(_where)/select_n | solution.py:21
  96.9 2.1 %fusion.86 = f32[8,128,128]{2,1,0:T(8,128)S(1)} fusion(f32[8,128,128]{2,1,0:T(8,128)S(1)} %get-tuple-element.507, f32[8,8,128,128]{3,2,1,0:T(8,128)} %get-tuple-element.519, s32[]{:T(128)} %get-tuple-element.506, f32[]{:T(128)} %bitcast.134, pred[]{:T(512)S(6)} %compare.6, pred[]{:T(512)S(6)} %lt.69), kind=kLoop, calls=%fused_computation.1.clone.1 | loop fusion | flops 524288 | bytes 1572874 | tf_op jit(solution)/shard_map/while/body/eval_jaxpr/jit(_where)/select_n | solution.py:21
  101.6 2.1 %fusion.86 = f32[8,128,128]{2,1,0:T(8,128)S(1)} fusion(f32[8,128,128]{2,1,0:T(8,128)S(1)} %get-tuple-element.507, f32[8,8,128,128]{3,2,1,0:T(8,128)} %get-tuple-element.519, s32[]{:T(128)} %get-tuple-element.506, f32[]{:T(128)} %bitcast.134, pred[]{:T(512)S(6)} %compare.6, pred[]{:T(512)S(6)} %lt.69), kind=kLoop, calls=%fused_computation.1.clone.1 | loop fusion | flops 524288 | bytes 1572874 | tf_op jit(solution)/shard_map/while/body/eval_jaxpr/jit(_where)/select_n | solution.py:21
  106.2 2.1 %fusion.86 = f32[8,128,128]{2,1,0:T(8,128)S(1)} fusion(f32[8,128,128]{2,1,0:T(8,128)S(1)} %get-tuple-element.507, f32[8,8,128,128]{3,2,1,0:T(8,128)} %get-tuple-element.519, s32[]{:T(128)} %get-tuple-element.506, f32[]{:T(128)} %bitcast.134, pred[]{:T(512)S(6)} %compare.6, pred[]{:T(512)S(6)} %lt.69), kind=kLoop, calls=%fused_computation.1.clone.1 | loop fusion | flops 524288 | bytes 1572874 | tf_op jit(solution)/shard_map/while/body/eval_jaxpr/jit(_where)/select_n | solution.py:21
  110.9 2.1 %fusion.86 = f32[8,128,128]{2,1,0:T(8,128)S(1)} fusion(f32[8,128,128]{2,1,0:T(8,128)S(1)} %get-tuple-element.507, f32[8,8,128,128]{3,2,1,0:T(8,128)} %get-tuple-element.519, s32[]{:T(128)} %get-tuple-element.506, f32[]{:T(128)} %bitcast.134, pred[]{:T(512)S(6)} %compare.6, pred[]{:T(512)S(6)} %lt.69), kind=kLoop, calls=%fused_computation.1.clone.1 | loop fusion | flops 524288 | bytes 1572874 | tf_op jit(solution)/shard_map/while/body/eval_jaxpr/jit(_where)/select_n | solution.py:21
  116.1 2.0 fusion.17
  123.3 2.4 %fusion.18 = f32[8,128,128]{2,1,0:T(8,128)} fusion(f32[128,8,128]{0,2,1:T(8,128)S(1)} %bitcast.147, f32[8]{0:T(128)} %get-tuple-element.394, f32[128]{0:T(128)S(1)} %compare_convert_fusion, f32[8,128]{1,0:T(8,128)S(1)} %get-tuple-element.405, f32[8,128,128]{1,2,0:T(8,128)} %copy-done.1), kind=kOutput, calls=%fused_computation.33 | convolution fusion | flops 34473088 | bytes 1577504 | tf_op jit(solution)/shard_map/transpose(jvp(hts,she->the))/dot_general | solution.py:82
  125.7 2.5 %multiply_reduce_fusion.1 = (f32[128,8]{0,1:T(8,128)S(1)}, f32[128,8,128]{0,2,1:T(8,128)}) fusion(f32[128,8]{0,1:T(8,128)S(1)} %multiply_divide_fusion.4, f32[128]{0:T(128)S(1)} %compare_convert_fusion, f32[8]{0:T(128)} %copy-done.9, f32[128,1024]{0,1:T(8,128)S(1)} %copy.53, f32[128,8,128]{0,2,1:T(8,128)S(1)} %select_n.147, ...), kind=kOutput, calls=%fused_computation.67 | convolution fusion | flops 202112000 | bytes 2105892 | tf_op jit(solution)/shard_map/jvp(thd,hde->the)/dot_general | solution.py:69
  128.2 2.3 %fusion.10 = f32[128,8,128]{0,2,1:T(8,128)} fusion(f32[8,128,128]{2,1,0:T(8,128)S(1)} %get-tuple-element.306, f32[8,128]{1,0:T(8,128)} %copy-done.6, f32[8,128]{1,0:T(8,128)S(1)} %get-tuple-element.404, f32[]{:T(128)} %bitcast, f32[128,8,128]{0,2,1:T(8,128)S(1)} %bitcast.148, f32[128,8]{0,1:T(8,128)} %copy-done.8, f32[128]{0:T(128)S(1)} %compare_convert_fusion, ...), kind=kOutput, calls=%fused_computation.21 | convolution fusion | flops 202113024 | bytes 1585700 | tf_op jit(solution)/shard_map/transpose(jvp(thd,hde->the))/dot_general | solution.py:69
  130.4 2.4 %fusion.26 = bf16[128,8,128]{0,2,1:T(8,128)(2,1)S(1)} fusion(bf16[128,8,128]{0,2,1:T(8,128)(2,1)} %bitcast.163, f32[128,8,128]{0,2,1:T(8,128)} %bitcast.168, f32[128,8,128]{0,2,1:T(8,128)} %bitcast.154, pred[128,8,128]{0,2,1:T(32,128)(4,1)} %bitcast.170, f32[128,8,128]{0,2,1:T(8,128)} %fusion.10, f32[8,128,128]{1,2,0:T(8,128)} %get-tuple-element.410, ...), kind=kOutput, calls=%fused_computation.43 | convolution fusion | flops 35521664 | bytes 3301376 | tf_op jit(solution)/shard_map/transpose(jvp(thd,shd->hts))/dot_general | solution.py:72
  134.7 8.8 %all-gather.4 = bf16[64,128]{1,0:T(8,128)(2,1)S(1)} all-gather(bf16[8,128]{1,0:T(8,128)(2,1)S(1)} %multiply_convert_fusion), channel_id=6, replica_groups=mesh['seq'=8,'head'=4] {'seq'}, dimensions={0}, use_global_device_ids=true | all-gather | bytes 18432 | tf_op jit(solution)/shard_map/all_gather | solution.py:29
  145.2 6.0 %convolution_bitcast_fusion = f32[4096,128]{0,1:T(8,128)} fusion(bf16[128,1024]{0,1:T(8,128)(2,1)S(1)} %bitcast.166, bf16[1024,4096]{1,0:T(8,128)(2,1)} %param.16), kind=kOutput, calls=%fused_computation.11 | convolution fusion | flops 1073741824 | bytes 10747904 | tf_op jit(solution)/shard_map/dot_general | solution.py:135
  151.3 25.6 %while.35 = (s32[]{:T(128)}, f32[8,128,128]{2,1,0:T(8,128)S(1)}, f32[8,128]{1,0:T(8,128)S(1)}, s32[]{:T(128)}, bf16[8,8,128,128]{3,2,1,0:T(8,128)(2,1)}, /*index...) while((s32[]{:T(128)}, f32[8,128,128]{2,1,0:T(8,128)S(1)}, ...), condition=%wide.region_9.10_spmd.clone, body=%wide.region_8.9_spmd.clone.sunk | while | flops 660489 | bytes 1321163 | solution.py:47
  155.1 1.9 fusion.89
  161.5 1.9 fusion.89
  164.7 1.9 fusion.89
  171.1 1.9 fusion.89
  174.3 1.9 fusion.89
  176.9 2.1 %fusion.16 = bf16[8,128,128]{2,1,0:T(8,128)(2,1)S(1)} fusion(f32[8,128,128]{2,1,0:T(8,128)} %fusion.18, f32[8,128,128]{2,1,0:T(8,128)S(1)} %get-tuple-element.309, f32[128]{0:T(128)S(1)} %compare_convert_fusion, pred[128,8,128]{0,2,1:T(32,128)(4,1)S(1)} %bitcast.158, f32[128,8,128]{0,2,1:T(8,128)S(1)} %bitcast.144, f32[128,8,128]{0,2,1:T(8,128)S(1)} %bitcast.141), kind=kOutput, calls=%fused_computation.30 | convolution fusion | flops 201981952 | bytes 2490880 | tf_op jit(solution)/shard_map/transpose(jvp(thd,the->hde))/dot_general | solution.py:58
  183.1 12.1 %reduce-scatter.2.cloned.1.call-done = f32[1024,128]{0,1:T(8,128)} async-done(((f32[4096,128]{0,1:T(8,128)}), f32[1024,128]{0,1:T(8,128)}) %reduce-scatter.2.cloned.1.call-update) | async-done | bytes 524304 | tf_op jit(solution)/shard_map/reduce_scatter | solution.py:134
  (111 shorter events, 66.5 us)
Async XLA Ops:
  7.2 43.9 %copy-start = (bf16[128,1024]{1,0:T(8,128)(2,1)S(1)}, bf16[128,1024]{1,0:T(8,128)(2,1)}, u32[]{:S(2)}) copy-start(bf16[128,1024]{1,0:T(8,128)(2,1)} %param.12) | copy-start | bytes 786436
  7.2 65.8 %all-gather.9.cloned.1.call-start = ((), (), s32[]{:S(2)}) async-start(), calls=%async_computation.2 | async-start | bytes 1310720 | tf_op jit(solution)/shard_map/all_gather | solution.py:145
  7.9 73.6 %all-gather.11.cloned.1.call-start = ((), (), s32[]{:S(2)}) async-start(), calls=%async_computation.3 | async-start | bytes 4718592 | tf_op jit(solution)/shard_map/all_gather | solution.py:14
  15.5 135.8 %all-gather.13.cloned.1.call-start = ((), (), s32[]{:S(2)}) async-start(), calls=%async_computation.4 | async-start | bytes 2359296 | tf_op jit(solution)/shard_map/all_gather | solution.py:29
  57.5 15.5 %copy-start.5 = (pred[128,1024]{0,1:T(32,128)(4,1)}, pred[128,1024]{0,1:T(32,128)(4,1)S(1)}, u32[]{:S(2)}) copy-start(pred[128,1024]{0,1:T(32,128)(4,1)S(1)} %copy.45) | copy-start | bytes 393220
  72.3 43.3 %copy-start.9 = (f32[8]{0:T(128)}, f32[8]{0:T(128)S(1)}, u32[]{:S(2)}) copy-start(f32[8]{0:T(128)S(1)} %get-tuple-element.395) | copy-start | bytes 100
  114.4 0.6 copy-start.6
  115.5 0.6 copy-start.8
  118.1 77.1 %reduce-scatter.2.cloned.1.call-start = ((), (), s32[]{:S(2)}) async-start(), calls=%async_computation.1 | async-start | bytes 2621440 | tf_op jit(solution)/shard_map/reduce_scatter | solution.py:134
  119.7 0.8 copy-start.1
  145.2 6.0 %copy-start.10 = (bf16[8]{0:T(256)(128)(2,1)S(1)}, bf16[8]{0:T(256)(128)(2,1)}, u32[]{:S(2)}) copy-start(bf16[8]{0:T(256)(128)(2,1)} %all-reduce.1) | copy-start | bytes 52
  151.2 29.3 %copy-start.2 = (bf16[128,1024]{0,1:T(8,128)(2,1)S(1)}, bf16[128,1024]{0,1:T(8,128)(2,1)}, u32[]{:S(2)}) copy-start(bf16[128,1024]{0,1:T(8,128)(2,1)} %copy.83) | copy-start | bytes 786436
  151.2 29.3 %copy-start.3 = (f32[8,128,128]{1,2,0:T(8,128)S(1)}, f32[8,128,128]{1,2,0:T(8,128)}, u32[]{:S(2)}) copy-start(f32[8,128,128]{1,2,0:T(8,128)} %get-tuple-element.410) | copy-start | bytes 1572868
  151.2 29.3 %copy-start.4 = (f32[128,1024]{0,1:T(8,128)S(1)}, f32[128,1024]{0,1:T(8,128)}, u32[]{:S(2)}) copy-start(f32[128,1024]{0,1:T(8,128)} %copy.61) | copy-start | bytes 1572868
  151.2 29.3 %copy-start.7 = (f32[8,128]{1,0:T(8,128)S(1)}, f32[8,128]{1,0:T(8,128)}, u32[]{:S(2)}) copy-start(f32[8,128]{1,0:T(8,128)} %neg.22) | copy-start | bytes 12292
Sparse Core Ops, SparseCore 0:
  9.6 30.6 all-gather.8
  42.1 36.3 all-gather.10
  118.2 27.8 all-gather.12
  151.3 43.7 reduce-scatter.1
where the time goes:
time: 205 us; the launch traced here: 203 us
  other arithmetic  69.4 us (34%)
  blocking collectives  47.1 us (23%)
  matrix products  37.6 us (18%)
  local copies, waits for them, and re-layouts  20 us (10%)
  between operations  15.8 us (8%)
  waiting for transfers between devices  12.9 us (6%)
    unnamed x2, blocking collectives  29.1 us
    select_n x14, other arithmetic, carried_turn(): jnp.where(position < mine, new, old)  24.2 us
    select_n x16, other arithmetic, entering_turn(): return jax.tree.map(lambda a, b: jnp.where(reached, a, b), new, before)  20.7 us
    reduce_scatter x1, waiting for transfers between devices, shards(): lax.psum_scatter(lax.dot_general(weight_part, mixed_heads, (((0,), (1,)),...  12.1 us
    all_gather x1, blocking collectives, carried_in(): pieces = jax.tree.map(lambda part: lax.all_gather(part, axis), value)  9.18 us
    all_gather x1, blocking collectives, entering(): lax.all_gather(part.astype(kind), axis)  8.83 us
    sub x7, other arithmetic, join_forward(): keep = 1.0 - later[0]  8.72 us
    unnamed x30, local copies, waits for them, and re-layouts  8.32 us
  transfers between devices with their start and end apart: 4, of which 1 were waited for; matrix products, arithmetic and copies ran while one was open for 43% of the time, Pallas kernels for 0%

commit v1 on v0

v1 whole, which is shorter than its diff:
```python
import functools

import jax
import jax.numpy as jnp
from jax import lax
from jax.experimental import pallas as pl
from jax.experimental.pallas import tpu as pltpu
from jax.sharding import PartitionSpec as P

DH = 128
ROWS = 136
SENT = 144
BF16 = jnp.bfloat16
F32 = jnp.float32
VMEM = pl.BlockSpec(memory_space=pltpu.VMEM)
SMEM = pl.BlockSpec(memory_space=pltpu.SMEM)


def call(kernel, outs, in_specs, args, flops=0, name=None):
    moved = sum(a.size * a.dtype.itemsize for a in args)
    moved += sum(o.size * o.dtype.itemsize for o in outs)
    return pl.pallas_call(
        kernel,
        out_shape=outs,
        in_specs=in_specs,
        out_specs=[VMEM] * len(outs),
        compiler_params=pltpu.CompilerParams(vmem_limit_bytes=48 * 1024 * 1024),
        cost_estimate=pl.CostEstimate(flops=flops, bytes_accessed=moved, transcendentals=0),
        name=name,
    )(*args)


def feature(x):
    return jnp.where(x > 0, x + 1.0, jnp.exp(jnp.minimum(x, 0.0)))


def slope(x):
    return jnp.where(x > 0, 1.0, jnp.where(x == 0, 0.5, jnp.exp(jnp.minimum(x, 0.0))))


def sigmoid(x):
    return 1.0 / (1.0 + jnp.exp(-x))


def dot(a, b, dims):
    return lax.dot_general(a, b, (dims, ((), ())), preferred_element_type=F32)


NN = ((1,), (0,))
NT = ((1,), (1,))
TN = ((0,), (0,))


def live_rows(valid_ref, length):
    where = lax.broadcasted_iota(jnp.int32, (length, 1), 0)
    return (where < valid_ref[0]).astype(F32)


def head(ref, h):
    return ref[:, h * DH : (h + 1) * DH]


def tail(rows, *values):
    where = lax.broadcasted_iota(jnp.int32, (rows, DH), 0)
    out = jnp.zeros((rows, DH), F32)
    for at, value in enumerate(values):
        out = jnp.where(where == at, value, out)
    return out


def split(x):
    top = x.astype(BF16)
    rest = x - top.astype(F32)
    return top, rest.astype(BF16)


def state_kernel(heads, valid_ref, starts_ref, k_ref, v_ref, state_ref):
    live = live_rows(valid_ref, k_ref.shape[0])
    opened = 1.0 - starts_ref[0].astype(F32)
    for h in range(heads):
        sig = (feature(head(k_ref, h).astype(F32)) * live).astype(BF16)
        state_ref[h, 0:DH, :] = dot(sig, head(v_ref, h), TN)
        norm = jnp.sum(sig.astype(F32), axis=0, keepdims=True)
        state_ref[h, DH:ROWS, :] = tail(ROWS - DH, norm, opened)


def pair_kernel(heads, forward, pos_ref, mine_ref, other_ref, sent_ref):
    half = lax.rem(pos_ref[0], 2)
    lower = half == 0
    for i in range(heads // 2):
        h = half * (heads // 2) + i
        mine, other = mine_ref[h], other_ref[h]
        first = jnp.where(lower, mine, other)
        second = jnp.where(lower, other, mine)
        open_first, open_second = first[DH + 1 : DH + 2], second[DH + 1 : DH + 2]
        if forward:
            total = open_second * first + second
        else:
            total = open_first * (first + open_second * second)
        memory, norm = total[0:DH], total[DH : DH + 1]
        norm_1, rest = split(norm)
        norm_1 = norm_1.astype(F32)
        norm_2 = rest.astype(F32)
        norm_3 = norm - norm_1 - norm_2
        if forward:
            weight = jnp.maximum(jnp.sum(norm, axis=1, keepdims=True), 1e-30)
            centre = jnp.sum(memory, axis=0, keepdims=True) / weight
            centre = centre.astype(BF16).astype(F32)
            norms = tail(16, norm_1, norm_2, norm_3).astype(BF16)
            centres = tail(16, centre, centre, centre).astype(BF16)
            memory = memory - dot(norms, centres, TN)
        else:
            centre = jnp.zeros_like(norm)
        sent_ref[i, 0:DH, :] = memory.astype(BF16)
        rows = tail(SENT - DH, norm_1, norm_2, norm_3, centre, open_first * open_second)
        sent_ref[i, DH:SENT, :] = rows.astype(BF16)


def join_kernel(heads, forward, pos_ref, x_ref, y_ref, d_ref, carry_ref):
    chip = pos_ref[0] // 2
    place = chip if forward else 3 - chip
    for i in range(heads // 2):
        totals = []
        for ref in (x_ref, y_ref, d_ref):
            memory = ref[i, 0:DH, :].astype(F32)
            rows = ref[i, DH:SENT, :].astype(F32)
            norm = rows[0:1] + rows[1:2] + rows[2:3]
            if forward:
                norms = tail(16, rows[0:1], rows[1:2], rows[2:3]).astype(BF16)
                centres = tail(16, rows[3:4], rows[3:4], rows[3:4]).astype(BF16)
                memory = memory + dot(norms, centres, TN)
            totals.append((memory, norm, rows[4:5]))
        (x_mem, x_norm, x_open), (y_mem, y_norm, y_open), (d_mem, d_norm, d_open) = totals
        on_y = jnp.where(place == 2, d_open, x_open)
        on_d = jnp.where(place == 2, 1.0, x_open * y_open)
        carry_ref[i, 0:DH, :] = x_mem + on_y * y_mem + on_d * d_mem
        carry_ref[i, DH:ROWS, :] = tail(ROWS - DH, x_norm + on_y * y_norm + on_d * d_norm)


def local_kernel(heads, valid_ref, q_ref, k_ref, v_ref, probs_ref, local_ref):
    length = q_ref.shape[0]
    row = lax.broadcasted_iota(jnp.int32, (length, length), 0)
    col = lax.broadcasted_iota(jnp.int32, (length, length), 1)
    allowed = (col <= row) & (col < valid_ref[0])
    for h in range(heads):
        scores = dot(head(q_ref, h), head(k_ref, h), NT) * DH ** (-0.5)
        scores = jnp.where(allowed, scores, -1e30)
        expo = jnp.exp(scores - jnp.max(scores, axis=1, keepdims=True))
        probs = (expo / jnp.sum(expo, axis=1, keepdims=True)).astype(BF16)
        probs_ref[h] = probs
        local_ref[:, h * DH : (h + 1) * DH] = dot(probs, head(v_ref, h), NN)


def read_kernel(
    heads, pos_ref, valid_ref, gate_ref, q_ref, mine_ref, other_ref, own_ref, far_ref, local_ref,
    mixed_ref, read_ref, memory_ref, norm_ref,
):
    length = q_ref.shape[0]
    live = live_rows(valid_ref, length)
    upper = lax.rem(pos_ref[0], 2) == 1
    for h in range(heads):
        i, part = h % (heads // 2), h // (heads // 2)
        own_here = upper if part else jnp.logical_not(upper)
        carry = jnp.where(own_here, own_ref[i], far_ref[i])
        other = other_ref[h]
        before = jnp.where(upper, other[DH + 1 : DH + 2] * carry + other, carry)
        state = mine_ref[h, DH + 1 : DH + 2, :] * before
        memory, norm = state[0:DH], state[DH : DH + 1]
        parts = jnp.concatenate(split(memory), axis=1)
        memory_ref[h] = parts
        norm_ref[h] = jnp.broadcast_to(norm, (8, DH))
        sig = feature(head(q_ref, h).astype(F32)).astype(BF16)
        numer = dot(sig, parts, NN)
        numer = numer[:, 0:DH] + numer[:, DH:]
        denom = jnp.sum(sig.astype(F32) * norm, axis=1, keepdims=True) + 1.0
        read = numer / denom
        gate = sigmoid(jnp.full((1, DH), gate_ref[h], F32))
        mixed = live * (gate * read + (1.0 - gate) * head(local_ref, h))
        read_ref[:, h * DH : (h + 1) * DH] = read
        mixed_ref[:, h * DH : (h + 1) * DH] = mixed.astype(BF16)


def spread_kernel(heads, valid_ref, starts_ref, gate_ref, q_ref, norm_ref, read_ref, grad_ref,
                  passed_ref, numer_ref, denom_ref):
    length = q_ref.shape[0]
    live = live_rows(valid_ref, length)
    opened = 1.0 - starts_ref[0].astype(F32)
    for h in range(heads):
        sig = feature(head(q_ref, h).astype(F32)).astype(BF16)
        sig_full = sig.astype(F32)
        denom = jnp.sum(sig_full * norm_ref[h, 0:1, :], axis=1, keepdims=True) + 1.0
        gate = sigmoid(jnp.full((1, DH), gate_ref[h], F32))
        numer_grad = (head(grad_ref, h).astype(F32) * gate * (live / denom)).astype(BF16)
        denom_grad = -jnp.sum(
            numer_grad.astype(F32) * head(read_ref, h), axis=1, keepdims=True
        )
        passed_ref[h, 0:DH, :] = dot(sig, numer_grad, TN)
        norm_grad = jnp.sum(sig_full * denom_grad, axis=0, keepdims=True)
        passed_ref[h, DH:ROWS, :] = tail(ROWS - DH, norm_grad, opened)
        numer_ref[:, h * DH : (h + 1) * DH] = numer_grad
        denom_ref[h] = denom_grad


def grads_kernel(heads, valid_ref, gate_ref, q_ref, k_ref, v_ref, probs_ref, grad_ref, numer_ref,
                 denom_ref, memory_ref, norm_ref, query_ref, key_ref, value_ref):
    length = q_ref.shape[0]
    live = live_rows(valid_ref, length)
    for h in range(heads):
        cut = slice(h * DH, (h + 1) * DH)
        q, k, v = head(q_ref, h), head(k_ref, h), head(v_ref, h)
        gate = sigmoid(jnp.full((1, DH), gate_ref[h], F32))
        grad = (head(grad_ref, h).astype(F32) * (1.0 - gate) * live).astype(BF16)
        probs = probs_ref[h]
        probs_grad = dot(grad, v, NT)
        full = probs.astype(F32)
        mean = jnp.sum(full * probs_grad, axis=1, keepdims=True)
        scores_grad = (full * (probs_grad - mean) * DH ** (-0.5)).astype(BF16)
        key_ref[:, cut] = dot(scores_grad, q, TN)
        value_ref[:, cut] = dot(probs, grad, TN)
        parts = memory_ref[h]
        numer = head(numer_ref, h)
        sig_grad = dot(numer, parts[:, 0:DH], NT) + dot(numer, parts[:, DH:], NT)
        sig_grad = sig_grad + denom_ref[h] * norm_ref[h, 0:1, :]
        total = dot(scores_grad, k, NN) + sig_grad * slope(q.astype(F32))
        query_ref[:, cut] = total.astype(BF16)


def last_kernel(heads, pos_ref, valid_ref, k_ref, v_ref, other_ref, own_ref, far_ref, key_ref,
                value_ref, key_out, value_out):
    length = k_ref.shape[0]
    live = live_rows(valid_ref, length)
    upper = lax.rem(pos_ref[0], 2) == 1
    for h in range(heads):
        cut = slice(h * DH, (h + 1) * DH)
        i, part = h % (heads // 2), h // (heads // 2)
        own_here = upper if part else jnp.logical_not(upper)
        carry = jnp.where(own_here, own_ref[i], far_ref[i])
        other = other_ref[h]
        back = jnp.where(upper, carry, other[DH + 1 : DH + 2] * (other + carry))
        memory, norm = back[0:DH], back[DH : DH + 1]
        top, low = split(memory)
        k, v = head(k_ref, h).astype(F32), head(v_ref, h)
        sig = (feature(k) * live).astype(BF16)
        sig_grad = (dot(v, top, NT) + dot(v, low, NT) + norm) * live
        key_out[:, cut] = (key_ref[:, cut] + sig_grad * slope(k)).astype(BF16)
        more = dot(sig, jnp.concatenate([top, low], axis=1), NN)
        value_out[:, cut] = (value_ref[:, cut] + more[:, 0:DH] + more[:, DH:]).astype(BF16)


def project_kernel(ids_ref, mixed_ref, weight_ref, out_ref):
    out_ref[0] = dot(mixed_ref[...], weight_ref[...], NN).astype(BF16)


def project(ids, mixed, weight, cols, name):
    count, (length, width) = ids.shape[0], mixed.shape
    return pl.pallas_call(
        project_kernel,
        grid_spec=pltpu.PrefetchScalarGridSpec(
            num_scalar_prefetch=1,
            grid=(count,),
            in_specs=[
                pl.BlockSpec((length, width), lambda s, ids: (0, 0)),
                pl.BlockSpec((width, cols), lambda s, ids: (0, ids[s])),
            ],
            out_specs=pl.BlockSpec((1, length, cols), lambda s, ids: (s, 0, 0)),
        ),
        out_shape=jax.ShapeDtypeStruct((count, length, cols), BF16),
        compiler_params=pltpu.CompilerParams(vmem_limit_bytes=48 * 1024 * 1024),
        cost_estimate=pl.CostEstimate(
            flops=2 * length * width * cols * count,
            bytes_accessed=2 * count * width * cols,
            transcendentals=0,
        ),
        name=name,
    )(ids, mixed, weight)


def unproject_kernel(blocks, grad_first, ids_ref, *refs):
    parts, (weight_ref, total_ref) = refs[:-2], refs[-2:]
    step = pl.program_id(0)
    for s, members in enumerate(blocks):

        @pl.when(step == s)
        def _():
            block = parts[members[0]][...]
            for more in members[1:]:
                block = block + parts[more][...]
            term = dot(block, weight_ref[...], NT)
            if s == 0 and grad_first:
                total_ref[...] = term
            elif s == 0:
                total_ref[...] = parts[-1][...] + term
            else:
                total_ref[...] += term


def unproject(ids, groups, weight, before, name):
    flat, blocks = [], []
    for group in groups:
        blocks.append(tuple(range(len(flat), len(flat) + len(group))))
        flat += group
    length, cols = flat[0].shape
    width = weight.shape[0]
    extra = [] if before is None else [before]
    return pl.pallas_call(
        functools.partial(unproject_kernel, blocks, before is None),
        grid_spec=pltpu.PrefetchScalarGridSpec(
            num_scalar_prefetch=1,
            grid=(len(groups),),
            in_specs=[pl.BlockSpec((length, cols), lambda s, ids: (0, 0)) for _ in flat]
            + [pl.BlockSpec((length, width), lambda s, ids: (0, 0)) for _ in extra]
            + [pl.BlockSpec((width, cols), lambda s, ids: (0, ids[s]))],
            out_specs=pl.BlockSpec((length, width), lambda s, ids: (0, 0)),
        ),
        out_shape=jax.ShapeDtypeStruct((length, width), F32),
        compiler_params=pltpu.CompilerParams(vmem_limit_bytes=48 * 1024 * 1024),
        cost_estimate=pl.CostEstimate(
            flops=2 * length * width * cols * len(groups),
            bytes_accessed=2 * len(groups) * width * cols,
            transcendentals=0,
        ),
        name=name,
    )(ids, *flat, *extra, weight)


def weighted(state, forward):
    count, mine = lax.axis_size("seq"), lax.axis_index("seq")
    states = lax.all_gather(state, "seq")
    total = jnp.zeros_like(state)
    weight = jnp.ones((), F32)

    def turn(step, carried):
        total, weight = carried
        at = mine - 1 - step if forward else mine + 1 + step
        inside = (at >= 0) & (at < count)
        one = lax.dynamic_index_in_dim(states, jnp.clip(at, 0, count - 1), keepdims=False)
        opened = one[0, DH + 1, 0]
        here = weight if forward else weight * opened
        total = jnp.where(inside, total + here * one, total)
        return total, weight * opened

    return lax.fori_loop(0, count - 1, turn, (total, weight))[0]


def scan_states(state, pos, heads, forward):
    count = lax.axis_size("seq")
    if count != 8:
        carry = weighted(state, forward)
        place = jnp.full_like(pos, 0 if forward else 1)
        own, far = carry[: heads // 2], carry[heads // 2 :]
        return (own, far, state, place) if forward else (far, own, state, place)
    pairs = [(s, s ^ 1) for s in range(count)]
    other = lax.ppermute(state, "seq", pairs)
    flops = heads * DH * DH * 40
    sent = call(
        functools.partial(pair_kernel, heads, forward),
        [jax.ShapeDtypeStruct((heads // 2, SENT, DH), BF16)],
        [SMEM, VMEM, VMEM],
        [pos, state, other],
        flops,
        name="pair",
    )[0]
    x = [(0, 2), (1, 3), (4, 6), (5, 7)]
    y = [(0, 4), (1, 5), (2, 6), (3, 7)]
    d = [(0, 6), (1, 7), (2, 4), (3, 5)]
    if not forward:
        x, y, d = ([(b, a) for a, b in ways] for ways in (x, y, d))
    arrived = [lax.ppermute(sent, "seq", ways) for ways in (d, x, y)]
    own = call(
        functools.partial(join_kernel, heads, forward),
        [jax.ShapeDtypeStruct((heads // 2, ROWS, DH), F32)],
        [SMEM, VMEM, VMEM, VMEM],
        [pos, arrived[1], arrived[2], arrived[0]],
        flops,
        name="join",
    )[0]
    far = lax.ppermute(own, "seq", pairs)
    return own, far, other, pos


def shards(queries, keys, values, gate, out_weight, out_grad, valid, starts):
    length, width = queries.shape
    heads = width // DH
    cols = out_grad.shape[1]
    groups = lax.axis_size("head")
    pos = lax.axis_index("seq").astype(jnp.int32).reshape(1)
    z = lax.axis_index("head").astype(jnp.int32)
    flat = jax.ShapeDtypeStruct((length, width), F32)
    low = jax.ShapeDtypeStruct((length, width), BF16)
    states = jax.ShapeDtypeStruct((heads, ROWS, DH), F32)
    square = 2 * heads * length * DH * DH

    state = call(
        functools.partial(state_kernel, heads), [states], [SMEM, SMEM, VMEM, VMEM],
        [valid, starts, keys, values], square, name="state",
    )[0]

    if groups == 4:
        swap = [(0, 1), (1, 0), (2, 3), (3, 2)]
        ends = [(0, 3), (3, 0)]
        skip_in, skip_out = [(0, 2), (3, 1)], [(1, 3), (2, 0)]
        middle = [(1, 2), (2, 1)]
        outward, inward = [(1, 0), (2, 3)], [(0, 1), (3, 2)]
        near = z + 1 - 2 * (z % 2)
        far_id = jnp.where(z < 2, 3, 0)
        mid_id = jnp.where(z < 2, 2, 1)
        from_mid = lax.ppermute(out_grad, "head", middle)
        from_near = lax.ppermute(out_grad, "head", swap)
        from_end = lax.ppermute(out_grad, "head", ends)
        from_skip = lax.ppermute(out_grad, "head", skip_in)
        from_out = lax.ppermute(from_mid, "head", outward)

    probs, local = call(
        functools.partial(local_kernel, heads),
        [jax.ShapeDtypeStruct((heads, length, length), BF16), flat],
        [SMEM, VMEM, VMEM, VMEM],
        [valid, queries, keys, values], 2 * square, name="local",
    )

    own, far, other, place = scan_states(state, pos, heads, True)
    mixed, read, memory, norm = call(
        functools.partial(read_kernel, heads),
        [low, flat, jax.ShapeDtypeStruct((heads, DH, 2 * DH), BF16),
         jax.ShapeDtypeStruct((heads, 8, DH), F32)],
        [SMEM, SMEM, SMEM] + [VMEM] * 6,
        [place, valid, gate, queries, state, other, own, far, local], 2 * square, name="read",
    )

    if groups == 4:
        first = project(jnp.stack([mid_id, far_id]), mixed, out_weight, cols, "project_far")
        to_in = lax.ppermute(first[0], "head", inward)
        end = lax.ppermute(first[1], "head", ends)
        skip = lax.ppermute(first[1], "head", skip_out)
        second = project(jnp.stack([near, z]), mixed, out_weight, cols, "project_near")
        next_to = lax.ppermute(second[0], "head", swap)
        mid = lax.ppermute(first[0] + to_in, "head", middle)
        output = second[1].astype(F32) + next_to.astype(F32) + end.astype(F32)
        output = (output + skip.astype(F32) + mid.astype(F32)).astype(BF16)
        total = unproject(
            jnp.stack([z, near, far_id]), [[out_grad], [from_near], [from_end, from_skip]],
            out_weight, None, "unproject_first",
        )
        total = unproject(
            mid_id.reshape(1), [[from_mid, from_out]], out_weight, total, "unproject_last"
        )
    else:
        part = dot(mixed, out_weight, NN)
        output = lax.psum_scatter(part, "head", scatter_dimension=1, tiled=True).astype(BF16)
        whole = lax.all_gather(out_grad, "head", axis=1, tiled=True)
        total = dot(whole, out_weight, NT)
    mixed_grad = total.astype(BF16)

    passed, numer_grad, denom_grad = call(
        functools.partial(spread_kernel, heads),
        [states, low, jax.ShapeDtypeStruct((heads, length, 1), F32)],
        [SMEM] * 3 + [VMEM] * 4,
        [valid, starts, gate, queries, norm, read, mixed_grad], square, name="spread",
    )
    query_grad, key_part, value_part = call(
        functools.partial(grads_kernel, heads),
        [low, flat, flat],
        [SMEM] * 2 + [VMEM] * 9,
        [valid, gate, queries, keys, values, probs, mixed_grad, numer_grad, denom_grad, memory, norm],
        6 * square, name="grads",
    )
    own, far, other, place = scan_states(passed, pos, heads, False)
    key_grad, value_grad = call(
        functools.partial(last_kernel, heads),
        [low, low],
        [SMEM] * 2 + [VMEM] * 7,
        [place, valid, keys, values, other, own, far, key_part, value_part], 4 * square, name="last",
    )
    return (output, query_grad, key_grad, value_grad)


def solution(mesh):
    placed = (
        P("seq", "head"),
        P("seq", "head"),
        P("seq", "head"),
        P("head"),
        P("head", None),
        P("seq", "head"),
        P("seq"),
        P("seq"),
    )
    return jax.shard_map(
        shards,
        mesh=mesh,
        in_specs=placed,
        out_specs=(P("seq", "head"), P("seq", "head"), P("seq", "head"), P("seq", "head")),
        check_vma=False,
    )
```

time: 205 us -> 89.7 us (0.44)
  other arithmetic: 69.4 us -> 1.21 us
  blocking collectives: 47.1 us -> 0 us
  matrix products: 37.6 us -> 0 us
  starting transfers between devices: 0.34 us -> 31.1 us
  Pallas kernels: 0 us -> 25.5 us
  local copies, waits for them, and re-layouts: 20 us -> 5.77 us
  between operations: 15.8 us -> 2.31 us
  waiting for transfers between devices: 12.9 us -> 23 us
    select_n x33 -> x0, other arithmetic: 49.3 us -> none  [the longest x14 24.2 us: carried_turn(): jnp.where(position < mine, new, old)]
    dot_general x16 -> x0, matrix products: 37.6 us -> none  [the longest x1 7.41 us: shards(): lax.dot_general(lax.all_gather(out_grad, 'head', axis=1, tiled=True), wei...]
    ppermute x0 -> x20, starting transfers between devices: none -> 31.1 us  [the longest x6 13.4 us: scan_states(): arrived = [lax.ppermute(sent, 'seq', ways) for ways in (d, x, y)]]
    unnamed x2 -> x0, blocking collectives: 29.1 us -> none
    pallas_call x0 -> x14, Pallas kernels: none -> 25.5 us  [the longest x10 11.1 us: call(): pl.pallas_call(kernel, out_shape=outs, in_specs=in_specs, out_specs=[VMEM...]
    ppermute x0 -> x20, waiting for transfers between devices: none -> 23 us  [the longest x6 11.6 us: scan_states(): arrived = [lax.ppermute(sent, 'seq', ways) for ways in (d, x, y)]]
    all_gather x2 -> x0, blocking collectives: 18 us -> none  [the longest x1 9.18 us: carried_in(): pieces = jax.tree.map(lambda part: lax.all_gather(part, axis), value)]
    sub x17 -> x0, other arithmetic: 15.1 us -> none  [the longest x7 8.72 us: join_forward(): keep = 1.0 - later[0]]
  transfers between devices with their start and end apart: 4 -> 20, of which waited for: 1 -> 6; matrix products, arithmetic and copies ran while one was open for 43% -> 1% of each run, Pallas kernels for 0% -> 24%
where the time goes in v1:
time: 89.7 us; the launch traced here: 89 us
  starting transfers between devices  31.1 us (35%)
  Pallas kernels  25.5 us (28%)
  waiting for transfers between devices  23 us (26%)
  local copies, waits for them, and re-layouts  5.77 us (6%)
  between operations  2.31 us (3%)
  other arithmetic  1.21 us (1%)
    ppermute x6, starting transfers between devices, scan_states(): arrived = [lax.ppermute(sent, 'seq', ways) for ways in (d, x, y)]  13.4 us
    ppermute x6, waiting for transfers between devices, scan_states(): arrived = [lax.ppermute(sent, 'seq', ways) for ways in (d, x, y)]  11.6 us
    pallas_call x10, Pallas kernels, call(): pl.pallas_call(kernel, out_shape=outs, in_specs=in_specs, out_specs=[VMEM...  11.1 us
    pallas_call x2, Pallas kernels, unproject(): pl.pallas_call(functools.partial(unproject_kernel, blocks, before is None...  7.85 us
    pallas_call x2, Pallas kernels, project(): pl.pallas_call(project_kernel, grid_spec=pltpu.PrefetchScalarGridSpec(num...  6.52 us
    unnamed x20, local copies, waits for them, and re-layouts  5.71 us
    ppermute x1, waiting for transfers between devices, shards(): to_in = lax.ppermute(first[0], 'head', inward)  5.61 us
    ppermute x1, starting transfers between devices, shards(): end = lax.ppermute(first[1], 'head', ends)  3.26 us
  transfers between devices with their start and end apart: 20, of which 6 were waited for; matrix products, arithmetic and copies ran while one was open for 1% of the time, Pallas kernels for 24%

profile of v1, /device:TPU:0, one launch (start us, length us, event | category | flops | bytes accessed | tf_op | source)
XLA Modules:
  0.0 89.0 jit_solution(17510369612662179846)
XLA Ops:
  2.9 0.9 %copy-done.5 = bf16[128,1024]{1,0:T(8,128)(2,1)S(1)} copy-done((bf16[128,1024]{1,0:T(8,128)(2,1)S(1)}, bf16[128,1024]{1,0:T(8,128)(2,1)}, u32[]{:S(2)}) %copy-start.5) | copy-done | bytes 262168
  6.6 4.8 %collective-permute-start.1 = (bf16[4,144,128]{2,1,0:T(8,128)(2,1)S(1)}, bf16[4,144,128]{2,1,0:T(8,128)(2,1)S(1)}, u32[]{:S(2)}, u32[]{:S(2)}) collective-permute-start(bf16[4,144,128]{2,1,0:T(8,128)(2,1)S(1)} %pair.2), channel_id=1, source_target_pairs={{0,8},{4,12},{16,24},{20,28},{1,9},{5,13},{17,25},{21,29},{2,10},{... | collective-permute-start | bytes 442376 | tf_op jit(solution)/shard_map/ppermute | solution.py:368
  11.4 3.4 %collective-permute-start.2 = (bf16[4,144,128]{2,1,0:T(8,128)(2,1)S(1)}, bf16[4,144,128]{2,1,0:T(8,128)(2,1)S(1)}, u32[]{:S(2)}, u32[]{:S(2)}) collective-permute-start(bf16[4,144,128]{2,1,0:T(8,128)(2,1)S(1)} %pair.2), channel_id=1, source_target_pairs={{0,16},{4,20},{8,24},{12,28},{1,17},{5,21},{9,25},{13,29},{2,18},{... | collective-permute-start | bytes 442376 | tf_op jit(solution)/shard_map/ppermute | solution.py:368
  14.8 1.3 %collective-permute-start.3 = (bf16[4,144,128]{2,1,0:T(8,128)(2,1)S(1)}, bf16[4,144,128]{2,1,0:T(8,128)(2,1)S(1)}, u32[]{:S(2)}, u32[]{:S(2)}) collective-permute-start(bf16[4,144,128]{2,1,0:T(8,128)(2,1)S(1)} %pair.2), channel_id=1, source_target_pairs={{0,24},{4,28},{8,16},{12,20},{1,25},{5,29},{9,17},{13,21},{2,26},{... | collective-permute-start | bytes 442376 | tf_op jit(solution)/shard_map/ppermute | solution.py:368
  16.1 3.2 %collective-permute-start.12 = (bf16[128,1024]{1,0:T(8,128)(2,1)}, bf16[128,1024]{1,0:T(8,128)(2,1)S(1)}, u32[]{:S(2)}, u32[]{:S(2)}) collective-permute-start(bf16[128,1024]{1,0:T(8,128)(2,1)} %refs_0_.1), channel_id=1, source_target_pairs={{0,1},{1,0},{2,3},{3,2},{4,5},{5,4},{6,7},{7,6},{8,9},{9,8},{10,11... | collective-permute-start | bytes 786440 | tf_op jit(solution)/shard_map/ppermute | solution.py:408
  19.3 3.2 %collective-permute-start.13 = (bf16[128,1024]{1,0:T(8,128)(2,1)}, bf16[128,1024]{1,0:T(8,128)(2,1)S(1)}, u32[]{:S(2)}, u32[]{:S(2)}) collective-permute-start(bf16[128,1024]{1,0:T(8,128)(2,1)} %refs_0_.1), channel_id=1, source_target_pairs={{0,3},{3,0},{4,7},{7,4},{8,11},{11,8},{12,15},{15,12},{16,19},{19,... | collective-permute-start | bytes 786440 | tf_op jit(solution)/shard_map/ppermute | solution.py:409
  22.6 1.3 %collective-permute-start.14 = (bf16[128,1024]{1,0:T(8,128)(2,1)}, bf16[128,1024]{1,0:T(8,128)(2,1)S(1)}, u32[]{:S(2)}, u32[]{:S(2)}) collective-permute-start(bf16[128,1024]{1,0:T(8,128)(2,1)} %refs_0_.1), channel_id=1, source_target_pairs={{0,2},{3,1},{4,6},{7,5},{8,10},{11,9},{12,14},{15,13},{16,18},{19,... | collective-permute-start | bytes 786440 | tf_op jit(solution)/shard_map/ppermute | solution.py:410
  24.0 0.9 %copy-done = bf16[128,1024]{1,0:T(8,128)(2,1)S(1)} copy-done((bf16[128,1024]{1,0:T(8,128)(2,1)S(1)}, bf16[128,1024]{1,0:T(8,128)(2,1)}, u32[]{:S(2)}) %copy-start) | copy-done | bytes 262168
  24.9 0.9 %copy-done.3 = bf16[128,1024]{1,0:T(8,128)(2,1)S(1)} copy-done((bf16[128,1024]{1,0:T(8,128)(2,1)S(1)}, bf16[128,1024]{1,0:T(8,128)(2,1)}, u32[]{:S(2)}) %copy-start.3) | copy-done | bytes 262168
  25.9 0.9 %copy-done.6 = bf16[128,1024]{1,0:T(8,128)(2,1)S(1)} copy-done((bf16[128,1024]{1,0:T(8,128)(2,1)S(1)}, bf16[128,1024]{1,0:T(8,128)(2,1)}, u32[]{:S(2)}) %copy-start.6) | copy-done | bytes 262168
  26.8 2.7 %local.1 = (bf16[8,128,128]{2,1,0:T(8,128)(2,1)S(1)}, f32[128,1024]{1,0:T(8,128)S(1)}) custom-call(s32[1]{0:T(128)S(6)} %copy.12.valid_ref, bf16[128,1024]{1,0:T(8,128)(2,1)S(1)} %copy-done, bf16[128,1024]{1,0:T(8,128)(2,1)S(1)} %copy-done.3, bf16[128,1024]{1,0:T(8,128)(2,1)S(1)} %copy-done.6), custom_call_target="tpu_custom_call" | custom-call | flops 67108864 | bytes 1572868 | tf_op jit(solution)/shard_map/local/pallas_call | solution.py:22
  29.5 1.3 %collective-permute-start.11 = (bf16[128,1024]{1,0:T(8,128)(2,1)S(1)}, bf16[128,1024]{1,0:T(8,128)(2,1)S(1)}, u32[]{:S(2)}, u32[]{:S(2)}) collective-permute-start(bf16[128,1024]{1,0:T(8,128)(2,1)S(1)} %collective-permute-done.10.refs_0_), channel_id=1, source_target_pairs={{1,0},{2,3},{5,4},{6,7},{9,8},{10,11},{13,12},{14,15},{17,16},{18,... | collective-permute-start | bytes 786440 | tf_op jit(solution)/shard_map/ppermute | solution.py:411
  31.4 2.3 %collective-permute-done.13.refs_2_ = bf16[128,1024]{1,0:T(8,128)(2,1)S(1)} collective-permute-done((bf16[128,1024]{1,0:T(8,128)(2,1)}, bf16[128,1024]{1,0:T(8,128)(2,1)S(1)}, u32[]{:S(2)}, u32[]{:S(2)}) %collective-permute-start.13) | collective-permute-done | bytes 262176 | tf_op jit(solution)/shard_map/ppermute | solution.py:409
  33.7 2.6 %collective-permute-done.14.refs_3_ = bf16[128,1024]{1,0:T(8,128)(2,1)S(1)} collective-permute-done((bf16[128,1024]{1,0:T(8,128)(2,1)}, bf16[128,1024]{1,0:T(8,128)(2,1)S(1)}, u32[]{:S(2)}, u32[]{:S(2)}) %collective-permute-start.14) | collective-permute-done | bytes 262176 | tf_op jit(solution)/shard_map/ppermute | solution.py:410
  36.3 0.9 %copy-done.8 = bf16[128,1024]{1,0:T(8,128)(2,1)S(1)} copy-done((bf16[128,1024]{1,0:T(8,128)(2,1)S(1)}, bf16[128,1024]{1,0:T(8,128)(2,1)}, u32[]{:S(2)}) %copy-start.8) | copy-done | bytes 262168
  37.2 5.4 %unproject_first.1.refs_2_ = f32[128,1024]{1,0:T(8,128)S(1)} custom-call(s32[3]{0:T(128)S(1)} %pad_add_fusion.2.ids_ref, bf16[128,1024]{1,0:T(8,128)(2,1)S(1)} %copy-done.8, bf16[128,1024]{1,0:T(8,128)(2,1)S(1)} %collective-permute-done.12.refs_1_, bf16[128,1024]{1,0:T(8,128)(2,1)S(1)} %collective-permute-done.13.refs_2_, ...), custom_call_target="tpu_custom_call" | custom-call | flops 805306368 | bytes 6291456 | tf_op jit(solution)/shard_map/unproject_first/pallas_call | solution.py:305
  42.6 2.4 %unproject_last.1 = f32[128,1024]{1,0:T(8,128)S(1)} custom-call(s32[1]{0:T(128)} %bitcast.5.ids_ref, bf16[128,1024]{1,0:T(8,128)(2,1)S(1)} %collective-permute-done.10.refs_0_, bf16[128,1024]{1,0:T(8,128)(2,1)S(1)} %collective-permute-done.11.refs_1_, f32[128,1024]{1,0:T(8,128)S(1)} %unproject_first.1.refs_2_, bf16[1024,4096]{1,0:T(8,128)(2,1)} %refs_3_.1), custom_call_target="tpu_custom_call" | custom-call | flops 268435456 | bytes 2097152 | tf_op jit(solution)/shard_map/unproject_last/pallas_call | solution.py:305
  45.1 1.1 %read.1 = (bf16[128,1024]{1,0:T(8,128)(2,1)S(1)}, f32[128,1024]{1,0:T(8,128)S(1)}, bf16[8,128,256]{2,1,0:T(8,128)(2,1)S(1)}, f32[8,8,128]{2,1,0:T(8,128)S(1)}) custom-call(s32[1]{0:T(128)} %bitcast.2.pos_ref, s32[1]{0:T(128)S(6)} %copy.12.valid_ref, f32[8]{0:T(128)S(1)} %copy-done.9, bf16[128,1024]{1,0:T(8,128)(2,1)S(1)} %copy-done.1, ...), custom_call_target="tpu_custom_call" | custom-call | flops 67108864 | bytes 3801128 | tf_op jit(solution)/shard_map/read/pallas_call | solution.py:22
  46.2 1.2 %spread.1 = (f32[8,136,128]{2,1,0:T(8,128)S(1)}, bf16[128,1024]{1,0:T(8,128)(2,1)S(1)}, f32[8,128,1]{2,1,0:T(8,128)S(1)}) custom-call(s32[1]{0:T(128)S(6)} %copy.12.valid_ref, s32[1]{0:T(128)S(6)} %copy.13.starts_ref, f32[8]{0:T(128)S(1)} %copy-done.9, bf16[128,1024]{1,0:T(8,128)(2,1)S(1)} %copy-done.1, f32[8,8,128]{2,1,0:T(8,128)S(1)} %get-tuple-element.21.norm_ref, ...), custom_call_target="tpu_custom_call" | custom-call | flops 33554432 | bytes 1904680 | tf_op jit(solution)/shard_map/spread/pallas_call | solution.py:22
  47.5 3.3 %project_far.1 = bf16[2,128,1024]{2,1,0:T(8,128)(2,1)S(1)} custom-call(s32[2]{0:T(128)S(1)} %pad_add_fusion.1.ids_ref, bf16[128,1024]{1,0:T(8,128)(2,1)S(1)} %get-tuple-element.19.mixed_ref, bf16[1024,4096]{1,0:T(8,128)(2,1)} %refs_3_.1), custom_call_target="tpu_custom_call" | custom-call | flops 536870912 | bytes 4194304 | tf_op jit(solution)/shard_map/project_far/pallas_call | solution.py:256
  50.8 1.4 %collective-permute-start.7 = (bf16[128,1024]{1,0:T(8,128)(2,1)S(1)}, bf16[128,1024]{1,0:T(8,128)(2,1)S(1)}, u32[]{:S(2)}, u32[]{:S(2)}) collective-permute-start(bf16[128,1024]{1,0:T(8,128)(2,1)S(1)} %get-tuple-element.32), channel_id=1, source_target_pairs={{1,3},{2,0},{5,7},{6,4},{9,11},{10,8},{13,15},{14,12},{17,19},{18,... | collective-permute-start | bytes 786440 | tf_op jit(solution)/shard_map/ppermute | solution.py:433
  52.3 3.3 %collective-permute-start.6 = (bf16[128,1024]{1,0:T(8,128)(2,1)S(1)}, bf16[128,1024]{1,0:T(8,128)(2,1)S(1)}, u32[]{:S(2)}, u32[]{:S(2)}) collective-permute-start(bf16[128,1024]{1,0:T(8,128)(2,1)S(1)} %get-tuple-element.32), channel_id=1, source_target_pairs={{0,3},{3,0},{4,7},{7,4},{8,11},{11,8},{12,15},{15,12},{16,19},{19,... | collective-permute-start | bytes 786440 | tf_op jit(solution)/shard_map/ppermute | solution.py:432
  55.5 1.9 %collective-permute-start.8 = (bf16[128,1024]{1,0:T(8,128)(2,1)S(1)}, bf16[128,1024]{1,0:T(8,128)(2,1)S(1)}, u32[]{:S(2)}, u32[]{:S(2)}) collective-permute-start(bf16[128,1024]{1,0:T(8,128)(2,1)S(1)} %get-tuple-element.33), channel_id=1, source_target_pairs={{0,1},{3,2},{4,5},{7,6},{8,9},{11,10},{12,13},{15,14},{16,17},{19,... | collective-permute-start | bytes 786440 | tf_op jit(solution)/shard_map/ppermute | solution.py:431
  57.4 3.3 %project_near.1 = bf16[2,128,1024]{2,1,0:T(8,128)(2,1)S(1)} custom-call(s32[2]{0:T(128)S(1)} %pad_add_fusion.ids_ref, bf16[128,1024]{1,0:T(8,128)(2,1)S(1)} %get-tuple-element.19.mixed_ref, bf16[1024,4096]{1,0:T(8,128)(2,1)} %refs_3_.1), custom_call_target="tpu_custom_call" | custom-call | flops 536870912 | bytes 4194304 | tf_op jit(solution)/shard_map/project_near/pallas_call | solution.py:256
  60.9 1.3 %collective-permute-start.16 = (bf16[4,144,128]{2,1,0:T(8,128)(2,1)S(1)}, bf16[4,144,128]{2,1,0:T(8,128)(2,1)S(1)}, u32[]{:S(2)}, u32[]{:S(2)}) collective-permute-start(bf16[4,144,128]{2,1,0:T(8,128)(2,1)S(1)} %pair.3), channel_id=1, source_target_pairs={{8,0},{12,4},{24,16},{28,20},{9,1},{13,5},{25,17},{29,21},{10,2},{... | collective-permute-start | bytes 442376 | tf_op jit(solution)/shard_map/ppermute | solution.py:368
  62.2 5.6 %collective-permute-done.8 = bf16[128,1024]{1,0:T(8,128)(2,1)S(1)} collective-permute-done((bf16[128,1024]{1,0:T(8,128)(2,1)S(1)}, bf16[128,1024]{1,0:T(8,128)(2,1)S(1)}, u32[]{:S(2)}, u32[]{:S(2)}) %collective-permute-start.8) | collective-permute-done | bytes 262176 | tf_op jit(solution)/shard_map/ppermute | solution.py:431
  67.8 1.3 %collective-permute-start.17 = (bf16[4,144,128]{2,1,0:T(8,128)(2,1)S(1)}, bf16[4,144,128]{2,1,0:T(8,128)(2,1)S(1)}, u32[]{:S(2)}, u32[]{:S(2)}) collective-permute-start(bf16[4,144,128]{2,1,0:T(8,128)(2,1)S(1)} %pair.3), channel_id=1, source_target_pairs={{16,0},{20,4},{24,8},{28,12},{17,1},{21,5},{25,9},{29,13},{18,2},{... | collective-permute-start | bytes 442376 | tf_op jit(solution)/shard_map/ppermute | solution.py:368
  69.8 5.0 %collective-permute-done.17.y_ref = bf16[4,144,128]{2,1,0:T(8,128)(2,1)S(1)} collective-permute-done((bf16[4,144,128]{2,1,0:T(8,128)(2,1)S(1)}, bf16[4,144,128]{2,1,0:T(8,128)(2,1)S(1)}, u32[]{:S(2)}, u32[]{:S(2)}) %collective-permute-start.17) | collective-permute-done | bytes 147488 | tf_op jit(solution)/shard_map/ppermute | solution.py:368
  74.8 1.3 %collective-permute-start.18 = (bf16[4,144,128]{2,1,0:T(8,128)(2,1)S(1)}, bf16[4,144,128]{2,1,0:T(8,128)(2,1)S(1)}, u32[]{:S(2)}, u32[]{:S(2)}) collective-permute-start(bf16[4,144,128]{2,1,0:T(8,128)(2,1)S(1)} %pair.3), channel_id=1, source_target_pairs={{24,0},{28,4},{16,8},{20,12},{25,1},{29,5},{17,9},{21,13},{26,2},{... | collective-permute-start | bytes 442376 | tf_op jit(solution)/shard_map/ppermute | solution.py:368
  76.1 6.6 %collective-permute-done.18.d_ref = bf16[4,144,128]{2,1,0:T(8,128)(2,1)S(1)} collective-permute-done((bf16[4,144,128]{2,1,0:T(8,128)(2,1)S(1)}, bf16[4,144,128]{2,1,0:T(8,128)(2,1)S(1)}, u32[]{:S(2)}, u32[]{:S(2)}) %collective-permute-start.18) | collective-permute-done | bytes 147488 | tf_op jit(solution)/shard_map/ppermute | solution.py:368
  82.9 3.6 %grads.1 = (bf16[128,1024]{1,0:T(8,128)(2,1)}, f32[128,1024]{1,0:T(8,128)S(1)}, f32[128,1024]{1,0:T(8,128)S(1)}) custom-call(s32[1]{0:T(128)S(6)} %copy.12.valid_ref, f32[8]{0:T(128)S(1)} %copy-done.9, bf16[128,1024]{1,0:T(8,128)(2,1)S(1)} %copy-done.1, bf16[128,1024]{1,0:T(8,128)(2,1)S(1)} %copy-done.4, bf16[128,1024]{1,0:T(8,128)(2,1)S(1)} %copy-done.7, ...), custom_call_target="tpu_custom_call" | custom-call | flops 201326592 | bytes 3444772 | tf_op jit(solution)/shard_map/grads/pallas_call | solution.py:22
  87.5 1.4 %last.1 = (bf16[128,1024]{1,0:T(8,128)(2,1)}, bf16[128,1024]{1,0:T(8,128)(2,1)}) custom-call(s32[1]{0:T(128)} %bitcast.2.pos_ref, s32[1]{0:T(128)S(6)} %copy.12.valid_ref, bf16[128,1024]{1,0:T(8,128)(2,1)S(1)} %copy-done.4, bf16[128,1024]{1,0:T(8,128)(2,1)S(1)} %copy-done.7, f32[8,136,128]{2,1,0:T(8,128)S(1)} %collective-permute-done.15.other_ref, ...), custom_call_target="tpu_custom_call" | custom-call | flops 134217728 | bytes 3211272 | tf_op jit(solution)/shard_map/last/pallas_call | solution.py:22
  (50 shorter events, 6.5 us)
Async XLA Ops:
  1.9 1.0 %copy-start.2 = (bf16[128,1024]{1,0:T(8,128)(2,1)S(1)}, bf16[128,1024]{1,0:T(8,128)(2,1)}, u32[]{:S(2)}) copy-start(bf16[128,1024]{1,0:T(8,128)(2,1)} %k_ref.7) | copy-start | bytes 786436
  2.9 0.9 %copy-start.5 = (bf16[128,1024]{1,0:T(8,128)(2,1)S(1)}, bf16[128,1024]{1,0:T(8,128)(2,1)}, u32[]{:S(2)}) copy-start(bf16[128,1024]{1,0:T(8,128)(2,1)} %v_ref.7) | copy-start | bytes 786436
  4.2 2.1 %collective-permute-start = (f32[8,136,128]{2,1,0:T(8,128)S(1)}, f32[8,136,128]{2,1,0:T(8,128)S(1)}, u32[]{:S(2)}, u32[]{:S(2)}) collective-permute-start(f32[8,136,128]{2,1,0:T(8,128)S(1)} %state.1.mine_ref), channel_id=1, source_target_pairs={{0,4},{4,0},{8,12},{12,8},{16,20},{20,16},{24,28},{28,24},{1,5},{5... | collective-permute-start | bytes 1671176 | tf_op jit(solution)/shard_map/ppermute | solution.py:353
  4.7 14.6 %collective-permute-start.10 = (bf16[128,1024]{1,0:T(8,128)(2,1)}, bf16[128,1024]{1,0:T(8,128)(2,1)S(1)}, u32[]{:S(2)}, u32[]{:S(2)}) collective-permute-start(bf16[128,1024]{1,0:T(8,128)(2,1)} %refs_0_.1), channel_id=1, source_target_pairs={{1,2},{2,1},{5,6},{6,5},{9,10},{10,9},{13,14},{14,13},{17,18},{18,... | collective-permute-start | bytes 786440 | tf_op jit(solution)/shard_map/ppermute | solution.py:407
  6.6 16.0 %collective-permute-start.1 = (bf16[4,144,128]{2,1,0:T(8,128)(2,1)S(1)}, bf16[4,144,128]{2,1,0:T(8,128)(2,1)S(1)}, u32[]{:S(2)}, u32[]{:S(2)}) collective-permute-start(bf16[4,144,128]{2,1,0:T(8,128)(2,1)S(1)} %pair.2), channel_id=1, source_target_pairs={{0,8},{4,12},{16,24},{20,28},{1,9},{5,13},{17,25},{21,29},{2,10},{... | collective-permute-start | bytes 442376 | tf_op jit(solution)/shard_map/ppermute | solution.py:368
  11.4 18.2 %collective-permute-start.2 = (bf16[4,144,128]{2,1,0:T(8,128)(2,1)S(1)}, bf16[4,144,128]{2,1,0:T(8,128)(2,1)S(1)}, u32[]{:S(2)}, u32[]{:S(2)}) collective-permute-start(bf16[4,144,128]{2,1,0:T(8,128)(2,1)S(1)} %pair.2), channel_id=1, source_target_pairs={{0,16},{4,20},{8,24},{12,28},{1,17},{5,21},{9,25},{13,29},{2,18},{... | collective-permute-start | bytes 442376 | tf_op jit(solution)/shard_map/ppermute | solution.py:368
  14.8 16.0 %collective-permute-start.3 = (bf16[4,144,128]{2,1,0:T(8,128)(2,1)S(1)}, bf16[4,144,128]{2,1,0:T(8,128)(2,1)S(1)}, u32[]{:S(2)}, u32[]{:S(2)}) collective-permute-start(bf16[4,144,128]{2,1,0:T(8,128)(2,1)S(1)} %pair.2), channel_id=1, source_target_pairs={{0,24},{4,28},{8,16},{12,20},{1,25},{5,29},{9,17},{13,21},{2,26},{... | collective-permute-start | bytes 442376 | tf_op jit(solution)/shard_map/ppermute | solution.py:368
  16.1 15.3 %collective-permute-start.12 = (bf16[128,1024]{1,0:T(8,128)(2,1)}, bf16[128,1024]{1,0:T(8,128)(2,1)S(1)}, u32[]{:S(2)}, u32[]{:S(2)}) collective-permute-start(bf16[128,1024]{1,0:T(8,128)(2,1)} %refs_0_.1), channel_id=1, source_target_pairs={{0,1},{1,0},{2,3},{3,2},{4,5},{5,4},{6,7},{7,6},{8,9},{9,8},{10,11... | collective-permute-start | bytes 786440 | tf_op jit(solution)/shard_map/ppermute | solution.py:408
  19.3 14.4 %collective-permute-start.13 = (bf16[128,1024]{1,0:T(8,128)(2,1)}, bf16[128,1024]{1,0:T(8,128)(2,1)S(1)}, u32[]{:S(2)}, u32[]{:S(2)}) collective-permute-start(bf16[128,1024]{1,0:T(8,128)(2,1)} %refs_0_.1), channel_id=1, source_target_pairs={{0,3},{3,0},{4,7},{7,4},{8,11},{11,8},{12,15},{15,12},{16,19},{19,... | collective-permute-start | bytes 786440 | tf_op jit(solution)/shard_map/ppermute | solution.py:409
  22.6 13.7 %collective-permute-start.14 = (bf16[128,1024]{1,0:T(8,128)(2,1)}, bf16[128,1024]{1,0:T(8,128)(2,1)S(1)}, u32[]{:S(2)}, u32[]{:S(2)}) collective-permute-start(bf16[128,1024]{1,0:T(8,128)(2,1)} %refs_0_.1), channel_id=1, source_target_pairs={{0,2},{3,1},{4,6},{7,5},{8,10},{11,9},{12,14},{15,13},{16,18},{19,... | collective-permute-start | bytes 786440 | tf_op jit(solution)/shard_map/ppermute | solution.py:410
  24.0 1.0 %copy-start = (bf16[128,1024]{1,0:T(8,128)(2,1)S(1)}, bf16[128,1024]{1,0:T(8,128)(2,1)}, u32[]{:S(2)}) copy-start(bf16[128,1024]{1,0:T(8,128)(2,1)} %q_ref.7) | copy-start | bytes 786436
  24.9 0.9 %copy-start.3 = (bf16[128,1024]{1,0:T(8,128)(2,1)S(1)}, bf16[128,1024]{1,0:T(8,128)(2,1)}, u32[]{:S(2)}) copy-start(bf16[128,1024]{1,0:T(8,128)(2,1)} %k_ref.7) | copy-start | bytes 786436
  25.9 0.9 %copy-start.6 = (bf16[128,1024]{1,0:T(8,128)(2,1)S(1)}, bf16[128,1024]{1,0:T(8,128)(2,1)}, u32[]{:S(2)}) copy-start(bf16[128,1024]{1,0:T(8,128)(2,1)} %v_ref.7) | copy-start | bytes 786436
  29.5 13.1 %collective-permute-start.11 = (bf16[128,1024]{1,0:T(8,128)(2,1)S(1)}, bf16[128,1024]{1,0:T(8,128)(2,1)S(1)}, u32[]{:S(2)}, u32[]{:S(2)}) collective-permute-start(bf16[128,1024]{1,0:T(8,128)(2,1)S(1)} %collective-permute-done.10.refs_0_), channel_id=1, source_target_pairs={{1,0},{2,3},{5,4},{6,7},{9,8},{10,11},{13,12},{14,15},{17,16},{18,... | collective-permute-start | bytes 786440 | tf_op jit(solution)/shard_map/ppermute | solution.py:411
  31.2 14.0 %collective-permute-start.4 = (f32[4,136,128]{2,1,0:T(8,128)S(1)}, f32[4,136,128]{2,1,0:T(8,128)S(1)}, u32[]{:S(2)}, u32[]{:S(2)}) collective-permute-start(f32[4,136,128]{2,1,0:T(8,128)S(1)} %join.2.own_ref), channel_id=1, source_target_pairs={{0,4},{4,0},{8,12},{12,8},{16,20},{20,16},{24,28},{28,24},{1,5},{5... | collective-permute-start | bytes 835592 | tf_op jit(solution)/shard_map/ppermute | solution.py:377
  31.3 13.8 %copy-start.9 = (f32[8]{0:T(128)S(1)}, f32[8]{0:T(128)}, u32[]{:S(2)}) copy-start(f32[8]{0:T(128)} %gate_ref.5) | copy-start | bytes 100
  31.4 13.7 %copy-start.1 = (bf16[128,1024]{1,0:T(8,128)(2,1)S(1)}, bf16[128,1024]{1,0:T(8,128)(2,1)}, u32[]{:S(2)}) copy-start(bf16[128,1024]{1,0:T(8,128)(2,1)} %q_ref.7) | copy-start | bytes 786436
  36.2 0.9 %copy-start.8 = (bf16[128,1024]{1,0:T(8,128)(2,1)S(1)}, bf16[128,1024]{1,0:T(8,128)(2,1)}, u32[]{:S(2)}) copy-start(bf16[128,1024]{1,0:T(8,128)(2,1)} %refs_0_.1) | copy-start | bytes 786436
  47.4 13.4 %collective-permute-start.15 = (f32[8,136,128]{2,1,0:T(8,128)S(1)}, f32[8,136,128]{2,1,0:T(8,128)S(1)}, u32[]{:S(2)}, u32[]{:S(2)}) collective-permute-start(f32[8,136,128]{2,1,0:T(8,128)S(1)} %get-tuple-element.27.mine_ref), channel_id=1, source_target_pairs={{0,4},{4,0},{8,12},{12,8},{16,20},{20,16},{24,28},{28,24},{1,5},{5... | collective-permute-start | bytes 1671176 | tf_op jit(solution)/shard_map/ppermute | solution.py:353
  50.8 32.2 %copy-start.4 = (bf16[128,1024]{1,0:T(8,128)(2,1)S(1)}, bf16[128,1024]{1,0:T(8,128)(2,1)}, u32[]{:S(2)}) copy-start(bf16[128,1024]{1,0:T(8,128)(2,1)} %k_ref.7) | copy-start | bytes 786436
  50.8 32.2 %copy-start.7 = (bf16[128,1024]{1,0:T(8,128)(2,1)S(1)}, bf16[128,1024]{1,0:T(8,128)(2,1)}, u32[]{:S(2)}) copy-start(bf16[128,1024]{1,0:T(8,128)(2,1)} %v_ref.7) | copy-start | bytes 786436
  50.8 35.7 %collective-permute-start.7 = (bf16[128,1024]{1,0:T(8,128)(2,1)S(1)}, bf16[128,1024]{1,0:T(8,128)(2,1)S(1)}, u32[]{:S(2)}, u32[]{:S(2)}) collective-permute-start(bf16[128,1024]{1,0:T(8,128)(2,1)S(1)} %get-tuple-element.32), channel_id=1, source_target_pairs={{1,3},{2,0},{5,7},{6,4},{9,11},{10,8},{13,15},{14,12},{17,19},{18,... | collective-permute-start | bytes 786440 | tf_op jit(solution)/shard_map/ppermute | solution.py:433
  52.3 34.3 %collective-permute-start.6 = (bf16[128,1024]{1,0:T(8,128)(2,1)S(1)}, bf16[128,1024]{1,0:T(8,128)(2,1)S(1)}, u32[]{:S(2)}, u32[]{:S(2)}) collective-permute-start(bf16[128,1024]{1,0:T(8,128)(2,1)S(1)} %get-tuple-element.32), channel_id=1, source_target_pairs={{0,3},{3,0},{4,7},{7,4},{8,11},{11,8},{12,15},{15,12},{16,19},{19,... | collective-permute-start | bytes 786440 | tf_op jit(solution)/shard_map/ppermute | solution.py:432
  55.5 12.3 %collective-permute-start.8 = (bf16[128,1024]{1,0:T(8,128)(2,1)S(1)}, bf16[128,1024]{1,0:T(8,128)(2,1)S(1)}, u32[]{:S(2)}, u32[]{:S(2)}) collective-permute-start(bf16[128,1024]{1,0:T(8,128)(2,1)S(1)} %get-tuple-element.33), channel_id=1, source_target_pairs={{0,1},{3,2},{4,5},{7,6},{8,9},{11,10},{12,13},{15,14},{16,17},{19,... | collective-permute-start | bytes 786440 | tf_op jit(solution)/shard_map/ppermute | solution.py:431
  60.7 25.9 %collective-permute-start.5 = (bf16[128,1024]{1,0:T(8,128)(2,1)S(1)}, bf16[128,1024]{1,0:T(8,128)(2,1)S(1)}, u32[]{:S(2)}, u32[]{:S(2)}) collective-permute-start(bf16[128,1024]{1,0:T(8,128)(2,1)S(1)} %slice_bitcast_fusion.2), channel_id=1, source_target_pairs={{0,1},{1,0},{2,3},{3,2},{4,5},{5,4},{6,7},{7,6},{8,9},{9,8},{10,11... | collective-permute-start | bytes 786440 | tf_op jit(solution)/shard_map/ppermute | solution.py:435
  60.9 8.2 %collective-permute-start.16 = (bf16[4,144,128]{2,1,0:T(8,128)(2,1)S(1)}, bf16[4,144,128]{2,1,0:T(8,128)(2,1)S(1)}, u32[]{:S(2)}, u32[]{:S(2)}) collective-permute-start(bf16[4,144,128]{2,1,0:T(8,128)(2,1)S(1)} %pair.3), channel_id=1, source_target_pairs={{8,0},{12,4},{24,16},{28,20},{9,1},{13,5},{25,17},{29,21},{10,2},{... | collective-permute-start | bytes 442376 | tf_op jit(solution)/shard_map/ppermute | solution.py:368
  67.8 7.0 %collective-permute-start.17 = (bf16[4,144,128]{2,1,0:T(8,128)(2,1)S(1)}, bf16[4,144,128]{2,1,0:T(8,128)(2,1)S(1)}, u32[]{:S(2)}, u32[]{:S(2)}) collective-permute-start(bf16[4,144,128]{2,1,0:T(8,128)(2,1)S(1)} %pair.3), channel_id=1, source_target_pairs={{16,0},{20,4},{24,8},{28,12},{17,1},{21,5},{25,9},{29,13},{18,2},{... | collective-permute-start | bytes 442376 | tf_op jit(solution)/shard_map/ppermute | solution.py:368
  69.1 17.5 %collective-permute-start.9 = (bf16[128,1024]{1,0:T(8,128)(2,1)S(1)}, bf16[128,1024]{1,0:T(8,128)(2,1)S(1)}, u32[]{:S(2)}, u32[]{:S(2)}) collective-permute-start(bf16[128,1024]{1,0:T(8,128)(2,1)S(1)} %fusion.4), channel_id=1, source_target_pairs={{1,2},{2,1},{5,6},{6,5},{9,10},{10,9},{13,14},{14,13},{17,18},{18,... | collective-permute-start | bytes 786440 | tf_op jit(solution)/shard_map/ppermute | solution.py:436
  74.8 7.9 %collective-permute-start.18 = (bf16[4,144,128]{2,1,0:T(8,128)(2,1)S(1)}, bf16[4,144,128]{2,1,0:T(8,128)(2,1)S(1)}, u32[]{:S(2)}, u32[]{:S(2)}) collective-permute-start(bf16[4,144,128]{2,1,0:T(8,128)(2,1)S(1)} %pair.3), channel_id=1, source_target_pairs={{24,0},{28,4},{16,8},{20,12},{25,1},{29,5},{17,9},{21,13},{26,2},{... | collective-permute-start | bytes 442376 | tf_op jit(solution)/shard_map/ppermute | solution.py:368
  82.8 4.7 %collective-permute-start.19 = (f32[4,136,128]{2,1,0:T(8,128)S(1)}, f32[4,136,128]{2,1,0:T(8,128)S(1)}, u32[]{:S(2)}, u32[]{:S(2)}) collective-permute-start(f32[4,136,128]{2,1,0:T(8,128)S(1)} %join.3.own_ref), channel_id=1, source_target_pairs={{0,4},{4,0},{8,12},{12,8},{16,20},{20,16},{24,28},{28,24},{1,5},{5... | collective-permute-start | bytes 835592 | tf_op jit(solution)/shard_map/ppermute | solution.py:377

commit v2 on v1

v2 whole, which is shorter than its diff:
```python
import functools

import jax
import jax.numpy as jnp
from jax import lax
from jax.experimental import pallas as pl
from jax.experimental.pallas import tpu as pltpu
from jax.sharding import PartitionSpec as P

DH = 128
ROWS = 136
SENT = 144
BF16 = jnp.bfloat16
F32 = jnp.float32
VMEM = pl.BlockSpec(memory_space=pltpu.VMEM)
SMEM = pl.BlockSpec(memory_space=pltpu.SMEM)


ANY = pl.BlockSpec(memory_space=pl.ANY)
DMA = pltpu.SemaphoreType.DMA


def call(kernel, outs, in_specs, args, flops=0, scratch=(), name=None):
    moved = sum(a.size * a.dtype.itemsize for a in args)
    moved += sum(o.size * o.dtype.itemsize for o in outs)
    return pl.pallas_call(
        kernel,
        out_shape=outs,
        in_specs=in_specs,
        out_specs=[VMEM] * len(outs),
        scratch_shapes=scratch,
        compiler_params=pltpu.CompilerParams(vmem_limit_bytes=24 * 1024 * 1024),
        cost_estimate=pl.CostEstimate(
            flops=flops, bytes_accessed=min(moved, 1 << 20), transcendentals=0
        ),
        name=name,
    )(*args)


def feature(x):
    return jnp.where(x > 0, x + 1.0, jnp.exp(jnp.minimum(x, 0.0)))


def slope(x):
    return jnp.where(x > 0, 1.0, jnp.where(x == 0, 0.5, jnp.exp(jnp.minimum(x, 0.0))))


def sigmoid(x):
    return 1.0 / (1.0 + jnp.exp(-x))


def dot(a, b, dims):
    return lax.dot_general(a, b, (dims, ((), ())), preferred_element_type=F32)


NN = ((1,), (0,))
NT = ((1,), (1,))
TN = ((0,), (0,))


def live_rows(info_ref, heads, length):
    where = lax.broadcasted_iota(jnp.int32, (length, 1), 0).astype(F32)
    return (where < info_ref[heads + 1 : heads + 2, 0:1]).astype(F32)


def head(ref, h):
    return ref[:, h * DH : (h + 1) * DH]


def tail(rows, *values):
    where = lax.broadcasted_iota(jnp.int32, (rows, DH), 0)
    out = jnp.zeros((rows, DH), F32)
    for at, value in enumerate(values):
        out = jnp.where(where == at, value, out)
    return out


def split(x):
    top = x.astype(BF16)
    rest = x - top.astype(F32)
    return top, rest.astype(BF16)


def load_kernel(
    heads, q_in, k_in, v_in, grad_in, valid_in, starts_in, gate_in,
    q_ref, k_ref, v_ref, grad_ref, info_ref, state_ref, valid_ref, starts_ref, gate_ref, sems,
):
    pairs = [(valid_in, valid_ref), (starts_in, starts_ref), (gate_in, gate_ref), (k_in, k_ref),
             (v_in, v_ref), (q_in, q_ref), (grad_in, grad_ref)]
    copies = [pltpu.make_async_copy(a, b, sems.at[i]) for i, (a, b) in enumerate(pairs)]
    for copy in copies:
        copy.start()
    for copy in copies[:3]:
        copy.wait()
    opened = 1.0 - starts_ref[0].astype(F32)
    valid = valid_ref[0].astype(F32)
    rows = [sigmoid(jnp.full((1, DH), gate_ref[h], F32)) for h in range(heads)]
    info_ref[...] = tail(heads + 8, *rows, opened, valid)
    live = live_rows(info_ref, heads, k_ref.shape[0])
    for copy in copies[3:5]:
        copy.wait()
    for h in range(heads):
        sig = (feature(head(k_ref, h).astype(F32)) * live).astype(BF16)
        state_ref[h, 0:DH, :] = dot(sig, head(v_ref, h), TN)
        norm = jnp.sum(sig.astype(F32), axis=0, keepdims=True)
        state_ref[h, DH:ROWS, :] = tail(ROWS - DH, norm, opened)
    for copy in copies[5:]:
        copy.wait()


def pair_kernel(heads, forward, pos_ref, mine_ref, other_ref, *refs):
    sent_ref = refs[-1]
    half = lax.rem(pos_ref[0], 2)
    lower = half == 0
    for i in range(heads // 2):
        h = half * (heads // 2) + i
        mine, other = mine_ref[h], other_ref[h]
        first = jnp.where(lower, mine, other)
        second = jnp.where(lower, other, mine)
        open_first, open_second = first[DH + 1 : DH + 2], second[DH + 1 : DH + 2]
        if forward:
            total = open_second * first + second
        else:
            total = open_first * (first + open_second * second)
        memory, norm = total[0:DH], total[DH : DH + 1]
        norm_1, rest = split(norm)
        norm_1 = norm_1.astype(F32)
        norm_2 = rest.astype(F32)
        norm_3 = norm - norm_1 - norm_2
        if forward:
            weight = jnp.maximum(jnp.sum(norm, axis=1, keepdims=True), 1e-30)
            centre = jnp.sum(memory, axis=0, keepdims=True) / weight
            centre = centre.astype(BF16).astype(F32)
            norms = tail(16, norm_1, norm_2, norm_3).astype(BF16)
            centres = tail(16, centre, centre, centre).astype(BF16)
            memory = memory - dot(norms, centres, TN)
        else:
            centre = jnp.zeros_like(norm)
        sent_ref[i, 0:DH, :] = memory.astype(BF16)
        rows = tail(SENT - DH, norm_1, norm_2, norm_3, centre, open_first * open_second)
        sent_ref[i, DH:SENT, :] = rows.astype(BF16)


def join_kernel(heads, forward, pos_ref, x_ref, y_ref, d_ref, *refs):
    carry_ref = refs[-1]
    chip = pos_ref[0] // 2
    place = chip if forward else 3 - chip
    for i in range(heads // 2):
        totals = []
        for ref in (x_ref, y_ref, d_ref):
            memory = ref[i, 0:DH, :].astype(F32)
            rows = ref[i, DH:SENT, :].astype(F32)
            norm = rows[0:1] + rows[1:2] + rows[2:3]
            if forward:
                norms = tail(16, rows[0:1], rows[1:2], rows[2:3]).astype(BF16)
                centres = tail(16, rows[3:4], rows[3:4], rows[3:4]).astype(BF16)
                memory = memory + dot(norms, centres, TN)
            totals.append((memory, norm, rows[4:5]))
        (x_mem, x_norm, x_open), (y_mem, y_norm, y_open), (d_mem, d_norm, d_open) = totals
        odd, high = lax.rem(place, 2) == 1, place >= 2
        on_x = jnp.where(odd, jnp.ones_like(x_open), 0.0)
        on_y = jnp.where(high, jnp.where(odd, x_open, d_open), 0.0)
        on_d = jnp.where(high, jnp.where(odd, x_open * y_open, 1.0), 0.0)
        norm = on_x * x_norm + on_y * y_norm + on_d * d_norm
        carry_ref[i, 0:DH, :] = on_x * x_mem + on_y * y_mem + on_d * d_mem
        carry_ref[i, DH:ROWS, :] = tail(ROWS - DH, norm)


def local_kernel(heads, info_ref, q_ref, k_ref, v_ref, after_ref, probs_ref, local_ref):
    length = q_ref.shape[0]
    row = lax.broadcasted_iota(jnp.int32, (length, length), 0)
    col = lax.broadcasted_iota(jnp.int32, (length, length), 1)
    allowed = (col <= row) & (col.astype(F32) < info_ref[heads + 1 : heads + 2, 0:1])
    for h in range(heads):
        scores = dot(head(q_ref, h), head(k_ref, h), NT) * DH ** (-0.5)
        scores = jnp.where(allowed, scores, -1e30)
        expo = jnp.exp(scores - jnp.max(scores, axis=1, keepdims=True))
        probs = (expo / jnp.sum(expo, axis=1, keepdims=True)).astype(BF16)
        probs_ref[h] = probs
        local_ref[:, h * DH : (h + 1) * DH] = dot(probs, head(v_ref, h), NN)


def fetch(weight_ref, ids_ref, slots, sems, rows, row_at=0):
    cols = slots.shape[-1]
    copies = []
    for s in range(slots.shape[0]):
        first = pl.multiple_of(ids_ref[s] * cols, DH)
        source = weight_ref.at[pl.ds(row_at, rows), pl.ds(first, cols)]
        copies.append(pltpu.make_async_copy(source, slots.at[s, pl.ds(row_at, rows)], sems.at[s]))
    for copy in copies:
        copy.start()
    return copies


def read_kernel(
    heads, project, pos_ref, ids_ref, info_ref, q_ref, mine_ref, other_ref, own_ref, far_ref,
    local_ref, *refs,
):
    if project:
        weight_ref, mixed_ref, read_ref, memory_ref, norm_ref, first_ref, slots, sems = refs
        (copy,) = fetch(weight_ref, ids_ref, slots, sems, weight_ref.shape[0])
    else:
        mixed_ref, read_ref, memory_ref, norm_ref = refs
    live = live_rows(info_ref, heads, q_ref.shape[0])
    upper = lax.rem(pos_ref[0], 2) == 1
    for h in range(heads):
        i, part = h % (heads // 2), h // (heads // 2)
        own_here = upper if part else jnp.logical_not(upper)
        carry = jnp.where(own_here, own_ref[i], far_ref[i])
        other = other_ref[h]
        before = jnp.where(upper, other[DH + 1 : DH + 2] * carry + other, carry)
        state = mine_ref[h, DH + 1 : DH + 2, :] * before
        memory, norm = state[0:DH], state[DH : DH + 1]
        parts = jnp.concatenate(split(memory), axis=1)
        memory_ref[h] = parts
        norm_ref[h] = jnp.broadcast_to(norm, (8, DH))
        sig = feature(head(q_ref, h).astype(F32)).astype(BF16)
        numer = dot(sig, parts, NN)
        numer = numer[:, 0:DH] + numer[:, DH:]
        denom = jnp.sum(sig.astype(F32) * norm, axis=1, keepdims=True) + 1.0
        read = numer / denom
        gate = info_ref[h : h + 1, :]
        mixed = live * (gate * read + (1.0 - gate) * head(local_ref, h))
        read_ref[:, h * DH : (h + 1) * DH] = read
        mixed_ref[:, h * DH : (h + 1) * DH] = mixed.astype(BF16)
    if project:
        copy.wait()
        first_ref[...] = dot(mixed_ref[...], slots[0], NN).astype(BF16)


def own_kernel(ids_ref, grad_ref, weight_ref, after_ref, total_ref, slots, sems):
    (copy,) = fetch(weight_ref, ids_ref, slots, sems, weight_ref.shape[0])
    copy.wait()
    total_ref[...] = dot(grad_ref[...], slots[0], NT)


def add_kernel(ids_ref, mixed_ref, weight_ref, more_ref, after_ref, out_ref, slots, sems):
    (copy,) = fetch(weight_ref, ids_ref, slots, sems, weight_ref.shape[0])
    copy.wait()
    part = dot(mixed_ref[...], slots[0], NN)
    out_ref[...] = (part + more_ref[...].astype(F32)).astype(BF16)


def rest_kernel(ids_ref, mixed_ref, weight_ref, after_ref, near_ref, own_ref, slots, sems):
    copies = fetch(weight_ref, ids_ref, slots, sems, weight_ref.shape[0])
    copies[0].wait()
    near_ref[...] = dot(mixed_ref[...], slots[0], NN).astype(BF16)
    copies[1].wait()
    own_ref[...] = dot(mixed_ref[...], slots[1], NN)


def spread_kernel(heads, blocks, ids_ref, info_ref, q_ref, norm_ref, read_ref, *refs):
    if blocks:
        parts, (total_ref, weight_ref) = refs[:blocks], refs[blocks : blocks + 2]
        refs = refs[blocks + 2 :]
        passed_ref, numer_ref, denom_ref, grad_ref, slots, sems = refs
        rows = 2 * DH
        copies = [
            fetch(weight_ref, ids_ref, slots, sems.at[at], rows, at * rows)
            for at in range(heads // 2)
        ]
    else:
        grad_ref, passed_ref, numer_ref, denom_ref = refs
    live = live_rows(info_ref, heads, q_ref.shape[0])
    opened = info_ref[heads : heads + 1, :]
    for h in range(heads):
        cut = slice(h * DH, (h + 1) * DH)
        if blocks and h % 2 == 0:
            wide = slice(h * DH, (h + 2) * DH)
            total = total_ref[:, wide]
            for s in range(blocks):
                copies[h // 2][s].wait()
                total = total + dot(parts[s][...], slots[s, h * DH : (h + 2) * DH, :], NT)
            grad_ref[:, wide] = total.astype(BF16)
        sig = feature(head(q_ref, h).astype(F32)).astype(BF16)
        sig_full = sig.astype(F32)
        denom = jnp.sum(sig_full * norm_ref[h, 0:1, :], axis=1, keepdims=True) + 1.0
        gate = info_ref[h : h + 1, :]
        numer_grad = (head(grad_ref, h).astype(F32) * gate * (live / denom)).astype(BF16)
        denom_grad = -jnp.sum(
            numer_grad.astype(F32) * head(read_ref, h), axis=1, keepdims=True
        )
        passed_ref[h, 0:DH, :] = dot(sig, numer_grad, TN)
        norm_grad = jnp.sum(sig_full * denom_grad, axis=0, keepdims=True)
        passed_ref[h, DH:ROWS, :] = tail(ROWS - DH, norm_grad, opened)
        numer_ref[:, cut] = numer_grad
        denom_ref[h] = denom_grad


def grads_kernel(heads, info_ref, q_ref, k_ref, v_ref, probs_ref, grad_ref, numer_ref,
                 denom_ref, memory_ref, norm_ref, after_ref, query_ref, key_ref, value_ref):
    length = q_ref.shape[0]
    live = live_rows(info_ref, heads, length)
    for h in range(heads):
        cut = slice(h * DH, (h + 1) * DH)
        q, k, v = head(q_ref, h), head(k_ref, h), head(v_ref, h)
        gate = info_ref[h : h + 1, :]
        grad = (head(grad_ref, h).astype(F32) * (1.0 - gate) * live).astype(BF16)
        probs = probs_ref[h]
        probs_grad = dot(grad, v, NT)
        full = probs.astype(F32)
        mean = jnp.sum(full * probs_grad, axis=1, keepdims=True)
        scores_grad = (full * (probs_grad - mean) * DH ** (-0.5)).astype(BF16)
        key_ref[:, cut] = dot(scores_grad, q, TN)
        value_ref[:, cut] = dot(probs, grad, TN)
        parts = memory_ref[h]
        numer = head(numer_ref, h)
        sig_grad = dot(numer, parts[:, 0:DH], NT) + dot(numer, parts[:, DH:], NT)
        sig_grad = sig_grad + denom_ref[h] * norm_ref[h, 0:1, :]
        total = dot(scores_grad, k, NN) + sig_grad * slope(q.astype(F32))
        query_ref[:, cut] = total.astype(BF16)


def last_kernel(heads, pos_ref, info_ref, k_ref, v_ref, other_ref, own_ref, far_ref, key_ref,
                value_ref, key_out, value_out):
    live = live_rows(info_ref, heads, k_ref.shape[0])
    upper = lax.rem(pos_ref[0], 2) == 1
    for h in range(heads):
        cut = slice(h * DH, (h + 1) * DH)
        i, part = h % (heads // 2), h // (heads // 2)
        own_here = upper if part else jnp.logical_not(upper)
        carry = jnp.where(own_here, own_ref[i], far_ref[i])
        other = other_ref[h]
        back = jnp.where(upper, carry, other[DH + 1 : DH + 2] * (other + carry))
        memory, norm = back[0:DH], back[DH : DH + 1]
        top, low = split(memory)
        k, v = head(k_ref, h).astype(F32), head(v_ref, h)
        sig = (feature(k) * live).astype(BF16)
        sig_grad = (dot(v, top, NT) + dot(v, low, NT) + norm) * live
        key_out[:, cut] = (key_ref[:, cut] + sig_grad * slope(k)).astype(BF16)
        more = dot(sig, jnp.concatenate([top, low], axis=1), NN)
        value_out[:, cut] = (value_ref[:, cut] + more[:, 0:DH] + more[:, DH:]).astype(BF16)


def weighted(state, forward):
    count, mine = lax.axis_size("seq"), lax.axis_index("seq")
    states = lax.all_gather(state, "seq")
    total = jnp.zeros_like(state)
    weight = jnp.ones((), F32)

    def turn(step, carried):
        total, weight = carried
        at = mine - 1 - step if forward else mine + 1 + step
        inside = (at >= 0) & (at < count)
        one = lax.dynamic_index_in_dim(states, jnp.clip(at, 0, count - 1), keepdims=False)
        opened = one[0, DH + 1, 0]
        here = weight if forward else weight * opened
        total = jnp.where(inside, total + here * one, total)
        return total, weight * opened

    return lax.fori_loop(0, count - 1, turn, (total, weight))[0]


def scan_states(state, pos, heads, forward, before_pair, before_join):
    count = lax.axis_size("seq")
    if count != 8:
        before_pair()
        before_join(state)
        carry = weighted(state, forward)
        place = jnp.full_like(pos, 0 if forward else 1)
        own, far = carry[: heads // 2], carry[heads // 2 :]
        return (own, far, state, place) if forward else (far, own, state, place)
    pairs = [(s, s ^ 1) for s in range(count)]
    other = lax.ppermute(state, "seq", pairs)
    flops = heads * DH * DH * 40
    after = before_pair()
    sent = call(
        functools.partial(pair_kernel, heads, forward),
        [jax.ShapeDtypeStruct((heads // 2, SENT, DH), BF16)],
        [SMEM, VMEM, VMEM] + [ANY] * len(after),
        [pos, state, other, *after],
        flops,
        name="pair",
    )[0]
    arrived = [
        lax.ppermute(sent, "seq", [(s, s ^ way) for s in range(count)]) for way in (6, 2, 4)
    ]
    after = before_join(sent)
    own = call(
        functools.partial(join_kernel, heads, forward),
        [jax.ShapeDtypeStruct((heads // 2, ROWS, DH), F32)],
        [SMEM, VMEM, VMEM, VMEM] + [ANY] * len(after),
        [pos, arrived[1], arrived[2], arrived[0], *after],
        flops,
        name="join",
    )[0]
    far = lax.ppermute(own, "seq", pairs)
    return own, far, other, pos


def shards(queries, keys, values, gate, out_weight, out_grad, valid, starts):
    length, width = queries.shape
    heads = width // DH
    cols = out_grad.shape[1]
    groups = lax.axis_size("head")
    direct = groups == 4
    pos = lax.axis_index("seq").astype(jnp.int32).reshape(1)
    z = lax.axis_index("head").astype(jnp.int32)
    flat = jax.ShapeDtypeStruct((length, width), F32)
    low = jax.ShapeDtypeStruct((length, width), BF16)
    part_low = jax.ShapeDtypeStruct((length, cols), BF16)
    part_full = jax.ShapeDtypeStruct((length, cols), F32)
    states = jax.ShapeDtypeStruct((heads, ROWS, DH), F32)
    square = 2 * heads * length * DH * DH
    block = 2 * length * width * cols

    def ids(*ways):
        return jnp.stack([z ^ way for way in ways])

    def slots(count):
        return pltpu.VMEM((count, width, cols), BF16)

    queries, keys, values, grad_here, info, state = call(
        functools.partial(load_kernel, heads),
        [low, low, low, part_low, jax.ShapeDtypeStruct((heads + 8, DH), F32), states],
        [ANY] * 7,
        [queries, keys, values, out_grad, valid, starts, gate], square,
        [pltpu.SMEM((1,), jnp.int32), pltpu.SMEM((1,), jnp.int32), pltpu.SMEM((heads,), F32),
         DMA((7,))],
        name="load",
    )

    def swap(array, way):
        return lax.ppermute(array, "head", [(s, s ^ way) for s in range(groups)])

    if direct:
        grad_3 = swap(grad_here, 3)
        grad_1 = swap(grad_here, 1)
        grad_2 = swap(grad_3, 1)

    kept = {}

    def beside_forward(sent):
        kept["local"] = call(
            functools.partial(local_kernel, heads),
            [jax.ShapeDtypeStruct((heads, length, length), BF16), flat],
            [VMEM] * 4 + [ANY],
            [info, queries, keys, values, sent], 2 * square, name="local",
        )
        if not direct:
            return []
        kept["total"] = call(
            own_kernel, [flat], [SMEM, VMEM, ANY, ANY],
            [ids(0), grad_here, out_weight, kept["local"][0]], block, [slots(1), DMA((1,))],
            name="unproject_own",
        )[0]
        return [kept["total"]]

    own, far, other, place = scan_states(state, pos, heads, True, lambda: [], beside_forward)
    probs, local = kept["local"]
    read_outs = [low, flat, jax.ShapeDtypeStruct((heads, DH, 2 * DH), BF16),
                 jax.ShapeDtypeStruct((heads, 8, DH), F32)]
    outs = call(
        functools.partial(read_kernel, heads, direct),
        read_outs + [part_low] * direct,
        [SMEM, SMEM] + [VMEM] * 7 + [ANY] * direct,
        [place, ids(2), info, queries, state, other, own, far, local] + [out_weight] * direct,
        2 * square + block * direct,
        [slots(1), DMA((1,))] if direct else [],
        name="read",
    )
    mixed, read, memory, norm = outs[:4]
    if direct:
        sum_2 = swap(outs[4], 1)
        grads_in = [grad_1, grad_3, grad_2, kept["total"], out_weight]
    else:
        part = dot(mixed, out_weight, NN)
        output = lax.psum_scatter(part, "head", scatter_dimension=1, tiled=True).astype(BF16)
        whole = lax.all_gather(out_grad, "head", axis=1, tiled=True)
        grads_in = [dot(whole, out_weight, NT).astype(BF16)]
    outs = call(
        functools.partial(spread_kernel, heads, 3 * direct),
        [states, low, jax.ShapeDtypeStruct((heads, length, 1), F32)] + [low] * direct,
        [SMEM] + [VMEM] * 4 + ([VMEM] * 4 + [ANY] if direct else [VMEM]),
        [ids(1, 3, 2), info, queries, norm, read, *grads_in],
        square + 3 * block * direct,
        [slots(3), DMA((heads // 2, 3))] if direct else [],
        name="spread",
    )
    passed, numer_grad, denom_grad = outs[:3]
    mixed_grad = outs[3] if direct else grads_in[0]

    def add_here():
        if not direct:
            return []
        kept["sum_3"] = call(
            add_kernel, [part_low], [SMEM, VMEM, ANY, VMEM, ANY],
            [ids(3), mixed, out_weight, sum_2, passed], block, [slots(1), DMA((1,))],
            name="project_add",
        )[0]
        kept["from_3"] = swap(kept["sum_3"], 3)
        return [kept["sum_3"]]

    def beside_back(sent):
        after = sent
        if direct:
            near, kept["own"] = call(
                rest_kernel, [part_low, part_full], [SMEM, VMEM, ANY, ANY],
                [ids(1, 0), mixed, out_weight, sent], 2 * block, [slots(2), DMA((2,))],
                name="project_rest",
            )
            kept["from_1"] = swap(near, 1)
            after = near
        kept["grads"] = call(
            functools.partial(grads_kernel, heads),
            [low, flat, flat],
            [VMEM] * 10 + [ANY],
            [info, queries, keys, values, probs, mixed_grad, numer_grad, denom_grad, memory, norm,
             after],
            6 * square, name="grads",
        )
        return [kept["grads"][1]]

    own, far, other, place = scan_states(passed, pos, heads, False, add_here, beside_back)
    query_grad, key_part, value_part = kept["grads"]
    if direct:
        output = kept["own"] + kept["from_1"].astype(F32) + kept["from_3"].astype(F32)
        output = output.astype(BF16)
    key_grad, value_grad = call(
        functools.partial(last_kernel, heads),
        [low, low],
        [SMEM] + [VMEM] * 8,
        [place, info, keys, values, other, own, far, key_part, value_part], 4 * square, name="last",
    )
    return (output, query_grad, key_grad, value_grad)


def solution(mesh):
    placed = (
        P("seq", "head"),
        P("seq", "head"),
        P("seq", "head"),
        P("head"),
        P("head", None),
        P("seq", "head"),
        P("seq"),
        P("seq"),
    )
    return jax.shard_map(
        shards,
        mesh=mesh,
        in_specs=placed,
        out_specs=(P("seq", "head"), P("seq", "head"), P("seq", "head"), P("seq", "head")),
        check_vma=False,
    )
```

time: 89.7 us -> 82.9 us (0.924)
  starting transfers between devices: 31.1 us -> 16.9 us
  local copies, waits for them, and re-layouts: 5.77 us -> 18 us
  waiting for transfers between devices: 23 us -> 19.6 us
    pallas_call x4 -> x0, Pallas kernels: 14.4 us -> none  [the longest x2 7.85 us: unproject(): pl.pallas_call(functools.partial(unproject_kernel, blocks, before is None...]
    ppermute x16 -> x12, starting transfers between devices: 30.4 us -> 16.2 us  [the longest x6 9.09 us: swap(): return lax.ppermute(array, 'head', [(s, s ^ way) for s in range(groups)])]
    pallas_call x10 -> x13, Pallas kernels: 11.1 us -> 24.8 us  [call(): pl.pallas_call(kernel, out_shape=outs, in_specs=in_specs, out_specs=[VMEM...]
    unnamed x20 -> x22, local copies, waits for them, and re-layouts: 5.71 us -> 18 us
    ppermute x16 -> x12, waiting for transfers between devices: 22.1 us -> 19.6 us  [the longest x6 16.4 us: swap(): return lax.ppermute(array, 'head', [(s, s ^ way) for s in range(groups)])]
    ppermute x2, waiting for transfers between devices: 0.91 us -> 0.01 us  [scan_states(): other = lax.ppermute(state, 'seq', pairs)]
  transfers between devices with their start and end apart: 20 -> 16, of which waited for: 6 -> 5; matrix products, arithmetic and copies ran while one was open for 1% -> 1% of each run, Pallas kernels for 24% -> 18%
where the time goes in v2:
time: 82.9 us; the launch traced here: 82.4 us
  Pallas kernels  24.8 us (30%)
  waiting for transfers between devices  19.6 us (24%)
  local copies, waits for them, and re-layouts  18 us (22%)
  starting transfers between devices  16.9 us (20%)
  between operations  2.13 us (3%)
  other arithmetic  0.96 us (1%)
    pallas_call x13, Pallas kernels, call(): pl.pallas_call(kernel, out_shape=outs, in_specs=in_specs, out_specs=[VMEM...  24.8 us
    unnamed x22, local copies, waits for them, and re-layouts  18 us
    ppermute x6, waiting for transfers between devices, swap(): return lax.ppermute(array, 'head', [(s, s ^ way) for s in range(groups)])  16.4 us
    ppermute x6, starting transfers between devices, swap(): return lax.ppermute(array, 'head', [(s, s ^ way) for s in range(groups)])  9.09 us
    ppermute x6, starting transfers between devices, scan_states(): lax.ppermute(sent, 'seq', [(s, s ^ way) for s in range(count)])  7.11 us
    ppermute x6, waiting for transfers between devices, scan_states(): lax.ppermute(sent, 'seq', [(s, s ^ way) for s in range(count)])  3.2 us
  transfers between devices with their start and end apart: 16, of which 5 were waited for; matrix products, arithmetic and copies ran while one was open for 1% of the time, Pallas kernels for 18%

profile of v2, /device:TPU:0, one launch (start us, length us, event | category | flops | bytes accessed | tf_op | source)
XLA Modules:
  0.0 82.4 jit_solution(10977271266046357181)
XLA Ops:
  1.9 0.9 %copy-done.4 = bf16[128,1024]{1,0:T(8,128)(2,1)S(1)} copy-done((bf16[128,1024]{1,0:T(8,128)(2,1)S(1)}, bf16[128,1024]{1,0:T(8,128)(2,1)}, u32[]{:S(2)}) %copy-start.4) | copy-done | bytes 262168
  2.9 0.9 %copy-done.5 = bf16[128,1024]{1,0:T(8,128)(2,1)S(1)} copy-done((bf16[128,1024]{1,0:T(8,128)(2,1)S(1)}, bf16[128,1024]{1,0:T(8,128)(2,1)}, u32[]{:S(2)}) %copy-start.5) | copy-done | bytes 262168
  3.8 0.9 %copy-done.6 = bf16[128,1024]{1,0:T(8,128)(2,1)S(1)} copy-done((bf16[128,1024]{1,0:T(8,128)(2,1)S(1)}, bf16[128,1024]{1,0:T(8,128)(2,1)}, u32[]{:S(2)}) %copy-start.6) | copy-done | bytes 262168
  4.8 0.9 %copy-done.7 = bf16[128,1024]{1,0:T(8,128)(2,1)S(1)} copy-done((bf16[128,1024]{1,0:T(8,128)(2,1)S(1)}, bf16[128,1024]{1,0:T(8,128)(2,1)}, u32[]{:S(2)}) %copy-start.7) | copy-done | bytes 262168
  5.7 0.7 copy-done.8
  6.4 1.7 %load.1 = (bf16[128,1024]{1,0:T(8,128)(2,1)S(1)}, bf16[128,1024]{1,0:T(8,128)(2,1)S(1)}, bf16[128,1024]{1,0:T(8,128)(2,1)S(1)}, bf16[128,1024]{1,0:T(8,128)(2,1)...) custom-call(bf16[128,1024]{1,0:T(8,128)(2,1)S(1)} %copy-done.4, bf16[128,1024]{1,0:T(8,128)(2,1)S(1)} %copy-done.5, ...), custom_call_target="tpu_custom_call" | custom-call | flops 33554432 | bytes 1048576 | tf_op jit(solution)/shard_map/load/pallas_call | solution.py:26
  8.7 4.7 %collective-permute-start.6 = (bf16[128,1024]{1,0:T(8,128)(2,1)}, bf16[128,1024]{1,0:T(8,128)(2,1)}, u32[]{:S(2)}, u32[]{:S(2)}) collective-permute-start(bf16[128,1024]{1,0:T(8,128)(2,1)} %get-tuple-element.31.grad_ref), channel_id=1, source_target_pairs={{0,3},{1,2},{2,1},{3,0},{4,7},{5,6},{6,5},{7,4},{8,11},{9,10},{10,... | collective-permute-start | bytes 786440 | tf_op jit(solution)/shard_map/ppermute | solution.py:424
  13.6 1.6 %collective-permute-start.1 = (bf16[4,144,128]{2,1,0:T(8,128)(2,1)S(1)}, bf16[4,144,128]{2,1,0:T(8,128)(2,1)}, u32[]{:S(2)}, u32[]{:S(2)}) collective-permute-start(bf16[4,144,128]{2,1,0:T(8,128)(2,1)S(1)} %pair.2.after_ref), channel_id=1, source_target_pairs={{0,8},{4,12},{8,0},{12,4},{16,24},{20,28},{24,16},{28,20},{1,9},{5... | collective-permute-start | bytes 442376 | tf_op jit(solution)/shard_map/ppermute | solution.py:376
  15.1 1.5 %collective-permute-start.2 = (bf16[4,144,128]{2,1,0:T(8,128)(2,1)S(1)}, bf16[4,144,128]{2,1,0:T(8,128)(2,1)}, u32[]{:S(2)}, u32[]{:S(2)}) collective-permute-start(bf16[4,144,128]{2,1,0:T(8,128)(2,1)S(1)} %pair.2.after_ref), channel_id=1, source_target_pairs={{0,16},{4,20},{8,24},{12,28},{16,0},{20,4},{24,8},{28,12},{1,17},{... | collective-permute-start | bytes 442376 | tf_op jit(solution)/shard_map/ppermute | solution.py:376
  17.1 2.7 %local.1 = (bf16[8,128,128]{2,1,0:T(8,128)(2,1)S(1)}, f32[128,1024]{1,0:T(8,128)S(1)}) custom-call(f32[16,128]{1,0:T(8,128)S(1)} %get-tuple-element.28.info_ref, bf16[128,1024]{1,0:T(8,128)(2,1)S(1)} %get-tuple-element.29.q_ref, bf16[128,1024]{1,0:T(8,128)(2,1)S(1)} %get-tuple-element.32.k_ref, bf16[128,1024]{1,0:T(8,128)(2,1)S(1)} %get-tuple-element.33.v_ref, ...), custom_call_target="tpu_custom_call" | custom-call | flops 67108864 | bytes 1048576 | tf_op jit(solution)/shard_map/local/pallas_call | solution.py:26
  19.8 3.4 %copy-done = bf16[1024,4096]{1,0:T(8,128)(2,1)S(1)} copy-done((bf16[1024,4096]{1,0:T(8,128)(2,1)S(1)}, bf16[1024,4096]{1,0:T(8,128)(2,1)}, u32[]{:S(2)}) %copy-start) | copy-done | bytes 8388632
  23.2 2.1 %unproject_own.1.refs_0_.refs_3_ = f32[128,1024]{1,0:T(8,128)S(1)} custom-call(s32[1]{0:T(128)} %bitcast.1.ids_ref, bf16[128,1024]{1,0:T(8,128)(2,1)} %get-tuple-element.31.grad_ref, bf16[1024,4096]{1,0:T(8,128)(2,1)S(1)} %copy-done, bf16[8,128,128]{2,1,0:T(8,128)(2,1)S(1)} %get-tuple-element.34.after_ref.probs_ref), custom_call_target="tpu_custom_call" | custom-call | flops 268435456 | bytes 1048576 | tf_op jit(solution)/shard_map/unproject_own/pallas_call | solution.py:26
  25.3 1.4 %join.2.own_ref = f32[4,136,128]{2,1,0:T(8,128)S(1)} custom-call(s32[1]{0:T(128)} %bitcast.2.pos_ref, bf16[4,144,128]{2,1,0:T(8,128)(2,1)} %collective-permute-done.1.x_ref, bf16[4,144,128]{2,1,0:T(8,128)(2,1)} %collective-permute-done.2.y_ref, bf16[4,144,128]{2,1,0:T(8,128)(2,1)} %collective-permute-done.3.d_ref, f32[128,1024]{1,0:T(8,128)S(1)} %unproject_own.1.refs_0_.refs_3_), custom_call_target="tpu_custom_call" | custom-call | flops 5242880 | bytes 1048576 | tf_op jit(solution)/shard_map/join/pallas_call | solution.py:26
  26.9 2.0 %collective-permute-start.7 = (bf16[128,1024]{1,0:T(8,128)(2,1)}, bf16[128,1024]{1,0:T(8,128)(2,1)}, u32[]{:S(2)}, u32[]{:S(2)}) collective-permute-start(bf16[128,1024]{1,0:T(8,128)(2,1)} %collective-permute-done.6.refs_1_), channel_id=1, source_target_pairs={{0,1},{1,0},{2,3},{3,2},{4,5},{5,4},{6,7},{7,6},{8,9},{9,8},{10,11... | collective-permute-start | bytes 786440 | tf_op jit(solution)/shard_map/ppermute | solution.py:424
  28.9 3.4 %copy-done.1 = bf16[1024,4096]{1,0:T(8,128)(2,1)S(1)} copy-done((bf16[1024,4096]{1,0:T(8,128)(2,1)S(1)}, bf16[1024,4096]{1,0:T(8,128)(2,1)}, u32[]{:S(2)}) %copy-start.1) | copy-done | bytes 8388632
  32.3 2.2 %read.1 = (bf16[128,1024]{1,0:T(8,128)(2,1)S(1)}, f32[128,1024]{1,0:T(8,128)S(1)}, bf16[8,128,256]{2,1,0:T(8,128)(2,1)S(1)}, f32[8,8,128]{2,1,0:T(8,128)S(1)}, bf16[128,1024]{1,0:T(8,128)(2,1)S(1)}) custom-call(s32[1]{0:T(128)} %bitcast.2.pos_ref, s32[1]{0:T(128)} %bitcast.3.ids_ref, f32[16,128]{1,0:T(8,128)S(1)} %get-tuple-element.28.info_ref, ...), custom_call_target="tpu_custom_call" | custom-call | flops 335544320 | bytes 1048576 | tf_op jit(solution)/shard_map/read/pallas_call | solution.py:26
  34.5 1.7 %collective-permute-done.5.refs_0_ = bf16[128,1024]{1,0:T(8,128)(2,1)} collective-permute-done((bf16[128,1024]{1,0:T(8,128)(2,1)}, bf16[128,1024]{1,0:T(8,128)(2,1)}, u32[]{:S(2)}, u32[]{:S(2)}) %collective-permute-start.5) | collective-permute-done | bytes 262176 | tf_op jit(solution)/shard_map/ppermute | solution.py:424
  36.2 5.2 %collective-permute-done.7.refs_2_ = bf16[128,1024]{1,0:T(8,128)(2,1)} collective-permute-done((bf16[128,1024]{1,0:T(8,128)(2,1)}, bf16[128,1024]{1,0:T(8,128)(2,1)}, u32[]{:S(2)}, u32[]{:S(2)}) %collective-permute-start.7) | collective-permute-done | bytes 262176 | tf_op jit(solution)/shard_map/ppermute | solution.py:424
  41.4 3.4 %copy-done.2 = bf16[1024,4096]{1,0:T(8,128)(2,1)S(1)} copy-done((bf16[1024,4096]{1,0:T(8,128)(2,1)S(1)}, bf16[1024,4096]{1,0:T(8,128)(2,1)}, u32[]{:S(2)}) %copy-start.2) | copy-done | bytes 8388632
  44.8 6.8 %spread.1 = (f32[8,136,128]{2,1,0:T(8,128)S(1)}, bf16[128,1024]{1,0:T(8,128)(2,1)S(1)}, f32[8,128,1]{2,1,0:T(8,128)S(1)}, bf16[128,1024]{1,0:T(8,128)(2,1)S(1)}) custom-call(s32[3]{0:T(128)S(1)} %pad_add_fusion.1.ids_ref, f32[16,128]{1,0:T(8,128)S(1)} %get-tuple-element.28.info_ref, bf16[128,1024]{1,0:T(8,128)(2,1)S(1)} %get-tuple-element.29.q_ref, ...), custom_call_target="tpu_custom_call" | custom-call | flops 838860800 | bytes 1048576 | tf_op jit(solution)/shard_map/spread/pallas_call | solution.py:26
  52.1 8.3 %collective-permute-done.9.more_ref = bf16[128,1024]{1,0:T(8,128)(2,1)S(1)} collective-permute-done((bf16[128,1024]{1,0:T(8,128)(2,1)S(1)}, bf16[128,1024]{1,0:T(8,128)(2,1)S(1)}, u32[]{:S(2)}, u32[]{:S(2)}) %collective-permute-start.9) | collective-permute-done | bytes 262176 | tf_op jit(solution)/shard_map/ppermute | solution.py:424
  60.4 3.4 %copy-done.3 = bf16[1024,4096]{1,0:T(8,128)(2,1)S(1)} copy-done((bf16[1024,4096]{1,0:T(8,128)(2,1)S(1)}, bf16[1024,4096]{1,0:T(8,128)(2,1)}, u32[]{:S(2)}) %copy-start.3) | copy-done | bytes 8388632
  63.8 0.9 %project_add.1.refs_0_ = bf16[128,1024]{1,0:T(8,128)(2,1)S(1)} custom-call(s32[1]{0:T(128)} %bitcast.4.ids_ref, bf16[128,1024]{1,0:T(8,128)(2,1)S(1)} %get-tuple-element.36.mixed_ref, bf16[1024,4096]{1,0:T(8,128)(2,1)S(1)} %copy-done.3, bf16[128,1024]{1,0:T(8,128)(2,1)S(1)} %collective-permute-done.9.more_ref, ...), custom_call_target="tpu_custom_call" | custom-call | flops 268435456 | bytes 1048576 | tf_op jit(solution)/shard_map/project_add/pallas_call | solution.py:26
  64.7 1.9 %collective-permute-start.11 = (bf16[128,1024]{1,0:T(8,128)(2,1)S(1)}, bf16[128,1024]{1,0:T(8,128)(2,1)S(1)}, u32[]{:S(2)}, u32[]{:S(2)}) collective-permute-start(bf16[128,1024]{1,0:T(8,128)(2,1)S(1)} %project_add.1.refs_0_), channel_id=1, source_target_pairs={{0,3},{1,2},{2,1},{3,0},{4,7},{5,6},{6,5},{7,4},{8,11},{9,10},{10,... | collective-permute-start | bytes 786440 | tf_op jit(solution)/shard_map/ppermute | solution.py:424
  66.7 2.0 %project_rest.1 = (bf16[128,1024]{1,0:T(8,128)(2,1)S(1)}, f32[128,1024]{1,0:T(8,128)S(1)}) custom-call(s32[2]{0:T(128)S(1)} %pad_add_fusion.ids_ref, bf16[128,1024]{1,0:T(8,128)(2,1)S(1)} %get-tuple-element.36.mixed_ref, bf16[1024,4096]{1,0:T(8,128)(2,1)S(1)} %bitcast.6, bf16[4,144,128]{2,1,0:T(8,128)(2,1)S(1)} %pair.3.after_ref), custom_call_target="tpu_custom_call" | custom-call | flops 536870912 | bytes 1048576 | tf_op jit(solution)/shard_map/project_rest/pallas_call | solution.py:26
  68.8 1.6 %collective-permute-start.12 = (bf16[4,144,128]{2,1,0:T(8,128)(2,1)S(1)}, bf16[4,144,128]{2,1,0:T(8,128)(2,1)S(1)}, u32[]{:S(2)}, u32[]{:S(2)}) collective-permute-start(bf16[4,144,128]{2,1,0:T(8,128)(2,1)S(1)} %pair.3.after_ref), channel_id=1, source_target_pairs={{0,8},{4,12},{8,0},{12,4},{16,24},{20,28},{24,16},{28,20},{1,9},{5... | collective-permute-start | bytes 442376 | tf_op jit(solution)/shard_map/ppermute | solution.py:376
  70.4 1.5 %collective-permute-start.13 = (bf16[4,144,128]{2,1,0:T(8,128)(2,1)S(1)}, bf16[4,144,128]{2,1,0:T(8,128)(2,1)S(1)}, u32[]{:S(2)}, u32[]{:S(2)}) collective-permute-start(bf16[4,144,128]{2,1,0:T(8,128)(2,1)S(1)} %pair.3.after_ref), channel_id=1, source_target_pairs={{0,16},{4,20},{8,24},{12,28},{16,0},{20,4},{24,8},{28,12},{1,17},{... | collective-permute-start | bytes 442376 | tf_op jit(solution)/shard_map/ppermute | solution.py:376
  72.4 3.1 %grads.1 = (bf16[128,1024]{1,0:T(8,128)(2,1)}, f32[128,1024]{1,0:T(8,128)S(1)}, f32[128,1024]{1,0:T(8,128)S(1)}) custom-call(f32[16,128]{1,0:T(8,128)S(1)} %get-tuple-element.28.info_ref, bf16[128,1024]{1,0:T(8,128)(2,1)S(1)} %get-tuple-element.29.q_ref, bf16[128,1024]{1,0:T(8,128)(2,1)S(1)} %get-tuple-element.32.k_ref, ...), custom_call_target="tpu_custom_call" | custom-call | flops 201326592 | bytes 1048576 | tf_op jit(solution)/shard_map/grads/pallas_call | solution.py:26
  75.5 3.2 %collective-permute-done.13.y_ref = bf16[4,144,128]{2,1,0:T(8,128)(2,1)S(1)} collective-permute-done((bf16[4,144,128]{2,1,0:T(8,128)(2,1)S(1)}, bf16[4,144,128]{2,1,0:T(8,128)(2,1)S(1)}, u32[]{:S(2)}, u32[]{:S(2)}) %collective-permute-start.13) | collective-permute-done | bytes 147488 | tf_op jit(solution)/shard_map/ppermute | solution.py:376
  78.9 1.2 %collective-permute-done.10 = bf16[128,1024]{1,0:T(8,128)(2,1)S(1)} collective-permute-done((bf16[128,1024]{1,0:T(8,128)(2,1)S(1)}, bf16[128,1024]{1,0:T(8,128)(2,1)S(1)}, u32[]{:S(2)}, u32[]{:S(2)}) %collective-permute-start.10) | collective-permute-done | bytes 262176 | tf_op jit(solution)/shard_map/ppermute | solution.py:424
  80.1 0.8 add_convert_fusion
  80.9 1.5 %last.1 = (bf16[128,1024]{1,0:T(8,128)(2,1)}, bf16[128,1024]{1,0:T(8,128)(2,1)}) custom-call(s32[1]{0:T(128)} %bitcast.2.pos_ref, f32[16,128]{1,0:T(8,128)S(1)} %get-tuple-element.28.info_ref, bf16[128,1024]{1,0:T(8,128)(2,1)S(1)} %get-tuple-element.32.k_ref, bf16[128,1024]{1,0:T(8,128)(2,1)S(1)} %get-tuple-element.33.v_ref, ...), custom_call_target="tpu_custom_call" | custom-call | flops 134217728 | bytes 1048576 | tf_op jit(solution)/shard_map/last/pallas_call | solution.py:26
  (39 shorter events, 2.8 us)
Async XLA Ops:
  1.9 1.0 %copy-start.4 = (bf16[128,1024]{1,0:T(8,128)(2,1)S(1)}, bf16[128,1024]{1,0:T(8,128)(2,1)}, u32[]{:S(2)}) copy-start(bf16[128,1024]{1,0:T(8,128)(2,1)} %q_in.1) | copy-start | bytes 786436
  2.9 0.9 %copy-start.5 = (bf16[128,1024]{1,0:T(8,128)(2,1)S(1)}, bf16[128,1024]{1,0:T(8,128)(2,1)}, u32[]{:S(2)}) copy-start(bf16[128,1024]{1,0:T(8,128)(2,1)} %k_in.1) | copy-start | bytes 786436
  3.8 0.9 %copy-start.6 = (bf16[128,1024]{1,0:T(8,128)(2,1)S(1)}, bf16[128,1024]{1,0:T(8,128)(2,1)}, u32[]{:S(2)}) copy-start(bf16[128,1024]{1,0:T(8,128)(2,1)} %v_in.1) | copy-start | bytes 786436
  4.8 0.9 %copy-start.7 = (bf16[128,1024]{1,0:T(8,128)(2,1)S(1)}, bf16[128,1024]{1,0:T(8,128)(2,1)}, u32[]{:S(2)}) copy-start(bf16[128,1024]{1,0:T(8,128)(2,1)} %grad_in.1) | copy-start | bytes 786436
  5.7 0.7 copy-start.8
  8.1 5.2 %collective-permute-start = (f32[8,136,128]{2,1,0:T(8,128)S(1)}, f32[8,136,128]{2,1,0:T(8,128)S(1)}, u32[]{:S(2)}, u32[]{:S(2)}) collective-permute-start(f32[8,136,128]{2,1,0:T(8,128)S(1)} %get-tuple-element.30.mine_ref), channel_id=1, source_target_pairs={{0,4},{4,0},{8,12},{12,8},{16,20},{20,16},{24,28},{28,24},{1,5},{5... | collective-permute-start | bytes 1671176 | tf_op jit(solution)/shard_map/ppermute | solution.py:364
  8.7 18.2 %collective-permute-start.6 = (bf16[128,1024]{1,0:T(8,128)(2,1)}, bf16[128,1024]{1,0:T(8,128)(2,1)}, u32[]{:S(2)}, u32[]{:S(2)}) collective-permute-start(bf16[128,1024]{1,0:T(8,128)(2,1)} %get-tuple-element.31.grad_ref), channel_id=1, source_target_pairs={{0,3},{1,2},{2,1},{3,0},{4,7},{5,6},{6,5},{7,4},{8,11},{9,10},{10,... | collective-permute-start | bytes 786440 | tf_op jit(solution)/shard_map/ppermute | solution.py:424
  13.6 11.7 %collective-permute-start.1 = (bf16[4,144,128]{2,1,0:T(8,128)(2,1)S(1)}, bf16[4,144,128]{2,1,0:T(8,128)(2,1)}, u32[]{:S(2)}, u32[]{:S(2)}) collective-permute-start(bf16[4,144,128]{2,1,0:T(8,128)(2,1)S(1)} %pair.2.after_ref), channel_id=1, source_target_pairs={{0,8},{4,12},{8,0},{12,4},{16,24},{20,28},{24,16},{28,20},{1,9},{5... | collective-permute-start | bytes 442376 | tf_op jit(solution)/shard_map/ppermute | solution.py:376
  15.1 10.1 %collective-permute-start.2 = (bf16[4,144,128]{2,1,0:T(8,128)(2,1)S(1)}, bf16[4,144,128]{2,1,0:T(8,128)(2,1)}, u32[]{:S(2)}, u32[]{:S(2)}) collective-permute-start(bf16[4,144,128]{2,1,0:T(8,128)(2,1)S(1)} %pair.2.after_ref), channel_id=1, source_target_pairs={{0,16},{4,20},{8,24},{12,28},{16,0},{20,4},{24,8},{28,12},{1,17},{... | collective-permute-start | bytes 442376 | tf_op jit(solution)/shard_map/ppermute | solution.py:376
  16.7 8.6 %collective-permute-start.3 = (bf16[4,144,128]{2,1,0:T(8,128)(2,1)S(1)}, bf16[4,144,128]{2,1,0:T(8,128)(2,1)}, u32[]{:S(2)}, u32[]{:S(2)}) collective-permute-start(bf16[4,144,128]{2,1,0:T(8,128)(2,1)S(1)} %pair.2.after_ref), channel_id=1, source_target_pairs={{0,24},{4,28},{8,16},{12,20},{16,8},{20,12},{24,0},{28,4},{1,25},{... | collective-permute-start | bytes 442376 | tf_op jit(solution)/shard_map/ppermute | solution.py:376
  19.8 3.4 %copy-start = (bf16[1024,4096]{1,0:T(8,128)(2,1)S(1)}, bf16[1024,4096]{1,0:T(8,128)(2,1)}, u32[]{:S(2)}) copy-start(bf16[1024,4096]{1,0:T(8,128)(2,1)} %weight_ref.5) | copy-start | bytes 25165828
  26.7 2.3 %collective-permute-start.4 = (f32[4,136,128]{2,1,0:T(8,128)S(1)}, f32[4,136,128]{2,1,0:T(8,128)}, u32[]{:S(2)}, u32[]{:S(2)}) collective-permute-start(f32[4,136,128]{2,1,0:T(8,128)S(1)} %join.2.own_ref), channel_id=1, source_target_pairs={{0,4},{4,0},{8,12},{12,8},{16,20},{20,16},{24,28},{28,24},{1,5},{5... | collective-permute-start | bytes 835592 | tf_op jit(solution)/shard_map/ppermute | solution.py:387
  26.8 9.5 %collective-permute-start.5 = (bf16[128,1024]{1,0:T(8,128)(2,1)}, bf16[128,1024]{1,0:T(8,128)(2,1)}, u32[]{:S(2)}, u32[]{:S(2)}) collective-permute-start(bf16[128,1024]{1,0:T(8,128)(2,1)} %get-tuple-element.31.grad_ref), channel_id=1, source_target_pairs={{0,1},{1,0},{2,3},{3,2},{4,5},{5,4},{6,7},{7,6},{8,9},{9,8},{10,11... | collective-permute-start | bytes 786440 | tf_op jit(solution)/shard_map/ppermute | solution.py:424
  26.9 14.6 %collective-permute-start.7 = (bf16[128,1024]{1,0:T(8,128)(2,1)}, bf16[128,1024]{1,0:T(8,128)(2,1)}, u32[]{:S(2)}, u32[]{:S(2)}) collective-permute-start(bf16[128,1024]{1,0:T(8,128)(2,1)} %collective-permute-done.6.refs_1_), channel_id=1, source_target_pairs={{0,1},{1,0},{2,3},{3,2},{4,5},{5,4},{6,7},{7,6},{8,9},{9,8},{10,11... | collective-permute-start | bytes 786440 | tf_op jit(solution)/shard_map/ppermute | solution.py:424
  28.9 3.4 %copy-start.1 = (bf16[1024,4096]{1,0:T(8,128)(2,1)S(1)}, bf16[1024,4096]{1,0:T(8,128)(2,1)}, u32[]{:S(2)}) copy-start(bf16[1024,4096]{1,0:T(8,128)(2,1)} %weight_ref.5) | copy-start | bytes 25165828
  41.4 3.4 %copy-start.2 = (bf16[1024,4096]{1,0:T(8,128)(2,1)S(1)}, bf16[1024,4096]{1,0:T(8,128)(2,1)}, u32[]{:S(2)}) copy-start(bf16[1024,4096]{1,0:T(8,128)(2,1)} %weight_ref.5) | copy-start | bytes 25165828
  44.8 21.9 %slice-start = ((s8[8388608]{0:T(1024)(128)(4,1)}), s8[4194304]{0:T(1024)(128)(4,1)S(1)}, s32[]{:S(2)}) async-start(s8[8388608]{0:T(1024)(128)(4,1)} %bitcast.5), calls=%async_computation | async-start | bytes 8388608
  51.6 15.0 %collective-permute-start.8 = (f32[8,136,128]{2,1,0:T(8,128)S(1)}, f32[8,136,128]{2,1,0:T(8,128)S(1)}, u32[]{:S(2)}, u32[]{:S(2)}) collective-permute-start(f32[8,136,128]{2,1,0:T(8,128)S(1)} %get-tuple-element.39.after_ref.mine_ref), channel_id=1, source_target_pairs={{0,4},{4,0},{8,12},{12,8},{16,20},{20,16},{24,28},{28,24},{1,5},{5... | collective-permute-start | bytes 1671176 | tf_op jit(solution)/shard_map/ppermute | solution.py:364
  51.7 8.7 %collective-permute-start.9 = (bf16[128,1024]{1,0:T(8,128)(2,1)S(1)}, bf16[128,1024]{1,0:T(8,128)(2,1)S(1)}, u32[]{:S(2)}, u32[]{:S(2)}) collective-permute-start(bf16[128,1024]{1,0:T(8,128)(2,1)S(1)} %get-tuple-element.40), channel_id=1, source_target_pairs={{0,1},{1,0},{2,3},{3,2},{4,5},{5,4},{6,7},{7,6},{8,9},{9,8},{10,11... | collective-permute-start | bytes 786440 | tf_op jit(solution)/shard_map/ppermute | solution.py:424
  60.4 3.4 %copy-start.3 = (bf16[1024,4096]{1,0:T(8,128)(2,1)S(1)}, bf16[1024,4096]{1,0:T(8,128)(2,1)}, u32[]{:S(2)}) copy-start(bf16[1024,4096]{1,0:T(8,128)(2,1)} %weight_ref.5) | copy-start | bytes 25165828
  63.8 2.9 %slice-start.1 = ((s8[8388608]{0:T(1024)(128)(4,1)}), s8[4194304]{0:T(1024)(128)(4,1)S(1)}, s32[]{:S(2)}) async-start(s8[8388608]{0:T(1024)(128)(4,1)} %bitcast.5), calls=%async_computation.1 | async-start | bytes 8388608
  64.7 14.2 %collective-permute-start.11 = (bf16[128,1024]{1,0:T(8,128)(2,1)S(1)}, bf16[128,1024]{1,0:T(8,128)(2,1)S(1)}, u32[]{:S(2)}, u32[]{:S(2)}) collective-permute-start(bf16[128,1024]{1,0:T(8,128)(2,1)S(1)} %project_add.1.refs_0_), channel_id=1, source_target_pairs={{0,3},{1,2},{2,1},{3,0},{4,7},{5,6},{6,5},{7,4},{8,11},{9,10},{10,... | collective-permute-start | bytes 786440 | tf_op jit(solution)/shard_map/ppermute | solution.py:424
  68.8 11.4 %collective-permute-start.10 = (bf16[128,1024]{1,0:T(8,128)(2,1)S(1)}, bf16[128,1024]{1,0:T(8,128)(2,1)S(1)}, u32[]{:S(2)}, u32[]{:S(2)}) collective-permute-start(bf16[128,1024]{1,0:T(8,128)(2,1)S(1)} %get-tuple-element.42.after_ref), channel_id=1, source_target_pairs={{0,1},{1,0},{2,3},{3,2},{4,5},{5,4},{6,7},{7,6},{8,9},{9,8},{10,11... | collective-permute-start | bytes 786440 | tf_op jit(solution)/shard_map/ppermute | solution.py:424
  68.8 6.7 %collective-permute-start.12 = (bf16[4,144,128]{2,1,0:T(8,128)(2,1)S(1)}, bf16[4,144,128]{2,1,0:T(8,128)(2,1)S(1)}, u32[]{:S(2)}, u32[]{:S(2)}) collective-permute-start(bf16[4,144,128]{2,1,0:T(8,128)(2,1)S(1)} %pair.3.after_ref), channel_id=1, source_target_pairs={{0,8},{4,12},{8,0},{12,4},{16,24},{20,28},{24,16},{28,20},{1,9},{5... | collective-permute-start | bytes 442376 | tf_op jit(solution)/shard_map/ppermute | solution.py:376
  70.4 8.3 %collective-permute-start.13 = (bf16[4,144,128]{2,1,0:T(8,128)(2,1)S(1)}, bf16[4,144,128]{2,1,0:T(8,128)(2,1)S(1)}, u32[]{:S(2)}, u32[]{:S(2)}) collective-permute-start(bf16[4,144,128]{2,1,0:T(8,128)(2,1)S(1)} %pair.3.after_ref), channel_id=1, source_target_pairs={{0,16},{4,20},{8,24},{12,28},{16,0},{20,4},{24,8},{28,12},{1,17},{... | collective-permute-start | bytes 442376 | tf_op jit(solution)/shard_map/ppermute | solution.py:376
  71.9 6.8 %collective-permute-start.14 = (bf16[4,144,128]{2,1,0:T(8,128)(2,1)S(1)}, bf16[4,144,128]{2,1,0:T(8,128)(2,1)S(1)}, u32[]{:S(2)}, u32[]{:S(2)}) collective-permute-start(bf16[4,144,128]{2,1,0:T(8,128)(2,1)S(1)} %pair.3.after_ref), channel_id=1, source_target_pairs={{0,24},{4,28},{8,16},{12,20},{16,8},{20,12},{24,0},{28,4},{1,25},{... | collective-permute-start | bytes 442376 | tf_op jit(solution)/shard_map/ppermute | solution.py:376
  78.8 2.1 %collective-permute-start.15 = (f32[4,136,128]{2,1,0:T(8,128)S(1)}, f32[4,136,128]{2,1,0:T(8,128)S(1)}, u32[]{:S(2)}, u32[]{:S(2)}) collective-permute-start(f32[4,136,128]{2,1,0:T(8,128)S(1)} %join.3.own_ref), channel_id=1, source_target_pairs={{0,4},{4,0},{8,12},{12,8},{16,20},{20,16},{24,28},{28,24},{1,5},{5... | collective-permute-start | bytes 835592 | tf_op jit(solution)/shard_map/ppermute | solution.py:387

commit v3 on v2

v3 whole, which is shorter than its diff:
```python
import functools

import jax
import jax.numpy as jnp
from jax import lax
from jax.experimental import pallas as pl
from jax.experimental.pallas import tpu as pltpu
from jax.sharding import PartitionSpec as P

DH = 128
ROWS = 136
SENT = 144
BF16 = jnp.bfloat16
F32 = jnp.float32
VMEM = pl.BlockSpec(memory_space=pltpu.VMEM)
SMEM = pl.BlockSpec(memory_space=pltpu.SMEM)


ANY = pl.BlockSpec(memory_space=pl.ANY)


def call(kernel, outs, in_specs, args, micros, name):
    return pl.pallas_call(
        kernel,
        out_shape=outs,
        in_specs=in_specs,
        out_specs=[VMEM] * len(outs),
        compiler_params=pltpu.CompilerParams(vmem_limit_bytes=24 * 1024 * 1024),
        cost_estimate=pl.CostEstimate(flops=int(micros * 1.15e9), bytes_accessed=1024, transcendentals=0),
        name=name,
    )(*args)


def feature(x):
    return jnp.where(x > 0, x + 1.0, jnp.exp(jnp.minimum(x, 0.0)))


def slope(x):
    return jnp.where(x > 0, 1.0, jnp.where(x == 0, 0.5, jnp.exp(jnp.minimum(x, 0.0))))


def sigmoid(x):
    return 1.0 / (1.0 + jnp.exp(-x))


def dot(a, b, dims):
    return lax.dot_general(a, b, (dims, ((), ())), preferred_element_type=F32)


NN = ((1,), (0,))
NT = ((1,), (1,))
TN = ((0,), (0,))


def live_rows(valid_ref, length):
    where = lax.broadcasted_iota(jnp.int32, (length, 1), 0)
    return (where < valid_ref[...]).astype(F32)


def opened(starts_ref):
    return 1.0 - starts_ref[...].astype(F32)


def gate_row(gate_ref, h):
    return sigmoid(jnp.full((1, DH), gate_ref[h], F32))


def head(ref, h):
    return ref[:, h * DH : (h + 1) * DH]


def tail(rows, *values):
    where = lax.broadcasted_iota(jnp.int32, (rows, DH), 0)
    out = jnp.zeros((rows, DH), F32)
    for at, value in enumerate(values):
        out = jnp.where(where == at, value, out)
    return out


def split(x):
    top = x.astype(BF16)
    rest = x - top.astype(F32)
    return top, rest.astype(BF16)


def state_kernel(heads, pos_ref, z_ref, valid_ref, starts_ref, k_ref, v_ref, state_ref):
    live = live_rows(valid_ref, k_ref.shape[0])
    for h in range(heads):
        sig = (feature(head(k_ref, h).astype(F32)) * live).astype(BF16)
        state_ref[h, 0:DH, :] = dot(sig, head(v_ref, h), TN)
        norm = jnp.sum(sig.astype(F32), axis=0, keepdims=True)
        state_ref[h, DH:ROWS, :] = tail(ROWS - DH, norm, opened(starts_ref))


def pair_kernel(heads, forward, pos_ref, mine_ref, other_ref, *refs):
    sent_ref = refs[-1]
    half = lax.rem(pos_ref[0], 2)
    lower = half == 0
    for i in range(heads // 2):
        h = half * (heads // 2) + i
        mine, other = mine_ref[h], other_ref[h]
        first = jnp.where(lower, mine, other)
        second = jnp.where(lower, other, mine)
        open_first, open_second = first[DH + 1 : DH + 2], second[DH + 1 : DH + 2]
        if forward:
            total = open_second * first + second
        else:
            total = open_first * (first + open_second * second)
        memory, norm = total[0:DH], total[DH : DH + 1]
        norm_1, rest = split(norm)
        norm_1 = norm_1.astype(F32)
        norm_2 = rest.astype(F32)
        norm_3 = norm - norm_1 - norm_2
        if forward:
            weight = jnp.maximum(jnp.sum(norm, axis=1, keepdims=True), 1e-30)
            centre = jnp.sum(memory, axis=0, keepdims=True) / weight
            centre = centre.astype(BF16).astype(F32)
            norms = tail(16, norm_1, norm_2, norm_3).astype(BF16)
            centres = tail(16, centre, centre, centre).astype(BF16)
            memory = memory - dot(norms, centres, TN)
        else:
            centre = jnp.zeros_like(norm)
        sent_ref[i, 0:DH, :] = memory.astype(BF16)
        rows = tail(SENT - DH, norm_1, norm_2, norm_3, centre, open_first * open_second)
        sent_ref[i, DH:SENT, :] = rows.astype(BF16)


def join_kernel(heads, forward, pos_ref, x_ref, y_ref, d_ref, *refs):
    carry_ref = refs[-1]
    chip = pos_ref[0] // 2
    place = chip if forward else 3 - chip
    for i in range(heads // 2):
        totals = []
        for ref in (x_ref, y_ref, d_ref):
            memory = ref[i, 0:DH, :].astype(F32)
            rows = ref[i, DH:SENT, :].astype(F32)
            norm = rows[0:1] + rows[1:2] + rows[2:3]
            if forward:
                norms = tail(16, rows[0:1], rows[1:2], rows[2:3]).astype(BF16)
                centres = tail(16, rows[3:4], rows[3:4], rows[3:4]).astype(BF16)
                memory = memory + dot(norms, centres, TN)
            totals.append((memory, norm, rows[4:5]))
        (x_mem, x_norm, x_open), (y_mem, y_norm, y_open), (d_mem, d_norm, d_open) = totals
        odd, high = lax.rem(place, 2) == 1, place >= 2
        on_x = jnp.where(odd, jnp.ones_like(x_open), 0.0)
        on_y = jnp.where(high, jnp.where(odd, x_open, d_open), 0.0)
        on_d = jnp.where(high, jnp.where(odd, x_open * y_open, 1.0), 0.0)
        norm = on_x * x_norm + on_y * y_norm + on_d * d_norm
        carry_ref[i, 0:DH, :] = on_x * x_mem + on_y * y_mem + on_d * d_mem
        carry_ref[i, DH:ROWS, :] = tail(ROWS - DH, norm)


def local_kernel(heads, valid_ref, q_ref, k_ref, v_ref, after_ref, probs_ref, local_ref):
    length = q_ref.shape[0]
    row = lax.broadcasted_iota(jnp.int32, (length, length), 0)
    col = lax.broadcasted_iota(jnp.int32, (length, length), 1)
    allowed = (col <= row) & (col < valid_ref[...])
    for h in range(heads):
        scores = dot(head(q_ref, h), head(k_ref, h), NT) * DH ** (-0.5)
        scores = jnp.where(allowed, scores, -1e30)
        expo = jnp.exp(scores - jnp.max(scores, axis=1, keepdims=True))
        probs = (expo / jnp.sum(expo, axis=1, keepdims=True)).astype(BF16)
        probs_ref[h] = probs
        local_ref[:, h * DH : (h + 1) * DH] = dot(probs, head(v_ref, h), NN)


def columns(z_ref, way, cols):
    return pl.ds(pl.multiple_of((z_ref[0] ^ way) * cols, DH), cols)


def read_kernel(
    heads, project, pos_ref, z_ref, valid_ref, gate_ref, q_ref, mine_ref, other_ref, own_ref, far_ref, local_ref,
    *refs,
):
    if project:
        weight_ref, after_ref, mixed_ref, read_ref, memory_ref, norm_ref, first_ref = refs
    else:
        mixed_ref, read_ref, memory_ref, norm_ref = refs
    live = live_rows(valid_ref, q_ref.shape[0])
    upper = lax.rem(pos_ref[0], 2) == 1
    for h in range(heads):
        i, part = h % (heads // 2), h // (heads // 2)
        own_here = upper if part else jnp.logical_not(upper)
        carry = jnp.where(own_here, own_ref[i], far_ref[i])
        other = other_ref[h]
        before = jnp.where(upper, other[DH + 1 : DH + 2] * carry + other, carry)
        state = mine_ref[h, DH + 1 : DH + 2, :] * before
        memory, norm = state[0:DH], state[DH : DH + 1]
        parts = jnp.concatenate(split(memory), axis=1)
        memory_ref[h] = parts
        norm_ref[h] = jnp.broadcast_to(norm, (8, DH))
        sig = feature(head(q_ref, h).astype(F32)).astype(BF16)
        numer = dot(sig, parts, NN)
        numer = numer[:, 0:DH] + numer[:, DH:]
        denom = jnp.sum(sig.astype(F32) * norm, axis=1, keepdims=True) + 1.0
        read = numer / denom
        gate = gate_row(gate_ref, h)
        mixed = live * (gate * read + (1.0 - gate) * head(local_ref, h))
        read_ref[:, h * DH : (h + 1) * DH] = read
        mixed_ref[:, h * DH : (h + 1) * DH] = mixed.astype(BF16)
    if project:
        block = weight_ref[:, columns(z_ref, 2, first_ref.shape[1])]
        first_ref[...] = dot(mixed_ref[...], block, NN).astype(BF16)


def more_kernel(ways, z_ref, *refs):
    grad_refs, (weight_ref, *before, after_ref, total_ref) = refs[: len(ways)], refs[len(ways) :]
    total = before[0][...] if before else None
    for way, grad_ref in zip(ways, grad_refs):
        block = weight_ref[:, columns(z_ref, way, grad_ref.shape[1])]
        part = dot(grad_ref[...], block, NT)
        total = part if total is None else total + part
    total_ref[...] = total


def add_kernel(z_ref, mixed_ref, weight_ref, more_ref, after_ref, out_ref):
    block = weight_ref[:, columns(z_ref, 3, out_ref.shape[1])]
    part = dot(mixed_ref[...], block, NN)
    out_ref[...] = (part + more_ref[...].astype(F32)).astype(BF16)


def rest_kernel(z_ref, mixed_ref, weight_ref, after_ref, near_ref, own_ref):
    cols = own_ref.shape[1]
    near = dot(mixed_ref[...], weight_ref[:, columns(z_ref, 1, cols)], NN)
    near_ref[...] = near.astype(BF16)
    own_ref[...] = dot(mixed_ref[...], weight_ref[:, columns(z_ref, 0, cols)], NN)


def spread_kernel(
    heads, ways, z_ref, valid_ref, starts_ref, gate_ref, q_ref, norm_ref, read_ref, *refs,
):
    if ways:
        parts, (total_ref, weight_ref) = refs[: len(ways)], refs[len(ways) : len(ways) + 2]
        passed_ref, numer_ref, denom_ref, grad_ref = refs[len(ways) + 3 :]
        total = total_ref[...]
        for way, part_ref in zip(ways, parts):
            block = weight_ref[:, columns(z_ref, way, part_ref.shape[1])]
            total = total + dot(part_ref[...], block, NT)
        grad_ref[...] = total.astype(BF16)
    else:
        grad_ref, passed_ref, numer_ref, denom_ref = refs
    live = live_rows(valid_ref, q_ref.shape[0])
    for h in range(heads):
        cut = slice(h * DH, (h + 1) * DH)
        sig = feature(head(q_ref, h).astype(F32)).astype(BF16)
        sig_full = sig.astype(F32)
        denom = jnp.sum(sig_full * norm_ref[h, 0:1, :], axis=1, keepdims=True) + 1.0
        gate = gate_row(gate_ref, h)
        numer_grad = (head(grad_ref, h).astype(F32) * gate * (live / denom)).astype(BF16)
        denom_grad = -jnp.sum(
            numer_grad.astype(F32) * head(read_ref, h), axis=1, keepdims=True
        )
        passed_ref[h, 0:DH, :] = dot(sig, numer_grad, TN)
        norm_grad = jnp.sum(sig_full * denom_grad, axis=0, keepdims=True)
        passed_ref[h, DH:ROWS, :] = tail(ROWS - DH, norm_grad, opened(starts_ref))
        numer_ref[:, cut] = numer_grad
        denom_ref[h] = denom_grad


def grads_kernel(heads, valid_ref, gate_ref, q_ref, k_ref, v_ref, probs_ref, grad_ref, numer_ref,
                 denom_ref, memory_ref, norm_ref, after_ref, query_ref, key_ref, value_ref):
    length = q_ref.shape[0]
    live = live_rows(valid_ref, length)
    for h in range(heads):
        cut = slice(h * DH, (h + 1) * DH)
        q, k, v = head(q_ref, h), head(k_ref, h), head(v_ref, h)
        gate = gate_row(gate_ref, h)
        grad = (head(grad_ref, h).astype(F32) * (1.0 - gate) * live).astype(BF16)
        probs = probs_ref[h]
        probs_grad = dot(grad, v, NT)
        full = probs.astype(F32)
        mean = jnp.sum(full * probs_grad, axis=1, keepdims=True)
        scores_grad = (full * (probs_grad - mean) * DH ** (-0.5)).astype(BF16)
        key_ref[:, cut] = dot(scores_grad, q, TN)
        value_ref[:, cut] = dot(probs, grad, TN)
        parts = memory_ref[h]
        numer = head(numer_ref, h)
        sig_grad = dot(numer, parts[:, 0:DH], NT) + dot(numer, parts[:, DH:], NT)
        sig_grad = sig_grad + denom_ref[h] * norm_ref[h, 0:1, :]
        total = dot(scores_grad, k, NN) + sig_grad * slope(q.astype(F32))
        query_ref[:, cut] = total.astype(BF16)


def last_kernel(heads, pos_ref, valid_ref, k_ref, v_ref, other_ref, own_ref, far_ref, key_ref,
                value_ref, key_out, value_out):
    live = live_rows(valid_ref, k_ref.shape[0])
    upper = lax.rem(pos_ref[0], 2) == 1
    for h in range(heads):
        cut = slice(h * DH, (h + 1) * DH)
        i, part = h % (heads // 2), h // (heads // 2)
        own_here = upper if part else jnp.logical_not(upper)
        carry = jnp.where(own_here, own_ref[i], far_ref[i])
        other = other_ref[h]
        back = jnp.where(upper, carry, other[DH + 1 : DH + 2] * (other + carry))
        memory, norm = back[0:DH], back[DH : DH + 1]
        top, low = split(memory)
        k, v = head(k_ref, h).astype(F32), head(v_ref, h)
        sig = (feature(k) * live).astype(BF16)
        sig_grad = (dot(v, top, NT) + dot(v, low, NT) + norm) * live
        key_out[:, cut] = (key_ref[:, cut] + sig_grad * slope(k)).astype(BF16)
        more = dot(sig, jnp.concatenate([top, low], axis=1), NN)
        value_out[:, cut] = (value_ref[:, cut] + more[:, 0:DH] + more[:, DH:]).astype(BF16)


def weighted(state, forward):
    count, mine = lax.axis_size("seq"), lax.axis_index("seq")
    states = lax.all_gather(state, "seq")
    total = jnp.zeros_like(state)
    weight = jnp.ones((), F32)

    def turn(step, carried):
        total, weight = carried
        at = mine - 1 - step if forward else mine + 1 + step
        inside = (at >= 0) & (at < count)
        one = lax.dynamic_index_in_dim(states, jnp.clip(at, 0, count - 1), keepdims=False)
        opened = one[0, DH + 1, 0]
        here = weight if forward else weight * opened
        total = jnp.where(inside, total + here * one, total)
        return total, weight * opened

    return lax.fori_loop(0, count - 1, turn, (total, weight))[0]


def scan_states(state, pos, heads, forward, before_pair, before_join):
    count = lax.axis_size("seq")
    if count != 8:
        before_pair()
        before_join(state)
        carry = weighted(state, forward)
        place = jnp.full_like(pos, 0 if forward else 1)
        own, far = carry[: heads // 2], carry[heads // 2 :]
        return (own, far, state, place) if forward else (far, own, state, place)
    pairs = [(s, s ^ 1) for s in range(count)]
    other = lax.ppermute(state, "seq", pairs)
    after = before_pair()
    sent = call(
        functools.partial(pair_kernel, heads, forward),
        [jax.ShapeDtypeStruct((heads // 2, SENT, DH), BF16)],
        [SMEM, VMEM, VMEM] + [ANY] * len(after),
        [pos, state, other, *after],
        0.3, "pair",
    )[0]
    arrived = [
        lax.ppermute(sent, "seq", [(s, s ^ way) for s in range(count)]) for way in (6, 2, 4)
    ]
    after = before_join(sent)
    own = call(
        functools.partial(join_kernel, heads, forward),
        [jax.ShapeDtypeStruct((heads // 2, ROWS, DH), F32)],
        [SMEM, VMEM, VMEM, VMEM] + [ANY] * len(after),
        [pos, arrived[1], arrived[2], arrived[0], *after],
        0.3, "join",
    )[0]
    far = lax.ppermute(own, "seq", pairs)
    return own, far, other, pos


def shards(queries, keys, values, gate, out_weight, out_grad, valid, starts):
    length, width = queries.shape
    heads = width // DH
    cols = out_grad.shape[1]
    groups = lax.axis_size("head")
    direct = groups == 4
    pos = lax.axis_index("seq").astype(jnp.int32).reshape(1)
    z = lax.axis_index("head").astype(jnp.int32).reshape(1)
    valid, starts = valid.reshape(1, 1), starts.reshape(1, 1)
    flat = jax.ShapeDtypeStruct((length, width), F32)
    low = jax.ShapeDtypeStruct((length, width), BF16)
    part_low = jax.ShapeDtypeStruct((length, cols), BF16)
    part_full = jax.ShapeDtypeStruct((length, cols), F32)
    states = jax.ShapeDtypeStruct((heads, ROWS, DH), F32)

    def swap(array, way):
        return lax.ppermute(array, "head", [(s, s ^ way) for s in range(groups)])

    state = call(
        functools.partial(state_kernel, heads), [states], [SMEM] * 2 + [VMEM] * 4,
        [pos, z, valid, starts, keys, values], 0.4, "state",
    )[0]
    if direct:
        grad_3 = swap(out_grad, 3)
        grad_1 = swap(out_grad, 1)
        grad_2 = swap(grad_3, 1)
    kept = {}

    def beside_forward(sent):
        kept["local"] = call(
            functools.partial(local_kernel, heads),
            [jax.ShapeDtypeStruct((heads, length, length), BF16), flat],
            [VMEM] * 4 + [ANY],
            [valid, queries, keys, values, sent], 2.7, "local",
        )
        return [kept["local"][1]]

    own, far, other, place = scan_states(state, pos, heads, True, lambda: [], beside_forward)
    probs, local = kept["local"]
    if direct:
        total = call(
            functools.partial(more_kernel, (0, 1)), [flat], [SMEM] + [VMEM] * 3 + [ANY],
            [z, out_grad, grad_1, out_weight, own], 1.5, "unproject_near",
        )[0]
    outs = call(
        functools.partial(read_kernel, heads, direct),
        [low, flat, jax.ShapeDtypeStruct((heads, DH, 2 * DH), BF16),
         jax.ShapeDtypeStruct((heads, 8, DH), F32)] + [part_low] * direct,
        [SMEM, SMEM, VMEM, SMEM] + [VMEM] * 6 + [VMEM, ANY] * direct,
        [place, z, valid, gate, queries, state, other, own, far, local]
        + ([out_weight, total] if direct else []),
        0.9, "read",
    )
    mixed, read, memory, norm = outs[:4]
    if direct:
        sum_2 = swap(outs[4], 1)
        total = call(
            functools.partial(more_kernel, (3,)), [flat], [SMEM] + [VMEM] * 3 + [ANY],
            [z, grad_3, out_weight, total, mixed], 0.9, "unproject_more",
        )[0]
        grads_in = [grad_2, total, out_weight]
    else:
        part = dot(mixed, out_weight, NN)
        output = lax.psum_scatter(part, "head", scatter_dimension=1, tiled=True).astype(BF16)
        whole = lax.all_gather(out_grad, "head", axis=1, tiled=True)
        grads_in = [dot(whole, out_weight, NT).astype(BF16)]
    outs = call(
        functools.partial(spread_kernel, heads, (2,) * direct),
        [states, low, jax.ShapeDtypeStruct((heads, length, 1), F32)] + [low] * direct,
        [SMEM, VMEM, VMEM, SMEM] + [VMEM] * (3 + len(grads_in)) + [ANY] * direct,
        [z, valid, starts, gate, queries, norm, read, *grads_in] + ([sum_2] if direct else []),
        2.5, "spread",
    )
    passed, numer_grad, denom_grad = outs[:3]
    mixed_grad = outs[3] if direct else grads_in[0]

    def add_here():
        if not direct:
            return []
        sum_3 = call(
            add_kernel, [part_low], [SMEM, VMEM, VMEM, VMEM, ANY],
            [z, mixed, out_weight, sum_2, passed], 0.5, "project_add",
        )[0]
        kept["from_3"] = swap(sum_3, 3)
        return [sum_3]

    def beside_back(sent):
        after = sent
        if direct:
            near, kept["own"] = call(
                rest_kernel, [part_low, part_full], [SMEM, VMEM, VMEM, ANY],
                [z, mixed, out_weight, sent], 1.3, "project_rest",
            )
            kept["from_1"] = swap(near, 1)
            after = near
        kept["grads"] = call(
            functools.partial(grads_kernel, heads),
            [low, flat, flat],
            [VMEM, SMEM] + [VMEM] * 9 + [ANY],
            [valid, gate, queries, keys, values, probs, mixed_grad, numer_grad, denom_grad, memory,
             norm, after],
            3.1, "grads",
        )
        return [kept["grads"][1]]

    own, far, other, place = scan_states(passed, pos, heads, False, add_here, beside_back)
    query_grad, key_part, value_part = kept["grads"]
    if direct:
        output = kept["own"] + kept["from_1"].astype(F32) + kept["from_3"].astype(F32)
        output = output.astype(BF16)
    key_grad, value_grad = call(
        functools.partial(last_kernel, heads),
        [low, low],
        [SMEM] + [VMEM] * 8,
        [place, valid, keys, values, other, own, far, key_part, value_part], 1.5, "last",
    )
    return (output, query_grad, key_grad, value_grad)


def solution(mesh):
    placed = (
        P("seq", "head"),
        P("seq", "head"),
        P("seq", "head"),
        P("head"),
        P("head", None),
        P("seq", "head"),
        P("seq"),
        P("seq"),
    )
    return jax.shard_map(
        shards,
        mesh=mesh,
        in_specs=placed,
        out_specs=(P("seq", "head"), P("seq", "head"), P("seq", "head"), P("seq", "head")),
        check_vma=False,
    )
```

time: 82.9 us -> 57.7 us (0.70)
  local copies, waits for them, and re-layouts: 18 us -> 4.78 us
  Pallas kernels: 24.8 us -> 15.8 us
  waiting for transfers between devices: 19.6 us -> 16.2 us
    unnamed x22 -> x24, local copies, waits for them, and re-layouts: 18 us -> 4.78 us
    pallas_call x13 -> x14, Pallas kernels: 24.8 us -> 15.8 us  [call(): pl.pallas_call(kernel, out_shape=outs, in_specs=in_specs, out_specs=[VMEM...]
    ppermute x6, waiting for transfers between devices: 16.4 us -> 12.7 us  [swap(): return lax.ppermute(array, 'head', [(s, s ^ way) for s in range(groups)])]
  transfers between devices with their start and end apart: 16 -> 16, of which waited for: 5 -> 6; matrix products, arithmetic and copies ran while one was open for 1% -> 1% of each run, Pallas kernels for 18% -> 21%
where the time goes in v3:
time: 57.7 us; the launch traced here: 57.4 us
  starting transfers between devices  17.1 us (30%)
  waiting for transfers between devices  16.2 us (28%)
  Pallas kernels  15.8 us (27%)
  local copies, waits for them, and re-layouts  4.78 us (8%)
  between operations  2.71 us (5%)
  other arithmetic  0.81 us (1%)
    pallas_call x14, Pallas kernels, call(): pl.pallas_call(kernel, out_shape=outs, in_specs=in_specs, out_specs=[VMEM...  15.8 us
    ppermute x6, waiting for transfers between devices, swap(): return lax.ppermute(array, 'head', [(s, s ^ way) for s in range(groups)])  12.7 us
    ppermute x6, starting transfers between devices, swap(): return lax.ppermute(array, 'head', [(s, s ^ way) for s in range(groups)])  9.3 us
    ppermute x6, starting transfers between devices, scan_states(): lax.ppermute(sent, 'seq', [(s, s ^ way) for s in range(count)])  7.11 us
    unnamed x24, local copies, waits for them, and re-layouts  4.78 us
    ppermute x6, waiting for transfers between devices, scan_states(): lax.ppermute(sent, 'seq', [(s, s ^ way) for s in range(count)])  3.43 us
  transfers between devices with their start and end apart: 16, of which 6 were waited for; matrix products, arithmetic and copies ran while one was open for 1% of the time, Pallas kernels for 21%

profile of v3, /device:TPU:0, one launch (start us, length us, event | category | flops | bytes accessed | tf_op | source)
XLA Modules:
  0.0 57.4 jit_solution(10911844656758779519)
XLA Ops:
  2.5 0.9 %copy-done.4 = bf16[128,1024]{1,0:T(8,128)(2,1)S(1)} copy-done((bf16[128,1024]{1,0:T(8,128)(2,1)S(1)}, bf16[128,1024]{1,0:T(8,128)(2,1)}, u32[]{:S(2)}) %copy-start.4) | copy-done | bytes 262168
  3.5 0.9 %copy-done.7 = bf16[128,1024]{1,0:T(8,128)(2,1)S(1)} copy-done((bf16[128,1024]{1,0:T(8,128)(2,1)S(1)}, bf16[128,1024]{1,0:T(8,128)(2,1)}, u32[]{:S(2)}) %copy-start.7) | copy-done | bytes 262168
  4.8 0.5 collective-permute-start
  5.3 2.6 %collective-permute-start.5 = (bf16[128,1024]{1,0:T(8,128)(2,1)}, bf16[128,1024]{1,0:T(8,128)(2,1)S(1)}, u32[]{:S(2)}, u32[]{:S(2)}) collective-permute-start(bf16[128,1024]{1,0:T(8,128)(2,1)} %refs_0_.2), channel_id=1, source_target_pairs={{0,1},{1,0},{2,3},{3,2},{4,5},{5,4},{6,7},{7,6},{8,9},{9,8},{10,11... | collective-permute-start | bytes 786440 | tf_op jit(solution)/shard_map/ppermute | solution.py:374
  8.0 2.5 %collective-permute-start.6 = (bf16[128,1024]{1,0:T(8,128)(2,1)}, bf16[128,1024]{1,0:T(8,128)(2,1)S(1)}, u32[]{:S(2)}, u32[]{:S(2)}) collective-permute-start(bf16[128,1024]{1,0:T(8,128)(2,1)} %refs_0_.2), channel_id=1, source_target_pairs={{0,3},{1,2},{2,1},{3,0},{4,7},{5,6},{6,5},{7,4},{8,11},{9,10},{10,... | collective-permute-start | bytes 786440 | tf_op jit(solution)/shard_map/ppermute | solution.py:374
  10.7 1.6 %collective-permute-start.1 = (bf16[4,144,128]{2,1,0:T(8,128)(2,1)S(1)}, bf16[4,144,128]{2,1,0:T(8,128)(2,1)S(1)}, u32[]{:S(2)}, u32[]{:S(2)}) collective-permute-start(bf16[4,144,128]{2,1,0:T(8,128)(2,1)S(1)} %pair.2.after_ref), channel_id=1, source_target_pairs={{0,8},{4,12},{8,0},{12,4},{16,24},{20,28},{24,16},{28,20},{1,9},{5... | collective-permute-start | bytes 442376 | tf_op jit(solution)/shard_map/ppermute | solution.py:344
  12.3 1.5 %collective-permute-start.2 = (bf16[4,144,128]{2,1,0:T(8,128)(2,1)S(1)}, bf16[4,144,128]{2,1,0:T(8,128)(2,1)S(1)}, u32[]{:S(2)}, u32[]{:S(2)}) collective-permute-start(bf16[4,144,128]{2,1,0:T(8,128)(2,1)S(1)} %pair.2.after_ref), channel_id=1, source_target_pairs={{0,16},{4,20},{8,24},{12,28},{16,0},{20,4},{24,8},{28,12},{1,17},{... | collective-permute-start | bytes 442376 | tf_op jit(solution)/shard_map/ppermute | solution.py:344
  14.3 0.9 %copy-done.1 = bf16[128,1024]{1,0:T(8,128)(2,1)S(1)} copy-done((bf16[128,1024]{1,0:T(8,128)(2,1)S(1)}, bf16[128,1024]{1,0:T(8,128)(2,1)}, u32[]{:S(2)}) %copy-start.1) | copy-done | bytes 262168
  15.2 0.9 %copy-done.5 = bf16[128,1024]{1,0:T(8,128)(2,1)S(1)} copy-done((bf16[128,1024]{1,0:T(8,128)(2,1)S(1)}, bf16[128,1024]{1,0:T(8,128)(2,1)}, u32[]{:S(2)}) %copy-start.5) | copy-done | bytes 262168
  16.2 0.9 %copy-done.8 = bf16[128,1024]{1,0:T(8,128)(2,1)S(1)} copy-done((bf16[128,1024]{1,0:T(8,128)(2,1)S(1)}, bf16[128,1024]{1,0:T(8,128)(2,1)}, u32[]{:S(2)}) %copy-start.8) | copy-done | bytes 262168
  17.1 2.7 %local.1 = (bf16[8,128,128]{2,1,0:T(8,128)(2,1)S(1)}, f32[128,1024]{1,0:T(8,128)S(1)}) custom-call(s32[1,1]{1,0:T(1,128)} %bitcast.5.valid_ref, bf16[128,1024]{1,0:T(8,128)(2,1)S(1)} %copy-done.1, bf16[128,1024]{1,0:T(8,128)(2,1)S(1)} %copy-done.5, bf16[128,1024]{1,0:T(8,128)(2,1)S(1)} %copy-done.8, bf16[4,144,128]{2,1,0:T(8,128)(2,1)S(1)} %pair.2.after_ref), custom_call_target="tpu_custom_call" | custom-call | flops 3104999936 | bytes 1024 | tf_op jit(solution)/shard_map/local/pallas_call | solution.py:23
  19.8 1.0 %collective-permute-done.2.y_ref = bf16[4,144,128]{2,1,0:T(8,128)(2,1)S(1)} collective-permute-done((bf16[4,144,128]{2,1,0:T(8,128)(2,1)S(1)}, bf16[4,144,128]{2,1,0:T(8,128)(2,1)S(1)}, u32[]{:S(2)}, u32[]{:S(2)}) %collective-permute-start.2) | collective-permute-done | bytes 147488 | tf_op jit(solution)/shard_map/ppermute | solution.py:344
  21.2 1.8 %collective-permute-done.6.refs_0_ = bf16[128,1024]{1,0:T(8,128)(2,1)S(1)} collective-permute-done((bf16[128,1024]{1,0:T(8,128)(2,1)}, bf16[128,1024]{1,0:T(8,128)(2,1)S(1)}, u32[]{:S(2)}, u32[]{:S(2)}) %collective-permute-start.6) | collective-permute-done | bytes 262176 | tf_op jit(solution)/shard_map/ppermute | solution.py:374
  23.0 0.6 %collective-permute-start.7 = (bf16[128,1024]{1,0:T(8,128)(2,1)S(1)}, bf16[128,1024]{1,0:T(8,128)(2,1)S(1)}, u32[]{:S(2)}, u32[]{:S(2)}) collective-permute-start(bf16[128,1024]{1,0:T(8,128)(2,1)S(1)} %collective-permute-done.6.refs_0_), channel_id=1, source_target_pairs={{0,1},{1,0},{2,3},{3,2},{4,5},{5,4},{6,7},{7,6},{8,9},{9,8},{10,11... | collective-permute-start | bytes 786440 | tf_op jit(solution)/shard_map/ppermute | solution.py:374
  23.7 1.5 %unproject_near.1.refs_1_.refs_2_ = f32[128,1024]{1,0:T(8,128)S(1)} custom-call(s32[1]{0:T(128)} %bitcast.z_ref, bf16[128,1024]{1,0:T(8,128)(2,1)S(1)} %copy-done, bf16[128,1024]{1,0:T(8,128)(2,1)S(1)} %collective-permute-done.5.refs_1_, bf16[1024,4096]{1,0:T(8,128)(2,1)S(1)} %bitcast.13, f32[4,136,128]{2,1,0:T(8,128)S(1)} %join.2.refs_3_.own_ref), custom_call_target="tpu_custom_call" | custom-call | flops 1724999936 | bytes 1024 | tf_op jit(solution)/shard_map/unproject_near/pallas_call | solution.py:23
  25.2 1.5 %read.1 = (bf16[128,1024]{1,0:T(8,128)(2,1)S(1)}, f32[128,1024]{1,0:T(8,128)S(1)}, bf16[8,128,256]{2,1,0:T(8,128)(2,1)S(1)}, f32[8,8,128]{2,1,0:T(8,128)S(1)}, bf16[128,1024]{1,0:T(8,128)(2,1)S(1)}) custom-call(s32[1]{0:T(128)} %bitcast.1.pos_ref, s32[1]{0:T(128)} %bitcast.z_ref, s32[1,1]{1,0:T(1,128)} %bitcast.6.valid_ref, f32[8]{0:T(128)S(1)} %copy-done.3, ...), custom_call_target="tpu_custom_call" | custom-call | flops 1035000000 | bytes 1024 | tf_op jit(solution)/shard_map/read/pallas_call | solution.py:23
  26.7 1.5 %collective-permute-start.8 = (bf16[128,1024]{1,0:T(8,128)(2,1)S(1)}, bf16[128,1024]{1,0:T(8,128)(2,1)S(1)}, u32[]{:S(2)}, u32[]{:S(2)}) collective-permute-start(bf16[128,1024]{1,0:T(8,128)(2,1)S(1)} %get-tuple-element.26), channel_id=1, source_target_pairs={{0,1},{1,0},{2,3},{3,2},{4,5},{5,4},{6,7},{7,6},{8,9},{9,8},{10,11... | collective-permute-start | bytes 786440 | tf_op jit(solution)/shard_map/ppermute | solution.py:374
  28.2 0.8 %unproject_more.1.refs_1_ = f32[128,1024]{1,0:T(8,128)S(1)} custom-call(s32[1]{0:T(128)} %bitcast.z_ref, bf16[128,1024]{1,0:T(8,128)(2,1)S(1)} %collective-permute-done.6.refs_0_, bf16[1024,4096]{1,0:T(8,128)(2,1)S(1)} %bitcast.13, f32[128,1024]{1,0:T(8,128)S(1)} %unproject_near.1.refs_1_.refs_2_, bf16[128,1024]{1,0:T(8,128)(2,1)S(1)} %get-tuple-element.23.refs_3_.mixed_ref), custom_call_target="tpu_custom_call" | custom-call | flops 1035000000 | bytes 1024 | tf_op jit(solution)/shard_map/unproject_more/pallas_call | solution.py:23
  29.0 3.2 %collective-permute-done.7.refs_0_ = bf16[128,1024]{1,0:T(8,128)(2,1)S(1)} collective-permute-done((bf16[128,1024]{1,0:T(8,128)(2,1)S(1)}, bf16[128,1024]{1,0:T(8,128)(2,1)S(1)}, u32[]{:S(2)}, u32[]{:S(2)}) %collective-permute-start.7) | collective-permute-done | bytes 262176 | tf_op jit(solution)/shard_map/ppermute | solution.py:374
  32.3 4.2 %collective-permute-done.8.refs_3_.more_ref = bf16[128,1024]{1,0:T(8,128)(2,1)S(1)} collective-permute-done((bf16[128,1024]{1,0:T(8,128)(2,1)S(1)}, bf16[128,1024]{1,0:T(8,128)(2,1)S(1)}, u32[]{:S(2)}, u32[]{:S(2)}) %collective-permute-start.8) | collective-permute-done | bytes 262176 | tf_op jit(solution)/shard_map/ppermute | solution.py:374
  36.5 1.8 %spread.1 = (f32[8,136,128]{2,1,0:T(8,128)S(1)}, bf16[128,1024]{1,0:T(8,128)(2,1)S(1)}, f32[8,128,1]{2,1,0:T(8,128)S(1)}, bf16[128,1024]{1,0:T(8,128)(2,1)S(1)}) custom-call(s32[1]{0:T(128)} %bitcast.z_ref, s32[1,1]{1,0:T(1,128)} %bitcast.7.valid_ref, s32[1,1]{1,0:T(1,128)} %bitcast.11.starts_ref, f32[8]{0:T(128)S(1)} %copy-done.3, ...), custom_call_target="tpu_custom_call" | custom-call | flops 2875000064 | bytes 1024 | tf_op jit(solution)/shard_map/spread/pallas_call | solution.py:23
  38.4 0.5 project_add.1.refs_0_
  38.8 1.4 %collective-permute-start.11 = (bf16[128,1024]{1,0:T(8,128)(2,1)S(1)}, bf16[128,1024]{1,0:T(8,128)(2,1)S(1)}, u32[]{:S(2)}, u32[]{:S(2)}) collective-permute-start(bf16[128,1024]{1,0:T(8,128)(2,1)S(1)} %project_add.1.refs_0_), channel_id=1, source_target_pairs={{0,3},{1,2},{2,1},{3,0},{4,7},{5,6},{6,5},{7,4},{8,11},{9,10},{10,... | collective-permute-start | bytes 786440 | tf_op jit(solution)/shard_map/ppermute | solution.py:374
  40.4 0.7 %project_rest.1 = (bf16[128,1024]{1,0:T(8,128)(2,1)S(1)}, f32[128,1024]{1,0:T(8,128)S(1)}) custom-call(s32[1]{0:T(128)} %bitcast.z_ref, bf16[128,1024]{1,0:T(8,128)(2,1)S(1)} %get-tuple-element.23.refs_3_.mixed_ref, bf16[1024,4096]{1,0:T(8,128)(2,1)S(1)} %bitcast.13, bf16[4,144,128]{2,1,0:T(8,128)(2,1)S(1)} %pair.3.after_ref), custom_call_target="tpu_custom_call" | custom-call | flops 1495000064 | bytes 1024 | tf_op jit(solution)/shard_map/project_rest/pallas_call | solution.py:23
  41.1 1.6 %collective-permute-start.12 = (bf16[4,144,128]{2,1,0:T(8,128)(2,1)S(1)}, bf16[4,144,128]{2,1,0:T(8,128)(2,1)S(1)}, u32[]{:S(2)}, u32[]{:S(2)}) collective-permute-start(bf16[4,144,128]{2,1,0:T(8,128)(2,1)S(1)} %pair.3.after_ref), channel_id=1, source_target_pairs={{0,8},{4,12},{8,0},{12,4},{16,24},{20,28},{24,16},{28,20},{1,9},{5... | collective-permute-start | bytes 442376 | tf_op jit(solution)/shard_map/ppermute | solution.py:344
  42.7 1.5 %collective-permute-start.13 = (bf16[4,144,128]{2,1,0:T(8,128)(2,1)S(1)}, bf16[4,144,128]{2,1,0:T(8,128)(2,1)S(1)}, u32[]{:S(2)}, u32[]{:S(2)}) collective-permute-start(bf16[4,144,128]{2,1,0:T(8,128)(2,1)S(1)} %pair.3.after_ref), channel_id=1, source_target_pairs={{0,16},{4,20},{8,24},{12,28},{16,0},{20,4},{24,8},{28,12},{1,17},{... | collective-permute-start | bytes 442376 | tf_op jit(solution)/shard_map/ppermute | solution.py:344
  44.7 0.7 %collective-permute-start.10 = (bf16[128,1024]{1,0:T(8,128)(2,1)S(1)}, bf16[128,1024]{1,0:T(8,128)(2,1)S(1)}, u32[]{:S(2)}, u32[]{:S(2)}) collective-permute-start(bf16[128,1024]{1,0:T(8,128)(2,1)S(1)} %get-tuple-element.29.after_ref), channel_id=1, source_target_pairs={{0,1},{1,0},{2,3},{3,2},{4,5},{5,4},{6,7},{7,6},{8,9},{9,8},{10,11... | collective-permute-start | bytes 786440 | tf_op jit(solution)/shard_map/ppermute | solution.py:374
  45.4 3.7 %grads.1 = (bf16[128,1024]{1,0:T(8,128)(2,1)}, f32[128,1024]{1,0:T(8,128)S(1)}, f32[128,1024]{1,0:T(8,128)S(1)}) custom-call(s32[1,1]{1,0:T(1,128)} %bitcast.8.valid_ref, f32[8]{0:T(128)S(1)} %copy-done.3, bf16[128,1024]{1,0:T(8,128)(2,1)S(1)} %copy-done.2, bf16[128,1024]{1,0:T(8,128)(2,1)S(1)} %copy-done.6, bf16[128,1024]{1,0:T(8,128)(2,1)S(1)} %copy-done.9, ...), custom_call_target="tpu_custom_call" | custom-call | flops 3564999936 | bytes 1024 | tf_op jit(solution)/shard_map/grads/pallas_call | solution.py:23
  49.0 2.4 %collective-permute-done.13.y_ref = bf16[4,144,128]{2,1,0:T(8,128)(2,1)S(1)} collective-permute-done((bf16[4,144,128]{2,1,0:T(8,128)(2,1)S(1)}, bf16[4,144,128]{2,1,0:T(8,128)(2,1)S(1)}, u32[]{:S(2)}, u32[]{:S(2)}) %collective-permute-start.13) | collective-permute-done | bytes 147488 | tf_op jit(solution)/shard_map/ppermute | solution.py:344
  51.7 3.4 %collective-permute-done.10 = bf16[128,1024]{1,0:T(8,128)(2,1)S(1)} collective-permute-done((bf16[128,1024]{1,0:T(8,128)(2,1)S(1)}, bf16[128,1024]{1,0:T(8,128)(2,1)S(1)}, u32[]{:S(2)}, u32[]{:S(2)}) %collective-permute-start.10) | collective-permute-done | bytes 262176 | tf_op jit(solution)/shard_map/ppermute | solution.py:374
  55.1 0.8 %add_convert_fusion = bf16[128,1024]{1,0:T(8,128)(2,1)} fusion(bf16[128,1024]{1,0:T(8,128)(2,1)S(1)} %collective-permute-done.11, f32[128,1024]{1,0:T(8,128)S(1)} %get-tuple-element.28, bf16[128,1024]{1,0:T(8,128)(2,1)S(1)} %collective-permute-done.10), kind=kLoop, calls=%fused_computation | loop fusion | flops 655360 | bytes 1310720 | tf_op jit(solution)/shard_map/convert_element_type | solution.py:467
  55.9 1.5 %last.1 = (bf16[128,1024]{1,0:T(8,128)(2,1)}, bf16[128,1024]{1,0:T(8,128)(2,1)}) custom-call(s32[1]{0:T(128)} %bitcast.1.pos_ref, s32[1,1]{1,0:T(1,128)} %bitcast.9.valid_ref, bf16[128,1024]{1,0:T(8,128)(2,1)S(1)} %copy-done.6, bf16[128,1024]{1,0:T(8,128)(2,1)S(1)} %copy-done.9, f32[8,136,128]{2,1,0:T(8,128)S(1)} %collective-permute-done.9.other_ref, ...), custom_call_target="tpu_custom_call" | custom-call | flops 1724999936 | bytes 1024 | tf_op jit(solution)/shard_map/last/pallas_call | solution.py:23
  (40 shorter events, 2.4 us)
Async XLA Ops:
  0.6 23.0 %copy-start = (bf16[128,1024]{1,0:T(8,128)(2,1)S(1)}, bf16[128,1024]{1,0:T(8,128)(2,1)}, u32[]{:S(2)}) copy-start(bf16[128,1024]{1,0:T(8,128)(2,1)} %refs_0_.2) | copy-start | bytes 786436
  0.6 23.0 %slice-start = ((s8[8388608]{0:T(1024)(128)(4,1)}), s8[4194304]{0:T(1024)(128)(4,1)S(1)}, s32[]{:S(2)}) async-start(s8[8388608]{0:T(1024)(128)(4,1)} %bitcast.12), calls=%async_computation | async-start | bytes 8388608
  2.5 1.0 %copy-start.4 = (bf16[128,1024]{1,0:T(8,128)(2,1)S(1)}, bf16[128,1024]{1,0:T(8,128)(2,1)}, u32[]{:S(2)}) copy-start(bf16[128,1024]{1,0:T(8,128)(2,1)} %k_ref.7) | copy-start | bytes 786436
  3.5 0.9 %copy-start.7 = (bf16[128,1024]{1,0:T(8,128)(2,1)S(1)}, bf16[128,1024]{1,0:T(8,128)(2,1)}, u32[]{:S(2)}) copy-start(bf16[128,1024]{1,0:T(8,128)(2,1)} %v_ref.7) | copy-start | bytes 786436
  4.8 5.6 %collective-permute-start = (f32[8,136,128]{2,1,0:T(8,128)S(1)}, f32[8,136,128]{2,1,0:T(8,128)S(1)}, u32[]{:S(2)}, u32[]{:S(2)}) collective-permute-start(f32[8,136,128]{2,1,0:T(8,128)S(1)} %state.1.mine_ref), channel_id=1, source_target_pairs={{0,4},{4,0},{8,12},{12,8},{16,20},{20,16},{24,28},{28,24},{1,5},{5... | collective-permute-start | bytes 1671176 | tf_op jit(solution)/shard_map/ppermute | solution.py:334
  5.3 18.3 %collective-permute-start.5 = (bf16[128,1024]{1,0:T(8,128)(2,1)}, bf16[128,1024]{1,0:T(8,128)(2,1)S(1)}, u32[]{:S(2)}, u32[]{:S(2)}) collective-permute-start(bf16[128,1024]{1,0:T(8,128)(2,1)} %refs_0_.2), channel_id=1, source_target_pairs={{0,1},{1,0},{2,3},{3,2},{4,5},{5,4},{6,7},{7,6},{8,9},{9,8},{10,11... | collective-permute-start | bytes 786440 | tf_op jit(solution)/shard_map/ppermute | solution.py:374
  8.0 15.0 %collective-permute-start.6 = (bf16[128,1024]{1,0:T(8,128)(2,1)}, bf16[128,1024]{1,0:T(8,128)(2,1)S(1)}, u32[]{:S(2)}, u32[]{:S(2)}) collective-permute-start(bf16[128,1024]{1,0:T(8,128)(2,1)} %refs_0_.2), channel_id=1, source_target_pairs={{0,3},{1,2},{2,1},{3,0},{4,7},{5,6},{6,5},{7,4},{8,11},{9,10},{10,... | collective-permute-start | bytes 786440 | tf_op jit(solution)/shard_map/ppermute | solution.py:374
  10.7 9.1 %collective-permute-start.1 = (bf16[4,144,128]{2,1,0:T(8,128)(2,1)S(1)}, bf16[4,144,128]{2,1,0:T(8,128)(2,1)S(1)}, u32[]{:S(2)}, u32[]{:S(2)}) collective-permute-start(bf16[4,144,128]{2,1,0:T(8,128)(2,1)S(1)} %pair.2.after_ref), channel_id=1, source_target_pairs={{0,8},{4,12},{8,0},{12,4},{16,24},{20,28},{24,16},{28,20},{1,9},{5... | collective-permute-start | bytes 442376 | tf_op jit(solution)/shard_map/ppermute | solution.py:344
  12.3 8.5 %collective-permute-start.2 = (bf16[4,144,128]{2,1,0:T(8,128)(2,1)S(1)}, bf16[4,144,128]{2,1,0:T(8,128)(2,1)S(1)}, u32[]{:S(2)}, u32[]{:S(2)}) collective-permute-start(bf16[4,144,128]{2,1,0:T(8,128)(2,1)S(1)} %pair.2.after_ref), channel_id=1, source_target_pairs={{0,16},{4,20},{8,24},{12,28},{16,0},{20,4},{24,8},{28,12},{1,17},{... | collective-permute-start | bytes 442376 | tf_op jit(solution)/shard_map/ppermute | solution.py:344
  13.8 7.0 %collective-permute-start.3 = (bf16[4,144,128]{2,1,0:T(8,128)(2,1)S(1)}, bf16[4,144,128]{2,1,0:T(8,128)(2,1)S(1)}, u32[]{:S(2)}, u32[]{:S(2)}) collective-permute-start(bf16[4,144,128]{2,1,0:T(8,128)(2,1)S(1)} %pair.2.after_ref), channel_id=1, source_target_pairs={{0,24},{4,28},{8,16},{12,20},{16,8},{20,12},{24,0},{28,4},{1,25},{... | collective-permute-start | bytes 442376 | tf_op jit(solution)/shard_map/ppermute | solution.py:344
  14.3 0.9 %copy-start.1 = (bf16[128,1024]{1,0:T(8,128)(2,1)S(1)}, bf16[128,1024]{1,0:T(8,128)(2,1)}, u32[]{:S(2)}) copy-start(bf16[128,1024]{1,0:T(8,128)(2,1)} %q_ref.7) | copy-start | bytes 786436
  15.2 0.9 %copy-start.5 = (bf16[128,1024]{1,0:T(8,128)(2,1)S(1)}, bf16[128,1024]{1,0:T(8,128)(2,1)}, u32[]{:S(2)}) copy-start(bf16[128,1024]{1,0:T(8,128)(2,1)} %k_ref.7) | copy-start | bytes 786436
  16.2 0.9 %copy-start.8 = (bf16[128,1024]{1,0:T(8,128)(2,1)S(1)}, bf16[128,1024]{1,0:T(8,128)(2,1)}, u32[]{:S(2)}) copy-start(bf16[128,1024]{1,0:T(8,128)(2,1)} %v_ref.7) | copy-start | bytes 786436
  17.1 6.5 %slice-start.1 = ((s8[8388608]{0:T(1024)(128)(4,1)}), s8[4194304]{0:T(1024)(128)(4,1)S(1)}, s32[]{:S(2)}) async-start(s8[8388608]{0:T(1024)(128)(4,1)} %bitcast.12), calls=%async_computation.1 | async-start | bytes 8388608
  17.1 8.1 %copy-start.2 = (bf16[128,1024]{1,0:T(8,128)(2,1)S(1)}, bf16[128,1024]{1,0:T(8,128)(2,1)}, u32[]{:S(2)}) copy-start(bf16[128,1024]{1,0:T(8,128)(2,1)} %q_ref.7) | copy-start | bytes 786436
  17.1 8.1 %copy-start.3 = (f32[8]{0:T(128)S(1)}, f32[8]{0:T(128)}, u32[]{:S(2)}) copy-start(f32[8]{0:T(128)} %gate_ref.5) | copy-start | bytes 100
  21.1 4.1 %collective-permute-start.4 = (f32[4,136,128]{2,1,0:T(8,128)S(1)}, f32[4,136,128]{2,1,0:T(8,128)S(1)}, u32[]{:S(2)}, u32[]{:S(2)}) collective-permute-start(f32[4,136,128]{2,1,0:T(8,128)S(1)} %join.2.refs_3_.own_ref), channel_id=1, source_target_pairs={{0,4},{4,0},{8,12},{12,8},{16,20},{20,16},{24,28},{28,24},{1,5},{5... | collective-permute-start | bytes 835592 | tf_op jit(solution)/shard_map/ppermute | solution.py:354
  23.0 9.2 %collective-permute-start.7 = (bf16[128,1024]{1,0:T(8,128)(2,1)S(1)}, bf16[128,1024]{1,0:T(8,128)(2,1)S(1)}, u32[]{:S(2)}, u32[]{:S(2)}) collective-permute-start(bf16[128,1024]{1,0:T(8,128)(2,1)S(1)} %collective-permute-done.6.refs_0_), channel_id=1, source_target_pairs={{0,1},{1,0},{2,3},{3,2},{4,5},{5,4},{6,7},{7,6},{8,9},{9,8},{10,11... | collective-permute-start | bytes 786440 | tf_op jit(solution)/shard_map/ppermute | solution.py:374
  26.7 9.7 %collective-permute-start.8 = (bf16[128,1024]{1,0:T(8,128)(2,1)S(1)}, bf16[128,1024]{1,0:T(8,128)(2,1)S(1)}, u32[]{:S(2)}, u32[]{:S(2)}) collective-permute-start(bf16[128,1024]{1,0:T(8,128)(2,1)S(1)} %get-tuple-element.26), channel_id=1, source_target_pairs={{0,1},{1,0},{2,3},{3,2},{4,5},{5,4},{6,7},{7,6},{8,9},{9,8},{10,11... | collective-permute-start | bytes 786440 | tf_op jit(solution)/shard_map/ppermute | solution.py:374
  38.3 7.1 %copy-start.6 = (bf16[128,1024]{1,0:T(8,128)(2,1)S(1)}, bf16[128,1024]{1,0:T(8,128)(2,1)}, u32[]{:S(2)}) copy-start(bf16[128,1024]{1,0:T(8,128)(2,1)} %k_ref.7) | copy-start | bytes 786436
  38.3 7.1 %copy-start.9 = (bf16[128,1024]{1,0:T(8,128)(2,1)S(1)}, bf16[128,1024]{1,0:T(8,128)(2,1)}, u32[]{:S(2)}) copy-start(bf16[128,1024]{1,0:T(8,128)(2,1)} %v_ref.7) | copy-start | bytes 786436
  38.3 2.0 %collective-permute-start.9 = (f32[8,136,128]{2,1,0:T(8,128)S(1)}, f32[8,136,128]{2,1,0:T(8,128)S(1)}, u32[]{:S(2)}, u32[]{:S(2)}) collective-permute-start(f32[8,136,128]{2,1,0:T(8,128)S(1)} %get-tuple-element.27.after_ref.mine_ref), channel_id=1, source_target_pairs={{0,4},{4,0},{8,12},{12,8},{16,20},{20,16},{24,28},{28,24},{1,5},{5... | collective-permute-start | bytes 1671176 | tf_op jit(solution)/shard_map/ppermute | solution.py:334
  38.8 12.8 %collective-permute-start.11 = (bf16[128,1024]{1,0:T(8,128)(2,1)S(1)}, bf16[128,1024]{1,0:T(8,128)(2,1)S(1)}, u32[]{:S(2)}, u32[]{:S(2)}) collective-permute-start(bf16[128,1024]{1,0:T(8,128)(2,1)S(1)} %project_add.1.refs_0_), channel_id=1, source_target_pairs={{0,3},{1,2},{2,1},{3,0},{4,7},{5,6},{6,5},{7,4},{8,11},{9,10},{10,... | collective-permute-start | bytes 786440 | tf_op jit(solution)/shard_map/ppermute | solution.py:374
  41.1 7.9 %collective-permute-start.12 = (bf16[4,144,128]{2,1,0:T(8,128)(2,1)S(1)}, bf16[4,144,128]{2,1,0:T(8,128)(2,1)S(1)}, u32[]{:S(2)}, u32[]{:S(2)}) collective-permute-start(bf16[4,144,128]{2,1,0:T(8,128)(2,1)S(1)} %pair.3.after_ref), channel_id=1, source_target_pairs={{0,8},{4,12},{8,0},{12,4},{16,24},{20,28},{24,16},{28,20},{1,9},{5... | collective-permute-start | bytes 442376 | tf_op jit(solution)/shard_map/ppermute | solution.py:344
  42.7 8.8 %collective-permute-start.13 = (bf16[4,144,128]{2,1,0:T(8,128)(2,1)S(1)}, bf16[4,144,128]{2,1,0:T(8,128)(2,1)S(1)}, u32[]{:S(2)}, u32[]{:S(2)}) collective-permute-start(bf16[4,144,128]{2,1,0:T(8,128)(2,1)S(1)} %pair.3.after_ref), channel_id=1, source_target_pairs={{0,16},{4,20},{8,24},{12,28},{16,0},{20,4},{24,8},{28,12},{1,17},{... | collective-permute-start | bytes 442376 | tf_op jit(solution)/shard_map/ppermute | solution.py:344
  44.2 7.3 %collective-permute-start.14 = (bf16[4,144,128]{2,1,0:T(8,128)(2,1)S(1)}, bf16[4,144,128]{2,1,0:T(8,128)(2,1)S(1)}, u32[]{:S(2)}, u32[]{:S(2)}) collective-permute-start(bf16[4,144,128]{2,1,0:T(8,128)(2,1)S(1)} %pair.3.after_ref), channel_id=1, source_target_pairs={{0,24},{4,28},{8,16},{12,20},{16,8},{20,12},{24,0},{28,4},{1,25},{... | collective-permute-start | bytes 442376 | tf_op jit(solution)/shard_map/ppermute | solution.py:344
  44.7 10.4 %collective-permute-start.10 = (bf16[128,1024]{1,0:T(8,128)(2,1)S(1)}, bf16[128,1024]{1,0:T(8,128)(2,1)S(1)}, u32[]{:S(2)}, u32[]{:S(2)}) collective-permute-start(bf16[128,1024]{1,0:T(8,128)(2,1)S(1)} %get-tuple-element.29.after_ref), channel_id=1, source_target_pairs={{0,1},{1,0},{2,3},{3,2},{4,5},{5,4},{6,7},{7,6},{8,9},{9,8},{10,11... | collective-permute-start | bytes 786440 | tf_op jit(solution)/shard_map/ppermute | solution.py:374
  51.6 4.3 %collective-permute-start.15 = (f32[4,136,128]{2,1,0:T(8,128)S(1)}, f32[4,136,128]{2,1,0:T(8,128)S(1)}, u32[]{:S(2)}, u32[]{:S(2)}) collective-permute-start(f32[4,136,128]{2,1,0:T(8,128)S(1)} %join.3.own_ref), channel_id=1, source_target_pairs={{0,4},{4,0},{8,12},{12,8},{16,20},{20,16},{24,28},{28,24},{1,5},{5... | collective-permute-start | bytes 835592 | tf_op jit(solution)/shard_map/ppermute | solution.py:354

commit v4 on v3

v4 whole, which is shorter than its diff:
```python
import functools

import jax
import jax.numpy as jnp
from jax import lax
from jax.experimental import pallas as pl
from jax.experimental.pallas import tpu as pltpu
from jax.sharding import PartitionSpec as P

DH = 128
ROWS = 136
SENT = 144
BF16 = jnp.bfloat16
F32 = jnp.float32
VMEM = pl.BlockSpec(memory_space=pltpu.VMEM)
SMEM = pl.BlockSpec(memory_space=pltpu.SMEM)


ANY = pl.BlockSpec(memory_space=pl.ANY)


def call(kernel, outs, in_specs, args, micros, name):
    return pl.pallas_call(
        kernel,
        out_shape=outs,
        in_specs=in_specs,
        out_specs=[VMEM] * len(outs),
        compiler_params=pltpu.CompilerParams(vmem_limit_bytes=24 * 1024 * 1024),
        cost_estimate=pl.CostEstimate(flops=int(micros * 1.15e9), bytes_accessed=1024, transcendentals=0),
        name=name,
    )(*args)


def feature(x):
    return jnp.where(x > 0, x + 1.0, jnp.exp(jnp.minimum(x, 0.0)))


def slope(x):
    return jnp.where(x > 0, 1.0, jnp.where(x == 0, 0.5, jnp.exp(jnp.minimum(x, 0.0))))


def sigmoid(x):
    return 1.0 / (1.0 + jnp.exp(-x))


def dot(a, b, dims):
    return lax.dot_general(a, b, (dims, ((), ())), preferred_element_type=F32)


NN = ((1,), (0,))
NT = ((1,), (1,))
TN = ((0,), (0,))


def live_rows(valid_ref, length):
    where = lax.broadcasted_iota(jnp.int32, (length, 1), 0)
    return (where < valid_ref[...]).astype(F32)


def opened(starts_ref):
    return 1.0 - starts_ref[...].astype(F32)


def gate_row(gate_ref, h):
    return sigmoid(jnp.full((1, DH), gate_ref[h], F32))


def head(ref, h):
    return ref[:, h * DH : (h + 1) * DH]


def tail(rows, *values):
    where = lax.broadcasted_iota(jnp.int32, (rows, DH), 0)
    out = jnp.zeros((rows, DH), F32)
    for at, value in enumerate(values):
        out = jnp.where(where == at, value, out)
    return out


def split(x):
    top = x.astype(BF16)
    rest = x - top.astype(F32)
    return top, rest.astype(BF16)


def cut(h):
    return pl.ds(h * DH if isinstance(h, int) else pl.multiple_of(h * DH, DH), DH)


def by_half(heads, pos_ref):
    half = lax.rem(pos_ref[0], 2)
    count = heads // 2
    for kept, first in ((True, half * count), (False, (1 - half) * count)):
        for i in range(count):
            yield kept, i, first + i


def state_kernel(
    heads, pos_ref, z_ref, valid_ref, starts_ref, k_ref, v_ref, keep_ref, give_ref
):
    live = live_rows(valid_ref, k_ref.shape[0])
    for kept, i, h in by_half(heads, pos_ref):
        out_ref = keep_ref if kept else give_ref
        sig = (feature(k_ref[:, cut(h)].astype(F32)) * live).astype(BF16)
        out_ref[i, 0:DH, :] = dot(sig, v_ref[:, cut(h)], TN)
        norm = jnp.sum(sig.astype(F32), axis=0, keepdims=True)
        out_ref[i, DH:ROWS, :] = tail(ROWS - DH, norm, opened(starts_ref))


def in_three(x):
    first = x.astype(BF16).astype(F32)
    second = (x - first).astype(BF16).astype(F32)
    return first, second, x - first - second


def store_sent(ref, i, memory, norm, flag, centre):
    ref[i, 0:DH, :] = memory.astype(BF16)
    ref[i, DH:SENT, :] = tail(SENT - DH, *in_three(norm), centre, flag).astype(BF16)


def load_sent(ref, i, centred):
    memory = ref[i, 0:DH, :].astype(F32)
    rows = ref[i, DH:SENT, :].astype(F32)
    if centred:
        norms = tail(16, rows[0:1], rows[1:2], rows[2:3]).astype(BF16)
        centres = tail(16, rows[3:4], rows[3:4], rows[3:4]).astype(BF16)
        memory = memory + dot(norms, centres, TN)
    return memory, rows[0:1] + rows[1:2] + rows[2:3], rows[4:5]


def load_state(ref, i):
    return ref[i, 0:DH, :], ref[i, DH : DH + 1, :], ref[i, DH + 1 : DH + 2, :]


def load_other(ref, i, forward):
    return load_state(ref, i) if forward else load_sent(ref, i, False)


def pair_kernel(heads, forward, pos_ref, keep_ref, other_ref, *refs):
    sent_ref = refs[-1]
    lower = lax.rem(pos_ref[0], 2) == 0
    for i in range(heads // 2):
        memory, norm, flag = load_state(keep_ref, i)
        other_memory, other_norm, other_flag = load_other(other_ref, i, forward)
        one = jnp.ones_like(flag)
        if forward:
            on_mine = jnp.where(lower, other_flag, one)
            on_other = jnp.where(lower, one, flag)
        else:
            on_mine = jnp.where(lower, flag, flag * other_flag)
            on_other = jnp.where(lower, flag * other_flag, other_flag)
        memory = on_mine * memory + on_other * other_memory
        norm = on_mine * norm + on_other * other_norm
        centre = jnp.zeros_like(norm)
        if forward:
            weight = jnp.maximum(jnp.sum(norm, axis=1, keepdims=True), 1e-30)
            centre = jnp.sum(memory, axis=0, keepdims=True) / weight
            centre = centre.astype(BF16).astype(F32)
            norms = tail(16, *in_three(norm)).astype(BF16)
            centres = tail(16, centre, centre, centre).astype(BF16)
            memory = memory - dot(norms, centres, TN)
        store_sent(sent_ref, i, memory, norm, flag * other_flag, centre)


def join_kernel(
    heads, forward, pos_ref, x_ref, y_ref, d_ref, keep_ref, other_ref, *refs
):
    own_ref, sent_ref = refs[-2:]
    lower = lax.rem(pos_ref[0], 2) == 0
    chip = pos_ref[0] // 2
    place = chip if forward else 3 - chip
    odd, high = lax.rem(place, 2) == 1, place >= 2
    for i in range(heads // 2):
        x_mem, x_norm, x_open = load_sent(x_ref, i, forward)
        y_mem, y_norm, y_open = load_sent(y_ref, i, forward)
        d_mem, d_norm, d_open = load_sent(d_ref, i, forward)
        on_x = jnp.where(odd, jnp.ones_like(x_open), 0.0)
        on_y = jnp.where(high, jnp.where(odd, x_open, d_open), 0.0)
        on_d = jnp.where(high, jnp.where(odd, x_open * y_open, 1.0), 0.0)
        memory = on_x * x_mem + on_y * y_mem + on_d * d_mem
        norm = on_x * x_norm + on_y * y_norm + on_d * d_norm
        mine_mem, mine_norm, mine_open = load_state(keep_ref, i)
        other_mem, other_norm, other_open = load_other(other_ref, i, forward)
        if forward:
            own = (
                jnp.where(lower, memory, other_open * memory + other_mem),
                jnp.where(lower, norm, other_open * norm + other_norm),
            )
            sent = (
                jnp.where(lower, mine_open * memory + mine_mem, memory),
                jnp.where(lower, mine_open * norm + mine_norm, norm),
            )
        else:
            own = (
                jnp.where(lower, other_open * (memory + other_mem), memory),
                jnp.where(lower, other_open * (norm + other_norm), norm),
            )
            sent = (
                jnp.where(lower, memory, mine_open * (memory + mine_mem)),
                jnp.where(lower, norm, mine_open * (norm + mine_norm)),
            )
        for ref, (value, sums) in ((own_ref, own), (sent_ref, sent)):
            ref[i, 0:DH, :] = value
            ref[i, DH:ROWS, :] = tail(ROWS - DH, sums)


def local_kernel(heads, valid_ref, q_ref, k_ref, v_ref, after_ref, probs_ref, local_ref):
    length = q_ref.shape[0]
    row = lax.broadcasted_iota(jnp.int32, (length, length), 0)
    col = lax.broadcasted_iota(jnp.int32, (length, length), 1)
    allowed = (col <= row) & (col < valid_ref[...])
    for h in range(heads):
        scores = dot(head(q_ref, h), head(k_ref, h), NT) * DH ** (-0.5)
        scores = jnp.where(allowed, scores, -1e30)
        expo = jnp.exp(scores - jnp.max(scores, axis=1, keepdims=True))
        probs = (expo / jnp.sum(expo, axis=1, keepdims=True)).astype(BF16)
        probs_ref[h] = probs
        local_ref[:, h * DH : (h + 1) * DH] = dot(probs, head(v_ref, h), NN)


def columns(z_ref, way, cols):
    return pl.ds(pl.multiple_of((z_ref[0] ^ way) * cols, DH), cols)


def read_kernel(
    heads, project, pos_ref, z_ref, valid_ref, gate_ref, q_ref, keep_ref, own_ref, far_ref,
    local_ref, *refs,
):
    if project:
        weight_ref, _, mixed_ref, read_ref, memory_ref, norm_ref, first_ref = refs
    else:
        mixed_ref, read_ref, memory_ref, norm_ref = refs
    live = live_rows(valid_ref, q_ref.shape[0])
    for kept, i, h in by_half(heads, pos_ref):
        carry, norm, _ = load_state(own_ref if kept else far_ref, i)
        flag = keep_ref[i, DH + 1 : DH + 2, :]
        norm = flag * norm
        parts = jnp.concatenate(split(flag * carry), axis=1)
        memory_ref[h] = parts
        norm_ref[h] = jnp.broadcast_to(norm, (8, DH))
        sig = feature(q_ref[:, cut(h)].astype(F32)).astype(BF16)
        numer = dot(sig, parts, NN)
        numer = numer[:, 0:DH] + numer[:, DH:]
        denom = jnp.sum(sig.astype(F32) * norm, axis=1, keepdims=True) + 1.0
        read = numer / denom
        gate = gate_row(gate_ref, h)
        mixed = live * (gate * read + (1.0 - gate) * local_ref[:, cut(h)])
        read_ref[:, cut(h)] = read
        mixed_ref[:, cut(h)] = mixed.astype(BF16)
    if project:
        block = weight_ref[:, columns(z_ref, 2, first_ref.shape[1])]
        first_ref[...] = dot(mixed_ref[...], block, NN).astype(BF16)


def pass_kernel(block_ref, after_ref, out_ref):
    out_ref[...] = block_ref[...]


def token_kernel(*refs):
    refs[-1][...] = jnp.zeros(refs[-1].shape, F32)


def more_kernel(ways, z_ref, *refs):
    grad_refs, (weight_ref, *before, after_ref, total_ref) = refs[: len(ways)], refs[len(ways) :]
    total = before[0][...] if before else None
    for way, grad_ref in zip(ways, grad_refs):
        block = weight_ref[:, columns(z_ref, way, grad_ref.shape[1])]
        part = dot(grad_ref[...], block, NT)
        total = part if total is None else total + part
    total_ref[...] = total


def add_kernel(z_ref, mixed_ref, weight_ref, more_ref, after_ref, out_ref):
    block = weight_ref[:, columns(z_ref, 3, out_ref.shape[1])]
    part = dot(mixed_ref[...], block, NN)
    out_ref[...] = (part + more_ref[...].astype(F32)).astype(BF16)


def rest_kernel(z_ref, mixed_ref, weight_ref, after_ref, near_ref, own_ref):
    cols = own_ref.shape[1]
    near = dot(mixed_ref[...], weight_ref[:, columns(z_ref, 1, cols)], NN)
    near_ref[...] = near.astype(BF16)
    own_ref[...] = dot(mixed_ref[...], weight_ref[:, columns(z_ref, 0, cols)], NN)


def spread_kernel(
    heads, ways, packed, pos_ref, z_ref, valid_ref, starts_ref, gate_ref, q_ref, norm_ref, read_ref, *refs,
):
    if ways:
        parts, (total_ref, weight_ref) = refs[: len(ways)], refs[len(ways) : len(ways) + 2]
        keep_ref, give_ref, numer_ref, denom_ref, grad_ref = refs[-5:]
        total = total_ref[...]
        for way, part_ref in zip(ways, parts):
            block = weight_ref[:, columns(z_ref, way, part_ref.shape[1])]
            total = total + dot(part_ref[...], block, NT)
        grad_ref[...] = total.astype(BF16)
    else:
        grad_ref, keep_ref, give_ref, numer_ref, denom_ref = refs
    live = live_rows(valid_ref, q_ref.shape[0])
    for kept, i, h in by_half(heads, pos_ref):
        sig = feature(q_ref[:, cut(h)].astype(F32)).astype(BF16)
        sig_full = sig.astype(F32)
        denom = jnp.sum(sig_full * norm_ref[h, 0:1, :], axis=1, keepdims=True) + 1.0
        gate = gate_row(gate_ref, h)
        numer_grad = (grad_ref[:, cut(h)].astype(F32) * gate * (live / denom)).astype(BF16)
        denom_grad = -jnp.sum(
            numer_grad.astype(F32) * read_ref[:, cut(h)], axis=1, keepdims=True
        )
        memory = dot(sig, numer_grad, TN)
        norm = jnp.sum(sig_full * denom_grad, axis=0, keepdims=True)
        numer_ref[:, cut(h)] = numer_grad
        denom_ref[h] = denom_grad
        flag = opened(starts_ref)
        if packed and not kept:
            store_sent(give_ref, i, memory, norm, flag, jnp.zeros_like(norm))
        else:
            out_ref = keep_ref if kept else give_ref
            out_ref[i, 0:DH, :] = memory
            out_ref[i, DH:ROWS, :] = tail(ROWS - DH, norm, flag)


def grads_kernel(heads, valid_ref, gate_ref, q_ref, k_ref, v_ref, probs_ref, grad_ref, numer_ref,
                 denom_ref, memory_ref, norm_ref, after_ref, query_ref, key_ref, value_ref):
    length = q_ref.shape[0]
    live = live_rows(valid_ref, length)
    for h in range(heads):
        here = slice(h * DH, (h + 1) * DH)
        q, k, v = head(q_ref, h), head(k_ref, h), head(v_ref, h)
        gate = gate_row(gate_ref, h)
        grad = (head(grad_ref, h).astype(F32) * (1.0 - gate) * live).astype(BF16)
        probs = probs_ref[h]
        probs_grad = dot(grad, v, NT)
        full = probs.astype(F32)
        mean = jnp.sum(full * probs_grad, axis=1, keepdims=True)
        scores_grad = (full * (probs_grad - mean) * DH ** (-0.5)).astype(BF16)
        key_ref[:, here] = dot(scores_grad, q, TN)
        value_ref[:, here] = dot(probs, grad, TN)
        parts = memory_ref[h]
        numer = head(numer_ref, h)
        sig_grad = dot(numer, parts[:, 0:DH], NT) + dot(numer, parts[:, DH:], NT)
        sig_grad = sig_grad + denom_ref[h] * norm_ref[h, 0:1, :]
        total = dot(scores_grad, k, NN) + sig_grad * slope(q.astype(F32))
        query_ref[:, here] = total.astype(BF16)


def last_kernel(heads, pos_ref, valid_ref, k_ref, v_ref, own_ref, far_ref, key_ref, value_ref,
                key_out, value_out):
    live = live_rows(valid_ref, k_ref.shape[0])
    for kept, i, h in by_half(heads, pos_ref):
        memory, norm, _ = load_state(own_ref if kept else far_ref, i)
        top, low = split(memory)
        k, v = k_ref[:, cut(h)].astype(F32), v_ref[:, cut(h)]
        sig = (feature(k) * live).astype(BF16)
        sig_grad = (dot(v, top, NT) + dot(v, low, NT) + norm) * live
        key_out[:, cut(h)] = (key_ref[:, cut(h)] + sig_grad * slope(k)).astype(BF16)
        more = dot(sig, jnp.concatenate([top, low], axis=1), NN)
        value_out[:, cut(h)] = (value_ref[:, cut(h)] + more[:, 0:DH] + more[:, DH:]).astype(BF16)


def weighted(state, forward):
    count, mine = lax.axis_size("seq"), lax.axis_index("seq")
    states = lax.all_gather(state, "seq")
    total = jnp.zeros_like(state)
    weight = jnp.ones((), F32)

    def turn(step, carried):
        total, weight = carried
        at = mine - 1 - step if forward else mine + 1 + step
        inside = (at >= 0) & (at < count)
        one = lax.dynamic_index_in_dim(states, jnp.clip(at, 0, count - 1), keepdims=False)
        opened = one[0, DH + 1, 0]
        here = weight if forward else weight * opened
        total = jnp.where(inside, total + here * one, total)
        return total, weight * opened

    return lax.fori_loop(0, count - 1, turn, (total, weight))[0]


def scan_states(keep, give, pos, heads, forward, before_pair, before_join):
    count = lax.axis_size("seq")
    half = heads // 2
    if count != 8:
        before_pair()
        before_join(keep)
        carry = weighted(jnp.concatenate([keep, give]), forward)
        return carry[:half], carry[half:]
    pairs = [(s, s ^ 1) for s in range(count)]
    other = lax.ppermute(give, "seq", pairs)
    after = before_pair()
    sent = call(
        functools.partial(pair_kernel, heads, forward),
        [jax.ShapeDtypeStruct((half, SENT, DH), BF16)],
        [SMEM, VMEM, VMEM] + [ANY] * len(after),
        [pos, keep, other, *after],
        0.3, "pair",
    )[0]
    arrived = [
        lax.ppermute(sent, "seq", [(s, s ^ way) for s in range(count)]) for way in (6, 2, 4)
    ]
    after = before_join(sent)
    own, passed = call(
        functools.partial(join_kernel, heads, forward),
        [jax.ShapeDtypeStruct((half, ROWS, DH), F32)] * 2,
        [SMEM] + [VMEM] * 5 + [ANY] * len(after),
        [pos, arrived[1], arrived[2], arrived[0], keep, other, *after],
        0.3, "join",
    )
    return own, lax.ppermute(passed, "seq", pairs)


def shards(queries, keys, values, gate, out_weight, out_grad, valid, starts):
    length, width = queries.shape
    heads = width // DH
    cols = out_grad.shape[1]
    groups = lax.axis_size("head")
    direct = groups == 4
    pos = lax.axis_index("seq").astype(jnp.int32).reshape(1)
    paired = lax.axis_size("seq") == 8
    if not paired:
        pos = jnp.zeros_like(pos)
    z = lax.axis_index("head").astype(jnp.int32).reshape(1)
    valid, starts = valid.reshape(1, 1), starts.reshape(1, 1)
    flat = jax.ShapeDtypeStruct((length, width), F32)
    low = jax.ShapeDtypeStruct((length, width), BF16)
    part_low = jax.ShapeDtypeStruct((length, cols), BF16)
    part_full = jax.ShapeDtypeStruct((length, cols), F32)
    states = jax.ShapeDtypeStruct((heads // 2, ROWS, DH), F32)
    packed = jax.ShapeDtypeStruct((heads // 2, SENT, DH), BF16)

    def swap(array, way):
        return lax.ppermute(array, "head", [(s, s ^ way) for s in range(groups)])

    keep, give = call(
        functools.partial(state_kernel, heads), [states] * 2, [SMEM] * 2 + [VMEM] * 4,
        [pos, z, valid, starts, keys, values], 0.4, "state",
    )
    if direct:
        grad_3 = swap(out_grad, 3)
        grad_1 = swap(out_grad, 1)
    kept = {}

    def beside_forward(sent):
        kept["local"] = call(
            functools.partial(local_kernel, heads),
            [jax.ShapeDtypeStruct((heads, length, length), BF16), flat],
            [VMEM] * 4 + [ANY],
            [valid, queries, keys, values, sent], 3, "local",
        )
        return [kept["local"][1]]

    own, far = scan_states(keep, give, pos, heads, True, lambda: [], beside_forward)
    probs, local = kept["local"]
    orders = []
    if direct:
        grad_2 = swap(
            call(pass_kernel, [part_low], [VMEM, ANY], [grad_3, own], 0.1, "pass_on")[0], 1
        )
        orders = call(
            token_kernel, [jax.ShapeDtypeStruct((8, DH), F32)], [ANY] * 2, [grad_1, own],
            3, "arrived",
        )
    outs = call(
        functools.partial(read_kernel, heads, direct),
        [low, flat, jax.ShapeDtypeStruct((heads, DH, 2 * DH), BF16),
         jax.ShapeDtypeStruct((heads, 8, DH), F32)] + [part_low] * direct,
        [SMEM, SMEM, VMEM, SMEM] + [VMEM] * 5 + [VMEM, ANY] * direct,
        [pos, z, valid, gate, queries, keep, own, far, local] + [out_weight, *orders] * direct,
        0.1, "read",
    )
    mixed, read, memory, norm = outs[:4]
    if direct:
        sum_2 = swap(outs[4], 1)
        total = call(
            functools.partial(more_kernel, (0, 1, 3)), [flat], [SMEM] + [VMEM] * 4 + [ANY],
            [z, out_grad, grad_1, grad_3, out_weight, mixed], 0.1, "unproject_more",
        )[0]
        near, mine = call(
            rest_kernel, [part_low, part_full], [SMEM, VMEM, VMEM, ANY],
            [z, mixed, out_weight, total], 0.1, "project_rest",
        )
        kept["from_1"] = swap(near, 1)
        grads_in = [grad_2, total, out_weight]
        orders = [near]
    else:
        part = dot(mixed, out_weight, NN)
        output = lax.psum_scatter(part, "head", scatter_dimension=1, tiled=True).astype(BF16)
        whole = lax.all_gather(out_grad, "head", axis=1, tiled=True)
        grads_in = [dot(whole, out_weight, NT).astype(BF16)]
        orders = []
    outs = call(
        functools.partial(spread_kernel, heads, (2,) * direct, paired),
        [states, packed if paired else states, low,
         jax.ShapeDtypeStruct((heads, length, 1), F32)] + [low] * direct,
        [SMEM, SMEM, VMEM, VMEM, SMEM] + [VMEM] * (3 + len(grads_in)) + [ANY] * len(orders),
        [pos, z, valid, starts, gate, queries, norm, read, *grads_in, *orders],
        0.5, "spread",
    )
    keep, give, numer_grad, denom_grad = outs[:4]
    mixed_grad = outs[4] if direct else grads_in[0]

    def add_here():
        if not direct:
            return []
        sum_3 = call(
            add_kernel, [part_low], [SMEM, VMEM, VMEM, VMEM, ANY],
            [z, mixed, out_weight, sum_2, numer_grad], 0.5, "project_add",
        )[0]
        kept["from_3"] = swap(sum_3, 3)
        return [sum_3]

    def beside_back(sent):
        kept["grads"] = call(
            functools.partial(grads_kernel, heads),
            [low, flat, flat],
            [VMEM, SMEM] + [VMEM] * 9 + [ANY],
            [valid, gate, queries, keys, values, probs, mixed_grad, numer_grad, denom_grad, memory,
             norm, sent],
            0.3, "grads",
        )
        return [kept["grads"][1]] + ([kept["from_1"]] if direct else [])

    own, far = scan_states(keep, give, pos, heads, False, add_here, beside_back)
    query_grad, key_part, value_part = kept["grads"]
    if direct:
        output = mine + kept["from_1"].astype(F32) + kept["from_3"].astype(F32)
        output = output.astype(BF16)
    key_grad, value_grad = call(
        functools.partial(last_kernel, heads),
        [low, low],
        [SMEM] + [VMEM] * 7,
        [pos, valid, keys, values, own, far, key_part, value_part], 1.5, "last",
    )
    return (output, query_grad, key_grad, value_grad)


def solution(mesh):
    placed = (
        P("seq", "head"),
        P("seq", "head"),
        P("seq", "head"),
        P("head"),
        P("head", None),
        P("seq", "head"),
        P("seq"),
        P("seq"),
    )
    return jax.shard_map(
        shards,
        mesh=mesh,
        in_specs=placed,
        out_specs=(P("seq", "head"), P("seq", "head"), P("seq", "head"), P("seq", "head")),
        check_vma=False,
    )
```

time: 57.7 us -> 51.6 us (0.89)
  waiting for transfers between devices: 16.2 us -> 10.5 us
  between operations: 2.71 us -> 2.09 us
  local copies, waits for them, and re-layouts: 4.78 us -> 5.39 us
    ppermute x6, waiting for transfers between devices: 12.7 us -> 6.28 us  [swap(): return lax.ppermute(array, 'head', [(s, s ^ way) for s in range(groups)])]
    ppermute x4, waiting for transfers between devices: 0.05 us -> 1.55 us  [the longest x2 1.54 us: scan_states(): return (own, lax.ppermute(passed, 'seq', pairs))]
    ppermute x6, waiting for transfers between devices: 3.43 us -> 2.67 us  [scan_states(): lax.ppermute(sent, 'seq', [(s, s ^ way) for s in range(count)])]
    unnamed x24, local copies, waits for them, and re-layouts: 4.78 us -> 5.39 us
    pallas_call x14 -> x15, Pallas kernels: 15.8 us -> 15.7 us  [call(): pl.pallas_call(kernel, out_shape=outs, in_specs=in_specs, out_specs=[VMEM...]
  transfers between devices with their start and end apart: 16 -> 16, of which waited for: 6 -> 8; matrix products, arithmetic and copies ran while one was open for 1% -> 2% of each run, Pallas kernels for 21% -> 27%
where the time goes in v4:
time: 51.6 us; the launch traced here: 51.3 us
  starting transfers between devices  16.7 us (32%)
  Pallas kernels  15.7 us (30%)
  waiting for transfers between devices  10.5 us (20%)
  local copies, waits for them, and re-layouts  5.39 us (10%)
  between operations  2.09 us (4%)
  other arithmetic  0.81 us (2%)
    pallas_call x15, Pallas kernels, call(): pl.pallas_call(kernel, out_shape=outs, in_specs=in_specs, out_specs=[VMEM...  15.7 us
    ppermute x6, starting transfers between devices, swap(): return lax.ppermute(array, 'head', [(s, s ^ way) for s in range(groups)])  8.98 us
    ppermute x6, starting transfers between devices, scan_states(): lax.ppermute(sent, 'seq', [(s, s ^ way) for s in range(count)])  7.11 us
    ppermute x6, waiting for transfers between devices, swap(): return lax.ppermute(array, 'head', [(s, s ^ way) for s in range(groups)])  6.28 us
    unnamed x24, local copies, waits for them, and re-layouts  5.39 us
    ppermute x6, waiting for transfers between devices, scan_states(): lax.ppermute(sent, 'seq', [(s, s ^ way) for s in range(count)])  2.67 us
    ppermute x2, waiting for transfers between devices, scan_states(): return (own, lax.ppermute(passed, 'seq', pairs))  1.54 us
  transfers between devices with their start and end apart: 16, of which 8 were waited for; matrix products, arithmetic and copies ran while one was open for 2% of the time, Pallas kernels for 27%

profile of v4, /device:TPU:0, one launch (start us, length us, event | category | flops | bytes accessed | tf_op | source)
XLA Modules:
  0.0 51.3 jit_solution(15968431885870639101)
XLA Ops:
  1.9 0.9 %copy-done.3 = bf16[128,1024]{1,0:T(8,128)(2,1)S(1)} copy-done((bf16[128,1024]{1,0:T(8,128)(2,1)S(1)}, bf16[128,1024]{1,0:T(8,128)(2,1)}, u32[]{:S(2)}) %copy-start.3) | copy-done | bytes 262168
  2.9 0.9 %copy-done.6 = bf16[128,1024]{1,0:T(8,128)(2,1)S(1)} copy-done((bf16[128,1024]{1,0:T(8,128)(2,1)S(1)}, bf16[128,1024]{1,0:T(8,128)(2,1)}, u32[]{:S(2)}) %copy-start.6) | copy-done | bytes 262168
  4.2 0.5 %collective-permute-start = (f32[4,136,128]{2,1,0:T(8,128)S(1)}, f32[4,136,128]{2,1,0:T(8,128)S(1)}, u32[]{:S(2)}, u32[]{:S(2)}) collective-permute-start(f32[4,136,128]{2,1,0:T(8,128)S(1)} %get-tuple-element.30), channel_id=1, source_target_pairs={{0,4},{4,0},{8,12},{12,8},{16,20},{20,16},{24,28},{28,24},{1,5},{5... | collective-permute-start | bytes 835592 | tf_op jit(solution)/shard_map/ppermute | solution.py:388
  4.7 2.6 %collective-permute-start.5 = (bf16[128,1024]{1,0:T(8,128)(2,1)}, bf16[128,1024]{1,0:T(8,128)(2,1)S(1)}, u32[]{:S(2)}, u32[]{:S(2)}) collective-permute-start(bf16[128,1024]{1,0:T(8,128)(2,1)} %refs_0_.3), channel_id=1, source_target_pairs={{0,1},{1,0},{2,3},{3,2},{4,5},{5,4},{6,7},{7,6},{8,9},{9,8},{10,11... | collective-permute-start | bytes 786440 | tf_op jit(solution)/shard_map/ppermute | solution.py:431
  7.4 2.5 %collective-permute-start.6 = (bf16[128,1024]{1,0:T(8,128)(2,1)}, bf16[128,1024]{1,0:T(8,128)(2,1)S(1)}, u32[]{:S(2)}, u32[]{:S(2)}) collective-permute-start(bf16[128,1024]{1,0:T(8,128)(2,1)} %refs_0_.3), channel_id=1, source_target_pairs={{0,3},{1,2},{2,1},{3,0},{4,7},{5,6},{6,5},{7,4},{8,11},{9,10},{10,... | collective-permute-start | bytes 786440 | tf_op jit(solution)/shard_map/ppermute | solution.py:431
  10.1 2.5 %collective-permute-start.3 = (bf16[4,144,128]{2,1,0:T(8,128)(2,1)S(1)}, bf16[4,144,128]{2,1,0:T(8,128)(2,1)S(1)}, u32[]{:S(2)}, u32[]{:S(2)}) collective-permute-start(bf16[4,144,128]{2,1,0:T(8,128)(2,1)S(1)} %pair.2.after_ref), channel_id=1, source_target_pairs={{0,24},{4,28},{8,16},{12,20},{16,8},{20,12},{24,0},{28,4},{1,25},{... | collective-permute-start | bytes 442376 | tf_op jit(solution)/shard_map/ppermute | solution.py:398
  12.7 0.5 collective-permute-start.2
  13.2 0.5 %collective-permute-start.1 = (bf16[4,144,128]{2,1,0:T(8,128)(2,1)S(1)}, bf16[4,144,128]{2,1,0:T(8,128)(2,1)S(1)}, u32[]{:S(2)}, u32[]{:S(2)}) collective-permute-start(bf16[4,144,128]{2,1,0:T(8,128)(2,1)S(1)} %pair.2.after_ref), channel_id=1, source_target_pairs={{0,8},{4,12},{8,0},{12,4},{16,24},{20,28},{24,16},{28,20},{1,9},{5... | collective-permute-start | bytes 442376 | tf_op jit(solution)/shard_map/ppermute | solution.py:398
  13.7 0.9 %copy-done = bf16[128,1024]{1,0:T(8,128)(2,1)S(1)} copy-done((bf16[128,1024]{1,0:T(8,128)(2,1)S(1)}, bf16[128,1024]{1,0:T(8,128)(2,1)}, u32[]{:S(2)}) %copy-start) | copy-done | bytes 262168
  14.6 0.9 %copy-done.4 = bf16[128,1024]{1,0:T(8,128)(2,1)S(1)} copy-done((bf16[128,1024]{1,0:T(8,128)(2,1)S(1)}, bf16[128,1024]{1,0:T(8,128)(2,1)}, u32[]{:S(2)}) %copy-start.4) | copy-done | bytes 262168
  15.6 0.9 %copy-done.7 = bf16[128,1024]{1,0:T(8,128)(2,1)S(1)} copy-done((bf16[128,1024]{1,0:T(8,128)(2,1)S(1)}, bf16[128,1024]{1,0:T(8,128)(2,1)}, u32[]{:S(2)}) %copy-start.7) | copy-done | bytes 262168
  16.5 2.7 %local.1 = (bf16[8,128,128]{2,1,0:T(8,128)(2,1)S(1)}, f32[128,1024]{1,0:T(8,128)S(1)}) custom-call(s32[1,1]{1,0:T(1,128)} %bitcast.5.valid_ref, bf16[128,1024]{1,0:T(8,128)(2,1)S(1)} %copy-done, bf16[128,1024]{1,0:T(8,128)(2,1)S(1)} %copy-done.4, bf16[128,1024]{1,0:T(8,128)(2,1)S(1)} %copy-done.7, bf16[4,144,128]{2,1,0:T(8,128)(2,1)S(1)} %pair.2.after_ref), custom_call_target="tpu_custom_call" | custom-call | flops 3449999872 | bytes 1024 | tf_op jit(solution)/shard_map/local/pallas_call | solution.py:23
  19.3 0.6 %collective-permute-done.2.y_ref = bf16[4,144,128]{2,1,0:T(8,128)(2,1)S(1)} collective-permute-done((bf16[4,144,128]{2,1,0:T(8,128)(2,1)S(1)}, bf16[4,144,128]{2,1,0:T(8,128)(2,1)S(1)}, u32[]{:S(2)}, u32[]{:S(2)}) %collective-permute-start.2) | collective-permute-done | bytes 147488 | tf_op jit(solution)/shard_map/ppermute | solution.py:398
  20.3 2.1 %collective-permute-done.6.refs_2_.block_ref = bf16[128,1024]{1,0:T(8,128)(2,1)S(1)} collective-permute-done((bf16[128,1024]{1,0:T(8,128)(2,1)}, bf16[128,1024]{1,0:T(8,128)(2,1)S(1)}, u32[]{:S(2)}, u32[]{:S(2)}) %collective-permute-start.6) | collective-permute-done | bytes 262176 | tf_op jit(solution)/shard_map/ppermute | solution.py:431
  22.5 0.7 %collective-permute-start.9 = (bf16[128,1024]{1,0:T(8,128)(2,1)S(1)}, bf16[128,1024]{1,0:T(8,128)(2,1)S(1)}, u32[]{:S(2)}, u32[]{:S(2)}) collective-permute-start(bf16[128,1024]{1,0:T(8,128)(2,1)S(1)} %pass_on.1), channel_id=1, source_target_pairs={{0,1},{1,0},{2,3},{3,2},{4,5},{5,4},{6,7},{7,6},{8,9},{9,8},{10,11... | collective-permute-start | bytes 786440 | tf_op jit(solution)/shard_map/ppermute | solution.py:431
  23.2 1.5 %collective-permute-done.4.far_ref = f32[4,136,128]{2,1,0:T(8,128)S(1)} collective-permute-done((f32[4,136,128]{2,1,0:T(8,128)S(1)}, f32[4,136,128]{2,1,0:T(8,128)S(1)}, u32[]{:S(2)}, u32[]{:S(2)}) %collective-permute-start.4) | collective-permute-done | bytes 278560 | tf_op jit(solution)/shard_map/ppermute | solution.py:408
  24.7 0.6 %slice-done.1 = s8[4194304]{0:T(1024)(128)(4,1)S(1)} async-done(((s8[8388608]{0:T(1024)(128)(4,1)}), s8[4194304]{0:T(1024)(128)(4,1)S(1)}, s32[]{:S(2)}) %slice-start.1) | async-done | bytes 4194328
  25.3 1.5 %read.1 = (bf16[128,1024]{1,0:T(8,128)(2,1)S(1)}, f32[128,1024]{1,0:T(8,128)S(1)}, bf16[8,128,256]{2,1,0:T(8,128)(2,1)S(1)}, f32[8,8,128]{2,1,0:T(8,128)S(1)}, bf16[128,1024]{1,0:T(8,128)(2,1)S(1)}) custom-call(s32[1]{0:T(128)} %bitcast.1.pos_ref, s32[1]{0:T(128)} %bitcast.z_ref, s32[1,1]{1,0:T(1,128)} %bitcast.6.valid_ref, f32[8]{0:T(128)S(1)} %copy-done.9, ...), custom_call_target="tpu_custom_call" | custom-call | flops 115000000 | bytes 1024 | tf_op jit(solution)/shard_map/read/pallas_call | solution.py:23
  26.8 1.5 %collective-permute-start.8 = (bf16[128,1024]{1,0:T(8,128)(2,1)S(1)}, bf16[128,1024]{1,0:T(8,128)(2,1)S(1)}, u32[]{:S(2)}, u32[]{:S(2)}) collective-permute-start(bf16[128,1024]{1,0:T(8,128)(2,1)S(1)} %get-tuple-element.37), channel_id=1, source_target_pairs={{0,1},{1,0},{2,3},{3,2},{4,5},{5,4},{6,7},{7,6},{8,9},{9,8},{10,11... | collective-permute-start | bytes 786440 | tf_op jit(solution)/shard_map/ppermute | solution.py:431
  28.3 2.2 %unproject_more.1.after_ref.refs_1_ = f32[128,1024]{1,0:T(8,128)S(1)} custom-call(s32[1]{0:T(128)} %bitcast.z_ref, bf16[128,1024]{1,0:T(8,128)(2,1)S(1)} %copy-done.2, bf16[128,1024]{1,0:T(8,128)(2,1)S(1)} %collective-permute-done.5.refs_0_.refs_1_, bf16[128,1024]{1,0:T(8,128)(2,1)S(1)} %collective-permute-done.6.refs_2_.block_ref, ...), custom_call_target="tpu_custom_call" | custom-call | flops 115000000 | bytes 1024 | tf_op jit(solution)/shard_map/unproject_more/pallas_call | solution.py:23
  30.5 0.7 %project_rest.1 = (bf16[128,1024]{1,0:T(8,128)(2,1)S(1)}, f32[128,1024]{1,0:T(8,128)S(1)}) custom-call(s32[1]{0:T(128)} %bitcast.z_ref, bf16[128,1024]{1,0:T(8,128)(2,1)S(1)} %get-tuple-element.34.refs_4_.mixed_ref, bf16[1024,4096]{1,0:T(8,128)(2,1)S(1)} %bitcast.13, f32[128,1024]{1,0:T(8,128)S(1)} %unproject_more.1.after_ref.refs_1_), custom_call_target="tpu_custom_call" | custom-call | flops 115000000 | bytes 1024 | tf_op jit(solution)/shard_map/project_rest/pallas_call | solution.py:23
  31.6 1.9 %spread.1 = (f32[4,136,128]{2,1,0:T(8,128)S(1)}, bf16[4,144,128]{2,1,0:T(8,128)(2,1)S(1)}, bf16[128,1024]{1,0:T(8,128)(2,1)S(1)}, f32[8,128,1]{2,1,0:T(8,128)S(1)}, bf16[128,1024]{1,0:T(8,128)(2,1)S(1)}) custom-call(s32[1]{0:T(128)} %bitcast.1.pos_ref, s32[1]{0:T(128)} %bitcast.z_ref, s32[1,1]{1,0:T(1,128)} %bitcast.7.valid_ref, s32[1,1]{1,0:T(1,128)} %bitcast.11.starts_ref, ...), custom_call_target="tpu_custom_call" | custom-call | flops 575000000 | bytes 1024 | tf_op jit(solution)/shard_map/spread/pallas_call | solution.py:23
  33.9 2.1 %collective-permute-done.8.more_ref = bf16[128,1024]{1,0:T(8,128)(2,1)S(1)} collective-permute-done((bf16[128,1024]{1,0:T(8,128)(2,1)S(1)}, bf16[128,1024]{1,0:T(8,128)(2,1)S(1)}, u32[]{:S(2)}, u32[]{:S(2)}) %collective-permute-start.8) | collective-permute-done | bytes 262176 | tf_op jit(solution)/shard_map/ppermute | solution.py:431
  36.4 1.4 %collective-permute-start.10 = (bf16[128,1024]{1,0:T(8,128)(2,1)S(1)}, bf16[128,1024]{1,0:T(8,128)(2,1)S(1)}, u32[]{:S(2)}, u32[]{:S(2)}) collective-permute-start(bf16[128,1024]{1,0:T(8,128)(2,1)S(1)} %project_add.1.refs_0_), channel_id=1, source_target_pairs={{0,3},{1,2},{2,1},{3,0},{4,7},{5,6},{6,5},{7,4},{8,11},{9,10},{10,... | collective-permute-start | bytes 786440 | tf_op jit(solution)/shard_map/ppermute | solution.py:431
  37.9 2.5 %collective-permute-start.14 = (bf16[4,144,128]{2,1,0:T(8,128)(2,1)S(1)}, bf16[4,144,128]{2,1,0:T(8,128)(2,1)S(1)}, u32[]{:S(2)}, u32[]{:S(2)}) collective-permute-start(bf16[4,144,128]{2,1,0:T(8,128)(2,1)S(1)} %pair.3.after_ref), channel_id=1, source_target_pairs={{0,24},{4,28},{8,16},{12,20},{16,8},{20,12},{24,0},{28,4},{1,25},{... | collective-permute-start | bytes 442376 | tf_op jit(solution)/shard_map/ppermute | solution.py:398
  40.4 0.5 collective-permute-start.13
  40.9 0.5 %collective-permute-start.12 = (bf16[4,144,128]{2,1,0:T(8,128)(2,1)S(1)}, bf16[4,144,128]{2,1,0:T(8,128)(2,1)S(1)}, u32[]{:S(2)}, u32[]{:S(2)}) collective-permute-start(bf16[4,144,128]{2,1,0:T(8,128)(2,1)S(1)} %pair.3.after_ref), channel_id=1, source_target_pairs={{0,8},{4,12},{8,0},{12,4},{16,24},{20,28},{24,16},{28,20},{1,9},{5... | collective-permute-start | bytes 442376 | tf_op jit(solution)/shard_map/ppermute | solution.py:398
  41.5 3.7 %grads.1 = (bf16[128,1024]{1,0:T(8,128)(2,1)}, f32[128,1024]{1,0:T(8,128)S(1)}, f32[128,1024]{1,0:T(8,128)S(1)}) custom-call(s32[1,1]{1,0:T(1,128)} %bitcast.8.valid_ref, f32[8]{0:T(128)S(1)} %copy-done.9, bf16[128,1024]{1,0:T(8,128)(2,1)S(1)} %copy-done.1, bf16[128,1024]{1,0:T(8,128)(2,1)S(1)} %copy-done.5, bf16[128,1024]{1,0:T(8,128)(2,1)S(1)} %copy-done.8, ...), custom_call_target="tpu_custom_call" | custom-call | flops 345000000 | bytes 1024 | tf_op jit(solution)/shard_map/grads/pallas_call | solution.py:23
  45.1 1.9 %collective-permute-done.13.y_ref = bf16[4,144,128]{2,1,0:T(8,128)(2,1)S(1)} collective-permute-done((bf16[4,144,128]{2,1,0:T(8,128)(2,1)S(1)}, bf16[4,144,128]{2,1,0:T(8,128)(2,1)S(1)}, u32[]{:S(2)}, u32[]{:S(2)}) %collective-permute-start.13) | collective-permute-done | bytes 147488 | tf_op jit(solution)/shard_map/ppermute | solution.py:398
  47.3 1.7 %collective-permute-done.10 = bf16[128,1024]{1,0:T(8,128)(2,1)S(1)} collective-permute-done((bf16[128,1024]{1,0:T(8,128)(2,1)S(1)}, bf16[128,1024]{1,0:T(8,128)(2,1)S(1)}, u32[]{:S(2)}, u32[]{:S(2)}) %collective-permute-start.10) | collective-permute-done | bytes 262176 | tf_op jit(solution)/shard_map/ppermute | solution.py:431
  49.0 0.8 %add_convert_fusion = bf16[128,1024]{1,0:T(8,128)(2,1)} fusion(bf16[128,1024]{1,0:T(8,128)(2,1)S(1)} %collective-permute-done.10, f32[128,1024]{1,0:T(8,128)S(1)} %get-tuple-element.35, bf16[128,1024]{1,0:T(8,128)(2,1)S(1)} %collective-permute-done.7.refs_1_), kind=kLoop, calls=%fused_computation | loop fusion | flops 655360 | bytes 1310720 | tf_op jit(solution)/shard_map/convert_element_type | solution.py:526
  49.8 1.4 %last.1 = (bf16[128,1024]{1,0:T(8,128)(2,1)}, bf16[128,1024]{1,0:T(8,128)(2,1)}) custom-call(s32[1]{0:T(128)} %bitcast.1.pos_ref, s32[1,1]{1,0:T(1,128)} %bitcast.9.valid_ref, bf16[128,1024]{1,0:T(8,128)(2,1)S(1)} %copy-done.5, bf16[128,1024]{1,0:T(8,128)(2,1)S(1)} %copy-done.8, f32[4,136,128]{2,1,0:T(8,128)S(1)} %get-tuple-element.49.own_ref, ...), custom_call_target="tpu_custom_call" | custom-call | flops 1724999936 | bytes 1024 | tf_op jit(solution)/shard_map/last/pallas_call | solution.py:23
  (41 shorter events, 2.8 us)
Async XLA Ops:
  1.9 1.0 %copy-start.3 = (bf16[128,1024]{1,0:T(8,128)(2,1)S(1)}, bf16[128,1024]{1,0:T(8,128)(2,1)}, u32[]{:S(2)}) copy-start(bf16[128,1024]{1,0:T(8,128)(2,1)} %k_ref.7) | copy-start | bytes 786436
  2.9 0.9 %copy-start.6 = (bf16[128,1024]{1,0:T(8,128)(2,1)S(1)}, bf16[128,1024]{1,0:T(8,128)(2,1)}, u32[]{:S(2)}) copy-start(bf16[128,1024]{1,0:T(8,128)(2,1)} %v_ref.7) | copy-start | bytes 786436
  4.2 5.6 %collective-permute-start = (f32[4,136,128]{2,1,0:T(8,128)S(1)}, f32[4,136,128]{2,1,0:T(8,128)S(1)}, u32[]{:S(2)}, u32[]{:S(2)}) collective-permute-start(f32[4,136,128]{2,1,0:T(8,128)S(1)} %get-tuple-element.30), channel_id=1, source_target_pairs={{0,4},{4,0},{8,12},{12,8},{16,20},{20,16},{24,28},{28,24},{1,5},{5... | collective-permute-start | bytes 835592 | tf_op jit(solution)/shard_map/ppermute | solution.py:388
  4.7 18.4 %collective-permute-start.5 = (bf16[128,1024]{1,0:T(8,128)(2,1)}, bf16[128,1024]{1,0:T(8,128)(2,1)S(1)}, u32[]{:S(2)}, u32[]{:S(2)}) collective-permute-start(bf16[128,1024]{1,0:T(8,128)(2,1)} %refs_0_.3), channel_id=1, source_target_pairs={{0,1},{1,0},{2,3},{3,2},{4,5},{5,4},{6,7},{7,6},{8,9},{9,8},{10,11... | collective-permute-start | bytes 786440 | tf_op jit(solution)/shard_map/ppermute | solution.py:431
  7.4 15.0 %collective-permute-start.6 = (bf16[128,1024]{1,0:T(8,128)(2,1)}, bf16[128,1024]{1,0:T(8,128)(2,1)S(1)}, u32[]{:S(2)}, u32[]{:S(2)}) collective-permute-start(bf16[128,1024]{1,0:T(8,128)(2,1)} %refs_0_.3), channel_id=1, source_target_pairs={{0,3},{1,2},{2,1},{3,0},{4,7},{5,6},{6,5},{7,4},{8,11},{9,10},{10,... | collective-permute-start | bytes 786440 | tf_op jit(solution)/shard_map/ppermute | solution.py:431
  10.1 9.1 %collective-permute-start.3 = (bf16[4,144,128]{2,1,0:T(8,128)(2,1)S(1)}, bf16[4,144,128]{2,1,0:T(8,128)(2,1)S(1)}, u32[]{:S(2)}, u32[]{:S(2)}) collective-permute-start(bf16[4,144,128]{2,1,0:T(8,128)(2,1)S(1)} %pair.2.after_ref), channel_id=1, source_target_pairs={{0,24},{4,28},{8,16},{12,20},{16,8},{20,12},{24,0},{28,4},{1,25},{... | collective-permute-start | bytes 442376 | tf_op jit(solution)/shard_map/ppermute | solution.py:398
  12.7 7.2 %collective-permute-start.2 = (bf16[4,144,128]{2,1,0:T(8,128)(2,1)S(1)}, bf16[4,144,128]{2,1,0:T(8,128)(2,1)S(1)}, u32[]{:S(2)}, u32[]{:S(2)}) collective-permute-start(bf16[4,144,128]{2,1,0:T(8,128)(2,1)S(1)} %pair.2.after_ref), channel_id=1, source_target_pairs={{0,16},{4,20},{8,24},{12,28},{16,0},{20,4},{24,8},{28,12},{1,17},{... | collective-permute-start | bytes 442376 | tf_op jit(solution)/shard_map/ppermute | solution.py:398
  13.2 6.8 %collective-permute-start.1 = (bf16[4,144,128]{2,1,0:T(8,128)(2,1)S(1)}, bf16[4,144,128]{2,1,0:T(8,128)(2,1)S(1)}, u32[]{:S(2)}, u32[]{:S(2)}) collective-permute-start(bf16[4,144,128]{2,1,0:T(8,128)(2,1)S(1)} %pair.2.after_ref), channel_id=1, source_target_pairs={{0,8},{4,12},{8,0},{12,4},{16,24},{20,28},{24,16},{28,20},{1,9},{5... | collective-permute-start | bytes 442376 | tf_op jit(solution)/shard_map/ppermute | solution.py:398
  13.7 0.9 %copy-start = (bf16[128,1024]{1,0:T(8,128)(2,1)S(1)}, bf16[128,1024]{1,0:T(8,128)(2,1)}, u32[]{:S(2)}) copy-start(bf16[128,1024]{1,0:T(8,128)(2,1)} %q_ref.7) | copy-start | bytes 786436
  14.6 0.9 %copy-start.4 = (bf16[128,1024]{1,0:T(8,128)(2,1)S(1)}, bf16[128,1024]{1,0:T(8,128)(2,1)}, u32[]{:S(2)}) copy-start(bf16[128,1024]{1,0:T(8,128)(2,1)} %k_ref.7) | copy-start | bytes 786436
  15.6 0.9 %copy-start.7 = (bf16[128,1024]{1,0:T(8,128)(2,1)S(1)}, bf16[128,1024]{1,0:T(8,128)(2,1)}, u32[]{:S(2)}) copy-start(bf16[128,1024]{1,0:T(8,128)(2,1)} %v_ref.7) | copy-start | bytes 786436
  19.2 5.5 %slice-start = ((s8[8388608]{0:T(1024)(128)(4,1)}), s8[4194304]{0:T(1024)(128)(4,1)S(1)}, s32[]{:S(2)}) async-start(s8[8388608]{0:T(1024)(128)(4,1)} %bitcast.12), calls=%async_computation | async-start | bytes 8388608
  19.2 5.5 %copy-start.1 = (bf16[128,1024]{1,0:T(8,128)(2,1)S(1)}, bf16[128,1024]{1,0:T(8,128)(2,1)}, u32[]{:S(2)}) copy-start(bf16[128,1024]{1,0:T(8,128)(2,1)} %q_ref.7) | copy-start | bytes 786436
  19.2 5.4 %copy-start.9 = (f32[8]{0:T(128)S(1)}, f32[8]{0:T(128)}, u32[]{:S(2)}) copy-start(f32[8]{0:T(128)} %gate_ref.5) | copy-start | bytes 100
  22.5 9.2 %collective-permute-start.9 = (bf16[128,1024]{1,0:T(8,128)(2,1)S(1)}, bf16[128,1024]{1,0:T(8,128)(2,1)S(1)}, u32[]{:S(2)}, u32[]{:S(2)}) collective-permute-start(bf16[128,1024]{1,0:T(8,128)(2,1)S(1)} %pass_on.1), channel_id=1, source_target_pairs={{0,1},{1,0},{2,3},{3,2},{4,5},{5,4},{6,7},{7,6},{8,9},{9,8},{10,11... | collective-permute-start | bytes 786440 | tf_op jit(solution)/shard_map/ppermute | solution.py:431
  23.1 2.2 %slice-start.1 = ((s8[8388608]{0:T(1024)(128)(4,1)}), s8[4194304]{0:T(1024)(128)(4,1)S(1)}, s32[]{:S(2)}) async-start(s8[8388608]{0:T(1024)(128)(4,1)} %bitcast.12), calls=%async_computation.1 | async-start | bytes 8388608
  23.1 5.1 %copy-start.2 = (bf16[128,1024]{1,0:T(8,128)(2,1)S(1)}, bf16[128,1024]{1,0:T(8,128)(2,1)}, u32[]{:S(2)}) copy-start(bf16[128,1024]{1,0:T(8,128)(2,1)} %refs_0_.3) | copy-start | bytes 786436
  23.1 1.6 %collective-permute-start.4 = (f32[4,136,128]{2,1,0:T(8,128)S(1)}, f32[4,136,128]{2,1,0:T(8,128)S(1)}, u32[]{:S(2)}, u32[]{:S(2)}) collective-permute-start(f32[4,136,128]{2,1,0:T(8,128)S(1)} %get-tuple-element.33), channel_id=1, source_target_pairs={{0,4},{4,0},{8,12},{12,8},{16,20},{20,16},{24,28},{28,24},{1,5},{5... | collective-permute-start | bytes 835592 | tf_op jit(solution)/shard_map/ppermute | solution.py:408
  26.8 9.2 %collective-permute-start.8 = (bf16[128,1024]{1,0:T(8,128)(2,1)S(1)}, bf16[128,1024]{1,0:T(8,128)(2,1)S(1)}, u32[]{:S(2)}, u32[]{:S(2)}) collective-permute-start(bf16[128,1024]{1,0:T(8,128)(2,1)S(1)} %get-tuple-element.37), channel_id=1, source_target_pairs={{0,1},{1,0},{2,3},{3,2},{4,5},{5,4},{6,7},{7,6},{8,9},{9,8},{10,11... | collective-permute-start | bytes 786440 | tf_op jit(solution)/shard_map/ppermute | solution.py:431
  31.6 9.8 %copy-start.5 = (bf16[128,1024]{1,0:T(8,128)(2,1)S(1)}, bf16[128,1024]{1,0:T(8,128)(2,1)}, u32[]{:S(2)}) copy-start(bf16[128,1024]{1,0:T(8,128)(2,1)} %k_ref.7) | copy-start | bytes 786436
  31.6 9.8 %copy-start.8 = (bf16[128,1024]{1,0:T(8,128)(2,1)S(1)}, bf16[128,1024]{1,0:T(8,128)(2,1)}, u32[]{:S(2)}) copy-start(bf16[128,1024]{1,0:T(8,128)(2,1)} %v_ref.7) | copy-start | bytes 786436
  33.5 4.3 %collective-permute-start.11 = (bf16[4,144,128]{2,1,0:T(8,128)(2,1)S(1)}, bf16[4,144,128]{2,1,0:T(8,128)(2,1)S(1)}, u32[]{:S(2)}, u32[]{:S(2)}) collective-permute-start(bf16[4,144,128]{2,1,0:T(8,128)(2,1)S(1)} %get-tuple-element.46), channel_id=1, source_target_pairs={{0,4},{4,0},{8,12},{12,8},{16,20},{20,16},{24,28},{28,24},{1,5},{5... | collective-permute-start | bytes 442376 | tf_op jit(solution)/shard_map/ppermute | solution.py:388
  33.6 11.6 %collective-permute-start.7 = (bf16[128,1024]{1,0:T(8,128)(2,1)S(1)}, bf16[128,1024]{1,0:T(8,128)(2,1)S(1)}, u32[]{:S(2)}, u32[]{:S(2)}) collective-permute-start(bf16[128,1024]{1,0:T(8,128)(2,1)S(1)} %get-tuple-element.36.refs_3_), channel_id=1, source_target_pairs={{0,1},{1,0},{2,3},{3,2},{4,5},{5,4},{6,7},{7,6},{8,9},{9,8},{10,11... | collective-permute-start | bytes 786440 | tf_op jit(solution)/shard_map/ppermute | solution.py:431
  36.4 12.6 %collective-permute-start.10 = (bf16[128,1024]{1,0:T(8,128)(2,1)S(1)}, bf16[128,1024]{1,0:T(8,128)(2,1)S(1)}, u32[]{:S(2)}, u32[]{:S(2)}) collective-permute-start(bf16[128,1024]{1,0:T(8,128)(2,1)S(1)} %project_add.1.refs_0_), channel_id=1, source_target_pairs={{0,3},{1,2},{2,1},{3,0},{4,7},{5,6},{6,5},{7,4},{8,11},{9,10},{10,... | collective-permute-start | bytes 786440 | tf_op jit(solution)/shard_map/ppermute | solution.py:431
  37.9 7.2 %collective-permute-start.14 = (bf16[4,144,128]{2,1,0:T(8,128)(2,1)S(1)}, bf16[4,144,128]{2,1,0:T(8,128)(2,1)S(1)}, u32[]{:S(2)}, u32[]{:S(2)}) collective-permute-start(bf16[4,144,128]{2,1,0:T(8,128)(2,1)S(1)} %pair.3.after_ref), channel_id=1, source_target_pairs={{0,24},{4,28},{8,16},{12,20},{16,8},{20,12},{24,0},{28,4},{1,25},{... | collective-permute-start | bytes 442376 | tf_op jit(solution)/shard_map/ppermute | solution.py:398
  40.4 6.6 %collective-permute-start.13 = (bf16[4,144,128]{2,1,0:T(8,128)(2,1)S(1)}, bf16[4,144,128]{2,1,0:T(8,128)(2,1)S(1)}, u32[]{:S(2)}, u32[]{:S(2)}) collective-permute-start(bf16[4,144,128]{2,1,0:T(8,128)(2,1)S(1)} %pair.3.after_ref), channel_id=1, source_target_pairs={{0,16},{4,20},{8,24},{12,28},{16,0},{20,4},{24,8},{28,12},{1,17},{... | collective-permute-start | bytes 442376 | tf_op jit(solution)/shard_map/ppermute | solution.py:398
  40.9 6.2 %collective-permute-start.12 = (bf16[4,144,128]{2,1,0:T(8,128)(2,1)S(1)}, bf16[4,144,128]{2,1,0:T(8,128)(2,1)S(1)}, u32[]{:S(2)}, u32[]{:S(2)}) collective-permute-start(bf16[4,144,128]{2,1,0:T(8,128)(2,1)S(1)} %pair.3.after_ref), channel_id=1, source_target_pairs={{0,8},{4,12},{8,0},{12,4},{16,24},{20,28},{24,16},{28,20},{1,9},{5... | collective-permute-start | bytes 442376 | tf_op jit(solution)/shard_map/ppermute | solution.py:398
  47.2 2.6 %collective-permute-start.15 = (f32[4,136,128]{2,1,0:T(8,128)S(1)}, f32[4,136,128]{2,1,0:T(8,128)S(1)}, u32[]{:S(2)}, u32[]{:S(2)}) collective-permute-start(f32[4,136,128]{2,1,0:T(8,128)S(1)} %get-tuple-element.50), channel_id=1, source_target_pairs={{0,4},{4,0},{8,12},{12,8},{16,20},{20,16},{24,28},{28,24},{1,5},{5... | collective-permute-start | bytes 835592 | tf_op jit(solution)/shard_map/ppermute | solution.py:408

commit v5 on v4

--- a/solution.py
+++ b/solution.py
@@ -5,6 +5,7 @@
 from jax import lax
 from jax.experimental import pallas as pl
 from jax.experimental.pallas import tpu as pltpu
+from jax.sharding import NamedSharding
 from jax.sharding import PartitionSpec as P
 
 DH = 128
@@ -52,13 +53,13 @@
 TN = ((0,), (0,))
 
 
-def live_rows(valid_ref, length):
+def live_rows(facts_ref, length):
     where = lax.broadcasted_iota(jnp.int32, (length, 1), 0)
-    return (where < valid_ref[...]).astype(F32)
-
-
-def opened(starts_ref):
-    return 1.0 - starts_ref[...].astype(F32)
+    return (where.astype(F32) < facts_ref[0:1, 0:1]).astype(F32)
+
+
+def opened(facts_ref):
+    return 1.0 - facts_ref[4:5, 0:1]
 
 
 def gate_row(gate_ref, h):
@@ -96,15 +97,15 @@
 
 
 def state_kernel(
-    heads, pos_ref, z_ref, valid_ref, starts_ref, k_ref, v_ref, keep_ref, give_ref
+    heads, pos_ref, z_ref, facts_ref, k_ref, v_ref, after_ref, keep_ref, give_ref
 ):
-    live = live_rows(valid_ref, k_ref.shape[0])
+    live = live_rows(facts_ref, k_ref.shape[0])
     for kept, i, h in by_half(heads, pos_ref):
         out_ref = keep_ref if kept else give_ref
         sig = (feature(k_ref[:, cut(h)].astype(F32)) * live).astype(BF16)
         out_ref[i, 0:DH, :] = dot(sig, v_ref[:, cut(h)], TN)
         norm = jnp.sum(sig.astype(F32), axis=0, keepdims=True)
-        out_ref[i, DH:ROWS, :] = tail(ROWS - DH, norm, opened(starts_ref))
+        out_ref[i, DH:ROWS, :] = tail(ROWS - DH, norm, opened(facts_ref))
 
 
 def in_three(x):
@@ -113,7 +114,15 @@
     return first, second, x - first - second
 
 
-def store_sent(ref, i, memory, norm, flag, centre):
+def store_sent(ref, i, memory, norm, flag, centred):
+    centre = jnp.zeros_like(norm)
+    if centred:
+        weight = jnp.maximum(jnp.sum(norm, axis=1, keepdims=True), 1e-30)
+        centre = jnp.sum(memory, axis=0, keepdims=True) / weight
+        centre = centre.astype(BF16).astype(F32)
+        norms = tail(16, *in_three(norm)).astype(BF16)
+        centres = tail(16, centre, centre, centre).astype(BF16)
+        memory = memory - dot(norms, centres, TN)
     ref[i, 0:DH, :] = memory.astype(BF16)
     ref[i, DH:SENT, :] = tail(SENT - DH, *in_three(norm), centre, flag).astype(BF16)
 
@@ -151,15 +160,7 @@
             on_other = jnp.where(lower, flag * other_flag, other_flag)
         memory = on_mine * memory + on_other * other_memory
         norm = on_mine * norm + on_other * other_norm
-        centre = jnp.zeros_like(norm)
-        if forward:
-            weight = jnp.maximum(jnp.sum(norm, axis=1, keepdims=True), 1e-30)
-            centre = jnp.sum(memory, axis=0, keepdims=True) / weight
-            centre = centre.astype(BF16).astype(F32)
-            norms = tail(16, *in_three(norm)).astype(BF16)
-            centres = tail(16, centre, centre, centre).astype(BF16)
-            memory = memory - dot(norms, centres, TN)
-        store_sent(sent_ref, i, memory, norm, flag * other_flag, centre)
+        store_sent(sent_ref, i, memory, norm, flag * other_flag, forward)
 
 
 def join_kernel(
@@ -199,16 +200,20 @@
                 jnp.where(lower, memory, mine_open * (memory + mine_mem)),
                 jnp.where(lower, norm, mine_open * (norm + mine_norm)),
             )
-        for ref, (value, sums) in ((own_ref, own), (sent_ref, sent)):
-            ref[i, 0:DH, :] = value
-            ref[i, DH:ROWS, :] = tail(ROWS - DH, sums)
-
-
-def local_kernel(heads, valid_ref, q_ref, k_ref, v_ref, after_ref, probs_ref, local_ref):
+        own_ref[i, 0:DH, :] = own[0]
+        own_ref[i, DH:ROWS, :] = tail(ROWS - DH, own[1])
+        if forward:
+            sent_ref[i, 0:DH, :] = sent[0]
+            sent_ref[i, DH:ROWS, :] = tail(ROWS - DH, sent[1])
+        else:
+            store_sent(sent_ref, i, *sent, mine_open, False)
+
+
+def local_kernel(heads, facts_ref, q_ref, k_ref, v_ref, after_ref, probs_ref, local_ref):
     length = q_ref.shape[0]
     row = lax.broadcasted_iota(jnp.int32, (length, length), 0)
     col = lax.broadcasted_iota(jnp.int32, (length, length), 1)
-    allowed = (col <= row) & (col < valid_ref[...])
+    allowed = (col <= row) & (col.astype(F32) < facts_ref[0:1, 0:1])
     for h in range(heads):
         scores = dot(head(q_ref, h), head(k_ref, h), NT) * DH ** (-0.5)
         scores = jnp.where(allowed, scores, -1e30)
@@ -223,14 +228,14 @@
 
 
 def read_kernel(
-    heads, project, pos_ref, z_ref, valid_ref, gate_ref, q_ref, keep_ref, own_ref, far_ref,
+    heads, project, pos_ref, z_ref, facts_ref, gate_ref, q_ref, keep_ref, own_ref, far_ref,
     local_ref, *refs,
 ):
     if project:
-        weight_ref, _, mixed_ref, read_ref, memory_ref, norm_ref, first_ref = refs
+        weight_ref, _, mixed_ref, read_ref, memory_ref, norm_ref, sig_ref, scale_ref, first_ref = refs
     else:
-        mixed_ref, read_ref, memory_ref, norm_ref = refs
-    live = live_rows(valid_ref, q_ref.shape[0])
+        mixed_ref, read_ref, memory_ref, norm_ref, sig_ref, scale_ref = refs
+    live = live_rows(facts_ref, q_ref.shape[0])
     for kept, i, h in by_half(heads, pos_ref):
         carry, norm, _ = load_state(own_ref if kept else far_ref, i)
         flag = keep_ref[i, DH + 1 : DH + 2, :]
@@ -245,6 +250,8 @@
         read = numer / denom
         gate = gate_row(gate_ref, h)
         mixed = live * (gate * read + (1.0 - gate) * local_ref[:, cut(h)])
+        sig_ref[:, cut(h)] = sig
+        scale_ref[h] = live * gate[:, 0:1] / denom
         read_ref[:, cut(h)] = read
         mixed_ref[:, cut(h)] = mixed.astype(BF16)
     if project:
@@ -284,7 +291,7 @@
 
 
 def spread_kernel(
-    heads, ways, packed, pos_ref, z_ref, valid_ref, starts_ref, gate_ref, q_ref, norm_ref, read_ref, *refs,
+    heads, ways, packed, pos_ref, z_ref, facts_ref, sig_ref, scale_ref, read_ref, *refs,
 ):
     if ways:
         parts, (total_ref, weight_ref) = refs[: len(ways)], refs[len(ways) : len(ways) + 2]
@@ -296,33 +303,30 @@
         grad_ref[...] = total.astype(BF16)
     else:
         grad_ref, keep_ref, give_ref, numer_ref, denom_ref = refs
-    live = live_rows(valid_ref, q_ref.shape[0])
     for kept, i, h in by_half(heads, pos_ref):
-        sig = feature(q_ref[:, cut(h)].astype(F32)).astype(BF16)
-        sig_full = sig.astype(F32)
-        denom = jnp.sum(sig_full * norm_ref[h, 0:1, :], axis=1, keepdims=True) + 1.0
-        gate = gate_row(gate_ref, h)
-        numer_grad = (grad_ref[:, cut(h)].astype(F32) * gate * (live / denom)).astype(BF16)
+        sig = sig_ref[:, cut(h)]
+        numer_grad = (grad_ref[:, cut(h)].astype(F32) * scale_ref[h]).astype(BF16)
         denom_grad = -jnp.sum(
             numer_grad.astype(F32) * read_ref[:, cut(h)], axis=1, keepdims=True
         )
         memory = dot(sig, numer_grad, TN)
-        norm = jnp.sum(sig_full * denom_grad, axis=0, keepdims=True)
+        norm = jnp.sum(sig.astype(F32) * denom_grad, axis=0, keepdims=True)
         numer_ref[:, cut(h)] = numer_grad
         denom_ref[h] = denom_grad
-        flag = opened(starts_ref)
+        flag = opened(facts_ref)
         if packed and not kept:
-            store_sent(give_ref, i, memory, norm, flag, jnp.zeros_like(norm))
+            store_sent(give_ref, i, memory, norm, flag, False)
         else:
             out_ref = keep_ref if kept else give_ref
             out_ref[i, 0:DH, :] = memory
             out_ref[i, DH:ROWS, :] = tail(ROWS - DH, norm, flag)
 
 
-def grads_kernel(heads, valid_ref, gate_ref, q_ref, k_ref, v_ref, probs_ref, grad_ref, numer_ref,
-                 denom_ref, memory_ref, norm_ref, after_ref, query_ref, key_ref, value_ref):
+def grads_kernel(heads, facts_ref, gate_ref, q_ref, k_ref, v_ref, probs_ref, grad_ref, numer_ref,
+                 denom_ref, memory_ref, norm_ref, *refs):
+    query_ref, key_ref, value_ref = refs[-3:]
     length = q_ref.shape[0]
-    live = live_rows(valid_ref, length)
+    live = live_rows(facts_ref, length)
     for h in range(heads):
         here = slice(h * DH, (h + 1) * DH)
         q, k, v = head(q_ref, h), head(k_ref, h), head(v_ref, h)
@@ -343,11 +347,15 @@
         query_ref[:, here] = total.astype(BF16)
 
 
-def last_kernel(heads, pos_ref, valid_ref, k_ref, v_ref, own_ref, far_ref, key_ref, value_ref,
-                key_out, value_out):
-    live = live_rows(valid_ref, k_ref.shape[0])
+def last_kernel(heads, packed, pos_ref, facts_ref, k_ref, v_ref, own_ref, far_ref, key_ref, value_ref,
+                *refs):
+    key_out, value_out = refs[-2:]
+    live = live_rows(facts_ref, k_ref.shape[0])
     for kept, i, h in by_half(heads, pos_ref):
-        memory, norm, _ = load_state(own_ref if kept else far_ref, i)
+        if kept or not packed:
+            memory, norm, _ = load_state(own_ref if kept else far_ref, i)
+        else:
+            memory, norm, _ = load_sent(far_ref, i, False)
         top, low = split(memory)
         k, v = k_ref[:, cut(h)].astype(F32), v_ref[:, cut(h)]
         sig = (feature(k) * live).astype(BF16)
@@ -392,7 +400,7 @@
         [jax.ShapeDtypeStruct((half, SENT, DH), BF16)],
         [SMEM, VMEM, VMEM] + [ANY] * len(after),
         [pos, keep, other, *after],
-        0.3, "pair",
+        0.01, "pair",
     )[0]
     arrived = [
         lax.ppermute(sent, "seq", [(s, s ^ way) for s in range(count)]) for way in (6, 2, 4)
@@ -400,7 +408,9 @@
     after = before_join(sent)
     own, passed = call(
         functools.partial(join_kernel, heads, forward),
-        [jax.ShapeDtypeStruct((half, ROWS, DH), F32)] * 2,
+        [jax.ShapeDtypeStruct((half, ROWS, DH), F32),
+         jax.ShapeDtypeStruct((half, ROWS, DH), F32) if forward
+         else jax.ShapeDtypeStruct((half, SENT, DH), BF16)],
         [SMEM] + [VMEM] * 5 + [ANY] * len(after),
         [pos, arrived[1], arrived[2], arrived[0], keep, other, *after],
         0.3, "join",
@@ -408,7 +418,7 @@
     return own, lax.ppermute(passed, "seq", pairs)
 
 
-def shards(queries, keys, values, gate, out_weight, out_grad, valid, starts):
+def shards(queries, keys, values, gate, out_weight, out_grad, facts):
     length, width = queries.shape
     heads = width // DH
     cols = out_grad.shape[1]
@@ -419,20 +429,22 @@
     if not paired:
         pos = jnp.zeros_like(pos)
     z = lax.axis_index("head").astype(jnp.int32).reshape(1)
-    valid, starts = valid.reshape(1, 1), starts.reshape(1, 1)
+    facts = facts[0]
     flat = jax.ShapeDtypeStruct((length, width), F32)
     low = jax.ShapeDtypeStruct((length, width), BF16)
     part_low = jax.ShapeDtypeStruct((length, cols), BF16)
     part_full = jax.ShapeDtypeStruct((length, cols), F32)
     states = jax.ShapeDtypeStruct((heads // 2, ROWS, DH), F32)
     packed = jax.ShapeDtypeStruct((heads // 2, SENT, DH), BF16)
+    column = jax.ShapeDtypeStruct((heads, length, 1), F32)
 
     def swap(array, way):
         return lax.ppermute(array, "head", [(s, s ^ way) for s in range(groups)])
 
+    first = call(token_kernel, [jax.ShapeDtypeStruct((8, DH), F32)], [VMEM], [facts], 10, "warm")
     keep, give = call(
-        functools.partial(state_kernel, heads), [states] * 2, [SMEM] * 2 + [VMEM] * 4,
-        [pos, z, valid, starts, keys, values], 0.4, "state",
+        functools.partial(state_kernel, heads), [states] * 2, [SMEM] * 2 + [VMEM] * 3 + [ANY],
+        [pos, z, facts, keys, values, *first], 0.4, "state",
     )
     if direct:
         grad_3 = swap(out_grad, 3)
@@ -444,39 +456,45 @@
             functools.partial(local_kernel, heads),
             [jax.ShapeDtypeStruct((heads, length, length), BF16), flat],
             [VMEM] * 4 + [ANY],
-            [valid, queries, keys, values, sent], 3, "local",
-        )
-        return [kept["local"][1]]
+            [facts, queries, keys, values, sent], 0.1, "local",
+        )
+        if not direct:
+            return [kept["local"][1]]
+        kept["total"] = call(
+            functools.partial(more_kernel, (0,)), [flat], [SMEM] + [VMEM] * 2 + [ANY],
+            [z, out_grad, out_weight, kept["local"][1]], 0.8, "unproject_own",
+        )[0]
+        return [kept["total"]]
 
     own, far = scan_states(keep, give, pos, heads, True, lambda: [], beside_forward)
     probs, local = kept["local"]
     orders = []
     if direct:
-        grad_2 = swap(
-            call(pass_kernel, [part_low], [VMEM, ANY], [grad_3, own], 0.1, "pass_on")[0], 1
-        )
         orders = call(
             token_kernel, [jax.ShapeDtypeStruct((8, DH), F32)], [ANY] * 2, [grad_1, own],
             3, "arrived",
         )
+        grad_2 = swap(
+            call(pass_kernel, [part_low], [VMEM, ANY], [grad_3, own], 0.1, "pass_on")[0], 1
+        )
     outs = call(
         functools.partial(read_kernel, heads, direct),
         [low, flat, jax.ShapeDtypeStruct((heads, DH, 2 * DH), BF16),
-         jax.ShapeDtypeStruct((heads, 8, DH), F32)] + [part_low] * direct,
+         jax.ShapeDtypeStruct((heads, 8, DH), F32), low, column] + [part_low] * direct,
         [SMEM, SMEM, VMEM, SMEM] + [VMEM] * 5 + [VMEM, ANY] * direct,
-        [pos, z, valid, gate, queries, keep, own, far, local] + [out_weight, *orders] * direct,
-        0.1, "read",
+        [pos, z, facts, gate, queries, keep, own, far, local] + [out_weight, *orders] * direct,
+        0.01, "read",
     )
-    mixed, read, memory, norm = outs[:4]
+    mixed, read, memory, norm, sig, scale = outs[:6]
     if direct:
-        sum_2 = swap(outs[4], 1)
+        sum_2 = swap(outs[6], 1)
         total = call(
-            functools.partial(more_kernel, (0, 1, 3)), [flat], [SMEM] + [VMEM] * 4 + [ANY],
-            [z, out_grad, grad_1, grad_3, out_weight, mixed], 0.1, "unproject_more",
+            functools.partial(more_kernel, (1, 3)), [flat], [SMEM] + [VMEM] * 4 + [ANY],
+            [z, grad_1, grad_3, out_weight, kept["total"], mixed], 0.01, "unproject_more",
         )[0]
         near, mine = call(
             rest_kernel, [part_low, part_full], [SMEM, VMEM, VMEM, ANY],
-            [z, mixed, out_weight, total], 0.1, "project_rest",
+            [z, mixed, out_weight, total], 0.01, "project_rest",
         )
         kept["from_1"] = swap(near, 1)
         grads_in = [grad_2, total, out_weight]
@@ -490,64 +508,63 @@
     outs = call(
         functools.partial(spread_kernel, heads, (2,) * direct, paired),
         [states, packed if paired else states, low,
-         jax.ShapeDtypeStruct((heads, length, 1), F32)] + [low] * direct,
-        [SMEM, SMEM, VMEM, VMEM, SMEM] + [VMEM] * (3 + len(grads_in)) + [ANY] * len(orders),
-        [pos, z, valid, starts, gate, queries, norm, read, *grads_in, *orders],
-        0.5, "spread",
+         column] + [low] * direct,
+        [SMEM, SMEM] + [VMEM] * (4 + len(grads_in)) + [ANY] * len(orders),
+        [pos, z, facts, sig, scale, read, *grads_in, *orders],
+        0.01, "spread",
     )
     keep, give, numer_grad, denom_grad = outs[:4]
     mixed_grad = outs[4] if direct else grads_in[0]
 
-    def add_here():
-        if not direct:
-            return []
-        sum_3 = call(
-            add_kernel, [part_low], [SMEM, VMEM, VMEM, VMEM, ANY],
-            [z, mixed, out_weight, sum_2, numer_grad], 0.5, "project_add",
-        )[0]
-        kept["from_3"] = swap(sum_3, 3)
-        return [sum_3]
-
     def beside_back(sent):
+        after = [sent]
+        if direct:
+            after = call(
+                add_kernel, [part_low], [SMEM, VMEM, VMEM, VMEM, ANY],
+                [z, mixed, out_weight, sum_2, sent], 0.01, "project_add",
+            )
+            kept["from_3"] = swap(after[0], 3)
         kept["grads"] = call(
             functools.partial(grads_kernel, heads),
             [low, flat, flat],
-            [VMEM, SMEM] + [VMEM] * 9 + [ANY],
-            [valid, gate, queries, keys, values, probs, mixed_grad, numer_grad, denom_grad, memory,
-             norm, sent],
-            0.3, "grads",
-        )
-        return [kept["grads"][1]] + ([kept["from_1"]] if direct else [])
-
-    own, far = scan_states(keep, give, pos, heads, False, add_here, beside_back)
+            [VMEM, SMEM] + [VMEM] * 9 + [ANY] * len(after),
+            [facts, gate, queries, keys, values, probs, mixed_grad, numer_grad, denom_grad, memory,
+             norm, *after],
+            0.01, "grads",
+        )
+        if not direct:
+            return [kept["grads"][1]]
+        return call(
+            token_kernel, [jax.ShapeDtypeStruct((8, DH), F32)], [ANY] * 2,
+            [kept["from_1"], kept["grads"][1]], 1.5, "settled",
+        )
+
+    own, far = scan_states(keep, give, pos, heads, False, lambda: [], beside_back)
     query_grad, key_part, value_part = kept["grads"]
     if direct:
         output = mine + kept["from_1"].astype(F32) + kept["from_3"].astype(F32)
         output = output.astype(BF16)
     key_grad, value_grad = call(
-        functools.partial(last_kernel, heads),
+        functools.partial(last_kernel, heads, paired),
         [low, low],
         [SMEM] + [VMEM] * 7,
-        [pos, valid, keys, values, own, far, key_part, value_part], 1.5, "last",
+        [pos, facts, keys, values, own, far, key_part, value_part],
+        0.01, "last",
     )
     return (output, query_grad, key_grad, value_grad)
 
 
 def solution(mesh):
-    placed = (
-        P("seq", "head"),
-        P("seq", "head"),
-        P("seq", "head"),
-        P("head"),
-        P("head", None),
-        P("seq", "head"),
-        P("seq"),
-        P("seq"),
+    tokens = P("seq", "head")
+    placed = (tokens, tokens, tokens, P("head"), P("head", None), tokens, P("seq", None, None))
+    parts = jax.shard_map(
+        shards, mesh=mesh, in_specs=placed, out_specs=(tokens,) * 4, check_vma=False
     )
-    return jax.shard_map(
-        shards,
-        mesh=mesh,
-        in_specs=placed,
-        out_specs=(P("seq", "head"), P("seq", "head"), P("seq", "head"), P("seq", "head")),
-        check_vma=False,
-    )
+
+    def whole(queries, keys, values, gate, out_weight, out_grad, valid, starts):
+        row = lax.broadcasted_iota(jnp.int32, (valid.shape[0], 8, DH), 1)
+        facts = jnp.where(row < 4, valid[:, None, None], starts[:, None, None]).astype(F32)
+        facts = lax.with_sharding_constraint(facts, NamedSharding(mesh, placed[-1]))
+        return parts(queries, keys, values, gate, out_weight, out_grad, facts)
+
+    return whole

time: 51.6 us -> 48.5 us (0.940)
  the two profiles are of different devices: /device:TPU:0 before, /device:TPU:10 now
where the time goes in v5:
time: 48.5 us; the launch traced here: 48.3 us
  Pallas kernels  15.3 us (32%)
  starting transfers between devices  15.3 us (32%)
  waiting for transfers between devices  13.5 us (28%)
  between operations  2.12 us (4%)
  local copies, waits for them, and re-layouts  1.25 us (3%)
  other arithmetic  0.82 us (2%)
    pallas_call x18, Pallas kernels, call(): pl.pallas_call(kernel, out_shape=outs, in_specs=in_specs, out_specs=[VMEM...  15.3 us
    ppermute x6, starting transfers between devices, swap(): return lax.ppermute(array, 'head', [(s, s ^ way) for s in range(groups)])  8.01 us
    ppermute x6, starting transfers between devices, scan_states(): lax.ppermute(sent, 'seq', [(s, s ^ way) for s in range(count)])  7.1 us
    ppermute x6, waiting for transfers between devices, swap(): return lax.ppermute(array, 'head', [(s, s ^ way) for s in range(groups)])  6.98 us
    ppermute x6, waiting for transfers between devices, scan_states(): lax.ppermute(sent, 'seq', [(s, s ^ way) for s in range(count)])  3.67 us
    ppermute x2, waiting for transfers between devices, scan_states(): return (own, lax.ppermute(passed, 'seq', pairs))  1.49 us
    ppermute x2, waiting for transfers between devices, scan_states(): other = lax.ppermute(give, 'seq', pairs)  1.36 us
    unnamed x14, local copies, waits for them, and re-layouts  1.18 us
  transfers between devices with their start and end apart: 16, of which 10 were waited for; matrix products, arithmetic and copies ran while one was open for 0% of the time, Pallas kernels for 31%

profile of v5, /device:TPU:10, one launch (start us, length us, event | category | flops | bytes accessed | tf_op | source)
XLA Modules:
  0.0 48.3 jit_solution(2041893567968182514)
XLA Ops:
  2.0 1.1 %copy-done.1 = bf16[128,1024]{1,0:T(8,128)(2,1)S(1)} copy-done((bf16[128,1024]{1,0:T(8,128)(2,1)S(1)}, bf16[128,1024]{1,0:T(8,128)(2,1)}, u32[]{:S(2)}) %copy-start.1) | copy-done | bytes 262168
  3.2 0.4 state.1
  3.7 1.6 %collective-permute-start.6 = (bf16[128,1024]{1,0:T(8,128)(2,1)S(1)}, bf16[128,1024]{1,0:T(8,128)(2,1)S(1)}, u32[]{:S(2)}, u32[]{:S(2)}) collective-permute-start(bf16[128,1024]{1,0:T(8,128)(2,1)S(1)} %copy-done.3), channel_id=1, source_target_pairs={{0,3},{1,2},{2,1},{3,0},{4,7},{5,6},{6,5},{7,4},{8,11},{9,10},{10,... | collective-permute-start | bytes 786440 | tf_op jit(solution)/shard_map/ppermute | solution.py:442
  5.4 2.5 %collective-permute-start.5 = (bf16[128,1024]{1,0:T(8,128)(2,1)S(1)}, bf16[128,1024]{1,0:T(8,128)(2,1)S(1)}, u32[]{:S(2)}, u32[]{:S(2)}) collective-permute-start(bf16[128,1024]{1,0:T(8,128)(2,1)S(1)} %copy-done.3), channel_id=1, source_target_pairs={{0,1},{1,0},{2,3},{3,2},{4,5},{5,4},{6,7},{7,6},{8,9},{9,8},{10,11... | collective-permute-start | bytes 786440 | tf_op jit(solution)/shard_map/ppermute | solution.py:442
  8.1 1.6 %collective-permute-start.3 = (bf16[4,144,128]{2,1,0:T(8,128)(2,1)S(1)}, bf16[4,144,128]{2,1,0:T(8,128)(2,1)S(1)}, u32[]{:S(2)}, u32[]{:S(2)}) collective-permute-start(bf16[4,144,128]{2,1,0:T(8,128)(2,1)S(1)} %pair.2.after_ref), channel_id=1, source_target_pairs={{0,24},{4,28},{8,16},{12,20},{16,8},{20,12},{24,0},{28,4},{1,25},{... | collective-permute-start | bytes 442376 | tf_op jit(solution)/shard_map/ppermute | solution.py:406
  9.7 0.5 %collective-permute-start.2 = (bf16[4,144,128]{2,1,0:T(8,128)(2,1)S(1)}, bf16[4,144,128]{2,1,0:T(8,128)(2,1)S(1)}, u32[]{:S(2)}, u32[]{:S(2)}) collective-permute-start(bf16[4,144,128]{2,1,0:T(8,128)(2,1)S(1)} %pair.2.after_ref), channel_id=1, source_target_pairs={{0,16},{4,20},{8,24},{12,28},{16,0},{20,4},{24,8},{28,12},{1,17},{... | collective-permute-start | bytes 442376 | tf_op jit(solution)/shard_map/ppermute | solution.py:406
  10.2 1.5 %collective-permute-start.1 = (bf16[4,144,128]{2,1,0:T(8,128)(2,1)S(1)}, bf16[4,144,128]{2,1,0:T(8,128)(2,1)S(1)}, u32[]{:S(2)}, u32[]{:S(2)}) collective-permute-start(bf16[4,144,128]{2,1,0:T(8,128)(2,1)S(1)} %pair.2.after_ref), channel_id=1, source_target_pairs={{0,8},{4,12},{8,0},{12,4},{16,24},{20,28},{24,16},{28,20},{1,9},{5... | collective-permute-start | bytes 442376 | tf_op jit(solution)/shard_map/ppermute | solution.py:406
  11.7 2.7 %local.1 = (bf16[8,128,128]{2,1,0:T(8,128)(2,1)S(1)}, f32[128,1024]{1,0:T(8,128)S(1)}) custom-call(f32[8,128]{1,0:T(8,128)S(1)} %broadcast.10.refs_0_.facts_ref, bf16[128,1024]{1,0:T(8,128)(2,1)S(1)} %copy-done, bf16[128,1024]{1,0:T(8,128)(2,1)S(1)} %copy-done.1, bf16[128,1024]{1,0:T(8,128)(2,1)S(1)} %copy-done.2, bf16[4,144,128]{2,1,0:T(8,128)(2,1)S(1)} %pair.2.after_ref), custom_call_target="tpu_custom_call" | custom-call | flops 115000000 | bytes 1024 | tf_op jit(solution)/shard_map/local/pallas_call | solution.py:24
  14.4 0.8 %unproject_own.1.refs_0_.refs_3_ = f32[128,1024]{1,0:T(8,128)S(1)} custom-call(s32[1]{0:T(128)} %bitcast.z_ref, bf16[128,1024]{1,0:T(8,128)(2,1)S(1)} %copy-done.3, bf16[1024,4096]{1,0:T(8,128)(2,1)S(1)} %bitcast.7, f32[128,1024]{1,0:T(8,128)S(1)} %get-tuple-element.33.refs_2_.local_ref), custom_call_target="tpu_custom_call" | custom-call | flops 920000000 | bytes 1024 | tf_op jit(solution)/shard_map/unproject_own/pallas_call | solution.py:24
  15.2 0.6 %collective-permute-done.3.d_ref = bf16[4,144,128]{2,1,0:T(8,128)(2,1)S(1)} collective-permute-done((bf16[4,144,128]{2,1,0:T(8,128)(2,1)S(1)}, bf16[4,144,128]{2,1,0:T(8,128)(2,1)S(1)}, u32[]{:S(2)}, u32[]{:S(2)}) %collective-permute-start.3) | collective-permute-done | bytes 147488 | tf_op jit(solution)/shard_map/ppermute | solution.py:406
  15.8 2.0 %collective-permute-done.2.y_ref = bf16[4,144,128]{2,1,0:T(8,128)(2,1)S(1)} collective-permute-done((bf16[4,144,128]{2,1,0:T(8,128)(2,1)S(1)}, bf16[4,144,128]{2,1,0:T(8,128)(2,1)S(1)}, u32[]{:S(2)}, u32[]{:S(2)}) %collective-permute-start.2) | collective-permute-done | bytes 147488 | tf_op jit(solution)/shard_map/ppermute | solution.py:406
  18.0 0.3 join.2
  18.3 0.3 collective-permute-start.9
  18.7 1.4 %collective-permute-done.5.refs_0_ = bf16[128,1024]{1,0:T(8,128)(2,1)S(1)} collective-permute-done((bf16[128,1024]{1,0:T(8,128)(2,1)S(1)}, bf16[128,1024]{1,0:T(8,128)(2,1)S(1)}, u32[]{:S(2)}, u32[]{:S(2)}) %collective-permute-start.5) | collective-permute-done | bytes 262176 | tf_op jit(solution)/shard_map/ppermute | solution.py:442
  20.3 1.5 %read.1 = (bf16[128,1024]{1,0:T(8,128)(2,1)S(1)}, f32[128,1024]{1,0:T(8,128)S(1)}, bf16[8,128,256]{2,1,0:T(8,128)(2,1)S(1)}, f32[8,8,128]{2,1,0:T(8,128)S(1)}, b...) custom-call(s32[1]{0:T(128)} %bitcast.1.pos_ref, s32[1]{0:T(128)} %bitcast.z_ref, ...), custom_call_target="tpu_custom_call" | custom-call | flops 11500000 | bytes 1024 | tf_op jit(solution)/shard_map/read/pallas_call | solution.py:24
  21.8 1.8 %collective-permute-start.8 = (bf16[128,1024]{1,0:T(8,128)(2,1)S(1)}, bf16[128,1024]{1,0:T(8,128)(2,1)S(1)}, u32[]{:S(2)}, u32[]{:S(2)}) collective-permute-start(bf16[128,1024]{1,0:T(8,128)(2,1)S(1)} %get-tuple-element.39), channel_id=1, source_target_pairs={{0,1},{1,0},{2,3},{3,2},{4,5},{5,4},{6,7},{7,6},{8,9},{9,8},{10,11... | collective-permute-start | bytes 786440 | tf_op jit(solution)/shard_map/ppermute | solution.py:442
  23.6 1.5 %unproject_more.1.after_ref.refs_1_ = f32[128,1024]{1,0:T(8,128)S(1)} custom-call(s32[1]{0:T(128)} %bitcast.z_ref, bf16[128,1024]{1,0:T(8,128)(2,1)S(1)} %collective-permute-done.5.refs_0_, bf16[128,1024]{1,0:T(8,128)(2,1)S(1)} %collective-permute-done.6.refs_1_.block_ref, bf16[1024,4096]{1,0:T(8,128)(2,1)S(1)} %bitcast.7, ...), custom_call_target="tpu_custom_call" | custom-call | flops 11500000 | bytes 1024 | tf_op jit(solution)/shard_map/unproject_more/pallas_call | solution.py:24
  25.1 0.7 %project_rest.1 = (bf16[128,1024]{1,0:T(8,128)(2,1)S(1)}, f32[128,1024]{1,0:T(8,128)S(1)}) custom-call(s32[1]{0:T(128)} %bitcast.z_ref, bf16[128,1024]{1,0:T(8,128)(2,1)S(1)} %get-tuple-element.36.refs_4_.mixed_ref, bf16[1024,4096]{1,0:T(8,128)(2,1)S(1)} %bitcast.7, f32[128,1024]{1,0:T(8,128)S(1)} %unproject_more.1.after_ref.refs_1_), custom_call_target="tpu_custom_call" | custom-call | flops 11500000 | bytes 1024 | tf_op jit(solution)/shard_map/project_rest/pallas_call | solution.py:24
  26.2 1.4 %collective-permute-done.9.refs_0_ = bf16[128,1024]{1,0:T(8,128)(2,1)S(1)} collective-permute-done((bf16[128,1024]{1,0:T(8,128)(2,1)S(1)}, bf16[128,1024]{1,0:T(8,128)(2,1)S(1)}, u32[]{:S(2)}, u32[]{:S(2)}) %collective-permute-start.9) | collective-permute-done | bytes 262176 | tf_op jit(solution)/shard_map/ppermute | solution.py:442
  27.6 1.2 %spread.1 = (f32[4,136,128]{2,1,0:T(8,128)S(1)}, bf16[4,144,128]{2,1,0:T(8,128)(2,1)S(1)}, bf16[128,1024]{1,0:T(8,128)(2,1)S(1)}, f32[8,128,1]{2,1,0:T(8,128)S(1)}, bf16[128,1024]{1,0:T(8,128)(2,1)S(1)}) custom-call(s32[1]{0:T(128)} %bitcast.1.pos_ref, s32[1]{0:T(128)} %bitcast.z_ref, f32[8,128]{1,0:T(8,128)S(1)} %broadcast.10.refs_0_.facts_ref, ...), custom_call_target="tpu_custom_call" | custom-call | flops 11500000 | bytes 1024 | tf_op jit(solution)/shard_map/spread/pallas_call | solution.py:24
  28.9 1.4 %collective-permute-done.10.other_ref = bf16[4,144,128]{2,1,0:T(8,128)(2,1)S(1)} collective-permute-done((bf16[4,144,128]{2,1,0:T(8,128)(2,1)S(1)}, bf16[4,144,128]{2,1,0:T(8,128)(2,1)S(1)}, u32[]{:S(2)}, u32[]{:S(2)}) %collective-permute-start.10) | collective-permute-done | bytes 147488 | tf_op jit(solution)/shard_map/ppermute | solution.py:396
  30.3 1.4 %collective-permute-start.14 = (bf16[4,144,128]{2,1,0:T(8,128)(2,1)S(1)}, bf16[4,144,128]{2,1,0:T(8,128)(2,1)S(1)}, u32[]{:S(2)}, u32[]{:S(2)}) collective-permute-start(bf16[4,144,128]{2,1,0:T(8,128)(2,1)S(1)} %pair.3.after_ref), channel_id=1, source_target_pairs={{0,24},{4,28},{8,16},{12,20},{16,8},{20,12},{24,0},{28,4},{1,25},{... | collective-permute-start | bytes 442376 | tf_op jit(solution)/shard_map/ppermute | solution.py:406
  31.7 0.6 %collective-permute-start.13 = (bf16[4,144,128]{2,1,0:T(8,128)(2,1)S(1)}, bf16[4,144,128]{2,1,0:T(8,128)(2,1)S(1)}, u32[]{:S(2)}, u32[]{:S(2)}) collective-permute-start(bf16[4,144,128]{2,1,0:T(8,128)(2,1)S(1)} %pair.3.after_ref), channel_id=1, source_target_pairs={{0,16},{4,20},{8,24},{12,28},{16,0},{20,4},{24,8},{28,12},{1,17},{... | collective-permute-start | bytes 442376 | tf_op jit(solution)/shard_map/ppermute | solution.py:406
  32.3 1.5 %collective-permute-start.12 = (bf16[4,144,128]{2,1,0:T(8,128)(2,1)S(1)}, bf16[4,144,128]{2,1,0:T(8,128)(2,1)S(1)}, u32[]{:S(2)}, u32[]{:S(2)}) collective-permute-start(bf16[4,144,128]{2,1,0:T(8,128)(2,1)S(1)} %pair.3.after_ref), channel_id=1, source_target_pairs={{0,8},{4,12},{8,0},{12,4},{16,24},{20,28},{24,16},{28,20},{1,9},{5... | collective-permute-start | bytes 442376 | tf_op jit(solution)/shard_map/ppermute | solution.py:406
  33.8 0.5 project_add.1.refs_0_
  34.3 1.4 %collective-permute-start.11 = (bf16[128,1024]{1,0:T(8,128)(2,1)S(1)}, bf16[128,1024]{1,0:T(8,128)(2,1)S(1)}, u32[]{:S(2)}, u32[]{:S(2)}) collective-permute-start(bf16[128,1024]{1,0:T(8,128)(2,1)S(1)} %project_add.1.refs_0_), channel_id=1, source_target_pairs={{0,3},{1,2},{2,1},{3,0},{4,7},{5,6},{6,5},{7,4},{8,11},{9,10},{10,... | collective-permute-start | bytes 786440 | tf_op jit(solution)/shard_map/ppermute | solution.py:442
  35.7 3.7 %grads.1 = (bf16[128,1024]{1,0:T(8,128)(2,1)}, f32[128,1024]{1,0:T(8,128)S(1)}, f32[128,1024]{1,0:T(8,128)S(1)}) custom-call(f32[8,128]{1,0:T(8,128)S(1)} %broadcast.10.refs_0_.facts_ref, f32[8]{0:T(128)S(1)} %copy-done.4, bf16[128,1024]{1,0:T(8,128)(2,1)S(1)} %copy-done, bf16[128,1024]{1,0:T(8,128)(2,1)S(1)} %copy-done.1, bf16[128,1024]{1,0:T(8,128)(2,1)S(1)} %copy-done.2, ...), custom_call_target="tpu_custom_call" | custom-call | flops 11500000 | bytes 1024 | tf_op jit(solution)/shard_map/grads/pallas_call | solution.py:24
  39.4 0.9 %collective-permute-done.13.y_ref = bf16[4,144,128]{2,1,0:T(8,128)(2,1)S(1)} collective-permute-done((bf16[4,144,128]{2,1,0:T(8,128)(2,1)S(1)}, bf16[4,144,128]{2,1,0:T(8,128)(2,1)S(1)}, u32[]{:S(2)}, u32[]{:S(2)}) %collective-permute-start.13) | collective-permute-done | bytes 147488 | tf_op jit(solution)/shard_map/ppermute | solution.py:406
  40.6 1.4 %collective-permute-done.15.far_ref = bf16[4,144,128]{2,1,0:T(8,128)(2,1)S(1)} collective-permute-done((bf16[4,144,128]{2,1,0:T(8,128)(2,1)S(1)}, bf16[4,144,128]{2,1,0:T(8,128)(2,1)S(1)}, u32[]{:S(2)}, u32[]{:S(2)}) %collective-permute-start.15) | collective-permute-done | bytes 147488 | tf_op jit(solution)/shard_map/ppermute | solution.py:418
  41.9 1.4 %last.1 = (bf16[128,1024]{1,0:T(8,128)(2,1)}, bf16[128,1024]{1,0:T(8,128)(2,1)}) custom-call(s32[1]{0:T(128)} %bitcast.1.pos_ref, f32[8,128]{1,0:T(8,128)S(1)} %broadcast.10.refs_0_.facts_ref, bf16[128,1024]{1,0:T(8,128)(2,1)S(1)} %copy-done.1, bf16[128,1024]{1,0:T(8,128)(2,1)S(1)} %copy-done.2, f32[4,136,128]{2,1,0:T(8,128)S(1)} %get-tuple-element.53.own_ref, ...), custom_call_target="tpu_custom_call" | custom-call | flops 11500000 | bytes 1024 | tf_op jit(solution)/shard_map/last/pallas_call | solution.py:24
  43.4 4.1 %collective-permute-done.11 = bf16[128,1024]{1,0:T(8,128)(2,1)S(1)} collective-permute-done((bf16[128,1024]{1,0:T(8,128)(2,1)S(1)}, bf16[128,1024]{1,0:T(8,128)(2,1)S(1)}, u32[]{:S(2)}, u32[]{:S(2)}) %collective-permute-start.11) | collective-permute-done | bytes 262176 | tf_op jit(solution)/shard_map/ppermute | solution.py:442
  47.5 0.8 %add_convert_fusion = bf16[128,1024]{1,0:T(8,128)(2,1)} fusion(bf16[128,1024]{1,0:T(8,128)(2,1)S(1)} %collective-permute-done.11, f32[128,1024]{1,0:T(8,128)S(1)} %get-tuple-element.37, bf16[128,1024]{1,0:T(8,128)(2,1)S(1)} %collective-permute-done.7.refs_0_), kind=kLoop, calls=%fused_computation | loop fusion | flops 655360 | bytes 1310720 | tf_op jit(solution)/shard_map/convert_element_type | solution.py:546
  (36 shorter events, 1.5 us)
Async XLA Ops:
  1.9 12.4 %slice-start = ((s8[8388608]{0:T(1024)(128)(4,1)}), s8[4194304]{0:T(1024)(128)(4,1)S(1)}, s32[]{:S(2)}) async-start(s8[8388608]{0:T(1024)(128)(4,1)} %bitcast.6), calls=%async_computation | async-start | bytes 8388608
  2.0 1.1 %copy-start.1 = (bf16[128,1024]{1,0:T(8,128)(2,1)S(1)}, bf16[128,1024]{1,0:T(8,128)(2,1)}, u32[]{:S(2)}) copy-start(bf16[128,1024]{1,0:T(8,128)(2,1)} %k_ref.7) | copy-start | bytes 786436
  2.0 1.2 %copy-start.2 = (bf16[128,1024]{1,0:T(8,128)(2,1)S(1)}, bf16[128,1024]{1,0:T(8,128)(2,1)}, u32[]{:S(2)}) copy-start(bf16[128,1024]{1,0:T(8,128)(2,1)} %v_ref.7) | copy-start | bytes 786436
  2.0 1.7 %copy-start.3 = (bf16[128,1024]{1,0:T(8,128)(2,1)S(1)}, bf16[128,1024]{1,0:T(8,128)(2,1)}, u32[]{:S(2)}) copy-start(bf16[128,1024]{1,0:T(8,128)(2,1)} %refs_0_.2) | copy-start | bytes 786436
  2.0 9.6 %copy-start = (bf16[128,1024]{1,0:T(8,128)(2,1)S(1)}, bf16[128,1024]{1,0:T(8,128)(2,1)}, u32[]{:S(2)}) copy-start(bf16[128,1024]{1,0:T(8,128)(2,1)} %q_ref.5) | copy-start | bytes 786436
  2.0 12.3 %slice-start.1 = ((s8[8388608]{0:T(1024)(128)(4,1)}), s8[4194304]{0:T(1024)(128)(4,1)S(1)}, s32[]{:S(2)}) async-start(s8[8388608]{0:T(1024)(128)(4,1)} %bitcast.6), calls=%async_computation.1 | async-start | bytes 8388608
  3.6 4.2 %collective-permute-start = (f32[4,136,128]{2,1,0:T(8,128)S(1)}, f32[4,136,128]{2,1,0:T(8,128)S(1)}, u32[]{:S(2)}, u32[]{:S(2)}) collective-permute-start(f32[4,136,128]{2,1,0:T(8,128)S(1)} %get-tuple-element.32), channel_id=1, source_target_pairs={{0,4},{4,0},{8,12},{12,8},{16,20},{20,16},{24,28},{28,24},{1,5},{5... | collective-permute-start | bytes 835592 | tf_op jit(solution)/shard_map/ppermute | solution.py:396
  3.7 14.6 %collective-permute-start.6 = (bf16[128,1024]{1,0:T(8,128)(2,1)S(1)}, bf16[128,1024]{1,0:T(8,128)(2,1)S(1)}, u32[]{:S(2)}, u32[]{:S(2)}) collective-permute-start(bf16[128,1024]{1,0:T(8,128)(2,1)S(1)} %copy-done.3), channel_id=1, source_target_pairs={{0,3},{1,2},{2,1},{3,0},{4,7},{5,6},{6,5},{7,4},{8,11},{9,10},{10,... | collective-permute-start | bytes 786440 | tf_op jit(solution)/shard_map/ppermute | solution.py:442
  5.4 14.8 %collective-permute-start.5 = (bf16[128,1024]{1,0:T(8,128)(2,1)S(1)}, bf16[128,1024]{1,0:T(8,128)(2,1)S(1)}, u32[]{:S(2)}, u32[]{:S(2)}) collective-permute-start(bf16[128,1024]{1,0:T(8,128)(2,1)S(1)} %copy-done.3), channel_id=1, source_target_pairs={{0,1},{1,0},{2,3},{3,2},{4,5},{5,4},{6,7},{7,6},{8,9},{9,8},{10,11... | collective-permute-start | bytes 786440 | tf_op jit(solution)/shard_map/ppermute | solution.py:442
  8.1 7.7 %collective-permute-start.3 = (bf16[4,144,128]{2,1,0:T(8,128)(2,1)S(1)}, bf16[4,144,128]{2,1,0:T(8,128)(2,1)S(1)}, u32[]{:S(2)}, u32[]{:S(2)}) collective-permute-start(bf16[4,144,128]{2,1,0:T(8,128)(2,1)S(1)} %pair.2.after_ref), channel_id=1, source_target_pairs={{0,24},{4,28},{8,16},{12,20},{16,8},{20,12},{24,0},{28,4},{1,25},{... | collective-permute-start | bytes 442376 | tf_op jit(solution)/shard_map/ppermute | solution.py:406
  9.7 8.2 %collective-permute-start.2 = (bf16[4,144,128]{2,1,0:T(8,128)(2,1)S(1)}, bf16[4,144,128]{2,1,0:T(8,128)(2,1)S(1)}, u32[]{:S(2)}, u32[]{:S(2)}) collective-permute-start(bf16[4,144,128]{2,1,0:T(8,128)(2,1)S(1)} %pair.2.after_ref), channel_id=1, source_target_pairs={{0,16},{4,20},{8,24},{12,28},{16,0},{20,4},{24,8},{28,12},{1,17},{... | collective-permute-start | bytes 442376 | tf_op jit(solution)/shard_map/ppermute | solution.py:406
  10.2 7.8 %collective-permute-start.1 = (bf16[4,144,128]{2,1,0:T(8,128)(2,1)S(1)}, bf16[4,144,128]{2,1,0:T(8,128)(2,1)S(1)}, u32[]{:S(2)}, u32[]{:S(2)}) collective-permute-start(bf16[4,144,128]{2,1,0:T(8,128)(2,1)S(1)} %pair.2.after_ref), channel_id=1, source_target_pairs={{0,8},{4,12},{8,0},{12,4},{16,24},{20,28},{24,16},{28,20},{1,9},{5... | collective-permute-start | bytes 442376 | tf_op jit(solution)/shard_map/ppermute | solution.py:406
  15.2 5.1 %copy-start.4 = (f32[8]{0:T(128)S(1)}, f32[8]{0:T(128)}, u32[]{:S(2)}) copy-start(f32[8]{0:T(128)} %gate_ref.3) | copy-start | bytes 100
  18.3 9.2 %collective-permute-start.9 = (bf16[128,1024]{1,0:T(8,128)(2,1)S(1)}, bf16[128,1024]{1,0:T(8,128)(2,1)S(1)}, u32[]{:S(2)}, u32[]{:S(2)}) collective-permute-start(bf16[128,1024]{1,0:T(8,128)(2,1)S(1)} %pass_on.1), channel_id=1, source_target_pairs={{0,1},{1,0},{2,3},{3,2},{4,5},{5,4},{6,7},{7,6},{8,9},{9,8},{10,11... | collective-permute-start | bytes 786440 | tf_op jit(solution)/shard_map/ppermute | solution.py:442
  18.7 1.6 %collective-permute-start.4 = (f32[4,136,128]{2,1,0:T(8,128)S(1)}, f32[4,136,128]{2,1,0:T(8,128)S(1)}, u32[]{:S(2)}, u32[]{:S(2)}) collective-permute-start(f32[4,136,128]{2,1,0:T(8,128)S(1)} %get-tuple-element.35), channel_id=1, source_target_pairs={{0,4},{4,0},{8,12},{12,8},{16,20},{20,16},{24,28},{28,24},{1,5},{5... | collective-permute-start | bytes 835592 | tf_op jit(solution)/shard_map/ppermute | solution.py:418
  21.8 12.1 %collective-permute-start.8 = (bf16[128,1024]{1,0:T(8,128)(2,1)S(1)}, bf16[128,1024]{1,0:T(8,128)(2,1)S(1)}, u32[]{:S(2)}, u32[]{:S(2)}) collective-permute-start(bf16[128,1024]{1,0:T(8,128)(2,1)S(1)} %get-tuple-element.39), channel_id=1, source_target_pairs={{0,1},{1,0},{2,3},{3,2},{4,5},{5,4},{6,7},{7,6},{8,9},{9,8},{10,11... | collective-permute-start | bytes 786440 | tf_op jit(solution)/shard_map/ppermute | solution.py:442
  25.8 13.5 %collective-permute-start.7 = (bf16[128,1024]{1,0:T(8,128)(2,1)S(1)}, bf16[128,1024]{1,0:T(8,128)(2,1)S(1)}, u32[]{:S(2)}, u32[]{:S(2)}) collective-permute-start(bf16[128,1024]{1,0:T(8,128)(2,1)S(1)} %get-tuple-element.38.refs_3_), channel_id=1, source_target_pairs={{0,1},{1,0},{2,3},{3,2},{4,5},{5,4},{6,7},{7,6},{8,9},{9,8},{10,11... | collective-permute-start | bytes 786440 | tf_op jit(solution)/shard_map/ppermute | solution.py:442
  28.8 1.4 %collective-permute-start.10 = (bf16[4,144,128]{2,1,0:T(8,128)(2,1)S(1)}, bf16[4,144,128]{2,1,0:T(8,128)(2,1)S(1)}, u32[]{:S(2)}, u32[]{:S(2)}) collective-permute-start(bf16[4,144,128]{2,1,0:T(8,128)(2,1)S(1)} %get-tuple-element.44), channel_id=1, source_target_pairs={{0,4},{4,0},{8,12},{12,8},{16,20},{20,16},{24,28},{28,24},{1,5},{5... | collective-permute-start | bytes 442376 | tf_op jit(solution)/shard_map/ppermute | solution.py:396
  30.3 9.1 %collective-permute-start.14 = (bf16[4,144,128]{2,1,0:T(8,128)(2,1)S(1)}, bf16[4,144,128]{2,1,0:T(8,128)(2,1)S(1)}, u32[]{:S(2)}, u32[]{:S(2)}) collective-permute-start(bf16[4,144,128]{2,1,0:T(8,128)(2,1)S(1)} %pair.3.after_ref), channel_id=1, source_target_pairs={{0,24},{4,28},{8,16},{12,20},{16,8},{20,12},{24,0},{28,4},{1,25},{... | collective-permute-start | bytes 442376 | tf_op jit(solution)/shard_map/ppermute | solution.py:406
  31.7 8.6 %collective-permute-start.13 = (bf16[4,144,128]{2,1,0:T(8,128)(2,1)S(1)}, bf16[4,144,128]{2,1,0:T(8,128)(2,1)S(1)}, u32[]{:S(2)}, u32[]{:S(2)}) collective-permute-start(bf16[4,144,128]{2,1,0:T(8,128)(2,1)S(1)} %pair.3.after_ref), channel_id=1, source_target_pairs={{0,16},{4,20},{8,24},{12,28},{16,0},{20,4},{24,8},{28,12},{1,17},{... | collective-permute-start | bytes 442376 | tf_op jit(solution)/shard_map/ppermute | solution.py:406
  32.3 8.0 %collective-permute-start.12 = (bf16[4,144,128]{2,1,0:T(8,128)(2,1)S(1)}, bf16[4,144,128]{2,1,0:T(8,128)(2,1)S(1)}, u32[]{:S(2)}, u32[]{:S(2)}) collective-permute-start(bf16[4,144,128]{2,1,0:T(8,128)(2,1)S(1)} %pair.3.after_ref), channel_id=1, source_target_pairs={{0,8},{4,12},{8,0},{12,4},{16,24},{20,28},{24,16},{28,20},{1,9},{5... | collective-permute-start | bytes 442376 | tf_op jit(solution)/shard_map/ppermute | solution.py:406
  34.3 13.2 %collective-permute-start.11 = (bf16[128,1024]{1,0:T(8,128)(2,1)S(1)}, bf16[128,1024]{1,0:T(8,128)(2,1)S(1)}, u32[]{:S(2)}, u32[]{:S(2)}) collective-permute-start(bf16[128,1024]{1,0:T(8,128)(2,1)S(1)} %project_add.1.refs_0_), channel_id=1, source_target_pairs={{0,3},{1,2},{2,1},{3,0},{4,7},{5,6},{6,5},{7,4},{8,11},{9,10},{10,... | collective-permute-start | bytes 786440 | tf_op jit(solution)/shard_map/ppermute | solution.py:442
  40.5 1.4 %collective-permute-start.15 = (bf16[4,144,128]{2,1,0:T(8,128)(2,1)S(1)}, bf16[4,144,128]{2,1,0:T(8,128)(2,1)S(1)}, u32[]{:S(2)}, u32[]{:S(2)}) collective-permute-start(bf16[4,144,128]{2,1,0:T(8,128)(2,1)S(1)} %get-tuple-element.54), channel_id=1, source_target_pairs={{0,4},{4,0},{8,12},{12,8},{16,20},{20,16},{24,28},{28,24},{1,5},{5... | collective-permute-start | bytes 442376 | tf_op jit(solution)/shard_map/ppermute | solution.py:418

commit v6 on v5

--- a/solution.py
+++ b/solution.py
@@ -10,7 +10,7 @@
 
 DH = 128
 ROWS = 136
-SENT = 144
+TAIL = 16
 BF16 = jnp.bfloat16
 F32 = jnp.float32
 VMEM = pl.BlockSpec(memory_space=pltpu.VMEM)
@@ -96,117 +96,137 @@
             yield kept, i, first + i
 
 
-def state_kernel(
-    heads, pos_ref, z_ref, facts_ref, k_ref, v_ref, after_ref, keep_ref, give_ref
-):
+def pack(ref, states, flag, centred):
+    count = len(states)
+    norms = [split(norm) for _, norm in states]
+    centres = [jnp.zeros_like(norm) for _, norm in states]
+    memories = [memory for memory, _ in states]
+    if centred:
+        sums = [jnp.sum(memory, axis=0, keepdims=True) for memory in memories]
+        weights = [jnp.sum(norm, axis=1, keepdims=True) for _, norm in states]
+        centres = [a / jnp.maximum(b, 1e-30) for a, b in zip(sums, weights)]
+        centres = [centre.astype(BF16).astype(F32) for centre in centres]
+        outers = [outer(*norm, centre) for norm, centre in zip(norms, centres)]
+        memories = [memory - less for memory, less in zip(memories, outers)]
+    for i, memory in enumerate(memories):
+        ref[i * DH : (i + 1) * DH, :] = memory.astype(BF16)
+    tops, lows = zip(*norms)
+    rows = tail(TAIL, *[x.astype(F32) for x in tops + lows], *centres, flag)
+    ref[count * DH : count * DH + TAIL, :] = rows.astype(BF16)
+
+
+def pack_parts(refs, states, flag, centred):
+    share = len(states) // len(refs)
+    for at, ref in enumerate(refs):
+        pack(ref, states[at * share : (at + 1) * share], flag, centred)
+
+
+def outer(top, low, centre):
+    norms = tail(TAIL, top.astype(F32), low.astype(F32)).astype(BF16)
+    return dot(norms, tail(TAIL, centre, centre).astype(BF16), TN)
+
+
+def unpack(ref, centred):
+    count = ref.shape[0] // DH
+    rows = ref[count * DH : count * DH + TAIL, :].astype(F32)
+    row = [rows[i : i + 1] for i in range(3 * count + 1)]
+    states = []
+    for i in range(count):
+        memory = ref[i * DH : (i + 1) * DH, :].astype(F32)
+        if centred:
+            memory = memory + outer(row[i], row[count + i], row[2 * count + i])
+        states.append((memory, row[i] + row[count + i]))
+    return states, row[3 * count]
+
+
+def load_states(ref):
+    states = [(ref[i, 0:DH, :], ref[i, DH : DH + 1, :]) for i in range(ref.shape[0])]
+    return states, ref[0, DH + 1 : DH + 2, :]
+
+
+def store_states(ref, states, flag):
+    for i, (memory, norm) in enumerate(states):
+        ref[i, 0:DH, :] = memory
+        ref[i, DH:ROWS, :] = tail(ROWS - DH, norm, flag)
+
+
+def scaled(scale, state):
+    return scale * state[0], scale * state[1]
+
+
+def added(*states):
+    return sum(memory for memory, _ in states), sum(norm for _, norm in states)
+
+
+def chosen(which, yes, no):
+    return jnp.where(which, yes[0], no[0]), jnp.where(which, yes[1], no[1])
+
+
+def state_kernel(heads, packed, pos_ref, z_ref, facts_ref, k_ref, v_ref, after_ref, *refs):
     live = live_rows(facts_ref, k_ref.shape[0])
-    for kept, i, h in by_half(heads, pos_ref):
-        out_ref = keep_ref if kept else give_ref
+    kept, given = [], []
+    for mine, i, h in by_half(heads, pos_ref):
         sig = (feature(k_ref[:, cut(h)].astype(F32)) * live).astype(BF16)
-        out_ref[i, 0:DH, :] = dot(sig, v_ref[:, cut(h)], TN)
+        memory = dot(sig, v_ref[:, cut(h)], TN)
         norm = jnp.sum(sig.astype(F32), axis=0, keepdims=True)
-        out_ref[i, DH:ROWS, :] = tail(ROWS - DH, norm, opened(facts_ref))
-
-
-def in_three(x):
-    first = x.astype(BF16).astype(F32)
-    second = (x - first).astype(BF16).astype(F32)
-    return first, second, x - first - second
-
-
-def store_sent(ref, i, memory, norm, flag, centred):
-    centre = jnp.zeros_like(norm)
-    if centred:
-        weight = jnp.maximum(jnp.sum(norm, axis=1, keepdims=True), 1e-30)
-        centre = jnp.sum(memory, axis=0, keepdims=True) / weight
-        centre = centre.astype(BF16).astype(F32)
-        norms = tail(16, *in_three(norm)).astype(BF16)
-        centres = tail(16, centre, centre, centre).astype(BF16)
-        memory = memory - dot(norms, centres, TN)
-    ref[i, 0:DH, :] = memory.astype(BF16)
-    ref[i, DH:SENT, :] = tail(SENT - DH, *in_three(norm), centre, flag).astype(BF16)
-
-
-def load_sent(ref, i, centred):
-    memory = ref[i, 0:DH, :].astype(F32)
-    rows = ref[i, DH:SENT, :].astype(F32)
-    if centred:
-        norms = tail(16, rows[0:1], rows[1:2], rows[2:3]).astype(BF16)
-        centres = tail(16, rows[3:4], rows[3:4], rows[3:4]).astype(BF16)
-        memory = memory + dot(norms, centres, TN)
-    return memory, rows[0:1] + rows[1:2] + rows[2:3], rows[4:5]
-
-
-def load_state(ref, i):
-    return ref[i, 0:DH, :], ref[i, DH : DH + 1, :], ref[i, DH + 1 : DH + 2, :]
-
-
-def load_other(ref, i, forward):
-    return load_state(ref, i) if forward else load_sent(ref, i, False)
-
-
-def pair_kernel(heads, forward, pos_ref, keep_ref, other_ref, *refs):
+        (kept if mine else given).append((memory, norm))
+    flag = jnp.broadcast_to(opened(facts_ref), (1, DH))
+    store_states(refs[0], kept, flag)
+    if packed:
+        pack_parts(refs[1:], given, flag, True)
+    else:
+        store_states(refs[1], given, flag)
+
+
+def load_others(refs, forward):
+    states = []
+    for ref in refs:
+        part, flag = unpack(ref, forward)
+        states += part
+    return states, flag
+
+
+def pair_kernel(heads, forward, count, pos_ref, keep_ref, *refs):
     sent_ref = refs[-1]
     lower = lax.rem(pos_ref[0], 2) == 0
-    for i in range(heads // 2):
-        memory, norm, flag = load_state(keep_ref, i)
-        other_memory, other_norm, other_flag = load_other(other_ref, i, forward)
-        one = jnp.ones_like(flag)
-        if forward:
-            on_mine = jnp.where(lower, other_flag, one)
-            on_other = jnp.where(lower, one, flag)
-        else:
-            on_mine = jnp.where(lower, flag, flag * other_flag)
-            on_other = jnp.where(lower, flag * other_flag, other_flag)
-        memory = on_mine * memory + on_other * other_memory
-        norm = on_mine * norm + on_other * other_norm
-        store_sent(sent_ref, i, memory, norm, flag * other_flag, forward)
-
-
-def join_kernel(
-    heads, forward, pos_ref, x_ref, y_ref, d_ref, keep_ref, other_ref, *refs
-):
-    own_ref, sent_ref = refs[-2:]
+    mine, flag = load_states(keep_ref)
+    others, other_flag = load_others(refs[:count], forward)
+    one = jnp.ones_like(flag)
+    if forward:
+        on_mine = jnp.where(lower, other_flag, one)
+        on_other = jnp.where(lower, one, flag)
+    else:
+        on_mine = jnp.where(lower, flag, flag * other_flag)
+        on_other = jnp.where(lower, flag * other_flag, other_flag)
+    totals = [added(scaled(on_mine, a), scaled(on_other, b)) for a, b in zip(mine, others)]
+    pack(sent_ref, totals, flag * other_flag, forward)
+
+
+def join_kernel(heads, forward, count, parts, pos_ref, x_ref, y_ref, d_ref, keep_ref, *refs):
+    own_ref, *sent_refs = refs[-1 - parts :]
     lower = lax.rem(pos_ref[0], 2) == 0
     chip = pos_ref[0] // 2
     place = chip if forward else 3 - chip
     odd, high = lax.rem(place, 2) == 1, place >= 2
-    for i in range(heads // 2):
-        x_mem, x_norm, x_open = load_sent(x_ref, i, forward)
-        y_mem, y_norm, y_open = load_sent(y_ref, i, forward)
-        d_mem, d_norm, d_open = load_sent(d_ref, i, forward)
-        on_x = jnp.where(odd, jnp.ones_like(x_open), 0.0)
-        on_y = jnp.where(high, jnp.where(odd, x_open, d_open), 0.0)
-        on_d = jnp.where(high, jnp.where(odd, x_open * y_open, 1.0), 0.0)
-        memory = on_x * x_mem + on_y * y_mem + on_d * d_mem
-        norm = on_x * x_norm + on_y * y_norm + on_d * d_norm
-        mine_mem, mine_norm, mine_open = load_state(keep_ref, i)
-        other_mem, other_norm, other_open = load_other(other_ref, i, forward)
+    xs, x_open = unpack(x_ref, forward)
+    ys, y_open = unpack(y_ref, forward)
+    ds, d_open = unpack(d_ref, forward)
+    on_x = jnp.where(odd, jnp.ones_like(x_open), 0.0)
+    on_y = jnp.where(high, jnp.where(odd, x_open, d_open), 0.0)
+    on_d = jnp.where(high, jnp.where(odd, x_open * y_open, 1.0), 0.0)
+    mines, mine_open = load_states(keep_ref)
+    others, other_open = load_others(refs[:count], forward)
+    own, sent = [], []
+    for x, y, d, mine, other in zip(xs, ys, ds, mines, others):
+        carry = added(scaled(on_x, x), scaled(on_y, y), scaled(on_d, d))
         if forward:
-            own = (
-                jnp.where(lower, memory, other_open * memory + other_mem),
-                jnp.where(lower, norm, other_open * norm + other_norm),
-            )
-            sent = (
-                jnp.where(lower, mine_open * memory + mine_mem, memory),
-                jnp.where(lower, mine_open * norm + mine_norm, norm),
-            )
+            own.append(chosen(lower, carry, added(scaled(other_open, carry), other)))
+            sent.append(chosen(lower, added(scaled(mine_open, carry), mine), carry))
         else:
-            own = (
-                jnp.where(lower, other_open * (memory + other_mem), memory),
-                jnp.where(lower, other_open * (norm + other_norm), norm),
-            )
-            sent = (
-                jnp.where(lower, memory, mine_open * (memory + mine_mem)),
-                jnp.where(lower, norm, mine_open * (norm + mine_norm)),
-            )
-        own_ref[i, 0:DH, :] = own[0]
-        own_ref[i, DH:ROWS, :] = tail(ROWS - DH, own[1])
-        if forward:
-            sent_ref[i, 0:DH, :] = sent[0]
-            sent_ref[i, DH:ROWS, :] = tail(ROWS - DH, sent[1])
-        else:
-            store_sent(sent_ref, i, *sent, mine_open, False)
+            own.append(chosen(lower, scaled(other_open, added(carry, other)), carry))
+            sent.append(chosen(lower, carry, scaled(mine_open, added(carry, mine))))
+    store_states(own_ref, own, mine_open)
+    pack_parts(sent_refs, sent, mine_open, forward)
 
 
 def local_kernel(heads, facts_ref, q_ref, k_ref, v_ref, after_ref, probs_ref, local_ref):
@@ -227,18 +247,25 @@
     return pl.ds(pl.multiple_of((z_ref[0] ^ way) * cols, DH), cols)
 
 
+def load_carries(own_ref, far_refs, packed, forward):
+    own, flag = load_states(own_ref)
+    far = load_others(far_refs, forward)[0] if packed else load_states(far_refs[0])[0]
+    return {True: own, False: far}, flag
+
+
 def read_kernel(
-    heads, project, pos_ref, z_ref, facts_ref, gate_ref, q_ref, keep_ref, own_ref, far_ref,
-    local_ref, *refs,
+    heads, project, packed, pos_ref, z_ref, facts_ref, gate_ref, q_ref, own_ref, local_ref, far_ref,
+    *refs,
 ):
     if project:
-        weight_ref, _, mixed_ref, read_ref, memory_ref, norm_ref, sig_ref, scale_ref, first_ref = refs
+        weight_ref = refs[0]
+        mixed_ref, read_ref, memory_ref, norm_ref, sig_ref, scale_ref, first_ref = refs[-7:]
     else:
         mixed_ref, read_ref, memory_ref, norm_ref, sig_ref, scale_ref = refs
     live = live_rows(facts_ref, q_ref.shape[0])
+    carries, flag = load_carries(own_ref, [far_ref], packed, True)
     for kept, i, h in by_half(heads, pos_ref):
-        carry, norm, _ = load_state(own_ref if kept else far_ref, i)
-        flag = keep_ref[i, DH + 1 : DH + 2, :]
+        carry, norm = carries[kept][i]
         norm = flag * norm
         parts = jnp.concatenate(split(flag * carry), axis=1)
         memory_ref[h] = parts
@@ -303,6 +330,7 @@
         grad_ref[...] = total.astype(BF16)
     else:
         grad_ref, keep_ref, give_ref, numer_ref, denom_ref = refs
+    mine, given = [], []
     for kept, i, h in by_half(heads, pos_ref):
         sig = sig_ref[:, cut(h)]
         numer_grad = (grad_ref[:, cut(h)].astype(F32) * scale_ref[h]).astype(BF16)
@@ -313,13 +341,13 @@
         norm = jnp.sum(sig.astype(F32) * denom_grad, axis=0, keepdims=True)
         numer_ref[:, cut(h)] = numer_grad
         denom_ref[h] = denom_grad
-        flag = opened(facts_ref)
-        if packed and not kept:
-            store_sent(give_ref, i, memory, norm, flag, False)
-        else:
-            out_ref = keep_ref if kept else give_ref
-            out_ref[i, 0:DH, :] = memory
-            out_ref[i, DH:ROWS, :] = tail(ROWS - DH, norm, flag)
+        (mine if kept else given).append((memory, norm))
+    flag = jnp.broadcast_to(opened(facts_ref), (1, DH))
+    store_states(keep_ref, mine, flag)
+    if packed:
+        pack(give_ref, given, flag, False)
+    else:
+        store_states(give_ref, given, flag)
 
 
 def grads_kernel(heads, facts_ref, gate_ref, q_ref, k_ref, v_ref, probs_ref, grad_ref, numer_ref,
@@ -347,15 +375,14 @@
         query_ref[:, here] = total.astype(BF16)
 
 
-def last_kernel(heads, packed, pos_ref, facts_ref, k_ref, v_ref, own_ref, far_ref, key_ref, value_ref,
-                *refs):
-    key_out, value_out = refs[-2:]
+def last_kernel(
+    heads, packed, pos_ref, facts_ref, k_ref, v_ref, own_ref, key_ref, value_ref, *refs
+):
+    far_refs, (key_out, value_out) = refs[:-2], refs[-2:]
     live = live_rows(facts_ref, k_ref.shape[0])
+    carries, _ = load_carries(own_ref, far_refs, packed, False)
     for kept, i, h in by_half(heads, pos_ref):
-        if kept or not packed:
-            memory, norm, _ = load_state(own_ref if kept else far_ref, i)
-        else:
-            memory, norm, _ = load_sent(far_ref, i, False)
+        memory, norm = carries[kept][i]
         top, low = split(memory)
         k, v = k_ref[:, cut(h)].astype(F32), v_ref[:, cut(h)]
         sig = (feature(k) * live).astype(BF16)
@@ -390,32 +417,33 @@
     if count != 8:
         before_pair()
         before_join(keep)
-        carry = weighted(jnp.concatenate([keep, give]), forward)
-        return carry[:half], carry[half:]
+        carry = weighted(jnp.concatenate([keep, *give]), forward)
+        return carry[:half], [carry[half:]]
     pairs = [(s, s ^ 1) for s in range(count)]
-    other = lax.ppermute(give, "seq", pairs)
+    others = [lax.ppermute(part, "seq", pairs) for part in give]
+    sent_shape = jax.ShapeDtypeStruct((half * DH + TAIL, DH), BF16)
     after = before_pair()
     sent = call(
-        functools.partial(pair_kernel, heads, forward),
-        [jax.ShapeDtypeStruct((half, SENT, DH), BF16)],
-        [SMEM, VMEM, VMEM] + [ANY] * len(after),
-        [pos, keep, other, *after],
+        functools.partial(pair_kernel, heads, forward, len(give)),
+        [sent_shape],
+        [SMEM, VMEM] + [VMEM] * len(give) + [ANY] * len(after),
+        [pos, keep, *others, *after],
         0.01, "pair",
     )[0]
     arrived = [
         lax.ppermute(sent, "seq", [(s, s ^ way) for s in range(count)]) for way in (6, 2, 4)
     ]
     after = before_join(sent)
-    own, passed = call(
-        functools.partial(join_kernel, heads, forward),
-        [jax.ShapeDtypeStruct((half, ROWS, DH), F32),
-         jax.ShapeDtypeStruct((half, ROWS, DH), F32) if forward
-         else jax.ShapeDtypeStruct((half, SENT, DH), BF16)],
-        [SMEM] + [VMEM] * 5 + [ANY] * len(after),
-        [pos, arrived[1], arrived[2], arrived[0], keep, other, *after],
-        0.3, "join",
+    parts = 1 if forward else 2
+    part = jax.ShapeDtypeStruct((half // parts * DH + TAIL, DH), BF16)
+    own, *passed = call(
+        functools.partial(join_kernel, heads, forward, len(give), parts),
+        [jax.ShapeDtypeStruct((half, ROWS, DH), F32)] + [part] * parts,
+        [SMEM] + [VMEM] * 4 + [VMEM] * len(give) + [ANY] * len(after),
+        [pos, arrived[1], arrived[2], arrived[0], keep, *others, *after],
+        0.01, "join",
     )
-    return own, lax.ppermute(passed, "seq", pairs)
+    return own, [lax.ppermute(part, "seq", pairs) for part in passed]
 
 
 def shards(queries, keys, values, gate, out_weight, out_grad, facts):
@@ -435,16 +463,22 @@
     part_low = jax.ShapeDtypeStruct((length, cols), BF16)
     part_full = jax.ShapeDtypeStruct((length, cols), F32)
     states = jax.ShapeDtypeStruct((heads // 2, ROWS, DH), F32)
-    packed = jax.ShapeDtypeStruct((heads // 2, SENT, DH), BF16)
+
+    def packed(count):
+        return jax.ShapeDtypeStruct((count * DH + TAIL, DH), BF16)
+
     column = jax.ShapeDtypeStruct((heads, length, 1), F32)
 
     def swap(array, way):
         return lax.ppermute(array, "head", [(s, s ^ way) for s in range(groups)])
 
     first = call(token_kernel, [jax.ShapeDtypeStruct((8, DH), F32)], [VMEM], [facts], 10, "warm")
-    keep, give = call(
-        functools.partial(state_kernel, heads), [states] * 2, [SMEM] * 2 + [VMEM] * 3 + [ANY],
-        [pos, z, facts, keys, values, *first], 0.4, "state",
+    shares = 2 if paired else 1
+    keep, *give = call(
+        functools.partial(state_kernel, heads, paired),
+        [states] + ([packed(heads // 2 // shares)] * shares if paired else [states]),
+        [SMEM] * 2 + [VMEM] * 3 + [ANY],
+        [pos, z, facts, keys, values, *first], 3, "state",
     )
     if direct:
         grad_3 = swap(out_grad, 3)
@@ -456,33 +490,29 @@
             functools.partial(local_kernel, heads),
             [jax.ShapeDtypeStruct((heads, length, length), BF16), flat],
             [VMEM] * 4 + [ANY],
-            [facts, queries, keys, values, sent], 0.1, "local",
+            [facts, queries, keys, values, sent], 0.01, "local",
         )
         if not direct:
             return [kept["local"][1]]
         kept["total"] = call(
             functools.partial(more_kernel, (0,)), [flat], [SMEM] + [VMEM] * 2 + [ANY],
-            [z, out_grad, out_weight, kept["local"][1]], 0.8, "unproject_own",
+            [z, out_grad, out_weight, kept["local"][1]], 0.01, "unproject_own",
         )[0]
-        return [kept["total"]]
+        passed = call(
+            pass_kernel, [part_low], [VMEM, ANY], [grad_3, kept["total"]], 0.01, "pass_on"
+        )
+        kept["grad_2"] = swap(passed[0], 1)
+        return [*passed, grad_1]
 
     own, far = scan_states(keep, give, pos, heads, True, lambda: [], beside_forward)
     probs, local = kept["local"]
     orders = []
-    if direct:
-        orders = call(
-            token_kernel, [jax.ShapeDtypeStruct((8, DH), F32)], [ANY] * 2, [grad_1, own],
-            3, "arrived",
-        )
-        grad_2 = swap(
-            call(pass_kernel, [part_low], [VMEM, ANY], [grad_3, own], 0.1, "pass_on")[0], 1
-        )
     outs = call(
-        functools.partial(read_kernel, heads, direct),
+        functools.partial(read_kernel, heads, direct, paired),
         [low, flat, jax.ShapeDtypeStruct((heads, DH, 2 * DH), BF16),
          jax.ShapeDtypeStruct((heads, 8, DH), F32), low, column] + [part_low] * direct,
-        [SMEM, SMEM, VMEM, SMEM] + [VMEM] * 5 + [VMEM, ANY] * direct,
-        [pos, z, facts, gate, queries, keep, own, far, local] + [out_weight, *orders] * direct,
+        [SMEM, SMEM, VMEM, SMEM] + [VMEM] * (4 + direct) + [ANY] * len(orders),
+        [pos, z, facts, gate, queries, own, local, *far] + [out_weight] * direct + orders,
         0.01, "read",
     )
     mixed, read, memory, norm, sig, scale = outs[:6]
@@ -492,29 +522,32 @@
             functools.partial(more_kernel, (1, 3)), [flat], [SMEM] + [VMEM] * 4 + [ANY],
             [z, grad_1, grad_3, out_weight, kept["total"], mixed], 0.01, "unproject_more",
         )[0]
-        near, mine = call(
-            rest_kernel, [part_low, part_full], [SMEM, VMEM, VMEM, ANY],
-            [z, mixed, out_weight, total], 0.01, "project_rest",
-        )
-        kept["from_1"] = swap(near, 1)
-        grads_in = [grad_2, total, out_weight]
-        orders = [near]
+        grads_in = [kept["grad_2"], total, out_weight]
     else:
         part = dot(mixed, out_weight, NN)
         output = lax.psum_scatter(part, "head", scatter_dimension=1, tiled=True).astype(BF16)
         whole = lax.all_gather(out_grad, "head", axis=1, tiled=True)
         grads_in = [dot(whole, out_weight, NT).astype(BF16)]
-        orders = []
     outs = call(
         functools.partial(spread_kernel, heads, (2,) * direct, paired),
-        [states, packed if paired else states, low,
+        [states, packed(heads // 2) if paired else states, low,
          column] + [low] * direct,
-        [SMEM, SMEM] + [VMEM] * (4 + len(grads_in)) + [ANY] * len(orders),
-        [pos, z, facts, sig, scale, read, *grads_in, *orders],
+        [SMEM, SMEM] + [VMEM] * (4 + len(grads_in)),
+        [pos, z, facts, sig, scale, read, *grads_in],
         0.01, "spread",
     )
     keep, give, numer_grad, denom_grad = outs[:4]
     mixed_grad = outs[4] if direct else grads_in[0]
+
+    def project_rest():
+        if not direct:
+            return []
+        near, kept["mine"] = call(
+            rest_kernel, [part_low, part_full], [SMEM, VMEM, VMEM, ANY],
+            [z, mixed, out_weight, numer_grad], 0.01, "project_rest",
+        )
+        kept["from_1"] = swap(near, 1)
+        return [near]
 
     def beside_back(sent):
         after = [sent]
@@ -532,25 +565,19 @@
              norm, *after],
             0.01, "grads",
         )
-        if not direct:
-            return [kept["grads"][1]]
-        return call(
-            token_kernel, [jax.ShapeDtypeStruct((8, DH), F32)], [ANY] * 2,
-            [kept["from_1"], kept["grads"][1]], 1.5, "settled",
-        )
-
-    own, far = scan_states(keep, give, pos, heads, False, lambda: [], beside_back)
+        return [kept["grads"][1]]
+
+    own, far = scan_states(keep, [give], pos, heads, False, project_rest, beside_back)
     query_grad, key_part, value_part = kept["grads"]
-    if direct:
-        output = mine + kept["from_1"].astype(F32) + kept["from_3"].astype(F32)
-        output = output.astype(BF16)
     key_grad, value_grad = call(
         functools.partial(last_kernel, heads, paired),
         [low, low],
-        [SMEM] + [VMEM] * 7,
-        [pos, facts, keys, values, own, far, key_part, value_part],
-        0.01, "last",
+        [SMEM] + [VMEM] * (6 + len(far)),
+        [pos, facts, keys, values, own, key_part, value_part, *far], 0.01, "last",
     )
+    if direct:
+        output = kept["mine"] + kept["from_1"].astype(F32) + kept["from_3"].astype(F32)
+        output = output.astype(BF16)
     return (output, query_grad, key_grad, value_grad)
 
 

time: 48.5 us -> 46.5 us (0.959)
  the two profiles are of different devices: /device:TPU:10 before, /device:TPU:0 now
where the time goes in v6:
time: 46.5 us; the launch traced here: 46.3 us
  starting transfers between devices  18.8 us (40%)
  Pallas kernels  15.8 us (34%)
  waiting for transfers between devices  7.57 us (16%)
  between operations  2.15 us (5%)
  local copies, waits for them, and re-layouts  1.25 us (3%)
  other arithmetic  0.81 us (2%)
    pallas_call x16, Pallas kernels, call(): pl.pallas_call(kernel, out_shape=outs, in_specs=in_specs, out_specs=[VMEM...  15.8 us
    ppermute x6, starting transfers between devices, swap(): return lax.ppermute(array, 'head', [(s, s ^ way) for s in range(groups)])  10.4 us
    ppermute x6, starting transfers between devices, scan_states(): lax.ppermute(sent, 'seq', [(s, s ^ way) for s in range(count)])  7.04 us
    ppermute x6, waiting for transfers between devices, swap(): return lax.ppermute(array, 'head', [(s, s ^ way) for s in range(groups)])  2.5 us
    ppermute x3, waiting for transfers between devices, scan_states(): return (own, [lax.ppermute(part, 'seq', pairs) for part in passed])  2.25 us
    ppermute x6, waiting for transfers between devices, scan_states(): lax.ppermute(sent, 'seq', [(s, s ^ way) for s in range(count)])  1.54 us
    ppermute x3, waiting for transfers between devices, scan_states(): others = [lax.ppermute(part, 'seq', pairs) for part in give]  1.29 us
    unnamed x14, local copies, waits for them, and re-layouts  1.18 us
  transfers between devices with their start and end apart: 18, of which 11 were waited for; matrix products, arithmetic and copies ran while one was open for 0% of the time, Pallas kernels for 34%

profile of v6, /device:TPU:0, one launch (start us, length us, event | category | flops | bytes accessed | tf_op | source)
XLA Modules:
  0.0 46.3 jit_solution(16009250843974312859)
XLA Ops:
  0.6 5.1 %collective-permute-start.5 = (bf16[128,1024]{1,0:T(8,128)(2,1)}, bf16[128,1024]{1,0:T(8,128)(2,1)S(1)}, u32[]{:S(2)}, u32[]{:S(2)}) collective-permute-start(bf16[128,1024]{1,0:T(8,128)(2,1)} %refs_0_.2), channel_id=1, source_target_pairs={{0,3},{1,2},{2,1},{3,0},{4,7},{5,6},{6,5},{7,4},{8,11},{9,10},{10,... | collective-permute-start | bytes 786440 | tf_op jit(solution)/shard_map/ppermute | solution.py:473
  7.2 1.1 %copy-done.1 = bf16[128,1024]{1,0:T(8,128)(2,1)S(1)} copy-done((bf16[128,1024]{1,0:T(8,128)(2,1)S(1)}, bf16[128,1024]{1,0:T(8,128)(2,1)}, u32[]{:S(2)}) %copy-start.1) | copy-done | bytes 262168
  8.3 0.6 %state.1 = (f32[4,136,128]{2,1,0:T(8,128)S(1)}, bf16[272,128]{1,0:T(8,128)(2,1)S(1)}, bf16[272,128]{1,0:T(8,128)(2,1)S(1)}) custom-call(s32[1]{0:T(128)} %bitcast.1.pos_ref, s32[1]{0:T(128)} %bitcast.z_ref, f32[8,128]{1,0:T(8,128)S(1)} %broadcast.10.refs_0_.facts_ref, bf16[128,1024]{1,0:T(8,128)(2,1)S(1)} %copy-done.1, bf16[128,1024]{1,0:T(8,128)(2,1)S(1)} %copy-done.2, ...), custom_call_target="tpu_custom_call" | custom-call | flops 3449999872 | bytes 1024 | tf_op jit(solution)/shard_map/state/pallas_call | solution.py:24
  9.0 0.5 %collective-permute-start.1 = (bf16[272,128]{1,0:T(8,128)(2,1)S(1)}, bf16[272,128]{1,0:T(8,128)(2,1)S(1)}, u32[]{:S(2)}, u32[]{:S(2)}) collective-permute-start(bf16[272,128]{1,0:T(8,128)(2,1)S(1)} %get-tuple-element.35), channel_id=1, source_target_pairs={{0,4},{4,0},{8,12},{12,8},{16,20},{20,16},{24,28},{28,24},{1,5},{5... | collective-permute-start | bytes 208904 | tf_op jit(solution)/shard_map/ppermute | solution.py:423
  9.5 0.7 %collective-permute-done.refs_0_ = bf16[272,128]{1,0:T(8,128)(2,1)S(1)} collective-permute-done((bf16[272,128]{1,0:T(8,128)(2,1)S(1)}, bf16[272,128]{1,0:T(8,128)(2,1)S(1)}, u32[]{:S(2)}, u32[]{:S(2)}) %collective-permute-start) | collective-permute-done | bytes 69664 | tf_op jit(solution)/shard_map/ppermute | solution.py:423
  10.4 0.4 pair.2.after_ref
  10.8 2.5 %collective-permute-start.4 = (bf16[528,128]{1,0:T(8,128)(2,1)S(1)}, bf16[528,128]{1,0:T(8,128)(2,1)S(1)}, u32[]{:S(2)}, u32[]{:S(2)}) collective-permute-start(bf16[528,128]{1,0:T(8,128)(2,1)S(1)} %pair.2.after_ref), channel_id=1, source_target_pairs={{0,24},{4,28},{8,16},{12,20},{16,8},{20,12},{24,0},{28,4},{1,25},{... | collective-permute-start | bytes 405512 | tf_op jit(solution)/shard_map/ppermute | solution.py:434
  13.3 0.5 %collective-permute-start.3 = (bf16[528,128]{1,0:T(8,128)(2,1)S(1)}, bf16[528,128]{1,0:T(8,128)(2,1)S(1)}, u32[]{:S(2)}, u32[]{:S(2)}) collective-permute-start(bf16[528,128]{1,0:T(8,128)(2,1)S(1)} %pair.2.after_ref), channel_id=1, source_target_pairs={{0,16},{4,20},{8,24},{12,28},{16,0},{20,4},{24,8},{28,12},{1,17},{... | collective-permute-start | bytes 405512 | tf_op jit(solution)/shard_map/ppermute | solution.py:434
  13.8 0.5 %collective-permute-start.2 = (bf16[528,128]{1,0:T(8,128)(2,1)S(1)}, bf16[528,128]{1,0:T(8,128)(2,1)S(1)}, u32[]{:S(2)}, u32[]{:S(2)}) collective-permute-start(bf16[528,128]{1,0:T(8,128)(2,1)S(1)} %pair.2.after_ref), channel_id=1, source_target_pairs={{0,8},{4,12},{8,0},{12,4},{16,24},{20,28},{24,16},{28,20},{1,9},{5... | collective-permute-start | bytes 405512 | tf_op jit(solution)/shard_map/ppermute | solution.py:434
  14.3 2.7 %local.1 = (bf16[8,128,128]{2,1,0:T(8,128)(2,1)S(1)}, f32[128,1024]{1,0:T(8,128)S(1)}) custom-call(f32[8,128]{1,0:T(8,128)S(1)} %broadcast.10.refs_0_.facts_ref, bf16[128,1024]{1,0:T(8,128)(2,1)S(1)} %copy-done, bf16[128,1024]{1,0:T(8,128)(2,1)S(1)} %copy-done.1, bf16[128,1024]{1,0:T(8,128)(2,1)S(1)} %copy-done.2, bf16[528,128]{1,0:T(8,128)(2,1)S(1)} %pair.2.after_ref), custom_call_target="tpu_custom_call" | custom-call | flops 11500000 | bytes 1024 | tf_op jit(solution)/shard_map/local/pallas_call | solution.py:24
  17.1 0.8 %unproject_own.1.after_ref.refs_3_ = f32[128,1024]{1,0:T(8,128)S(1)} custom-call(s32[1]{0:T(128)} %bitcast.z_ref, bf16[128,1024]{1,0:T(8,128)(2,1)S(1)} %copy-done.3, bf16[1024,4096]{1,0:T(8,128)(2,1)S(1)} %bitcast.7, f32[128,1024]{1,0:T(8,128)S(1)} %get-tuple-element.36.refs_2_.local_ref), custom_call_target="tpu_custom_call" | custom-call | flops 11500000 | bytes 1024 | tf_op jit(solution)/shard_map/unproject_own/pallas_call | solution.py:24
  17.9 2.1 %collective-permute-start.8 = (bf16[128,1024]{1,0:T(8,128)(2,1)S(1)}, bf16[128,1024]{1,0:T(8,128)(2,1)S(1)}, u32[]{:S(2)}, u32[]{:S(2)}) collective-permute-start(bf16[128,1024]{1,0:T(8,128)(2,1)S(1)} %pass_on.1.refs_2_), channel_id=1, source_target_pairs={{0,1},{1,0},{2,3},{3,2},{4,5},{5,4},{6,7},{7,6},{8,9},{9,8},{10,11... | collective-permute-start | bytes 786440 | tf_op jit(solution)/shard_map/ppermute | solution.py:473
  20.0 0.5 collective-permute-done.3.y_ref
  20.6 0.6 %join.2 = (f32[4,136,128]{2,1,0:T(8,128)S(1)}, bf16[528,128]{1,0:T(8,128)(2,1)S(1)}) custom-call(s32[1]{0:T(128)} %bitcast.1.pos_ref, bf16[528,128]{1,0:T(8,128)(2,1)S(1)} %collective-permute-done.2.x_ref, bf16[528,128]{1,0:T(8,128)(2,1)S(1)} %collective-permute-done.3.y_ref, bf16[528,128]{1,0:T(8,128)(2,1)S(1)} %collective-permute-done.4.d_ref, ...), custom_call_target="tpu_custom_call" | custom-call | flops 11500000 | bytes 1024 | tf_op jit(solution)/shard_map/join/pallas_call | solution.py:24
  21.2 1.3 %collective-permute-done.7.far_ref = bf16[528,128]{1,0:T(8,128)(2,1)S(1)} collective-permute-done((bf16[528,128]{1,0:T(8,128)(2,1)S(1)}, bf16[528,128]{1,0:T(8,128)(2,1)S(1)}, u32[]{:S(2)}, u32[]{:S(2)}) %collective-permute-start.7) | collective-permute-done | bytes 135200 | tf_op jit(solution)/shard_map/ppermute | solution.py:446
  22.6 1.6 %read.1 = (bf16[128,1024]{1,0:T(8,128)(2,1)S(1)}, f32[128,1024]{1,0:T(8,128)S(1)}, bf16[8,128,256]{2,1,0:T(8,128)(2,1)S(1)}, f32[8,8,128]{2,1,0:T(8,128)S(1)}, b...) custom-call(s32[1]{0:T(128)} %bitcast.1.pos_ref, s32[1]{0:T(128)} %bitcast.z_ref, ...), custom_call_target="tpu_custom_call" | custom-call | flops 11500000 | bytes 1024 | tf_op jit(solution)/shard_map/read/pallas_call | solution.py:24
  24.1 2.1 %collective-permute-start.10 = (bf16[128,1024]{1,0:T(8,128)(2,1)S(1)}, bf16[128,1024]{1,0:T(8,128)(2,1)S(1)}, u32[]{:S(2)}, u32[]{:S(2)}) collective-permute-start(bf16[128,1024]{1,0:T(8,128)(2,1)S(1)} %get-tuple-element.46), channel_id=1, source_target_pairs={{0,1},{1,0},{2,3},{3,2},{4,5},{5,4},{6,7},{7,6},{8,9},{9,8},{10,11... | collective-permute-start | bytes 786440 | tf_op jit(solution)/shard_map/ppermute | solution.py:473
  26.2 1.5 %unproject_more.1.refs_1_ = f32[128,1024]{1,0:T(8,128)S(1)} custom-call(s32[1]{0:T(128)} %bitcast.z_ref, bf16[128,1024]{1,0:T(8,128)(2,1)S(1)} %collective-permute-done.6.refs_3_.refs_0_, bf16[128,1024]{1,0:T(8,128)(2,1)S(1)} %collective-permute-done.5.block_ref.refs_1_, bf16[1024,4096]{1,0:T(8,128)(2,1)S(1)} %bitcast.7, ...), custom_call_target="tpu_custom_call" | custom-call | flops 11500000 | bytes 1024 | tf_op jit(solution)/shard_map/unproject_more/pallas_call | solution.py:24
  27.8 1.2 %spread.1 = (f32[4,136,128]{2,1,0:T(8,128)S(1)}, bf16[528,128]{1,0:T(8,128)(2,1)S(1)}, bf16[128,1024]{1,0:T(8,128)(2,1)S(1)}, f32[8,128,1]{2,1,0:T(8,128)S(1)}, bf16[128,1024]{1,0:T(8,128)(2,1)S(1)}) custom-call(s32[1]{0:T(128)} %bitcast.1.pos_ref, s32[1]{0:T(128)} %bitcast.z_ref, f32[8,128]{1,0:T(8,128)S(1)} %broadcast.10.refs_0_.facts_ref, ...), custom_call_target="tpu_custom_call" | custom-call | flops 11500000 | bytes 1024 | tf_op jit(solution)/shard_map/spread/pallas_call | solution.py:24
  29.0 0.7 %project_rest.1 = (bf16[128,1024]{1,0:T(8,128)(2,1)S(1)}, f32[128,1024]{1,0:T(8,128)S(1)}) custom-call(s32[1]{0:T(128)} %bitcast.z_ref, bf16[128,1024]{1,0:T(8,128)(2,1)S(1)} %get-tuple-element.39.refs_4_.mixed_ref, bf16[1024,4096]{1,0:T(8,128)(2,1)S(1)} %bitcast.7, bf16[128,1024]{1,0:T(8,128)(2,1)S(1)} %get-tuple-element.43.after_ref.numer_ref), custom_call_target="tpu_custom_call" | custom-call | flops 11500000 | bytes 1024 | tf_op jit(solution)/shard_map/project_rest/pallas_call | solution.py:24
  30.4 2.5 %collective-permute-done.10.more_ref = bf16[128,1024]{1,0:T(8,128)(2,1)S(1)} collective-permute-done((bf16[128,1024]{1,0:T(8,128)(2,1)S(1)}, bf16[128,1024]{1,0:T(8,128)(2,1)S(1)}, u32[]{:S(2)}, u32[]{:S(2)}) %collective-permute-start.10) | collective-permute-done | bytes 262176 | tf_op jit(solution)/shard_map/ppermute | solution.py:473
  32.9 0.5 project_add.1.refs_0_
  33.4 0.9 %collective-permute-start.12 = (bf16[128,1024]{1,0:T(8,128)(2,1)S(1)}, bf16[128,1024]{1,0:T(8,128)(2,1)S(1)}, u32[]{:S(2)}, u32[]{:S(2)}) collective-permute-start(bf16[128,1024]{1,0:T(8,128)(2,1)S(1)} %project_add.1.refs_0_), channel_id=1, source_target_pairs={{0,3},{1,2},{2,1},{3,0},{4,7},{5,6},{6,5},{7,4},{8,11},{9,10},{10,... | collective-permute-start | bytes 786440 | tf_op jit(solution)/shard_map/ppermute | solution.py:473
  34.3 1.8 %collective-permute-start.15 = (bf16[528,128]{1,0:T(8,128)(2,1)S(1)}, bf16[528,128]{1,0:T(8,128)(2,1)S(1)}, u32[]{:S(2)}, u32[]{:S(2)}) collective-permute-start(bf16[528,128]{1,0:T(8,128)(2,1)S(1)} %pair.3.after_ref), channel_id=1, source_target_pairs={{0,24},{4,28},{8,16},{12,20},{16,8},{20,12},{24,0},{28,4},{1,25},{... | collective-permute-start | bytes 405512 | tf_op jit(solution)/shard_map/ppermute | solution.py:434
  36.0 1.2 %collective-permute-start.14 = (bf16[528,128]{1,0:T(8,128)(2,1)S(1)}, bf16[528,128]{1,0:T(8,128)(2,1)S(1)}, u32[]{:S(2)}, u32[]{:S(2)}) collective-permute-start(bf16[528,128]{1,0:T(8,128)(2,1)S(1)} %pair.3.after_ref), channel_id=1, source_target_pairs={{0,16},{4,20},{8,24},{12,28},{16,0},{20,4},{24,8},{28,12},{1,17},{... | collective-permute-start | bytes 405512 | tf_op jit(solution)/shard_map/ppermute | solution.py:434
  37.2 0.6 %collective-permute-start.13 = (bf16[528,128]{1,0:T(8,128)(2,1)S(1)}, bf16[528,128]{1,0:T(8,128)(2,1)S(1)}, u32[]{:S(2)}, u32[]{:S(2)}) collective-permute-start(bf16[528,128]{1,0:T(8,128)(2,1)S(1)} %pair.3.after_ref), channel_id=1, source_target_pairs={{0,8},{4,12},{8,0},{12,4},{16,24},{20,28},{24,16},{28,20},{1,9},{5... | collective-permute-start | bytes 405512 | tf_op jit(solution)/shard_map/ppermute | solution.py:434
  37.8 3.7 %grads.1 = (bf16[128,1024]{1,0:T(8,128)(2,1)}, f32[128,1024]{1,0:T(8,128)S(1)}, f32[128,1024]{1,0:T(8,128)S(1)}) custom-call(f32[8,128]{1,0:T(8,128)S(1)} %broadcast.10.refs_0_.facts_ref, f32[8]{0:T(128)S(1)} %copy-done.4, bf16[128,1024]{1,0:T(8,128)(2,1)S(1)} %copy-done, bf16[128,1024]{1,0:T(8,128)(2,1)S(1)} %copy-done.1, bf16[128,1024]{1,0:T(8,128)(2,1)S(1)} %copy-done.2, ...), custom_call_target="tpu_custom_call" | custom-call | flops 11500000 | bytes 1024 | tf_op jit(solution)/shard_map/grads/pallas_call | solution.py:24
  41.4 0.9 %collective-permute-done.14.y_ref = bf16[528,128]{1,0:T(8,128)(2,1)S(1)} collective-permute-done((bf16[528,128]{1,0:T(8,128)(2,1)S(1)}, bf16[528,128]{1,0:T(8,128)(2,1)S(1)}, u32[]{:S(2)}, u32[]{:S(2)}) %collective-permute-start.14) | collective-permute-done | bytes 135200 | tf_op jit(solution)/shard_map/ppermute | solution.py:434
  42.7 0.5 %collective-permute-start.17 = (bf16[272,128]{1,0:T(8,128)(2,1)S(1)}, bf16[272,128]{1,0:T(8,128)(2,1)S(1)}, u32[]{:S(2)}, u32[]{:S(2)}) collective-permute-start(bf16[272,128]{1,0:T(8,128)(2,1)S(1)} %get-tuple-element.59), channel_id=1, source_target_pairs={{0,4},{4,0},{8,12},{12,8},{16,20},{20,16},{24,28},{28,24},{1,5},{5... | collective-permute-start | bytes 208904 | tf_op jit(solution)/shard_map/ppermute | solution.py:446
  43.2 0.7 %collective-permute-done.16.refs_0_ = bf16[272,128]{1,0:T(8,128)(2,1)S(1)} collective-permute-done((bf16[272,128]{1,0:T(8,128)(2,1)S(1)}, bf16[272,128]{1,0:T(8,128)(2,1)S(1)}, u32[]{:S(2)}, u32[]{:S(2)}) %collective-permute-start.16) | collective-permute-done | bytes 69664 | tf_op jit(solution)/shard_map/ppermute | solution.py:446
  44.1 1.4 %last.1 = (bf16[128,1024]{1,0:T(8,128)(2,1)}, bf16[128,1024]{1,0:T(8,128)(2,1)}) custom-call(s32[1]{0:T(128)} %bitcast.1.pos_ref, f32[8,128]{1,0:T(8,128)S(1)} %broadcast.10.refs_0_.facts_ref, bf16[128,1024]{1,0:T(8,128)(2,1)S(1)} %copy-done.1, bf16[128,1024]{1,0:T(8,128)(2,1)S(1)} %copy-done.2, f32[4,136,128]{2,1,0:T(8,128)S(1)} %get-tuple-element.56.own_ref, ...), custom_call_target="tpu_custom_call" | custom-call | flops 11500000 | bytes 1024 | tf_op jit(solution)/shard_map/last/pallas_call | solution.py:24
  45.5 0.8 %add_convert_fusion = bf16[128,1024]{1,0:T(8,128)(2,1)} fusion(bf16[128,1024]{1,0:T(8,128)(2,1)S(1)} %collective-permute-done.12, f32[128,1024]{1,0:T(8,128)S(1)} %get-tuple-element.44, bf16[128,1024]{1,0:T(8,128)(2,1)S(1)} %collective-permute-done.9), kind=kLoop, calls=%fused_computation | loop fusion | flops 655360 | bytes 1310720 | tf_op jit(solution)/shard_map/convert_element_type | solution.py:580
  (38 shorter events, 1.8 us)
Async XLA Ops:
  0.6 17.3 %collective-permute-start.5 = (bf16[128,1024]{1,0:T(8,128)(2,1)}, bf16[128,1024]{1,0:T(8,128)(2,1)S(1)}, u32[]{:S(2)}, u32[]{:S(2)}) collective-permute-start(bf16[128,1024]{1,0:T(8,128)(2,1)} %refs_0_.2), channel_id=1, source_target_pairs={{0,3},{1,2},{2,1},{3,0},{4,7},{5,6},{6,5},{7,4},{8,11},{9,10},{10,... | collective-permute-start | bytes 786440 | tf_op jit(solution)/shard_map/ppermute | solution.py:473
  5.7 14.8 %collective-permute-start.6 = (bf16[128,1024]{1,0:T(8,128)(2,1)}, bf16[128,1024]{1,0:T(8,128)(2,1)S(1)}, u32[]{:S(2)}, u32[]{:S(2)}) collective-permute-start(bf16[128,1024]{1,0:T(8,128)(2,1)} %refs_0_.2), channel_id=1, source_target_pairs={{0,1},{1,0},{2,3},{3,2},{4,5},{5,4},{6,7},{7,6},{8,9},{9,8},{10,11... | collective-permute-start | bytes 786440 | tf_op jit(solution)/shard_map/ppermute | solution.py:473
  7.1 10.0 %slice-start = ((s8[8388608]{0:T(1024)(128)(4,1)}), s8[4194304]{0:T(1024)(128)(4,1)S(1)}, s32[]{:S(2)}) async-start(s8[8388608]{0:T(1024)(128)(4,1)} %bitcast.6), calls=%async_computation | async-start | bytes 8388608
  7.1 1.1 %copy-start.1 = (bf16[128,1024]{1,0:T(8,128)(2,1)S(1)}, bf16[128,1024]{1,0:T(8,128)(2,1)}, u32[]{:S(2)}) copy-start(bf16[128,1024]{1,0:T(8,128)(2,1)} %k_ref.7) | copy-start | bytes 786436
  7.1 1.2 %copy-start.2 = (bf16[128,1024]{1,0:T(8,128)(2,1)S(1)}, bf16[128,1024]{1,0:T(8,128)(2,1)}, u32[]{:S(2)}) copy-start(bf16[128,1024]{1,0:T(8,128)(2,1)} %v_ref.7) | copy-start | bytes 786436
  7.1 9.9 %slice-start.1 = ((s8[8388608]{0:T(1024)(128)(4,1)}), s8[4194304]{0:T(1024)(128)(4,1)S(1)}, s32[]{:S(2)}) async-start(s8[8388608]{0:T(1024)(128)(4,1)} %bitcast.6), calls=%async_computation.1 | async-start | bytes 8388608
  7.1 7.2 %copy-start = (bf16[128,1024]{1,0:T(8,128)(2,1)S(1)}, bf16[128,1024]{1,0:T(8,128)(2,1)}, u32[]{:S(2)}) copy-start(bf16[128,1024]{1,0:T(8,128)(2,1)} %q_ref.5) | copy-start | bytes 786436
  7.2 9.9 %copy-start.3 = (bf16[128,1024]{1,0:T(8,128)(2,1)S(1)}, bf16[128,1024]{1,0:T(8,128)(2,1)}, u32[]{:S(2)}) copy-start(bf16[128,1024]{1,0:T(8,128)(2,1)} %refs_0_.2) | copy-start | bytes 786436
  8.9 13.7 %copy-start.4 = (f32[8]{0:T(128)S(1)}, f32[8]{0:T(128)}, u32[]{:S(2)}) copy-start(f32[8]{0:T(128)} %gate_ref.3) | copy-start | bytes 100
  8.9 1.3 %collective-permute-start = (bf16[272,128]{1,0:T(8,128)(2,1)S(1)}, bf16[272,128]{1,0:T(8,128)(2,1)S(1)}, u32[]{:S(2)}, u32[]{:S(2)}) collective-permute-start(bf16[272,128]{1,0:T(8,128)(2,1)S(1)} %get-tuple-element.34), channel_id=1, source_target_pairs={{0,4},{4,0},{8,12},{12,8},{16,20},{20,16},{24,28},{28,24},{1,5},{5... | collective-permute-start | bytes 208904 | tf_op jit(solution)/shard_map/ppermute | solution.py:423
  9.0 1.4 %collective-permute-start.1 = (bf16[272,128]{1,0:T(8,128)(2,1)S(1)}, bf16[272,128]{1,0:T(8,128)(2,1)S(1)}, u32[]{:S(2)}, u32[]{:S(2)}) collective-permute-start(bf16[272,128]{1,0:T(8,128)(2,1)S(1)} %get-tuple-element.35), channel_id=1, source_target_pairs={{0,4},{4,0},{8,12},{12,8},{16,20},{20,16},{24,28},{28,24},{1,5},{5... | collective-permute-start | bytes 208904 | tf_op jit(solution)/shard_map/ppermute | solution.py:423
  10.8 9.2 %collective-permute-start.4 = (bf16[528,128]{1,0:T(8,128)(2,1)S(1)}, bf16[528,128]{1,0:T(8,128)(2,1)S(1)}, u32[]{:S(2)}, u32[]{:S(2)}) collective-permute-start(bf16[528,128]{1,0:T(8,128)(2,1)S(1)} %pair.2.after_ref), channel_id=1, source_target_pairs={{0,24},{4,28},{8,16},{12,20},{16,8},{20,12},{24,0},{28,4},{1,25},{... | collective-permute-start | bytes 405512 | tf_op jit(solution)/shard_map/ppermute | solution.py:434
  13.3 7.2 %collective-permute-start.3 = (bf16[528,128]{1,0:T(8,128)(2,1)S(1)}, bf16[528,128]{1,0:T(8,128)(2,1)S(1)}, u32[]{:S(2)}, u32[]{:S(2)}) collective-permute-start(bf16[528,128]{1,0:T(8,128)(2,1)S(1)} %pair.2.after_ref), channel_id=1, source_target_pairs={{0,16},{4,20},{8,24},{12,28},{16,0},{20,4},{24,8},{28,12},{1,17},{... | collective-permute-start | bytes 405512 | tf_op jit(solution)/shard_map/ppermute | solution.py:434
  13.8 6.8 %collective-permute-start.2 = (bf16[528,128]{1,0:T(8,128)(2,1)S(1)}, bf16[528,128]{1,0:T(8,128)(2,1)S(1)}, u32[]{:S(2)}, u32[]{:S(2)}) collective-permute-start(bf16[528,128]{1,0:T(8,128)(2,1)S(1)} %pair.2.after_ref), channel_id=1, source_target_pairs={{0,8},{4,12},{8,0},{12,4},{16,24},{20,28},{24,16},{28,20},{1,9},{5... | collective-permute-start | bytes 405512 | tf_op jit(solution)/shard_map/ppermute | solution.py:434
  17.9 9.8 %collective-permute-start.8 = (bf16[128,1024]{1,0:T(8,128)(2,1)S(1)}, bf16[128,1024]{1,0:T(8,128)(2,1)S(1)}, u32[]{:S(2)}, u32[]{:S(2)}) collective-permute-start(bf16[128,1024]{1,0:T(8,128)(2,1)S(1)} %pass_on.1.refs_2_), channel_id=1, source_target_pairs={{0,1},{1,0},{2,3},{3,2},{4,5},{5,4},{6,7},{7,6},{8,9},{9,8},{10,11... | collective-permute-start | bytes 786440 | tf_op jit(solution)/shard_map/ppermute | solution.py:473
  21.2 1.4 %collective-permute-start.7 = (bf16[528,128]{1,0:T(8,128)(2,1)S(1)}, bf16[528,128]{1,0:T(8,128)(2,1)S(1)}, u32[]{:S(2)}, u32[]{:S(2)}) collective-permute-start(bf16[528,128]{1,0:T(8,128)(2,1)S(1)} %get-tuple-element.38), channel_id=1, source_target_pairs={{0,4},{4,0},{8,12},{12,8},{16,20},{20,16},{24,28},{28,24},{1,5},{5... | collective-permute-start | bytes 405512 | tf_op jit(solution)/shard_map/ppermute | solution.py:446
  24.1 8.8 %collective-permute-start.10 = (bf16[128,1024]{1,0:T(8,128)(2,1)S(1)}, bf16[128,1024]{1,0:T(8,128)(2,1)S(1)}, u32[]{:S(2)}, u32[]{:S(2)}) collective-permute-start(bf16[128,1024]{1,0:T(8,128)(2,1)S(1)} %get-tuple-element.46), channel_id=1, source_target_pairs={{0,1},{1,0},{2,3},{3,2},{4,5},{5,4},{6,7},{7,6},{8,9},{9,8},{10,11... | collective-permute-start | bytes 786440 | tf_op jit(solution)/shard_map/ppermute | solution.py:473
  28.9 1.4 %collective-permute-start.11 = (bf16[528,128]{1,0:T(8,128)(2,1)S(1)}, bf16[528,128]{1,0:T(8,128)(2,1)S(1)}, u32[]{:S(2)}, u32[]{:S(2)}) collective-permute-start(bf16[528,128]{1,0:T(8,128)(2,1)S(1)} %get-tuple-element.48), channel_id=1, source_target_pairs={{0,4},{4,0},{8,12},{12,8},{16,20},{20,16},{24,28},{28,24},{1,5},{5... | collective-permute-start | bytes 405512 | tf_op jit(solution)/shard_map/ppermute | solution.py:423
  29.7 15.8 %collective-permute-start.9 = (bf16[128,1024]{1,0:T(8,128)(2,1)S(1)}, bf16[128,1024]{1,0:T(8,128)(2,1)S(1)}, u32[]{:S(2)}, u32[]{:S(2)}) collective-permute-start(bf16[128,1024]{1,0:T(8,128)(2,1)S(1)} %get-tuple-element.45.refs_1_), channel_id=1, source_target_pairs={{0,1},{1,0},{2,3},{3,2},{4,5},{5,4},{6,7},{7,6},{8,9},{9,8},{10,11... | collective-permute-start | bytes 786440 | tf_op jit(solution)/shard_map/ppermute | solution.py:473
  33.4 12.1 %collective-permute-start.12 = (bf16[128,1024]{1,0:T(8,128)(2,1)S(1)}, bf16[128,1024]{1,0:T(8,128)(2,1)S(1)}, u32[]{:S(2)}, u32[]{:S(2)}) collective-permute-start(bf16[128,1024]{1,0:T(8,128)(2,1)S(1)} %project_add.1.refs_0_), channel_id=1, source_target_pairs={{0,3},{1,2},{2,1},{3,0},{4,7},{5,6},{6,5},{7,4},{8,11},{9,10},{10,... | collective-permute-start | bytes 786440 | tf_op jit(solution)/shard_map/ppermute | solution.py:473
  34.3 7.2 %collective-permute-start.15 = (bf16[528,128]{1,0:T(8,128)(2,1)S(1)}, bf16[528,128]{1,0:T(8,128)(2,1)S(1)}, u32[]{:S(2)}, u32[]{:S(2)}) collective-permute-start(bf16[528,128]{1,0:T(8,128)(2,1)S(1)} %pair.3.after_ref), channel_id=1, source_target_pairs={{0,24},{4,28},{8,16},{12,20},{16,8},{20,12},{24,0},{28,4},{1,25},{... | collective-permute-start | bytes 405512 | tf_op jit(solution)/shard_map/ppermute | solution.py:434
  36.0 6.3 %collective-permute-start.14 = (bf16[528,128]{1,0:T(8,128)(2,1)S(1)}, bf16[528,128]{1,0:T(8,128)(2,1)S(1)}, u32[]{:S(2)}, u32[]{:S(2)}) collective-permute-start(bf16[528,128]{1,0:T(8,128)(2,1)S(1)} %pair.3.after_ref), channel_id=1, source_target_pairs={{0,16},{4,20},{8,24},{12,28},{16,0},{20,4},{24,8},{28,12},{1,17},{... | collective-permute-start | bytes 405512 | tf_op jit(solution)/shard_map/ppermute | solution.py:434
  37.2 5.2 %collective-permute-start.13 = (bf16[528,128]{1,0:T(8,128)(2,1)S(1)}, bf16[528,128]{1,0:T(8,128)(2,1)S(1)}, u32[]{:S(2)}, u32[]{:S(2)}) collective-permute-start(bf16[528,128]{1,0:T(8,128)(2,1)S(1)} %pair.3.after_ref), channel_id=1, source_target_pairs={{0,8},{4,12},{8,0},{12,4},{16,24},{20,28},{24,16},{28,20},{1,9},{5... | collective-permute-start | bytes 405512 | tf_op jit(solution)/shard_map/ppermute | solution.py:434
  42.6 1.3 %collective-permute-start.16 = (bf16[272,128]{1,0:T(8,128)(2,1)S(1)}, bf16[272,128]{1,0:T(8,128)(2,1)S(1)}, u32[]{:S(2)}, u32[]{:S(2)}) collective-permute-start(bf16[272,128]{1,0:T(8,128)(2,1)S(1)} %get-tuple-element.58), channel_id=1, source_target_pairs={{0,4},{4,0},{8,12},{12,8},{16,20},{20,16},{24,28},{28,24},{1,5},{5... | collective-permute-start | bytes 208904 | tf_op jit(solution)/shard_map/ppermute | solution.py:446
  42.7 1.4 %collective-permute-start.17 = (bf16[272,128]{1,0:T(8,128)(2,1)S(1)}, bf16[272,128]{1,0:T(8,128)(2,1)S(1)}, u32[]{:S(2)}, u32[]{:S(2)}) collective-permute-start(bf16[272,128]{1,0:T(8,128)(2,1)S(1)} %get-tuple-element.59), channel_id=1, source_target_pairs={{0,4},{4,0},{8,12},{12,8},{16,20},{20,16},{24,28},{28,24},{1,5},{5... | collective-permute-start | bytes 208904 | tf_op jit(solution)/shard_map/ppermute | solution.py:446

commit v7 on v6

--- a/solution.py
+++ b/solution.py
@@ -264,23 +264,30 @@
         mixed_ref, read_ref, memory_ref, norm_ref, sig_ref, scale_ref = refs
     live = live_rows(facts_ref, q_ref.shape[0])
     carries, flag = load_carries(own_ref, [far_ref], packed, True)
-    for kept, i, h in by_half(heads, pos_ref):
-        carry, norm = carries[kept][i]
-        norm = flag * norm
-        parts = jnp.concatenate(split(flag * carry), axis=1)
-        memory_ref[h] = parts
-        norm_ref[h] = jnp.broadcast_to(norm, (8, DH))
-        sig = feature(q_ref[:, cut(h)].astype(F32)).astype(BF16)
-        numer = dot(sig, parts, NN)
-        numer = numer[:, 0:DH] + numer[:, DH:]
-        denom = jnp.sum(sig.astype(F32) * norm, axis=1, keepdims=True) + 1.0
-        read = numer / denom
-        gate = gate_row(gate_ref, h)
-        mixed = live * (gate * read + (1.0 - gate) * local_ref[:, cut(h)])
-        sig_ref[:, cut(h)] = sig
-        scale_ref[h] = live * gate[:, 0:1] / denom
-        read_ref[:, cut(h)] = read
-        mixed_ref[:, cut(h)] = mixed.astype(BF16)
+    order = list(by_half(heads, pos_ref))
+    for at in range(0, heads, 4):
+        some = order[at : at + 4]
+        states = [scaled(flag, carries[kept][i]) for kept, i, _ in some]
+        sigs = [feature(q_ref[:, cut(h)].astype(F32)).astype(BF16) for _, _, h in some]
+        parts = [jnp.concatenate(split(memory), axis=1) for memory, _ in states]
+        numers = [dot(sig, part, NN) for sig, part in zip(sigs, parts)]
+        denoms = [
+            jnp.sum(sig.astype(F32) * norm, axis=1, keepdims=True) + 1.0
+            for sig, (_, norm) in zip(sigs, states)
+        ]
+        inverses = [1.0 / denom for denom in denoms]
+        reads = [(n[:, 0:DH] + n[:, DH:]) * d for n, d in zip(numers, inverses)]
+        for (_, _, h), state, sig, part, inverse, read in zip(
+            some, states, sigs, parts, inverses, reads
+        ):
+            gate = gate_row(gate_ref, h)
+            mixed = live * (gate * read + (1.0 - gate) * local_ref[:, cut(h)])
+            mixed_ref[:, cut(h)] = mixed.astype(BF16)
+            read_ref[:, cut(h)] = read
+            memory_ref[h] = part
+            norm_ref[h] = jnp.broadcast_to(state[1], (8, DH))
+            sig_ref[:, cut(h)] = sig
+            scale_ref[h] = live * gate[:, 0:1] * inverse
     if project:
         block = weight_ref[:, columns(z_ref, 2, first_ref.shape[1])]
         first_ref[...] = dot(mixed_ref[...], block, NN).astype(BF16)
@@ -376,9 +383,9 @@
 
 
 def last_kernel(
-    heads, packed, pos_ref, facts_ref, k_ref, v_ref, own_ref, key_ref, value_ref, *refs
+    heads, packed, far, pos_ref, facts_ref, k_ref, v_ref, own_ref, key_ref, value_ref, *refs
 ):
-    far_refs, (key_out, value_out) = refs[:-2], refs[-2:]
+    far_refs, (key_out, value_out) = refs[:far], refs[-2:]
     live = live_rows(facts_ref, k_ref.shape[0])
     carries, _ = load_carries(own_ref, far_refs, packed, False)
     for kept, i, h in by_half(heads, pos_ref):
@@ -472,8 +479,8 @@
     def swap(array, way):
         return lax.ppermute(array, "head", [(s, s ^ way) for s in range(groups)])
 
-    first = call(token_kernel, [jax.ShapeDtypeStruct((8, DH), F32)], [VMEM], [facts], 10, "warm")
-    shares = 2 if paired else 1
+    first = call(token_kernel, [jax.ShapeDtypeStruct((8, DH), F32)], [SMEM], [pos], 10, "warm")
+    shares = 1 if paired else 1
     keep, *give = call(
         functools.partial(state_kernel, heads, paired),
         [states] + ([packed(heads // 2 // shares)] * shares if paired else [states]),
@@ -494,25 +501,30 @@
         )
         if not direct:
             return [kept["local"][1]]
+        passed = call(
+            pass_kernel, [part_low], [VMEM, ANY], [grad_3, kept["local"][1]], 0.01, "pass_on"
+        )
+        kept["grad_2"] = swap(passed[0], 1)
         kept["total"] = call(
             functools.partial(more_kernel, (0,)), [flat], [SMEM] + [VMEM] * 2 + [ANY],
-            [z, out_grad, out_weight, kept["local"][1]], 0.01, "unproject_own",
+            [z, out_grad, out_weight, passed[0]], 0.8, "unproject_own",
         )[0]
-        passed = call(
-            pass_kernel, [part_low], [VMEM, ANY], [grad_3, kept["total"]], 0.01, "pass_on"
-        )
-        kept["grad_2"] = swap(passed[0], 1)
-        return [*passed, grad_1]
+        return [kept["total"]]
 
     own, far = scan_states(keep, give, pos, heads, True, lambda: [], beside_forward)
     probs, local = kept["local"]
     orders = []
+    if direct:
+        orders = call(
+            token_kernel, [jax.ShapeDtypeStruct((8, DH), F32)], [ANY] * 2, [grad_1, own],
+            0.5, "arrived",
+        )
     outs = call(
         functools.partial(read_kernel, heads, direct, paired),
         [low, flat, jax.ShapeDtypeStruct((heads, DH, 2 * DH), BF16),
          jax.ShapeDtypeStruct((heads, 8, DH), F32), low, column] + [part_low] * direct,
         [SMEM, SMEM, VMEM, SMEM] + [VMEM] * (4 + direct) + [ANY] * len(orders),
-        [pos, z, facts, gate, queries, own, local, *far] + [out_weight] * direct + orders,
+        [pos, z, facts, gate, queries, own, local, *far] + [out_weight] * direct + [*orders],
         0.01, "read",
     )
     mixed, read, memory, norm, sig, scale = outs[:6]
@@ -569,13 +581,15 @@
 
     own, far = scan_states(keep, [give], pos, heads, False, project_rest, beside_back)
     query_grad, key_part, value_part = kept["grads"]
+    orders = [kept["from_1"]] if direct else []
     key_grad, value_grad = call(
-        functools.partial(last_kernel, heads, paired),
+        functools.partial(last_kernel, heads, paired, len(far)),
         [low, low],
-        [SMEM] + [VMEM] * (6 + len(far)),
-        [pos, facts, keys, values, own, key_part, value_part, *far], 0.01, "last",
+        [SMEM] + [VMEM] * (6 + len(far)) + [ANY] * len(orders),
+        [pos, facts, keys, values, own, key_part, value_part, *far, *orders], 1, "last",
     )
     if direct:
+        kept["mine"], key_grad = lax.optimization_barrier((kept["mine"], key_grad))
         output = kept["mine"] + kept["from_1"].astype(F32) + kept["from_3"].astype(F32)
         output = output.astype(BF16)
     return (output, query_grad, key_grad, value_grad)

time: 46.5 us -> 45.7 us (0.983)
  starting transfers between devices: 18.8 us -> 17.2 us
  waiting for transfers between devices: 7.57 us -> 8.58 us
    ppermute x6, starting transfers between devices: 10.4 us -> 9.31 us  [swap(): return lax.ppermute(array, 'head', [(s, s ^ way) for s in range(groups)])]
    ppermute x6, waiting for transfers between devices: 2.5 us -> 3.62 us  [swap(): return lax.ppermute(array, 'head', [(s, s ^ way) for s in range(groups)])]
    ppermute x3, waiting for transfers between devices: 2.25 us -> 1.32 us  [scan_states(): return (own, [lax.ppermute(part, 'seq', pairs) for part in passed])]
    ppermute x6, waiting for transfers between devices: 1.54 us -> 2.38 us  [scan_states(): lax.ppermute(sent, 'seq', [(s, s ^ way) for s in range(count)])]
    ppermute x3 -> x2, starting transfers between devices: 0.64 us -> 0.14 us  [scan_states(): others = [lax.ppermute(part, 'seq', pairs) for part in give]]
    ppermute x3 -> x2, waiting for transfers between devices: 1.29 us -> 1.25 us  [scan_states(): others = [lax.ppermute(part, 'seq', pairs) for part in give]]
    pallas_call x16 -> x17, Pallas kernels: 15.8 us -> 15.8 us  [call(): pl.pallas_call(kernel, out_shape=outs, in_specs=in_specs, out_specs=[VMEM...]
  transfers between devices with their start and end apart: 18 -> 17, of which waited for: 11 -> 6; matrix products, arithmetic and copies ran while one was open for 0% -> 0% of each run, Pallas kernels for 34% -> 35%
where the time goes in v7:
time: 45.7 us; the launch traced here: 45.5 us
  starting transfers between devices  17.2 us (38%)
  Pallas kernels  15.8 us (35%)
  waiting for transfers between devices  8.58 us (19%)
  between operations  2.17 us (5%)
  local copies, waits for them, and re-layouts  0.98 us (2%)
  other arithmetic  0.82 us (2%)
    pallas_call x17, Pallas kernels, call(): pl.pallas_call(kernel, out_shape=outs, in_specs=in_specs, out_specs=[VMEM...  15.8 us
    ppermute x6, starting transfers between devices, swap(): return lax.ppermute(array, 'head', [(s, s ^ way) for s in range(groups)])  9.31 us
    ppermute x6, starting transfers between devices, scan_states(): lax.ppermute(sent, 'seq', [(s, s ^ way) for s in range(count)])  7.11 us
    ppermute x6, waiting for transfers between devices, swap(): return lax.ppermute(array, 'head', [(s, s ^ way) for s in range(groups)])  3.62 us
    ppermute x6, waiting for transfers between devices, scan_states(): lax.ppermute(sent, 'seq', [(s, s ^ way) for s in range(count)])  2.38 us
    ppermute x3, waiting for transfers between devices, scan_states(): return (own, [lax.ppermute(part, 'seq', pairs) for part in passed])  1.32 us
    ppermute x2, waiting for transfers between devices, scan_states(): others = [lax.ppermute(part, 'seq', pairs) for part in give]  1.25 us
    unnamed x14, local copies, waits for them, and re-layouts  0.91 us
  transfers between devices with their start and end apart: 17, of which 6 were waited for; matrix products, arithmetic and copies ran while one was open for 0% of the time, Pallas kernels for 35%

profile of v7, /device:TPU:0, one launch (start us, length us, event | category | flops | bytes accessed | tf_op | source)
XLA Modules:
  0.0 45.5 jit_solution(7841842404399555044)
XLA Ops:
  0.6 5.1 %collective-permute-start.4 = (bf16[128,1024]{1,0:T(8,128)(2,1)}, bf16[128,1024]{1,0:T(8,128)(2,1)S(1)}, u32[]{:S(2)}, u32[]{:S(2)}) collective-permute-start(bf16[128,1024]{1,0:T(8,128)(2,1)} %refs_0_.2), channel_id=1, source_target_pairs={{0,3},{1,2},{2,1},{3,0},{4,7},{5,6},{6,5},{7,4},{8,11},{9,10},{10,... | collective-permute-start | bytes 786440 | tf_op jit(solution)/shard_map/ppermute | solution.py:480
  7.2 0.8 %copy-done.1 = bf16[128,1024]{1,0:T(8,128)(2,1)S(1)} copy-done((bf16[128,1024]{1,0:T(8,128)(2,1)S(1)}, bf16[128,1024]{1,0:T(8,128)(2,1)}, u32[]{:S(2)}) %copy-start.1) | copy-done | bytes 262168
  8.1 0.5 %state.1 = (f32[4,136,128]{2,1,0:T(8,128)S(1)}, bf16[528,128]{1,0:T(8,128)(2,1)S(1)}) custom-call(s32[1]{0:T(128)} %bitcast.1.refs_0_.pos_ref, s32[1]{0:T(128)} %bitcast.z_ref, f32[8,128]{1,0:T(8,128)S(1)} %broadcast.10.facts_ref, bf16[128,1024]{1,0:T(8,128)(2,1)S(1)} %copy-done.1, bf16[128,1024]{1,0:T(8,128)(2,1)S(1)} %copy-done.2, f32[8,128]{1,0:T(8,128)S(1)} %warm.1.after_ref), custom_call_target="tpu_custom_call" | custom-call | flops 3449999872 | bytes 1024 | tf_op jit(solution)/shard_map/state/pallas_call | solution.py:24
  8.8 1.3 %collective-permute-done.refs_0_ = bf16[528,128]{1,0:T(8,128)(2,1)S(1)} collective-permute-done((bf16[528,128]{1,0:T(8,128)(2,1)S(1)}, bf16[528,128]{1,0:T(8,128)(2,1)S(1)}, u32[]{:S(2)}, u32[]{:S(2)}) %collective-permute-start) | collective-permute-done | bytes 135200 | tf_op jit(solution)/shard_map/ppermute | solution.py:430
  10.1 0.4 pair.2.after_ref
  10.5 2.5 %collective-permute-start.3 = (bf16[528,128]{1,0:T(8,128)(2,1)S(1)}, bf16[528,128]{1,0:T(8,128)(2,1)S(1)}, u32[]{:S(2)}, u32[]{:S(2)}) collective-permute-start(bf16[528,128]{1,0:T(8,128)(2,1)S(1)} %pair.2.after_ref), channel_id=1, source_target_pairs={{0,24},{4,28},{8,16},{12,20},{16,8},{20,12},{24,0},{28,4},{1,25},{... | collective-permute-start | bytes 405512 | tf_op jit(solution)/shard_map/ppermute | solution.py:441
  13.0 0.5 %collective-permute-start.2 = (bf16[528,128]{1,0:T(8,128)(2,1)S(1)}, bf16[528,128]{1,0:T(8,128)(2,1)S(1)}, u32[]{:S(2)}, u32[]{:S(2)}) collective-permute-start(bf16[528,128]{1,0:T(8,128)(2,1)S(1)} %pair.2.after_ref), channel_id=1, source_target_pairs={{0,16},{4,20},{8,24},{12,28},{16,0},{20,4},{24,8},{28,12},{1,17},{... | collective-permute-start | bytes 405512 | tf_op jit(solution)/shard_map/ppermute | solution.py:441
  13.5 0.5 %collective-permute-start.1 = (bf16[528,128]{1,0:T(8,128)(2,1)S(1)}, bf16[528,128]{1,0:T(8,128)(2,1)S(1)}, u32[]{:S(2)}, u32[]{:S(2)}) collective-permute-start(bf16[528,128]{1,0:T(8,128)(2,1)S(1)} %pair.2.after_ref), channel_id=1, source_target_pairs={{0,8},{4,12},{8,0},{12,4},{16,24},{20,28},{24,16},{28,20},{1,9},{5... | collective-permute-start | bytes 405512 | tf_op jit(solution)/shard_map/ppermute | solution.py:441
  14.0 2.7 %local.1 = (bf16[8,128,128]{2,1,0:T(8,128)(2,1)S(1)}, f32[128,1024]{1,0:T(8,128)S(1)}) custom-call(f32[8,128]{1,0:T(8,128)S(1)} %broadcast.10.facts_ref, bf16[128,1024]{1,0:T(8,128)(2,1)S(1)} %copy-done, bf16[128,1024]{1,0:T(8,128)(2,1)S(1)} %copy-done.1, bf16[128,1024]{1,0:T(8,128)(2,1)S(1)} %copy-done.2, bf16[528,128]{1,0:T(8,128)(2,1)S(1)} %pair.2.after_ref), custom_call_target="tpu_custom_call" | custom-call | flops 11500000 | bytes 1024 | tf_op jit(solution)/shard_map/local/pallas_call | solution.py:24
  16.8 0.9 %collective-permute-start.7 = (bf16[128,1024]{1,0:T(8,128)(2,1)S(1)}, bf16[128,1024]{1,0:T(8,128)(2,1)S(1)}, u32[]{:S(2)}, u32[]{:S(2)}) collective-permute-start(bf16[128,1024]{1,0:T(8,128)(2,1)S(1)} %pass_on.1.refs_2_), channel_id=1, source_target_pairs={{0,1},{1,0},{2,3},{3,2},{4,5},{5,4},{6,7},{7,6},{8,9},{9,8},{10,11... | collective-permute-start | bytes 786440 | tf_op jit(solution)/shard_map/ppermute | solution.py:480
  17.7 0.8 %unproject_own.1.refs_1_.refs_3_ = f32[128,1024]{1,0:T(8,128)S(1)} custom-call(s32[1]{0:T(128)} %bitcast.z_ref, bf16[128,1024]{1,0:T(8,128)(2,1)S(1)} %copy-done.3, bf16[1024,4096]{1,0:T(8,128)(2,1)S(1)} %bitcast.7, bf16[128,1024]{1,0:T(8,128)(2,1)S(1)} %pass_on.1.refs_2_), custom_call_target="tpu_custom_call" | custom-call | flops 920000000 | bytes 1024 | tf_op jit(solution)/shard_map/unproject_own/pallas_call | solution.py:24
  18.5 1.4 %collective-permute-done.2.y_ref = bf16[528,128]{1,0:T(8,128)(2,1)S(1)} collective-permute-done((bf16[528,128]{1,0:T(8,128)(2,1)S(1)}, bf16[528,128]{1,0:T(8,128)(2,1)S(1)}, u32[]{:S(2)}, u32[]{:S(2)}) %collective-permute-start.2) | collective-permute-done | bytes 135200 | tf_op jit(solution)/shard_map/ppermute | solution.py:441
  20.1 0.5 %join.2 = (f32[4,136,128]{2,1,0:T(8,128)S(1)}, bf16[528,128]{1,0:T(8,128)(2,1)S(1)}) custom-call(s32[1]{0:T(128)} %bitcast.1.refs_0_.pos_ref, bf16[528,128]{1,0:T(8,128)(2,1)S(1)} %collective-permute-done.1.x_ref, bf16[528,128]{1,0:T(8,128)(2,1)S(1)} %collective-permute-done.2.y_ref, bf16[528,128]{1,0:T(8,128)(2,1)S(1)} %collective-permute-done.3.d_ref, ...), custom_call_target="tpu_custom_call" | custom-call | flops 11500000 | bytes 1024 | tf_op jit(solution)/shard_map/join/pallas_call | solution.py:24
  20.7 1.3 %collective-permute-done.5.far_ref = bf16[528,128]{1,0:T(8,128)(2,1)S(1)} collective-permute-done((bf16[528,128]{1,0:T(8,128)(2,1)S(1)}, bf16[528,128]{1,0:T(8,128)(2,1)S(1)}, u32[]{:S(2)}, u32[]{:S(2)}) %collective-permute-start.5) | collective-permute-done | bytes 135200 | tf_op jit(solution)/shard_map/ppermute | solution.py:453
  22.0 1.6 %read.1 = (bf16[128,1024]{1,0:T(8,128)(2,1)S(1)}, f32[128,1024]{1,0:T(8,128)S(1)}, bf16[8,128,256]{2,1,0:T(8,128)(2,1)S(1)}, f32[8,8,128]{2,1,0:T(8,128)S(1)}, b...) custom-call(s32[1]{0:T(128)} %bitcast.1.refs_0_.pos_ref, s32[1]{0:T(128)} %bitcast.z_ref, ...), custom_call_target="tpu_custom_call" | custom-call | flops 11500000 | bytes 1024 | tf_op jit(solution)/shard_map/read/pallas_call | solution.py:24
  23.6 0.8 %collective-permute-start.12 = (bf16[128,1024]{1,0:T(8,128)(2,1)S(1)}, bf16[128,1024]{1,0:T(8,128)(2,1)S(1)}, u32[]{:S(2)}, u32[]{:S(2)}) collective-permute-start(bf16[128,1024]{1,0:T(8,128)(2,1)S(1)} %get-tuple-element.53), channel_id=1, source_target_pairs={{0,1},{1,0},{2,3},{3,2},{4,5},{5,4},{6,7},{7,6},{8,9},{9,8},{10,11... | collective-permute-start | bytes 786440 | tf_op jit(solution)/shard_map/ppermute | solution.py:480
  24.4 1.5 %unproject_more.1.refs_1_ = f32[128,1024]{1,0:T(8,128)S(1)} custom-call(s32[1]{0:T(128)} %bitcast.z_ref, bf16[128,1024]{1,0:T(8,128)(2,1)S(1)} %collective-permute-done.6.refs_0_, bf16[128,1024]{1,0:T(8,128)(2,1)S(1)} %collective-permute-done.4.block_ref.refs_1_, bf16[1024,4096]{1,0:T(8,128)(2,1)S(1)} %bitcast.7, ...), custom_call_target="tpu_custom_call" | custom-call | flops 11500000 | bytes 1024 | tf_op jit(solution)/shard_map/unproject_more/pallas_call | solution.py:24
  26.0 1.2 %spread.1 = (f32[4,136,128]{2,1,0:T(8,128)S(1)}, bf16[528,128]{1,0:T(8,128)(2,1)S(1)}, bf16[128,1024]{1,0:T(8,128)(2,1)S(1)}, f32[8,128,1]{2,1,0:T(8,128)S(1)}, bf16[128,1024]{1,0:T(8,128)(2,1)S(1)}) custom-call(s32[1]{0:T(128)} %bitcast.1.refs_0_.pos_ref, s32[1]{0:T(128)} %bitcast.z_ref, f32[8,128]{1,0:T(8,128)S(1)} %broadcast.10.facts_ref, ...), custom_call_target="tpu_custom_call" | custom-call | flops 11500000 | bytes 1024 | tf_op jit(solution)/shard_map/spread/pallas_call | solution.py:24
  27.2 0.7 %project_rest.1 = (bf16[128,1024]{1,0:T(8,128)(2,1)S(1)}, f32[128,1024]{1,0:T(8,128)S(1)}) custom-call(s32[1]{0:T(128)} %bitcast.z_ref, bf16[128,1024]{1,0:T(8,128)(2,1)S(1)} %get-tuple-element.39.refs_4_.mixed_ref, bf16[1024,4096]{1,0:T(8,128)(2,1)S(1)} %bitcast.7, bf16[128,1024]{1,0:T(8,128)(2,1)S(1)} %get-tuple-element.43.after_ref.numer_ref), custom_call_target="tpu_custom_call" | custom-call | flops 11500000 | bytes 1024 | tf_op jit(solution)/shard_map/project_rest/pallas_call | solution.py:24
  28.0 1.3 %collective-permute-start.15 = (bf16[128,1024]{1,0:T(8,128)(2,1)S(1)}, bf16[128,1024]{1,0:T(8,128)(2,1)S(1)}, u32[]{:S(2)}, u32[]{:S(2)}) collective-permute-start(bf16[128,1024]{1,0:T(8,128)(2,1)S(1)} %get-tuple-element.47.refs_1_), channel_id=1, source_target_pairs={{0,1},{1,0},{2,3},{3,2},{4,5},{5,4},{6,7},{7,6},{8,9},{9,8},{10,11... | collective-permute-start | bytes 786440 | tf_op jit(solution)/shard_map/ppermute | solution.py:480
  29.3 1.7 %collective-permute-start.11 = (bf16[528,128]{1,0:T(8,128)(2,1)S(1)}, bf16[528,128]{1,0:T(8,128)(2,1)S(1)}, u32[]{:S(2)}, u32[]{:S(2)}) collective-permute-start(bf16[528,128]{1,0:T(8,128)(2,1)S(1)} %pair.3.after_ref), channel_id=1, source_target_pairs={{0,24},{4,28},{8,16},{12,20},{16,8},{20,12},{24,0},{28,4},{1,25},{... | collective-permute-start | bytes 405512 | tf_op jit(solution)/shard_map/ppermute | solution.py:441
  31.1 1.3 %collective-permute-start.10 = (bf16[528,128]{1,0:T(8,128)(2,1)S(1)}, bf16[528,128]{1,0:T(8,128)(2,1)S(1)}, u32[]{:S(2)}, u32[]{:S(2)}) collective-permute-start(bf16[528,128]{1,0:T(8,128)(2,1)S(1)} %pair.3.after_ref), channel_id=1, source_target_pairs={{0,16},{4,20},{8,24},{12,28},{16,0},{20,4},{24,8},{28,12},{1,17},{... | collective-permute-start | bytes 405512 | tf_op jit(solution)/shard_map/ppermute | solution.py:441
  32.4 0.5 %collective-permute-start.9 = (bf16[528,128]{1,0:T(8,128)(2,1)S(1)}, bf16[528,128]{1,0:T(8,128)(2,1)S(1)}, u32[]{:S(2)}, u32[]{:S(2)}) collective-permute-start(bf16[528,128]{1,0:T(8,128)(2,1)S(1)} %pair.3.after_ref), channel_id=1, source_target_pairs={{0,8},{4,12},{8,0},{12,4},{16,24},{20,28},{24,16},{28,20},{1,9},{5... | collective-permute-start | bytes 405512 | tf_op jit(solution)/shard_map/ppermute | solution.py:441
  32.9 0.5 project_add.1.refs_0_
  33.4 1.0 %collective-permute-start.16 = (bf16[128,1024]{1,0:T(8,128)(2,1)S(1)}, bf16[128,1024]{1,0:T(8,128)(2,1)S(1)}, u32[]{:S(2)}, u32[]{:S(2)}) collective-permute-start(bf16[128,1024]{1,0:T(8,128)(2,1)S(1)} %project_add.1.refs_0_), channel_id=1, source_target_pairs={{0,3},{1,2},{2,1},{3,0},{4,7},{5,6},{6,5},{7,4},{8,11},{9,10},{10,... | collective-permute-start | bytes 786440 | tf_op jit(solution)/shard_map/ppermute | solution.py:480
  34.4 3.7 %grads.1 = (bf16[128,1024]{1,0:T(8,128)(2,1)}, f32[128,1024]{1,0:T(8,128)S(1)}, f32[128,1024]{1,0:T(8,128)S(1)}) custom-call(f32[8,128]{1,0:T(8,128)S(1)} %broadcast.10.facts_ref, f32[8]{0:T(128)S(1)} %copy-done.4, bf16[128,1024]{1,0:T(8,128)(2,1)S(1)} %copy-done, bf16[128,1024]{1,0:T(8,128)(2,1)S(1)} %copy-done.1, bf16[128,1024]{1,0:T(8,128)(2,1)S(1)} %copy-done.2, ...), custom_call_target="tpu_custom_call" | custom-call | flops 11500000 | bytes 1024 | tf_op jit(solution)/shard_map/grads/pallas_call | solution.py:24
  38.1 0.8 %collective-permute-done.10.y_ref = bf16[528,128]{1,0:T(8,128)(2,1)S(1)} collective-permute-done((bf16[528,128]{1,0:T(8,128)(2,1)S(1)}, bf16[528,128]{1,0:T(8,128)(2,1)S(1)}, u32[]{:S(2)}, u32[]{:S(2)}) %collective-permute-start.10) | collective-permute-done | bytes 135200 | tf_op jit(solution)/shard_map/ppermute | solution.py:441
  38.9 0.2 join.3
  39.2 0.5 %collective-permute-start.14 = (bf16[272,128]{1,0:T(8,128)(2,1)S(1)}, bf16[272,128]{1,0:T(8,128)(2,1)S(1)}, u32[]{:S(2)}, u32[]{:S(2)}) collective-permute-start(bf16[272,128]{1,0:T(8,128)(2,1)S(1)} %get-tuple-element.58), channel_id=1, source_target_pairs={{0,4},{4,0},{8,12},{12,8},{16,20},{20,16},{24,28},{28,24},{1,5},{5... | collective-permute-start | bytes 208904 | tf_op jit(solution)/shard_map/ppermute | solution.py:453
  39.7 3.6 %collective-permute-done.15.refs_2_ = bf16[128,1024]{1,0:T(8,128)(2,1)S(1)} collective-permute-done((bf16[128,1024]{1,0:T(8,128)(2,1)S(1)}, bf16[128,1024]{1,0:T(8,128)(2,1)S(1)}, u32[]{:S(2)}, u32[]{:S(2)}) %collective-permute-start.15) | collective-permute-done | bytes 262176 | tf_op jit(solution)/shard_map/ppermute | solution.py:480
  43.3 1.4 %last.1 = (bf16[128,1024]{1,0:T(8,128)(2,1)}, bf16[128,1024]{1,0:T(8,128)(2,1)}) custom-call(s32[1]{0:T(128)} %bitcast.1.refs_0_.pos_ref, f32[8,128]{1,0:T(8,128)S(1)} %broadcast.10.facts_ref, bf16[128,1024]{1,0:T(8,128)(2,1)S(1)} %copy-done.1, bf16[128,1024]{1,0:T(8,128)(2,1)S(1)} %copy-done.2, f32[4,136,128]{2,1,0:T(8,128)S(1)} %get-tuple-element.55.own_ref, ...), custom_call_target="tpu_custom_call" | custom-call | flops 1150000000 | bytes 1024 | tf_op jit(solution)/shard_map/last/pallas_call | solution.py:24
  44.7 0.8 %add_convert_fusion = bf16[128,1024]{1,0:T(8,128)(2,1)} fusion(bf16[128,1024]{1,0:T(8,128)(2,1)S(1)} %collective-permute-done.16, f32[128,1024]{1,0:T(8,128)S(1)} %get-tuple-element.60, bf16[128,1024]{1,0:T(8,128)(2,1)S(1)} %collective-permute-done.15.refs_2_), kind=kLoop, calls=%fused_computation | loop fusion | flops 655360 | bytes 1310720 | tf_op jit(solution)/shard_map/convert_element_type | solution.py:594
  (37 shorter events, 0.8 us)
Async XLA Ops:
  0.6 16.1 %collective-permute-start.4 = (bf16[128,1024]{1,0:T(8,128)(2,1)}, bf16[128,1024]{1,0:T(8,128)(2,1)S(1)}, u32[]{:S(2)}, u32[]{:S(2)}) collective-permute-start(bf16[128,1024]{1,0:T(8,128)(2,1)} %refs_0_.2), channel_id=1, source_target_pairs={{0,3},{1,2},{2,1},{3,0},{4,7},{5,6},{6,5},{7,4},{8,11},{9,10},{10,... | collective-permute-start | bytes 786440 | tf_op jit(solution)/shard_map/ppermute | solution.py:480
  7.0 1.0 %copy-start.1 = (bf16[128,1024]{1,0:T(8,128)(2,1)S(1)}, bf16[128,1024]{1,0:T(8,128)(2,1)}, u32[]{:S(2)}) copy-start(bf16[128,1024]{1,0:T(8,128)(2,1)} %k_ref.7) | copy-start | bytes 786436
  7.1 1.0 %copy-start.2 = (bf16[128,1024]{1,0:T(8,128)(2,1)S(1)}, bf16[128,1024]{1,0:T(8,128)(2,1)}, u32[]{:S(2)}) copy-start(bf16[128,1024]{1,0:T(8,128)(2,1)} %v_ref.7) | copy-start | bytes 786436
  7.1 1.7 %copy-start.3 = (bf16[128,1024]{1,0:T(8,128)(2,1)S(1)}, bf16[128,1024]{1,0:T(8,128)(2,1)}, u32[]{:S(2)}) copy-start(bf16[128,1024]{1,0:T(8,128)(2,1)} %refs_0_.2) | copy-start | bytes 786436
  7.1 6.9 %copy-start = (bf16[128,1024]{1,0:T(8,128)(2,1)S(1)}, bf16[128,1024]{1,0:T(8,128)(2,1)}, u32[]{:S(2)}) copy-start(bf16[128,1024]{1,0:T(8,128)(2,1)} %q_ref.5) | copy-start | bytes 786436
  7.1 10.6 %slice-start = ((s8[8388608]{0:T(1024)(128)(4,1)}), s8[4194304]{0:T(1024)(128)(4,1)S(1)}, s32[]{:S(2)}) async-start(s8[8388608]{0:T(1024)(128)(4,1)} %bitcast.6), calls=%async_computation | async-start | bytes 8388608
  8.1 9.6 %slice-start.1 = ((s8[8388608]{0:T(1024)(128)(4,1)}), s8[4194304]{0:T(1024)(128)(4,1)S(1)}, s32[]{:S(2)}) async-start(s8[8388608]{0:T(1024)(128)(4,1)} %bitcast.6), calls=%async_computation.1 | async-start | bytes 8388608
  8.6 13.4 %copy-start.4 = (f32[8]{0:T(128)S(1)}, f32[8]{0:T(128)}, u32[]{:S(2)}) copy-start(f32[8]{0:T(128)} %gate_ref.3) | copy-start | bytes 100
  8.6 1.4 %collective-permute-start = (bf16[528,128]{1,0:T(8,128)(2,1)S(1)}, bf16[528,128]{1,0:T(8,128)(2,1)S(1)}, u32[]{:S(2)}, u32[]{:S(2)}) collective-permute-start(bf16[528,128]{1,0:T(8,128)(2,1)S(1)} %get-tuple-element.35), channel_id=1, source_target_pairs={{0,4},{4,0},{8,12},{12,8},{16,20},{20,16},{24,28},{28,24},{1,5},{5... | collective-permute-start | bytes 405512 | tf_op jit(solution)/shard_map/ppermute | solution.py:430
  8.7 12.0 %collective-permute-start.6 = (bf16[128,1024]{1,0:T(8,128)(2,1)S(1)}, bf16[128,1024]{1,0:T(8,128)(2,1)S(1)}, u32[]{:S(2)}, u32[]{:S(2)}) collective-permute-start(bf16[128,1024]{1,0:T(8,128)(2,1)S(1)} %copy-done.3), channel_id=1, source_target_pairs={{0,1},{1,0},{2,3},{3,2},{4,5},{5,4},{6,7},{7,6},{8,9},{9,8},{10,11... | collective-permute-start | bytes 786440 | tf_op jit(solution)/shard_map/ppermute | solution.py:480
  10.5 8.1 %collective-permute-start.3 = (bf16[528,128]{1,0:T(8,128)(2,1)S(1)}, bf16[528,128]{1,0:T(8,128)(2,1)S(1)}, u32[]{:S(2)}, u32[]{:S(2)}) collective-permute-start(bf16[528,128]{1,0:T(8,128)(2,1)S(1)} %pair.2.after_ref), channel_id=1, source_target_pairs={{0,24},{4,28},{8,16},{12,20},{16,8},{20,12},{24,0},{28,4},{1,25},{... | collective-permute-start | bytes 405512 | tf_op jit(solution)/shard_map/ppermute | solution.py:441
  13.0 7.0 %collective-permute-start.2 = (bf16[528,128]{1,0:T(8,128)(2,1)S(1)}, bf16[528,128]{1,0:T(8,128)(2,1)S(1)}, u32[]{:S(2)}, u32[]{:S(2)}) collective-permute-start(bf16[528,128]{1,0:T(8,128)(2,1)S(1)} %pair.2.after_ref), channel_id=1, source_target_pairs={{0,16},{4,20},{8,24},{12,28},{16,0},{20,4},{24,8},{28,12},{1,17},{... | collective-permute-start | bytes 405512 | tf_op jit(solution)/shard_map/ppermute | solution.py:441
  13.5 6.6 %collective-permute-start.1 = (bf16[528,128]{1,0:T(8,128)(2,1)S(1)}, bf16[528,128]{1,0:T(8,128)(2,1)S(1)}, u32[]{:S(2)}, u32[]{:S(2)}) collective-permute-start(bf16[528,128]{1,0:T(8,128)(2,1)S(1)} %pair.2.after_ref), channel_id=1, source_target_pairs={{0,8},{4,12},{8,0},{12,4},{16,24},{20,28},{24,16},{28,20},{1,9},{5... | collective-permute-start | bytes 405512 | tf_op jit(solution)/shard_map/ppermute | solution.py:441
  16.8 9.2 %collective-permute-start.7 = (bf16[128,1024]{1,0:T(8,128)(2,1)S(1)}, bf16[128,1024]{1,0:T(8,128)(2,1)S(1)}, u32[]{:S(2)}, u32[]{:S(2)}) collective-permute-start(bf16[128,1024]{1,0:T(8,128)(2,1)S(1)} %pass_on.1.refs_2_), channel_id=1, source_target_pairs={{0,1},{1,0},{2,3},{3,2},{4,5},{5,4},{6,7},{7,6},{8,9},{9,8},{10,11... | collective-permute-start | bytes 786440 | tf_op jit(solution)/shard_map/ppermute | solution.py:480
  20.6 1.4 %collective-permute-start.5 = (bf16[528,128]{1,0:T(8,128)(2,1)S(1)}, bf16[528,128]{1,0:T(8,128)(2,1)S(1)}, u32[]{:S(2)}, u32[]{:S(2)}) collective-permute-start(bf16[528,128]{1,0:T(8,128)(2,1)S(1)} %get-tuple-element.38), channel_id=1, source_target_pairs={{0,4},{4,0},{8,12},{12,8},{16,20},{20,16},{24,28},{28,24},{1,5},{5... | collective-permute-start | bytes 405512 | tf_op jit(solution)/shard_map/ppermute | solution.py:453
  23.6 9.3 %collective-permute-start.12 = (bf16[128,1024]{1,0:T(8,128)(2,1)S(1)}, bf16[128,1024]{1,0:T(8,128)(2,1)S(1)}, u32[]{:S(2)}, u32[]{:S(2)}) collective-permute-start(bf16[128,1024]{1,0:T(8,128)(2,1)S(1)} %get-tuple-element.53), channel_id=1, source_target_pairs={{0,1},{1,0},{2,3},{3,2},{4,5},{5,4},{6,7},{7,6},{8,9},{9,8},{10,11... | collective-permute-start | bytes 786440 | tf_op jit(solution)/shard_map/ppermute | solution.py:480
  27.1 2.1 %collective-permute-start.8 = (bf16[528,128]{1,0:T(8,128)(2,1)S(1)}, bf16[528,128]{1,0:T(8,128)(2,1)S(1)}, u32[]{:S(2)}, u32[]{:S(2)}) collective-permute-start(bf16[528,128]{1,0:T(8,128)(2,1)S(1)} %get-tuple-element.46), channel_id=1, source_target_pairs={{0,4},{4,0},{8,12},{12,8},{16,20},{20,16},{24,28},{28,24},{1,5},{5... | collective-permute-start | bytes 405512 | tf_op jit(solution)/shard_map/ppermute | solution.py:430
  28.0 15.3 %collective-permute-start.15 = (bf16[128,1024]{1,0:T(8,128)(2,1)S(1)}, bf16[128,1024]{1,0:T(8,128)(2,1)S(1)}, u32[]{:S(2)}, u32[]{:S(2)}) collective-permute-start(bf16[128,1024]{1,0:T(8,128)(2,1)S(1)} %get-tuple-element.47.refs_1_), channel_id=1, source_target_pairs={{0,1},{1,0},{2,3},{3,2},{4,5},{5,4},{6,7},{7,6},{8,9},{9,8},{10,11... | collective-permute-start | bytes 786440 | tf_op jit(solution)/shard_map/ppermute | solution.py:480
  29.3 8.7 %collective-permute-start.11 = (bf16[528,128]{1,0:T(8,128)(2,1)S(1)}, bf16[528,128]{1,0:T(8,128)(2,1)S(1)}, u32[]{:S(2)}, u32[]{:S(2)}) collective-permute-start(bf16[528,128]{1,0:T(8,128)(2,1)S(1)} %pair.3.after_ref), channel_id=1, source_target_pairs={{0,24},{4,28},{8,16},{12,20},{16,8},{20,12},{24,0},{28,4},{1,25},{... | collective-permute-start | bytes 405512 | tf_op jit(solution)/shard_map/ppermute | solution.py:441
  31.1 7.8 %collective-permute-start.10 = (bf16[528,128]{1,0:T(8,128)(2,1)S(1)}, bf16[528,128]{1,0:T(8,128)(2,1)S(1)}, u32[]{:S(2)}, u32[]{:S(2)}) collective-permute-start(bf16[528,128]{1,0:T(8,128)(2,1)S(1)} %pair.3.after_ref), channel_id=1, source_target_pairs={{0,16},{4,20},{8,24},{12,28},{16,0},{20,4},{24,8},{28,12},{1,17},{... | collective-permute-start | bytes 405512 | tf_op jit(solution)/shard_map/ppermute | solution.py:441
  32.4 6.5 %collective-permute-start.9 = (bf16[528,128]{1,0:T(8,128)(2,1)S(1)}, bf16[528,128]{1,0:T(8,128)(2,1)S(1)}, u32[]{:S(2)}, u32[]{:S(2)}) collective-permute-start(bf16[528,128]{1,0:T(8,128)(2,1)S(1)} %pair.3.after_ref), channel_id=1, source_target_pairs={{0,8},{4,12},{8,0},{12,4},{16,24},{20,28},{24,16},{28,20},{1,9},{5... | collective-permute-start | bytes 405512 | tf_op jit(solution)/shard_map/ppermute | solution.py:441
  33.4 11.3 %collective-permute-start.16 = (bf16[128,1024]{1,0:T(8,128)(2,1)S(1)}, bf16[128,1024]{1,0:T(8,128)(2,1)S(1)}, u32[]{:S(2)}, u32[]{:S(2)}) collective-permute-start(bf16[128,1024]{1,0:T(8,128)(2,1)S(1)} %project_add.1.refs_0_), channel_id=1, source_target_pairs={{0,3},{1,2},{2,1},{3,0},{4,7},{5,6},{6,5},{7,4},{8,11},{9,10},{10,... | collective-permute-start | bytes 786440 | tf_op jit(solution)/shard_map/ppermute | solution.py:480
  39.1 4.2 %collective-permute-start.13 = (bf16[272,128]{1,0:T(8,128)(2,1)S(1)}, bf16[272,128]{1,0:T(8,128)(2,1)S(1)}, u32[]{:S(2)}, u32[]{:S(2)}) collective-permute-start(bf16[272,128]{1,0:T(8,128)(2,1)S(1)} %get-tuple-element.57), channel_id=1, source_target_pairs={{0,4},{4,0},{8,12},{12,8},{16,20},{20,16},{24,28},{28,24},{1,5},{5... | collective-permute-start | bytes 208904 | tf_op jit(solution)/shard_map/ppermute | solution.py:453
  39.2 4.1 %collective-permute-start.14 = (bf16[272,128]{1,0:T(8,128)(2,1)S(1)}, bf16[272,128]{1,0:T(8,128)(2,1)S(1)}, u32[]{:S(2)}, u32[]{:S(2)}) collective-permute-start(bf16[272,128]{1,0:T(8,128)(2,1)S(1)} %get-tuple-element.58), channel_id=1, source_target_pairs={{0,4},{4,0},{8,12},{12,8},{16,20},{20,16},{24,28},{28,24},{1,5},{5... | collective-permute-start | bytes 208904 | tf_op jit(solution)/shard_map/ppermute | solution.py:453

commit v8 on v7

--- a/solution.py
+++ b/solution.py
@@ -425,6 +425,7 @@
         before_pair()
         before_join(keep)
         carry = weighted(jnp.concatenate([keep, *give]), forward)
+        carry = carry.at[:, DH + 1].set(keep[0, DH + 1])
         return carry[:half], [carry[half:]]
     pairs = [(s, s ^ 1) for s in range(count)]
     others = [lax.ppermute(part, "seq", pairs) for part in give]

time: 45.7 us -> 45.7 us (level)
  no operation moved by 1% of the time
where the time goes in v8:
time: 45.7 us; the launch traced here: 45.5 us
  starting transfers between devices  17.2 us (38%)
  Pallas kernels  15.8 us (35%)
  waiting for transfers between devices  8.58 us (19%)
  between operations  2.17 us (5%)
  local copies, waits for them, and re-layouts  0.98 us (2%)
  other arithmetic  0.82 us (2%)
    pallas_call x17, Pallas kernels, call(): pl.pallas_call(kernel, out_shape=outs, in_specs=in_specs, out_specs=[VMEM...  15.8 us
    ppermute x6, starting transfers between devices, swap(): return lax.ppermute(array, 'head', [(s, s ^ way) for s in range(groups)])  9.31 us
    ppermute x6, starting transfers between devices, scan_states(): lax.ppermute(sent, 'seq', [(s, s ^ way) for s in range(count)])  7.11 us
    ppermute x6, waiting for transfers between devices, swap(): return lax.ppermute(array, 'head', [(s, s ^ way) for s in range(groups)])  3.62 us
    ppermute x6, waiting for transfers between devices, scan_states(): lax.ppermute(sent, 'seq', [(s, s ^ way) for s in range(count)])  2.38 us
    ppermute x3, waiting for transfers between devices, scan_states(): return (own, [lax.ppermute(part, 'seq', pairs) for part in passed])  1.32 us
    ppermute x2, waiting for transfers between devices, scan_states(): others = [lax.ppermute(part, 'seq', pairs) for part in give]  1.25 us
    unnamed x14, local copies, waits for them, and re-layouts  0.91 us
  transfers between devices with their start and end apart: 17, of which 6 were waited for; matrix products, arithmetic and copies ran while one was open for 0% of the time, Pallas kernels for 35%

profile of v8, /device:TPU:0, one launch (start us, length us, event | category | flops | bytes accessed | tf_op | source)
XLA Modules:
  0.0 45.5 jit_solution(7841842404399555044)
XLA Ops:
  0.6 5.1 %collective-permute-start.4 = (bf16[128,1024]{1,0:T(8,128)(2,1)}, bf16[128,1024]{1,0:T(8,128)(2,1)S(1)}, u32[]{:S(2)}, u32[]{:S(2)}) collective-permute-start(bf16[128,1024]{1,0:T(8,128)(2,1)} %refs_0_.2), channel_id=1, source_target_pairs={{0,3},{1,2},{2,1},{3,0},{4,7},{5,6},{6,5},{7,4},{8,11},{9,10},{10,... | collective-permute-start | bytes 786440 | tf_op jit(solution)/shard_map/ppermute | solution.py:481
  7.2 0.8 %copy-done.1 = bf16[128,1024]{1,0:T(8,128)(2,1)S(1)} copy-done((bf16[128,1024]{1,0:T(8,128)(2,1)S(1)}, bf16[128,1024]{1,0:T(8,128)(2,1)}, u32[]{:S(2)}) %copy-start.1) | copy-done | bytes 262168
  8.1 0.5 %state.1 = (f32[4,136,128]{2,1,0:T(8,128)S(1)}, bf16[528,128]{1,0:T(8,128)(2,1)S(1)}) custom-call(s32[1]{0:T(128)} %bitcast.1.refs_0_.pos_ref, s32[1]{0:T(128)} %bitcast.z_ref, f32[8,128]{1,0:T(8,128)S(1)} %broadcast.10.facts_ref, bf16[128,1024]{1,0:T(8,128)(2,1)S(1)} %copy-done.1, bf16[128,1024]{1,0:T(8,128)(2,1)S(1)} %copy-done.2, f32[8,128]{1,0:T(8,128)S(1)} %warm.1.after_ref), custom_call_target="tpu_custom_call" | custom-call | flops 3449999872 | bytes 1024 | tf_op jit(solution)/shard_map/state/pallas_call | solution.py:24
  8.8 1.3 %collective-permute-done.refs_0_ = bf16[528,128]{1,0:T(8,128)(2,1)S(1)} collective-permute-done((bf16[528,128]{1,0:T(8,128)(2,1)S(1)}, bf16[528,128]{1,0:T(8,128)(2,1)S(1)}, u32[]{:S(2)}, u32[]{:S(2)}) %collective-permute-start) | collective-permute-done | bytes 135200 | tf_op jit(solution)/shard_map/ppermute | solution.py:431
  10.1 0.4 pair.2.after_ref
  10.5 2.5 %collective-permute-start.3 = (bf16[528,128]{1,0:T(8,128)(2,1)S(1)}, bf16[528,128]{1,0:T(8,128)(2,1)S(1)}, u32[]{:S(2)}, u32[]{:S(2)}) collective-permute-start(bf16[528,128]{1,0:T(8,128)(2,1)S(1)} %pair.2.after_ref), channel_id=1, source_target_pairs={{0,24},{4,28},{8,16},{12,20},{16,8},{20,12},{24,0},{28,4},{1,25},{... | collective-permute-start | bytes 405512 | tf_op jit(solution)/shard_map/ppermute | solution.py:442
  13.0 0.5 %collective-permute-start.2 = (bf16[528,128]{1,0:T(8,128)(2,1)S(1)}, bf16[528,128]{1,0:T(8,128)(2,1)S(1)}, u32[]{:S(2)}, u32[]{:S(2)}) collective-permute-start(bf16[528,128]{1,0:T(8,128)(2,1)S(1)} %pair.2.after_ref), channel_id=1, source_target_pairs={{0,16},{4,20},{8,24},{12,28},{16,0},{20,4},{24,8},{28,12},{1,17},{... | collective-permute-start | bytes 405512 | tf_op jit(solution)/shard_map/ppermute | solution.py:442
  13.5 0.5 %collective-permute-start.1 = (bf16[528,128]{1,0:T(8,128)(2,1)S(1)}, bf16[528,128]{1,0:T(8,128)(2,1)S(1)}, u32[]{:S(2)}, u32[]{:S(2)}) collective-permute-start(bf16[528,128]{1,0:T(8,128)(2,1)S(1)} %pair.2.after_ref), channel_id=1, source_target_pairs={{0,8},{4,12},{8,0},{12,4},{16,24},{20,28},{24,16},{28,20},{1,9},{5... | collective-permute-start | bytes 405512 | tf_op jit(solution)/shard_map/ppermute | solution.py:442
  14.0 2.7 %local.1 = (bf16[8,128,128]{2,1,0:T(8,128)(2,1)S(1)}, f32[128,1024]{1,0:T(8,128)S(1)}) custom-call(f32[8,128]{1,0:T(8,128)S(1)} %broadcast.10.facts_ref, bf16[128,1024]{1,0:T(8,128)(2,1)S(1)} %copy-done, bf16[128,1024]{1,0:T(8,128)(2,1)S(1)} %copy-done.1, bf16[128,1024]{1,0:T(8,128)(2,1)S(1)} %copy-done.2, bf16[528,128]{1,0:T(8,128)(2,1)S(1)} %pair.2.after_ref), custom_call_target="tpu_custom_call" | custom-call | flops 11500000 | bytes 1024 | tf_op jit(solution)/shard_map/local/pallas_call | solution.py:24
  16.8 0.9 %collective-permute-start.7 = (bf16[128,1024]{1,0:T(8,128)(2,1)S(1)}, bf16[128,1024]{1,0:T(8,128)(2,1)S(1)}, u32[]{:S(2)}, u32[]{:S(2)}) collective-permute-start(bf16[128,1024]{1,0:T(8,128)(2,1)S(1)} %pass_on.1.refs_2_), channel_id=1, source_target_pairs={{0,1},{1,0},{2,3},{3,2},{4,5},{5,4},{6,7},{7,6},{8,9},{9,8},{10,11... | collective-permute-start | bytes 786440 | tf_op jit(solution)/shard_map/ppermute | solution.py:481
  17.7 0.8 %unproject_own.1.refs_1_.refs_3_ = f32[128,1024]{1,0:T(8,128)S(1)} custom-call(s32[1]{0:T(128)} %bitcast.z_ref, bf16[128,1024]{1,0:T(8,128)(2,1)S(1)} %copy-done.3, bf16[1024,4096]{1,0:T(8,128)(2,1)S(1)} %bitcast.7, bf16[128,1024]{1,0:T(8,128)(2,1)S(1)} %pass_on.1.refs_2_), custom_call_target="tpu_custom_call" | custom-call | flops 920000000 | bytes 1024 | tf_op jit(solution)/shard_map/unproject_own/pallas_call | solution.py:24
  18.5 1.4 %collective-permute-done.2.y_ref = bf16[528,128]{1,0:T(8,128)(2,1)S(1)} collective-permute-done((bf16[528,128]{1,0:T(8,128)(2,1)S(1)}, bf16[528,128]{1,0:T(8,128)(2,1)S(1)}, u32[]{:S(2)}, u32[]{:S(2)}) %collective-permute-start.2) | collective-permute-done | bytes 135200 | tf_op jit(solution)/shard_map/ppermute | solution.py:442
  20.1 0.5 %join.2 = (f32[4,136,128]{2,1,0:T(8,128)S(1)}, bf16[528,128]{1,0:T(8,128)(2,1)S(1)}) custom-call(s32[1]{0:T(128)} %bitcast.1.refs_0_.pos_ref, bf16[528,128]{1,0:T(8,128)(2,1)S(1)} %collective-permute-done.1.x_ref, bf16[528,128]{1,0:T(8,128)(2,1)S(1)} %collective-permute-done.2.y_ref, bf16[528,128]{1,0:T(8,128)(2,1)S(1)} %collective-permute-done.3.d_ref, ...), custom_call_target="tpu_custom_call" | custom-call | flops 11500000 | bytes 1024 | tf_op jit(solution)/shard_map/join/pallas_call | solution.py:24
  20.7 1.3 %collective-permute-done.5.far_ref = bf16[528,128]{1,0:T(8,128)(2,1)S(1)} collective-permute-done((bf16[528,128]{1,0:T(8,128)(2,1)S(1)}, bf16[528,128]{1,0:T(8,128)(2,1)S(1)}, u32[]{:S(2)}, u32[]{:S(2)}) %collective-permute-start.5) | collective-permute-done | bytes 135200 | tf_op jit(solution)/shard_map/ppermute | solution.py:454
  22.0 1.6 %read.1 = (bf16[128,1024]{1,0:T(8,128)(2,1)S(1)}, f32[128,1024]{1,0:T(8,128)S(1)}, bf16[8,128,256]{2,1,0:T(8,128)(2,1)S(1)}, f32[8,8,128]{2,1,0:T(8,128)S(1)}, b...) custom-call(s32[1]{0:T(128)} %bitcast.1.refs_0_.pos_ref, s32[1]{0:T(128)} %bitcast.z_ref, ...), custom_call_target="tpu_custom_call" | custom-call | flops 11500000 | bytes 1024 | tf_op jit(solution)/shard_map/read/pallas_call | solution.py:24
  23.6 0.8 %collective-permute-start.12 = (bf16[128,1024]{1,0:T(8,128)(2,1)S(1)}, bf16[128,1024]{1,0:T(8,128)(2,1)S(1)}, u32[]{:S(2)}, u32[]{:S(2)}) collective-permute-start(bf16[128,1024]{1,0:T(8,128)(2,1)S(1)} %get-tuple-element.53), channel_id=1, source_target_pairs={{0,1},{1,0},{2,3},{3,2},{4,5},{5,4},{6,7},{7,6},{8,9},{9,8},{10,11... | collective-permute-start | bytes 786440 | tf_op jit(solution)/shard_map/ppermute | solution.py:481
  24.4 1.5 %unproject_more.1.refs_1_ = f32[128,1024]{1,0:T(8,128)S(1)} custom-call(s32[1]{0:T(128)} %bitcast.z_ref, bf16[128,1024]{1,0:T(8,128)(2,1)S(1)} %collective-permute-done.6.refs_0_, bf16[128,1024]{1,0:T(8,128)(2,1)S(1)} %collective-permute-done.4.block_ref.refs_1_, bf16[1024,4096]{1,0:T(8,128)(2,1)S(1)} %bitcast.7, ...), custom_call_target="tpu_custom_call" | custom-call | flops 11500000 | bytes 1024 | tf_op jit(solution)/shard_map/unproject_more/pallas_call | solution.py:24
  26.0 1.2 %spread.1 = (f32[4,136,128]{2,1,0:T(8,128)S(1)}, bf16[528,128]{1,0:T(8,128)(2,1)S(1)}, bf16[128,1024]{1,0:T(8,128)(2,1)S(1)}, f32[8,128,1]{2,1,0:T(8,128)S(1)}, bf16[128,1024]{1,0:T(8,128)(2,1)S(1)}) custom-call(s32[1]{0:T(128)} %bitcast.1.refs_0_.pos_ref, s32[1]{0:T(128)} %bitcast.z_ref, f32[8,128]{1,0:T(8,128)S(1)} %broadcast.10.facts_ref, ...), custom_call_target="tpu_custom_call" | custom-call | flops 11500000 | bytes 1024 | tf_op jit(solution)/shard_map/spread/pallas_call | solution.py:24
  27.2 0.7 %project_rest.1 = (bf16[128,1024]{1,0:T(8,128)(2,1)S(1)}, f32[128,1024]{1,0:T(8,128)S(1)}) custom-call(s32[1]{0:T(128)} %bitcast.z_ref, bf16[128,1024]{1,0:T(8,128)(2,1)S(1)} %get-tuple-element.39.refs_4_.mixed_ref, bf16[1024,4096]{1,0:T(8,128)(2,1)S(1)} %bitcast.7, bf16[128,1024]{1,0:T(8,128)(2,1)S(1)} %get-tuple-element.43.after_ref.numer_ref), custom_call_target="tpu_custom_call" | custom-call | flops 11500000 | bytes 1024 | tf_op jit(solution)/shard_map/project_rest/pallas_call | solution.py:24
  28.0 1.3 %collective-permute-start.15 = (bf16[128,1024]{1,0:T(8,128)(2,1)S(1)}, bf16[128,1024]{1,0:T(8,128)(2,1)S(1)}, u32[]{:S(2)}, u32[]{:S(2)}) collective-permute-start(bf16[128,1024]{1,0:T(8,128)(2,1)S(1)} %get-tuple-element.47.refs_1_), channel_id=1, source_target_pairs={{0,1},{1,0},{2,3},{3,2},{4,5},{5,4},{6,7},{7,6},{8,9},{9,8},{10,11... | collective-permute-start | bytes 786440 | tf_op jit(solution)/shard_map/ppermute | solution.py:481
  29.3 1.7 %collective-permute-start.11 = (bf16[528,128]{1,0:T(8,128)(2,1)S(1)}, bf16[528,128]{1,0:T(8,128)(2,1)S(1)}, u32[]{:S(2)}, u32[]{:S(2)}) collective-permute-start(bf16[528,128]{1,0:T(8,128)(2,1)S(1)} %pair.3.after_ref), channel_id=1, source_target_pairs={{0,24},{4,28},{8,16},{12,20},{16,8},{20,12},{24,0},{28,4},{1,25},{... | collective-permute-start | bytes 405512 | tf_op jit(solution)/shard_map/ppermute | solution.py:442
  31.1 1.3 %collective-permute-start.10 = (bf16[528,128]{1,0:T(8,128)(2,1)S(1)}, bf16[528,128]{1,0:T(8,128)(2,1)S(1)}, u32[]{:S(2)}, u32[]{:S(2)}) collective-permute-start(bf16[528,128]{1,0:T(8,128)(2,1)S(1)} %pair.3.after_ref), channel_id=1, source_target_pairs={{0,16},{4,20},{8,24},{12,28},{16,0},{20,4},{24,8},{28,12},{1,17},{... | collective-permute-start | bytes 405512 | tf_op jit(solution)/shard_map/ppermute | solution.py:442
  32.4 0.5 %collective-permute-start.9 = (bf16[528,128]{1,0:T(8,128)(2,1)S(1)}, bf16[528,128]{1,0:T(8,128)(2,1)S(1)}, u32[]{:S(2)}, u32[]{:S(2)}) collective-permute-start(bf16[528,128]{1,0:T(8,128)(2,1)S(1)} %pair.3.after_ref), channel_id=1, source_target_pairs={{0,8},{4,12},{8,0},{12,4},{16,24},{20,28},{24,16},{28,20},{1,9},{5... | collective-permute-start | bytes 405512 | tf_op jit(solution)/shard_map/ppermute | solution.py:442
  32.9 0.5 project_add.1.refs_0_
  33.4 1.0 %collective-permute-start.16 = (bf16[128,1024]{1,0:T(8,128)(2,1)S(1)}, bf16[128,1024]{1,0:T(8,128)(2,1)S(1)}, u32[]{:S(2)}, u32[]{:S(2)}) collective-permute-start(bf16[128,1024]{1,0:T(8,128)(2,1)S(1)} %project_add.1.refs_0_), channel_id=1, source_target_pairs={{0,3},{1,2},{2,1},{3,0},{4,7},{5,6},{6,5},{7,4},{8,11},{9,10},{10,... | collective-permute-start | bytes 786440 | tf_op jit(solution)/shard_map/ppermute | solution.py:481
  34.4 3.7 %grads.1 = (bf16[128,1024]{1,0:T(8,128)(2,1)}, f32[128,1024]{1,0:T(8,128)S(1)}, f32[128,1024]{1,0:T(8,128)S(1)}) custom-call(f32[8,128]{1,0:T(8,128)S(1)} %broadcast.10.facts_ref, f32[8]{0:T(128)S(1)} %copy-done.4, bf16[128,1024]{1,0:T(8,128)(2,1)S(1)} %copy-done, bf16[128,1024]{1,0:T(8,128)(2,1)S(1)} %copy-done.1, bf16[128,1024]{1,0:T(8,128)(2,1)S(1)} %copy-done.2, ...), custom_call_target="tpu_custom_call" | custom-call | flops 11500000 | bytes 1024 | tf_op jit(solution)/shard_map/grads/pallas_call | solution.py:24
  38.1 0.8 %collective-permute-done.10.y_ref = bf16[528,128]{1,0:T(8,128)(2,1)S(1)} collective-permute-done((bf16[528,128]{1,0:T(8,128)(2,1)S(1)}, bf16[528,128]{1,0:T(8,128)(2,1)S(1)}, u32[]{:S(2)}, u32[]{:S(2)}) %collective-permute-start.10) | collective-permute-done | bytes 135200 | tf_op jit(solution)/shard_map/ppermute | solution.py:442
  38.9 0.2 join.3
  39.2 0.5 %collective-permute-start.14 = (bf16[272,128]{1,0:T(8,128)(2,1)S(1)}, bf16[272,128]{1,0:T(8,128)(2,1)S(1)}, u32[]{:S(2)}, u32[]{:S(2)}) collective-permute-start(bf16[272,128]{1,0:T(8,128)(2,1)S(1)} %get-tuple-element.58), channel_id=1, source_target_pairs={{0,4},{4,0},{8,12},{12,8},{16,20},{20,16},{24,28},{28,24},{1,5},{5... | collective-permute-start | bytes 208904 | tf_op jit(solution)/shard_map/ppermute | solution.py:454
  39.7 3.6 %collective-permute-done.15.refs_2_ = bf16[128,1024]{1,0:T(8,128)(2,1)S(1)} collective-permute-done((bf16[128,1024]{1,0:T(8,128)(2,1)S(1)}, bf16[128,1024]{1,0:T(8,128)(2,1)S(1)}, u32[]{:S(2)}, u32[]{:S(2)}) %collective-permute-start.15) | collective-permute-done | bytes 262176 | tf_op jit(solution)/shard_map/ppermute | solution.py:481
  43.3 1.4 %last.1 = (bf16[128,1024]{1,0:T(8,128)(2,1)}, bf16[128,1024]{1,0:T(8,128)(2,1)}) custom-call(s32[1]{0:T(128)} %bitcast.1.refs_0_.pos_ref, f32[8,128]{1,0:T(8,128)S(1)} %broadcast.10.facts_ref, bf16[128,1024]{1,0:T(8,128)(2,1)S(1)} %copy-done.1, bf16[128,1024]{1,0:T(8,128)(2,1)S(1)} %copy-done.2, f32[4,136,128]{2,1,0:T(8,128)S(1)} %get-tuple-element.55.own_ref, ...), custom_call_target="tpu_custom_call" | custom-call | flops 1150000000 | bytes 1024 | tf_op jit(solution)/shard_map/last/pallas_call | solution.py:24
  44.7 0.8 %add_convert_fusion = bf16[128,1024]{1,0:T(8,128)(2,1)} fusion(bf16[128,1024]{1,0:T(8,128)(2,1)S(1)} %collective-permute-done.16, f32[128,1024]{1,0:T(8,128)S(1)} %get-tuple-element.60, bf16[128,1024]{1,0:T(8,128)(2,1)S(1)} %collective-permute-done.15.refs_2_), kind=kLoop, calls=%fused_computation | loop fusion | flops 655360 | bytes 1310720 | tf_op jit(solution)/shard_map/convert_element_type | solution.py:595
  (37 shorter events, 0.8 us)
Async XLA Ops:
  0.6 16.1 %collective-permute-start.4 = (bf16[128,1024]{1,0:T(8,128)(2,1)}, bf16[128,1024]{1,0:T(8,128)(2,1)S(1)}, u32[]{:S(2)}, u32[]{:S(2)}) collective-permute-start(bf16[128,1024]{1,0:T(8,128)(2,1)} %refs_0_.2), channel_id=1, source_target_pairs={{0,3},{1,2},{2,1},{3,0},{4,7},{5,6},{6,5},{7,4},{8,11},{9,10},{10,... | collective-permute-start | bytes 786440 | tf_op jit(solution)/shard_map/ppermute | solution.py:481
  7.0 1.0 %copy-start.1 = (bf16[128,1024]{1,0:T(8,128)(2,1)S(1)}, bf16[128,1024]{1,0:T(8,128)(2,1)}, u32[]{:S(2)}) copy-start(bf16[128,1024]{1,0:T(8,128)(2,1)} %k_ref.7) | copy-start | bytes 786436
  7.1 1.0 %copy-start.2 = (bf16[128,1024]{1,0:T(8,128)(2,1)S(1)}, bf16[128,1024]{1,0:T(8,128)(2,1)}, u32[]{:S(2)}) copy-start(bf16[128,1024]{1,0:T(8,128)(2,1)} %v_ref.7) | copy-start | bytes 786436
  7.1 1.7 %copy-start.3 = (bf16[128,1024]{1,0:T(8,128)(2,1)S(1)}, bf16[128,1024]{1,0:T(8,128)(2,1)}, u32[]{:S(2)}) copy-start(bf16[128,1024]{1,0:T(8,128)(2,1)} %refs_0_.2) | copy-start | bytes 786436
  7.1 6.9 %copy-start = (bf16[128,1024]{1,0:T(8,128)(2,1)S(1)}, bf16[128,1024]{1,0:T(8,128)(2,1)}, u32[]{:S(2)}) copy-start(bf16[128,1024]{1,0:T(8,128)(2,1)} %q_ref.5) | copy-start | bytes 786436
  7.1 10.6 %slice-start = ((s8[8388608]{0:T(1024)(128)(4,1)}), s8[4194304]{0:T(1024)(128)(4,1)S(1)}, s32[]{:S(2)}) async-start(s8[8388608]{0:T(1024)(128)(4,1)} %bitcast.6), calls=%async_computation | async-start | bytes 8388608
  8.1 9.6 %slice-start.1 = ((s8[8388608]{0:T(1024)(128)(4,1)}), s8[4194304]{0:T(1024)(128)(4,1)S(1)}, s32[]{:S(2)}) async-start(s8[8388608]{0:T(1024)(128)(4,1)} %bitcast.6), calls=%async_computation.1 | async-start | bytes 8388608
  8.6 13.4 %copy-start.4 = (f32[8]{0:T(128)S(1)}, f32[8]{0:T(128)}, u32[]{:S(2)}) copy-start(f32[8]{0:T(128)} %gate_ref.3) | copy-start | bytes 100
  8.6 1.4 %collective-permute-start = (bf16[528,128]{1,0:T(8,128)(2,1)S(1)}, bf16[528,128]{1,0:T(8,128)(2,1)S(1)}, u32[]{:S(2)}, u32[]{:S(2)}) collective-permute-start(bf16[528,128]{1,0:T(8,128)(2,1)S(1)} %get-tuple-element.35), channel_id=1, source_target_pairs={{0,4},{4,0},{8,12},{12,8},{16,20},{20,16},{24,28},{28,24},{1,5},{5... | collective-permute-start | bytes 405512 | tf_op jit(solution)/shard_map/ppermute | solution.py:431
  8.7 12.0 %collective-permute-start.6 = (bf16[128,1024]{1,0:T(8,128)(2,1)S(1)}, bf16[128,1024]{1,0:T(8,128)(2,1)S(1)}, u32[]{:S(2)}, u32[]{:S(2)}) collective-permute-start(bf16[128,1024]{1,0:T(8,128)(2,1)S(1)} %copy-done.3), channel_id=1, source_target_pairs={{0,1},{1,0},{2,3},{3,2},{4,5},{5,4},{6,7},{7,6},{8,9},{9,8},{10,11... | collective-permute-start | bytes 786440 | tf_op jit(solution)/shard_map/ppermute | solution.py:481
  10.5 8.1 %collective-permute-start.3 = (bf16[528,128]{1,0:T(8,128)(2,1)S(1)}, bf16[528,128]{1,0:T(8,128)(2,1)S(1)}, u32[]{:S(2)}, u32[]{:S(2)}) collective-permute-start(bf16[528,128]{1,0:T(8,128)(2,1)S(1)} %pair.2.after_ref), channel_id=1, source_target_pairs={{0,24},{4,28},{8,16},{12,20},{16,8},{20,12},{24,0},{28,4},{1,25},{... | collective-permute-start | bytes 405512 | tf_op jit(solution)/shard_map/ppermute | solution.py:442
  13.0 7.0 %collective-permute-start.2 = (bf16[528,128]{1,0:T(8,128)(2,1)S(1)}, bf16[528,128]{1,0:T(8,128)(2,1)S(1)}, u32[]{:S(2)}, u32[]{:S(2)}) collective-permute-start(bf16[528,128]{1,0:T(8,128)(2,1)S(1)} %pair.2.after_ref), channel_id=1, source_target_pairs={{0,16},{4,20},{8,24},{12,28},{16,0},{20,4},{24,8},{28,12},{1,17},{... | collective-permute-start | bytes 405512 | tf_op jit(solution)/shard_map/ppermute | solution.py:442
  13.5 6.6 %collective-permute-start.1 = (bf16[528,128]{1,0:T(8,128)(2,1)S(1)}, bf16[528,128]{1,0:T(8,128)(2,1)S(1)}, u32[]{:S(2)}, u32[]{:S(2)}) collective-permute-start(bf16[528,128]{1,0:T(8,128)(2,1)S(1)} %pair.2.after_ref), channel_id=1, source_target_pairs={{0,8},{4,12},{8,0},{12,4},{16,24},{20,28},{24,16},{28,20},{1,9},{5... | collective-permute-start | bytes 405512 | tf_op jit(solution)/shard_map/ppermute | solution.py:442
  16.8 9.2 %collective-permute-start.7 = (bf16[128,1024]{1,0:T(8,128)(2,1)S(1)}, bf16[128,1024]{1,0:T(8,128)(2,1)S(1)}, u32[]{:S(2)}, u32[]{:S(2)}) collective-permute-start(bf16[128,1024]{1,0:T(8,128)(2,1)S(1)} %pass_on.1.refs_2_), channel_id=1, source_target_pairs={{0,1},{1,0},{2,3},{3,2},{4,5},{5,4},{6,7},{7,6},{8,9},{9,8},{10,11... | collective-permute-start | bytes 786440 | tf_op jit(solution)/shard_map/ppermute | solution.py:481
  20.6 1.4 %collective-permute-start.5 = (bf16[528,128]{1,0:T(8,128)(2,1)S(1)}, bf16[528,128]{1,0:T(8,128)(2,1)S(1)}, u32[]{:S(2)}, u32[]{:S(2)}) collective-permute-start(bf16[528,128]{1,0:T(8,128)(2,1)S(1)} %get-tuple-element.38), channel_id=1, source_target_pairs={{0,4},{4,0},{8,12},{12,8},{16,20},{20,16},{24,28},{28,24},{1,5},{5... | collective-permute-start | bytes 405512 | tf_op jit(solution)/shard_map/ppermute | solution.py:454
  23.6 9.3 %collective-permute-start.12 = (bf16[128,1024]{1,0:T(8,128)(2,1)S(1)}, bf16[128,1024]{1,0:T(8,128)(2,1)S(1)}, u32[]{:S(2)}, u32[]{:S(2)}) collective-permute-start(bf16[128,1024]{1,0:T(8,128)(2,1)S(1)} %get-tuple-element.53), channel_id=1, source_target_pairs={{0,1},{1,0},{2,3},{3,2},{4,5},{5,4},{6,7},{7,6},{8,9},{9,8},{10,11... | collective-permute-start | bytes 786440 | tf_op jit(solution)/shard_map/ppermute | solution.py:481
  27.1 2.1 %collective-permute-start.8 = (bf16[528,128]{1,0:T(8,128)(2,1)S(1)}, bf16[528,128]{1,0:T(8,128)(2,1)S(1)}, u32[]{:S(2)}, u32[]{:S(2)}) collective-permute-start(bf16[528,128]{1,0:T(8,128)(2,1)S(1)} %get-tuple-element.46), channel_id=1, source_target_pairs={{0,4},{4,0},{8,12},{12,8},{16,20},{20,16},{24,28},{28,24},{1,5},{5... | collective-permute-start | bytes 405512 | tf_op jit(solution)/shard_map/ppermute | solution.py:431
  28.0 15.3 %collective-permute-start.15 = (bf16[128,1024]{1,0:T(8,128)(2,1)S(1)}, bf16[128,1024]{1,0:T(8,128)(2,1)S(1)}, u32[]{:S(2)}, u32[]{:S(2)}) collective-permute-start(bf16[128,1024]{1,0:T(8,128)(2,1)S(1)} %get-tuple-element.47.refs_1_), channel_id=1, source_target_pairs={{0,1},{1,0},{2,3},{3,2},{4,5},{5,4},{6,7},{7,6},{8,9},{9,8},{10,11... | collective-permute-start | bytes 786440 | tf_op jit(solution)/shard_map/ppermute | solution.py:481
  29.3 8.7 %collective-permute-start.11 = (bf16[528,128]{1,0:T(8,128)(2,1)S(1)}, bf16[528,128]{1,0:T(8,128)(2,1)S(1)}, u32[]{:S(2)}, u32[]{:S(2)}) collective-permute-start(bf16[528,128]{1,0:T(8,128)(2,1)S(1)} %pair.3.after_ref), channel_id=1, source_target_pairs={{0,24},{4,28},{8,16},{12,20},{16,8},{20,12},{24,0},{28,4},{1,25},{... | collective-permute-start | bytes 405512 | tf_op jit(solution)/shard_map/ppermute | solution.py:442
  31.1 7.8 %collective-permute-start.10 = (bf16[528,128]{1,0:T(8,128)(2,1)S(1)}, bf16[528,128]{1,0:T(8,128)(2,1)S(1)}, u32[]{:S(2)}, u32[]{:S(2)}) collective-permute-start(bf16[528,128]{1,0:T(8,128)(2,1)S(1)} %pair.3.after_ref), channel_id=1, source_target_pairs={{0,16},{4,20},{8,24},{12,28},{16,0},{20,4},{24,8},{28,12},{1,17},{... | collective-permute-start | bytes 405512 | tf_op jit(solution)/shard_map/ppermute | solution.py:442
  32.4 6.5 %collective-permute-start.9 = (bf16[528,128]{1,0:T(8,128)(2,1)S(1)}, bf16[528,128]{1,0:T(8,128)(2,1)S(1)}, u32[]{:S(2)}, u32[]{:S(2)}) collective-permute-start(bf16[528,128]{1,0:T(8,128)(2,1)S(1)} %pair.3.after_ref), channel_id=1, source_target_pairs={{0,8},{4,12},{8,0},{12,4},{16,24},{20,28},{24,16},{28,20},{1,9},{5... | collective-permute-start | bytes 405512 | tf_op jit(solution)/shard_map/ppermute | solution.py:442
  33.4 11.3 %collective-permute-start.16 = (bf16[128,1024]{1,0:T(8,128)(2,1)S(1)}, bf16[128,1024]{1,0:T(8,128)(2,1)S(1)}, u32[]{:S(2)}, u32[]{:S(2)}) collective-permute-start(bf16[128,1024]{1,0:T(8,128)(2,1)S(1)} %project_add.1.refs_0_), channel_id=1, source_target_pairs={{0,3},{1,2},{2,1},{3,0},{4,7},{5,6},{6,5},{7,4},{8,11},{9,10},{10,... | collective-permute-start | bytes 786440 | tf_op jit(solution)/shard_map/ppermute | solution.py:481
  39.1 4.2 %collective-permute-start.13 = (bf16[272,128]{1,0:T(8,128)(2,1)S(1)}, bf16[272,128]{1,0:T(8,128)(2,1)S(1)}, u32[]{:S(2)}, u32[]{:S(2)}) collective-permute-start(bf16[272,128]{1,0:T(8,128)(2,1)S(1)} %get-tuple-element.57), channel_id=1, source_target_pairs={{0,4},{4,0},{8,12},{12,8},{16,20},{20,16},{24,28},{28,24},{1,5},{5... | collective-permute-start | bytes 208904 | tf_op jit(solution)/shard_map/ppermute | solution.py:454
  39.2 4.1 %collective-permute-start.14 = (bf16[272,128]{1,0:T(8,128)(2,1)S(1)}, bf16[272,128]{1,0:T(8,128)(2,1)S(1)}, u32[]{:S(2)}, u32[]{:S(2)}) collective-permute-start(bf16[272,128]{1,0:T(8,128)(2,1)S(1)} %get-tuple-element.58), channel_id=1, source_target_pairs={{0,4},{4,0},{8,12},{12,8},{16,20},{20,16},{24,28},{28,24},{1,5},{5... | collective-permute-start | bytes 208904 | tf_op jit(solution)/shard_map/ppermute | solution.py:454

commit v9 on v8

--- a/solution.py
+++ b/solution.py
@@ -385,7 +385,12 @@
 def last_kernel(
     heads, packed, far, pos_ref, facts_ref, k_ref, v_ref, own_ref, key_ref, value_ref, *refs
 ):
-    far_refs, (key_out, value_out) = refs[:far], refs[-2:]
+    far_refs, sum_refs = refs[:far], refs[far:-2]
+    key_out, value_out = refs[-2:]
+    if sum_refs:
+        own_sum, near_sum, key_out = sum_refs
+        value_out, partial_ref = refs[-2:]
+        partial_ref[...] = own_sum[...] + near_sum[...].astype(F32)
     live = live_rows(facts_ref, k_ref.shape[0])
     carries, _ = load_carries(own_ref, far_refs, packed, False)
     for kept, i, h in by_half(heads, pos_ref):
@@ -520,6 +525,11 @@
             token_kernel, [jax.ShapeDtypeStruct((8, DH), F32)], [ANY] * 2, [grad_1, own],
             0.5, "arrived",
         )
+        kept["total"] = call(
+            functools.partial(more_kernel, (3,)), [flat], [SMEM] + [VMEM] * 3 + [ANY],
+            [z, grad_3, out_weight, kept["total"], own], 0.01, "unproject_end",
+        )[0]
+        orders = [*orders, kept["total"]]
     outs = call(
         functools.partial(read_kernel, heads, direct, paired),
         [low, flat, jax.ShapeDtypeStruct((heads, DH, 2 * DH), BF16),
@@ -532,8 +542,8 @@
     if direct:
         sum_2 = swap(outs[6], 1)
         total = call(
-            functools.partial(more_kernel, (1, 3)), [flat], [SMEM] + [VMEM] * 4 + [ANY],
-            [z, grad_1, grad_3, out_weight, kept["total"], mixed], 0.01, "unproject_more",
+            functools.partial(more_kernel, (1,)), [flat], [SMEM] + [VMEM] * 3 + [ANY],
+            [z, grad_1, out_weight, kept["total"], mixed], 0.01, "unproject_near",
         )[0]
         grads_in = [kept["grad_2"], total, out_weight]
     else:
@@ -582,17 +592,15 @@
 
     own, far = scan_states(keep, [give], pos, heads, False, project_rest, beside_back)
     query_grad, key_part, value_part = kept["grads"]
-    orders = [kept["from_1"]] if direct else []
-    key_grad, value_grad = call(
+    sums = [kept["mine"], kept["from_1"]] if direct else []
+    key_grad, value_grad, *partial = call(
         functools.partial(last_kernel, heads, paired, len(far)),
-        [low, low],
-        [SMEM] + [VMEM] * (6 + len(far)) + [ANY] * len(orders),
-        [pos, facts, keys, values, own, key_part, value_part, *far, *orders], 1, "last",
+        [low, low] + [part_full] * direct,
+        [SMEM] + [VMEM] * (6 + len(far) + len(sums)),
+        [pos, facts, keys, values, own, key_part, value_part, *far, *sums], 1, "last",
     )
     if direct:
-        kept["mine"], key_grad = lax.optimization_barrier((kept["mine"], key_grad))
-        output = kept["mine"] + kept["from_1"].astype(F32) + kept["from_3"].astype(F32)
-        output = output.astype(BF16)
+        output = (partial[0] + kept["from_3"].astype(F32)).astype(BF16)
     return (output, query_grad, key_grad, value_grad)
 
 

time: 45.7 us -> 45.7 us (level)
    ppermute x6, waiting for transfers between devices: 3.62 us -> 4.9 us  [swap(): return lax.ppermute(array, 'head', [(s, s ^ way) for s in range(groups)])]
    ppermute x3, waiting for transfers between devices: 1.32 us -> 0.48 us  [scan_states(): return (own, [lax.ppermute(part, 'seq', pairs) for part in passed])]
    ppermute x6, waiting for transfers between devices: 2.38 us -> 1.83 us  [scan_states(): lax.ppermute(sent, 'seq', [(s, s ^ way) for s in range(count)])]
    pallas_call x17 -> x18, Pallas kernels: 15.8 us -> 16 us  [call(): pl.pallas_call(kernel, out_shape=outs, in_specs=in_specs, out_specs=[VMEM...]
  transfers between devices with their start and end apart: 17 -> 17, of which waited for: 6 -> 7; matrix products, arithmetic and copies ran while one was open for 0% -> 0% of each run, Pallas kernels for 35% -> 35%
where the time goes in v9:
time: 45.7 us; the launch traced here: 45.5 us
  starting transfers between devices  17.1 us (37%)
  Pallas kernels  16 us (35%)
  waiting for transfers between devices  8.46 us (19%)
  between operations  2.18 us (5%)
  local copies, waits for them, and re-layouts  0.98 us (2%)
  other arithmetic  0.77 us (2%)
    pallas_call x18, Pallas kernels, call(): pl.pallas_call(kernel, out_shape=outs, in_specs=in_specs, out_specs=[VMEM...  16 us
    ppermute x6, starting transfers between devices, swap(): return lax.ppermute(array, 'head', [(s, s ^ way) for s in range(groups)])  9.24 us
    ppermute x6, starting transfers between devices, scan_states(): lax.ppermute(sent, 'seq', [(s, s ^ way) for s in range(count)])  7.11 us
    ppermute x6, waiting for transfers between devices, swap(): return lax.ppermute(array, 'head', [(s, s ^ way) for s in range(groups)])  4.9 us
    ppermute x6, waiting for transfers between devices, scan_states(): lax.ppermute(sent, 'seq', [(s, s ^ way) for s in range(count)])  1.83 us
    ppermute x2, waiting for transfers between devices, scan_states(): others = [lax.ppermute(part, 'seq', pairs) for part in give]  1.25 us
    unnamed x14, local copies, waits for them, and re-layouts  0.91 us
  transfers between devices with their start and end apart: 17, of which 7 were waited for; matrix products, arithmetic and copies ran while one was open for 0% of the time, Pallas kernels for 35%

profile of v9, /device:TPU:0, one launch (start us, length us, event | category | flops | bytes accessed | tf_op | source)
XLA Modules:
  0.0 45.5 jit_solution(11486067523699089553)
XLA Ops:
  0.6 5.1 %collective-permute-start.4 = (bf16[128,1024]{1,0:T(8,128)(2,1)}, bf16[128,1024]{1,0:T(8,128)(2,1)S(1)}, u32[]{:S(2)}, u32[]{:S(2)}) collective-permute-start(bf16[128,1024]{1,0:T(8,128)(2,1)} %refs_0_.2), channel_id=1, source_target_pairs={{0,3},{1,2},{2,1},{3,0},{4,7},{5,6},{6,5},{7,4},{8,11},{9,10},{10,... | collective-permute-start | bytes 786440 | tf_op jit(solution)/shard_map/ppermute | solution.py:486
  7.2 0.8 %copy-done.1 = bf16[128,1024]{1,0:T(8,128)(2,1)S(1)} copy-done((bf16[128,1024]{1,0:T(8,128)(2,1)S(1)}, bf16[128,1024]{1,0:T(8,128)(2,1)}, u32[]{:S(2)}) %copy-start.1) | copy-done | bytes 262168
  8.1 0.5 %state.1 = (f32[4,136,128]{2,1,0:T(8,128)S(1)}, bf16[528,128]{1,0:T(8,128)(2,1)S(1)}) custom-call(s32[1]{0:T(128)} %bitcast.refs_0_.pos_ref, s32[1]{0:T(128)} %bitcast.3.z_ref, f32[8,128]{1,0:T(8,128)S(1)} %broadcast.10.facts_ref, bf16[128,1024]{1,0:T(8,128)(2,1)S(1)} %copy-done.1, bf16[128,1024]{1,0:T(8,128)(2,1)S(1)} %copy-done.2, f32[8,128]{1,0:T(8,128)S(1)} %warm.1.after_ref), custom_call_target="tpu_custom_call" | custom-call | flops 3449999872 | bytes 1024 | tf_op jit(solution)/shard_map/state/pallas_call | solution.py:24
  8.8 1.3 %collective-permute-done.refs_0_ = bf16[528,128]{1,0:T(8,128)(2,1)S(1)} collective-permute-done((bf16[528,128]{1,0:T(8,128)(2,1)S(1)}, bf16[528,128]{1,0:T(8,128)(2,1)S(1)}, u32[]{:S(2)}, u32[]{:S(2)}) %collective-permute-start) | collective-permute-done | bytes 135200 | tf_op jit(solution)/shard_map/ppermute | solution.py:436
  10.1 0.4 pair.2.after_ref
  10.5 2.5 %collective-permute-start.3 = (bf16[528,128]{1,0:T(8,128)(2,1)S(1)}, bf16[528,128]{1,0:T(8,128)(2,1)S(1)}, u32[]{:S(2)}, u32[]{:S(2)}) collective-permute-start(bf16[528,128]{1,0:T(8,128)(2,1)S(1)} %pair.2.after_ref), channel_id=1, source_target_pairs={{0,24},{4,28},{8,16},{12,20},{16,8},{20,12},{24,0},{28,4},{1,25},{... | collective-permute-start | bytes 405512 | tf_op jit(solution)/shard_map/ppermute | solution.py:447
  13.0 0.5 %collective-permute-start.2 = (bf16[528,128]{1,0:T(8,128)(2,1)S(1)}, bf16[528,128]{1,0:T(8,128)(2,1)S(1)}, u32[]{:S(2)}, u32[]{:S(2)}) collective-permute-start(bf16[528,128]{1,0:T(8,128)(2,1)S(1)} %pair.2.after_ref), channel_id=1, source_target_pairs={{0,16},{4,20},{8,24},{12,28},{16,0},{20,4},{24,8},{28,12},{1,17},{... | collective-permute-start | bytes 405512 | tf_op jit(solution)/shard_map/ppermute | solution.py:447
  13.5 0.5 %collective-permute-start.1 = (bf16[528,128]{1,0:T(8,128)(2,1)S(1)}, bf16[528,128]{1,0:T(8,128)(2,1)S(1)}, u32[]{:S(2)}, u32[]{:S(2)}) collective-permute-start(bf16[528,128]{1,0:T(8,128)(2,1)S(1)} %pair.2.after_ref), channel_id=1, source_target_pairs={{0,8},{4,12},{8,0},{12,4},{16,24},{20,28},{24,16},{28,20},{1,9},{5... | collective-permute-start | bytes 405512 | tf_op jit(solution)/shard_map/ppermute | solution.py:447
  14.0 2.7 %local.1 = (bf16[8,128,128]{2,1,0:T(8,128)(2,1)S(1)}, f32[128,1024]{1,0:T(8,128)S(1)}) custom-call(f32[8,128]{1,0:T(8,128)S(1)} %broadcast.10.facts_ref, bf16[128,1024]{1,0:T(8,128)(2,1)S(1)} %copy-done, bf16[128,1024]{1,0:T(8,128)(2,1)S(1)} %copy-done.1, bf16[128,1024]{1,0:T(8,128)(2,1)S(1)} %copy-done.2, bf16[528,128]{1,0:T(8,128)(2,1)S(1)} %pair.2.after_ref), custom_call_target="tpu_custom_call" | custom-call | flops 11500000 | bytes 1024 | tf_op jit(solution)/shard_map/local/pallas_call | solution.py:24
  16.7 0.9 %collective-permute-start.7 = (bf16[128,1024]{1,0:T(8,128)(2,1)S(1)}, bf16[128,1024]{1,0:T(8,128)(2,1)S(1)}, u32[]{:S(2)}, u32[]{:S(2)}) collective-permute-start(bf16[128,1024]{1,0:T(8,128)(2,1)S(1)} %pass_on.1.refs_2_), channel_id=1, source_target_pairs={{0,1},{1,0},{2,3},{3,2},{4,5},{5,4},{6,7},{7,6},{8,9},{9,8},{10,11... | collective-permute-start | bytes 786440 | tf_op jit(solution)/shard_map/ppermute | solution.py:486
  17.7 0.8 %unproject_own.1.refs_1_.refs_2_ = f32[128,1024]{1,0:T(8,128)S(1)} custom-call(s32[1]{0:T(128)} %bitcast.3.z_ref, bf16[128,1024]{1,0:T(8,128)(2,1)S(1)} %copy-done.3, bf16[1024,4096]{1,0:T(8,128)(2,1)S(1)} %bitcast.7, bf16[128,1024]{1,0:T(8,128)(2,1)S(1)} %pass_on.1.refs_2_), custom_call_target="tpu_custom_call" | custom-call | flops 920000000 | bytes 1024 | tf_op jit(solution)/shard_map/unproject_own/pallas_call | solution.py:24
  18.5 1.4 %collective-permute-done.2.y_ref = bf16[528,128]{1,0:T(8,128)(2,1)S(1)} collective-permute-done((bf16[528,128]{1,0:T(8,128)(2,1)S(1)}, bf16[528,128]{1,0:T(8,128)(2,1)S(1)}, u32[]{:S(2)}, u32[]{:S(2)}) %collective-permute-start.2) | collective-permute-done | bytes 135200 | tf_op jit(solution)/shard_map/ppermute | solution.py:447
  20.0 0.5 %join.2 = (f32[4,136,128]{2,1,0:T(8,128)S(1)}, bf16[528,128]{1,0:T(8,128)(2,1)S(1)}) custom-call(s32[1]{0:T(128)} %bitcast.refs_0_.pos_ref, bf16[528,128]{1,0:T(8,128)(2,1)S(1)} %collective-permute-done.1.x_ref, bf16[528,128]{1,0:T(8,128)(2,1)S(1)} %collective-permute-done.2.y_ref, bf16[528,128]{1,0:T(8,128)(2,1)S(1)} %collective-permute-done.3.d_ref, ...), custom_call_target="tpu_custom_call" | custom-call | flops 11500000 | bytes 1024 | tf_op jit(solution)/shard_map/join/pallas_call | solution.py:24
  20.7 0.8 %unproject_end.1.refs_2_ = f32[128,1024]{1,0:T(8,128)S(1)} custom-call(s32[1]{0:T(128)} %bitcast.3.z_ref, bf16[128,1024]{1,0:T(8,128)(2,1)S(1)} %collective-permute-done.4.block_ref.refs_0_, bf16[1024,4096]{1,0:T(8,128)(2,1)S(1)} %bitcast.7, f32[128,1024]{1,0:T(8,128)S(1)} %unproject_own.1.refs_1_.refs_2_, ...), custom_call_target="tpu_custom_call" | custom-call | flops 11500000 | bytes 1024 | tf_op jit(solution)/shard_map/unproject_end/pallas_call | solution.py:24
  21.5 0.5 %collective-permute-done.5.far_ref = bf16[528,128]{1,0:T(8,128)(2,1)S(1)} collective-permute-done((bf16[528,128]{1,0:T(8,128)(2,1)S(1)}, bf16[528,128]{1,0:T(8,128)(2,1)S(1)}, u32[]{:S(2)}, u32[]{:S(2)}) %collective-permute-start.5) | collective-permute-done | bytes 135200 | tf_op jit(solution)/shard_map/ppermute | solution.py:459
  22.0 1.6 %read.1 = (bf16[128,1024]{1,0:T(8,128)(2,1)S(1)}, f32[128,1024]{1,0:T(8,128)S(1)}, bf16[8,128,256]{2,1,0:T(8,128)(2,1)S(1)}, f32[8,8,128]{2,1,0:T(8,128)S(1)}, b...) custom-call(s32[1]{0:T(128)} %bitcast.refs_0_.pos_ref, s32[1]{0:T(128)} %bitcast.3.z_ref, ...), custom_call_target="tpu_custom_call" | custom-call | flops 11500000 | bytes 1024 | tf_op jit(solution)/shard_map/read/pallas_call | solution.py:24
  23.6 0.8 %collective-permute-start.12 = (bf16[128,1024]{1,0:T(8,128)(2,1)S(1)}, bf16[128,1024]{1,0:T(8,128)(2,1)S(1)}, u32[]{:S(2)}, u32[]{:S(2)}) collective-permute-start(bf16[128,1024]{1,0:T(8,128)(2,1)S(1)} %get-tuple-element.51), channel_id=1, source_target_pairs={{0,1},{1,0},{2,3},{3,2},{4,5},{5,4},{6,7},{7,6},{8,9},{9,8},{10,11... | collective-permute-start | bytes 786440 | tf_op jit(solution)/shard_map/ppermute | solution.py:486
  24.4 0.8 %unproject_near.1.refs_1_ = f32[128,1024]{1,0:T(8,128)S(1)} custom-call(s32[1]{0:T(128)} %bitcast.3.z_ref, bf16[128,1024]{1,0:T(8,128)(2,1)S(1)} %collective-permute-done.6.refs_0_, bf16[1024,4096]{1,0:T(8,128)(2,1)S(1)} %bitcast.7, f32[128,1024]{1,0:T(8,128)S(1)} %unproject_end.1.refs_2_, bf16[128,1024]{1,0:T(8,128)(2,1)S(1)} %get-tuple-element.41.refs_3_.mixed_ref), custom_call_target="tpu_custom_call" | custom-call | flops 11500000 | bytes 1024 | tf_op jit(solution)/shard_map/unproject_near/pallas_call | solution.py:24
  25.3 1.2 %spread.1 = (f32[4,136,128]{2,1,0:T(8,128)S(1)}, bf16[528,128]{1,0:T(8,128)(2,1)S(1)}, bf16[128,1024]{1,0:T(8,128)(2,1)S(1)}, f32[8,128,1]{2,1,0:T(8,128)S(1)}, bf16[128,1024]{1,0:T(8,128)(2,1)S(1)}) custom-call(s32[1]{0:T(128)} %bitcast.refs_0_.pos_ref, s32[1]{0:T(128)} %bitcast.3.z_ref, f32[8,128]{1,0:T(8,128)S(1)} %broadcast.10.facts_ref, ...), custom_call_target="tpu_custom_call" | custom-call | flops 11500000 | bytes 1024 | tf_op jit(solution)/shard_map/spread/pallas_call | solution.py:24
  26.5 0.7 %project_rest.1 = (bf16[128,1024]{1,0:T(8,128)(2,1)S(1)}, f32[128,1024]{1,0:T(8,128)S(1)}) custom-call(s32[1]{0:T(128)} %bitcast.3.z_ref, bf16[128,1024]{1,0:T(8,128)(2,1)S(1)} %get-tuple-element.41.refs_3_.mixed_ref, bf16[1024,4096]{1,0:T(8,128)(2,1)S(1)} %bitcast.7, bf16[128,1024]{1,0:T(8,128)(2,1)S(1)} %get-tuple-element.44.after_ref.numer_ref), custom_call_target="tpu_custom_call" | custom-call | flops 11500000 | bytes 1024 | tf_op jit(solution)/shard_map/project_rest/pallas_call | solution.py:24
  27.3 1.3 %collective-permute-start.15 = (bf16[128,1024]{1,0:T(8,128)(2,1)S(1)}, bf16[128,1024]{1,0:T(8,128)(2,1)S(1)}, u32[]{:S(2)}, u32[]{:S(2)}) collective-permute-start(bf16[128,1024]{1,0:T(8,128)(2,1)S(1)} %get-tuple-element.45.refs_1_), channel_id=1, source_target_pairs={{0,1},{1,0},{2,3},{3,2},{4,5},{5,4},{6,7},{7,6},{8,9},{9,8},{10,11... | collective-permute-start | bytes 786440 | tf_op jit(solution)/shard_map/ppermute | solution.py:486
  28.7 1.7 %collective-permute-start.11 = (bf16[528,128]{1,0:T(8,128)(2,1)S(1)}, bf16[528,128]{1,0:T(8,128)(2,1)S(1)}, u32[]{:S(2)}, u32[]{:S(2)}) collective-permute-start(bf16[528,128]{1,0:T(8,128)(2,1)S(1)} %pair.3.after_ref), channel_id=1, source_target_pairs={{0,24},{4,28},{8,16},{12,20},{16,8},{20,12},{24,0},{28,4},{1,25},{... | collective-permute-start | bytes 405512 | tf_op jit(solution)/shard_map/ppermute | solution.py:447
  30.4 1.3 %collective-permute-start.10 = (bf16[528,128]{1,0:T(8,128)(2,1)S(1)}, bf16[528,128]{1,0:T(8,128)(2,1)S(1)}, u32[]{:S(2)}, u32[]{:S(2)}) collective-permute-start(bf16[528,128]{1,0:T(8,128)(2,1)S(1)} %pair.3.after_ref), channel_id=1, source_target_pairs={{0,16},{4,20},{8,24},{12,28},{16,0},{20,4},{24,8},{28,12},{1,17},{... | collective-permute-start | bytes 405512 | tf_op jit(solution)/shard_map/ppermute | solution.py:447
  31.7 0.5 %collective-permute-start.9 = (bf16[528,128]{1,0:T(8,128)(2,1)S(1)}, bf16[528,128]{1,0:T(8,128)(2,1)S(1)}, u32[]{:S(2)}, u32[]{:S(2)}) collective-permute-start(bf16[528,128]{1,0:T(8,128)(2,1)S(1)} %pair.3.after_ref), channel_id=1, source_target_pairs={{0,8},{4,12},{8,0},{12,4},{16,24},{20,28},{24,16},{28,20},{1,9},{5... | collective-permute-start | bytes 405512 | tf_op jit(solution)/shard_map/ppermute | solution.py:447
  32.2 0.6 %collective-permute-done.12.more_ref = bf16[128,1024]{1,0:T(8,128)(2,1)S(1)} collective-permute-done((bf16[128,1024]{1,0:T(8,128)(2,1)S(1)}, bf16[128,1024]{1,0:T(8,128)(2,1)S(1)}, u32[]{:S(2)}, u32[]{:S(2)}) %collective-permute-start.12) | collective-permute-done | bytes 262176 | tf_op jit(solution)/shard_map/ppermute | solution.py:486
  32.8 0.5 %project_add.1.refs_0_ = bf16[128,1024]{1,0:T(8,128)(2,1)S(1)} custom-call(s32[1]{0:T(128)} %bitcast.3.z_ref, bf16[128,1024]{1,0:T(8,128)(2,1)S(1)} %get-tuple-element.41.refs_3_.mixed_ref, bf16[1024,4096]{1,0:T(8,128)(2,1)S(1)} %bitcast.7, bf16[128,1024]{1,0:T(8,128)(2,1)S(1)} %collective-permute-done.12.more_ref, bf16[528,128]{1,0:T(8,128)(2,1)S(1)} %pair.3.after_ref), custom_call_target="tpu_custom_call" | custom-call | flops 11500000 | bytes 1024 | tf_op jit(solution)/shard_map/project_add/pallas_call | solution.py:24
  33.3 1.0 %collective-permute-start.16 = (bf16[128,1024]{1,0:T(8,128)(2,1)S(1)}, bf16[128,1024]{1,0:T(8,128)(2,1)S(1)}, u32[]{:S(2)}, u32[]{:S(2)}) collective-permute-start(bf16[128,1024]{1,0:T(8,128)(2,1)S(1)} %project_add.1.refs_0_), channel_id=1, source_target_pairs={{0,3},{1,2},{2,1},{3,0},{4,7},{5,6},{6,5},{7,4},{8,11},{9,10},{10,... | collective-permute-start | bytes 786440 | tf_op jit(solution)/shard_map/ppermute | solution.py:486
  34.2 3.7 %grads.1 = (bf16[128,1024]{1,0:T(8,128)(2,1)}, f32[128,1024]{1,0:T(8,128)S(1)}, f32[128,1024]{1,0:T(8,128)S(1)}) custom-call(f32[8,128]{1,0:T(8,128)S(1)} %broadcast.10.facts_ref, f32[8]{0:T(128)S(1)} %copy-done.4, bf16[128,1024]{1,0:T(8,128)(2,1)S(1)} %copy-done, bf16[128,1024]{1,0:T(8,128)(2,1)S(1)} %copy-done.1, bf16[128,1024]{1,0:T(8,128)(2,1)S(1)} %copy-done.2, ...), custom_call_target="tpu_custom_call" | custom-call | flops 11500000 | bytes 1024 | tf_op jit(solution)/shard_map/grads/pallas_call | solution.py:24
  38.5 0.5 %collective-permute-start.14 = (bf16[272,128]{1,0:T(8,128)(2,1)S(1)}, bf16[272,128]{1,0:T(8,128)(2,1)S(1)}, u32[]{:S(2)}, u32[]{:S(2)}) collective-permute-start(bf16[272,128]{1,0:T(8,128)(2,1)S(1)} %get-tuple-element.56), channel_id=1, source_target_pairs={{0,4},{4,0},{8,12},{12,8},{16,20},{20,16},{24,28},{28,24},{1,5},{5... | collective-permute-start | bytes 208904 | tf_op jit(solution)/shard_map/ppermute | solution.py:459
  39.0 4.3 %collective-permute-done.15.refs_3_ = bf16[128,1024]{1,0:T(8,128)(2,1)S(1)} collective-permute-done((bf16[128,1024]{1,0:T(8,128)(2,1)S(1)}, bf16[128,1024]{1,0:T(8,128)(2,1)S(1)}, u32[]{:S(2)}, u32[]{:S(2)}) %collective-permute-start.15) | collective-permute-done | bytes 262176 | tf_op jit(solution)/shard_map/ppermute | solution.py:486
  43.3 1.5 %last.1 = (bf16[128,1024]{1,0:T(8,128)(2,1)}, bf16[128,1024]{1,0:T(8,128)(2,1)}, f32[128,1024]{1,0:T(8,128)S(1)}) custom-call(s32[1]{0:T(128)} %bitcast.refs_0_.pos_ref, f32[8,128]{1,0:T(8,128)S(1)} %broadcast.10.facts_ref, bf16[128,1024]{1,0:T(8,128)(2,1)S(1)} %copy-done.1, bf16[128,1024]{1,0:T(8,128)(2,1)S(1)} %copy-done.2, ...), custom_call_target="tpu_custom_call" | custom-call | flops 1150000000 | bytes 1024 | tf_op jit(solution)/shard_map/last/pallas_call | solution.py:24
  44.7 0.8 %add_convert_fusion = bf16[128,1024]{1,0:T(8,128)(2,1)} fusion(f32[128,1024]{1,0:T(8,128)S(1)} %get-tuple-element.58, bf16[128,1024]{1,0:T(8,128)(2,1)S(1)} %collective-permute-done.16), kind=kLoop, calls=%fused_computation | loop fusion | flops 393216 | bytes 1048576 | tf_op jit(solution)/shard_map/convert_element_type | solution.py:603
  (38 shorter events, 1.2 us)
Async XLA Ops:
  0.6 16.1 %collective-permute-start.4 = (bf16[128,1024]{1,0:T(8,128)(2,1)}, bf16[128,1024]{1,0:T(8,128)(2,1)S(1)}, u32[]{:S(2)}, u32[]{:S(2)}) collective-permute-start(bf16[128,1024]{1,0:T(8,128)(2,1)} %refs_0_.2), channel_id=1, source_target_pairs={{0,3},{1,2},{2,1},{3,0},{4,7},{5,6},{6,5},{7,4},{8,11},{9,10},{10,... | collective-permute-start | bytes 786440 | tf_op jit(solution)/shard_map/ppermute | solution.py:486
  7.0 1.0 %copy-start.1 = (bf16[128,1024]{1,0:T(8,128)(2,1)S(1)}, bf16[128,1024]{1,0:T(8,128)(2,1)}, u32[]{:S(2)}) copy-start(bf16[128,1024]{1,0:T(8,128)(2,1)} %k_ref.7) | copy-start | bytes 786436
  7.1 1.0 %copy-start.2 = (bf16[128,1024]{1,0:T(8,128)(2,1)S(1)}, bf16[128,1024]{1,0:T(8,128)(2,1)}, u32[]{:S(2)}) copy-start(bf16[128,1024]{1,0:T(8,128)(2,1)} %v_ref.7) | copy-start | bytes 786436
  7.1 1.6 %copy-start.3 = (bf16[128,1024]{1,0:T(8,128)(2,1)S(1)}, bf16[128,1024]{1,0:T(8,128)(2,1)}, u32[]{:S(2)}) copy-start(bf16[128,1024]{1,0:T(8,128)(2,1)} %refs_0_.2) | copy-start | bytes 786436
  7.1 6.9 %copy-start = (bf16[128,1024]{1,0:T(8,128)(2,1)S(1)}, bf16[128,1024]{1,0:T(8,128)(2,1)}, u32[]{:S(2)}) copy-start(bf16[128,1024]{1,0:T(8,128)(2,1)} %q_ref.5) | copy-start | bytes 786436
  7.1 10.6 %slice-start = ((s8[8388608]{0:T(1024)(128)(4,1)}), s8[4194304]{0:T(1024)(128)(4,1)S(1)}, s32[]{:S(2)}) async-start(s8[8388608]{0:T(1024)(128)(4,1)} %bitcast.6), calls=%async_computation | async-start | bytes 8388608
  8.1 9.6 %slice-start.1 = ((s8[8388608]{0:T(1024)(128)(4,1)}), s8[4194304]{0:T(1024)(128)(4,1)S(1)}, s32[]{:S(2)}) async-start(s8[8388608]{0:T(1024)(128)(4,1)} %bitcast.6), calls=%async_computation.1 | async-start | bytes 8388608
  8.6 1.4 %collective-permute-start = (bf16[528,128]{1,0:T(8,128)(2,1)S(1)}, bf16[528,128]{1,0:T(8,128)(2,1)S(1)}, u32[]{:S(2)}, u32[]{:S(2)}) collective-permute-start(bf16[528,128]{1,0:T(8,128)(2,1)S(1)} %get-tuple-element.34), channel_id=1, source_target_pairs={{0,4},{4,0},{8,12},{12,8},{16,20},{20,16},{24,28},{28,24},{1,5},{5... | collective-permute-start | bytes 405512 | tf_op jit(solution)/shard_map/ppermute | solution.py:436
  8.7 12.8 %collective-permute-start.6 = (bf16[128,1024]{1,0:T(8,128)(2,1)S(1)}, bf16[128,1024]{1,0:T(8,128)(2,1)S(1)}, u32[]{:S(2)}, u32[]{:S(2)}) collective-permute-start(bf16[128,1024]{1,0:T(8,128)(2,1)S(1)} %copy-done.3), channel_id=1, source_target_pairs={{0,1},{1,0},{2,3},{3,2},{4,5},{5,4},{6,7},{7,6},{8,9},{9,8},{10,11... | collective-permute-start | bytes 786440 | tf_op jit(solution)/shard_map/ppermute | solution.py:486
  10.5 8.1 %collective-permute-start.3 = (bf16[528,128]{1,0:T(8,128)(2,1)S(1)}, bf16[528,128]{1,0:T(8,128)(2,1)S(1)}, u32[]{:S(2)}, u32[]{:S(2)}) collective-permute-start(bf16[528,128]{1,0:T(8,128)(2,1)S(1)} %pair.2.after_ref), channel_id=1, source_target_pairs={{0,24},{4,28},{8,16},{12,20},{16,8},{20,12},{24,0},{28,4},{1,25},{... | collective-permute-start | bytes 405512 | tf_op jit(solution)/shard_map/ppermute | solution.py:447
  13.0 7.0 %collective-permute-start.2 = (bf16[528,128]{1,0:T(8,128)(2,1)S(1)}, bf16[528,128]{1,0:T(8,128)(2,1)S(1)}, u32[]{:S(2)}, u32[]{:S(2)}) collective-permute-start(bf16[528,128]{1,0:T(8,128)(2,1)S(1)} %pair.2.after_ref), channel_id=1, source_target_pairs={{0,16},{4,20},{8,24},{12,28},{16,0},{20,4},{24,8},{28,12},{1,17},{... | collective-permute-start | bytes 405512 | tf_op jit(solution)/shard_map/ppermute | solution.py:447
  13.5 6.6 %collective-permute-start.1 = (bf16[528,128]{1,0:T(8,128)(2,1)S(1)}, bf16[528,128]{1,0:T(8,128)(2,1)S(1)}, u32[]{:S(2)}, u32[]{:S(2)}) collective-permute-start(bf16[528,128]{1,0:T(8,128)(2,1)S(1)} %pair.2.after_ref), channel_id=1, source_target_pairs={{0,8},{4,12},{8,0},{12,4},{16,24},{20,28},{24,16},{28,20},{1,9},{5... | collective-permute-start | bytes 405512 | tf_op jit(solution)/shard_map/ppermute | solution.py:447
  16.7 8.5 %collective-permute-start.7 = (bf16[128,1024]{1,0:T(8,128)(2,1)S(1)}, bf16[128,1024]{1,0:T(8,128)(2,1)S(1)}, u32[]{:S(2)}, u32[]{:S(2)}) collective-permute-start(bf16[128,1024]{1,0:T(8,128)(2,1)S(1)} %pass_on.1.refs_2_), channel_id=1, source_target_pairs={{0,1},{1,0},{2,3},{3,2},{4,5},{5,4},{6,7},{7,6},{8,9},{9,8},{10,11... | collective-permute-start | bytes 786440 | tf_op jit(solution)/shard_map/ppermute | solution.py:486
  18.5 3.5 %copy-start.4 = (f32[8]{0:T(128)S(1)}, f32[8]{0:T(128)}, u32[]{:S(2)}) copy-start(f32[8]{0:T(128)} %gate_ref.3) | copy-start | bytes 100
  20.6 1.4 %collective-permute-start.5 = (bf16[528,128]{1,0:T(8,128)(2,1)S(1)}, bf16[528,128]{1,0:T(8,128)(2,1)S(1)}, u32[]{:S(2)}, u32[]{:S(2)}) collective-permute-start(bf16[528,128]{1,0:T(8,128)(2,1)S(1)} %get-tuple-element.37), channel_id=1, source_target_pairs={{0,4},{4,0},{8,12},{12,8},{16,20},{20,16},{24,28},{28,24},{1,5},{5... | collective-permute-start | bytes 405512 | tf_op jit(solution)/shard_map/ppermute | solution.py:459
  23.6 9.2 %collective-permute-start.12 = (bf16[128,1024]{1,0:T(8,128)(2,1)S(1)}, bf16[128,1024]{1,0:T(8,128)(2,1)S(1)}, u32[]{:S(2)}, u32[]{:S(2)}) collective-permute-start(bf16[128,1024]{1,0:T(8,128)(2,1)S(1)} %get-tuple-element.51), channel_id=1, source_target_pairs={{0,1},{1,0},{2,3},{3,2},{4,5},{5,4},{6,7},{7,6},{8,9},{9,8},{10,11... | collective-permute-start | bytes 786440 | tf_op jit(solution)/shard_map/ppermute | solution.py:486
  26.5 2.1 %collective-permute-start.8 = (bf16[528,128]{1,0:T(8,128)(2,1)S(1)}, bf16[528,128]{1,0:T(8,128)(2,1)S(1)}, u32[]{:S(2)}, u32[]{:S(2)}) collective-permute-start(bf16[528,128]{1,0:T(8,128)(2,1)S(1)} %get-tuple-element.43), channel_id=1, source_target_pairs={{0,4},{4,0},{8,12},{12,8},{16,20},{20,16},{24,28},{28,24},{1,5},{5... | collective-permute-start | bytes 405512 | tf_op jit(solution)/shard_map/ppermute | solution.py:436
  27.3 16.0 %collective-permute-start.15 = (bf16[128,1024]{1,0:T(8,128)(2,1)S(1)}, bf16[128,1024]{1,0:T(8,128)(2,1)S(1)}, u32[]{:S(2)}, u32[]{:S(2)}) collective-permute-start(bf16[128,1024]{1,0:T(8,128)(2,1)S(1)} %get-tuple-element.45.refs_1_), channel_id=1, source_target_pairs={{0,1},{1,0},{2,3},{3,2},{4,5},{5,4},{6,7},{7,6},{8,9},{9,8},{10,11... | collective-permute-start | bytes 786440 | tf_op jit(solution)/shard_map/ppermute | solution.py:486
  28.7 9.2 %collective-permute-start.11 = (bf16[528,128]{1,0:T(8,128)(2,1)S(1)}, bf16[528,128]{1,0:T(8,128)(2,1)S(1)}, u32[]{:S(2)}, u32[]{:S(2)}) collective-permute-start(bf16[528,128]{1,0:T(8,128)(2,1)S(1)} %pair.3.after_ref), channel_id=1, source_target_pairs={{0,24},{4,28},{8,16},{12,20},{16,8},{20,12},{24,0},{28,4},{1,25},{... | collective-permute-start | bytes 405512 | tf_op jit(solution)/shard_map/ppermute | solution.py:447
  30.4 7.8 %collective-permute-start.10 = (bf16[528,128]{1,0:T(8,128)(2,1)S(1)}, bf16[528,128]{1,0:T(8,128)(2,1)S(1)}, u32[]{:S(2)}, u32[]{:S(2)}) collective-permute-start(bf16[528,128]{1,0:T(8,128)(2,1)S(1)} %pair.3.after_ref), channel_id=1, source_target_pairs={{0,16},{4,20},{8,24},{12,28},{16,0},{20,4},{24,8},{28,12},{1,17},{... | collective-permute-start | bytes 405512 | tf_op jit(solution)/shard_map/ppermute | solution.py:447
  31.7 6.5 %collective-permute-start.9 = (bf16[528,128]{1,0:T(8,128)(2,1)S(1)}, bf16[528,128]{1,0:T(8,128)(2,1)S(1)}, u32[]{:S(2)}, u32[]{:S(2)}) collective-permute-start(bf16[528,128]{1,0:T(8,128)(2,1)S(1)} %pair.3.after_ref), channel_id=1, source_target_pairs={{0,8},{4,12},{8,0},{12,4},{16,24},{20,28},{24,16},{28,20},{1,9},{5... | collective-permute-start | bytes 405512 | tf_op jit(solution)/shard_map/ppermute | solution.py:447
  33.3 11.5 %collective-permute-start.16 = (bf16[128,1024]{1,0:T(8,128)(2,1)S(1)}, bf16[128,1024]{1,0:T(8,128)(2,1)S(1)}, u32[]{:S(2)}, u32[]{:S(2)}) collective-permute-start(bf16[128,1024]{1,0:T(8,128)(2,1)S(1)} %project_add.1.refs_0_), channel_id=1, source_target_pairs={{0,3},{1,2},{2,1},{3,0},{4,7},{5,6},{6,5},{7,4},{8,11},{9,10},{10,... | collective-permute-start | bytes 786440 | tf_op jit(solution)/shard_map/ppermute | solution.py:486
  38.4 4.9 %collective-permute-start.13 = (bf16[272,128]{1,0:T(8,128)(2,1)S(1)}, bf16[272,128]{1,0:T(8,128)(2,1)S(1)}, u32[]{:S(2)}, u32[]{:S(2)}) collective-permute-start(bf16[272,128]{1,0:T(8,128)(2,1)S(1)} %get-tuple-element.55), channel_id=1, source_target_pairs={{0,4},{4,0},{8,12},{12,8},{16,20},{20,16},{24,28},{28,24},{1,5},{5... | collective-permute-start | bytes 208904 | tf_op jit(solution)/shard_map/ppermute | solution.py:459
  38.5 4.8 %collective-permute-start.14 = (bf16[272,128]{1,0:T(8,128)(2,1)S(1)}, bf16[272,128]{1,0:T(8,128)(2,1)S(1)}, u32[]{:S(2)}, u32[]{:S(2)}) collective-permute-start(bf16[272,128]{1,0:T(8,128)(2,1)S(1)} %get-tuple-element.56), channel_id=1, source_target_pairs={{0,4},{4,0},{8,12},{12,8},{16,20},{20,16},{24,28},{28,24},{1,5},{5... | collective-permute-start | bytes 208904 | tf_op jit(solution)/shard_map/ppermute | solution.py:459
